TPU v7x, 32 devices: a whole 2x2x4 slice. The times are simulated.
32 devices in a mesh: section: 4 (over z), dp: 8 (over y, x, core).
Axes of the slice: x: 2, y: 2, z: 4, core: 2. Of those that a mesh axis runs over, the one named last changes fastest.
Arguments:
- inputs: bfloat16 [4, 8, 256, 1024], P(None, 'dp'), may hold values from -8 to 8
- cotangent: bfloat16 [4, 8, 256, 1024], P(None, 'dp'), may hold values from -6 to 6
- w_qkv: bfloat16 [3, 1024, 2048], P(None, None, 'section'), may hold values from -0.1875 to 0.1875
- w_beta: bfloat16 [1024, 16], P(None, 'section'), may hold values from -0.1875 to 0.1875
- conv_taps: float32 [3, 4, 2048], P(None, None, 'section'), may hold values from -3 to 3
- w_out: bfloat16 [2048, 1024], P('section'), may hold values from -0.1875 to 0.1875
- w_gate_up: bfloat16 [2, 1024, 5632], P(None, None, 'section'), may hold values from -0.1875 to 0.1875
- w_down: bfloat16 [5632, 1024], P('section'), may hold values from -0.109375 to 0.109375
- norm_gains: float32 [2, 2048], P(None, 'section'), may hold values from 0.1 to 1.9
- out_gains: float32 [256], P('section'), may hold values from 0.1 to 1.9
Outputs:
- outputs: bfloat16 [4, 8, 256, 1024], P(None, 'dp', None, 'section')
- input_grad: bfloat16 [4, 8, 256, 1024], P(None, 'dp', None, 'section')
- grad_qkv: float32 [3, 1024, 2048], P(None, 'dp', 'section')
- grad_beta: float32 [1024, 16], P('dp', 'section')
- grad_taps: float32 [3, 4, 2048], P(None, None, ('section', 'dp'))
- grad_out: float32 [2048, 1024], P(('section', 'dp'))
- grad_gate_up: float32 [2, 1024, 5632], P(None, 'dp', 'section')
- grad_down: float32 [5632, 1024], P(('section', 'dp'))
- grad_norm_gains: float32 [2, 2048], P(None, ('section', 'dp'))
- grad_out_gains: float32 [256], P(('section', 'dp'))
All inputs are finite; a program needn't handle non-finite values.
Results may differ from a plain program's by a relative error of at most 0.024.
Values may be sent and summed in bfloat16 or wider, within the bound.
No kernel may reach another device: no remote copies, remote signals or barrier semaphores. Data moves between devices by JAX's collectives and lax.ppermute only.
A program may use at most 640 MiB of HBM per device.

v0:
```python
from functools import partial

import jax
import jax.numpy as jnp
from jax import lax
from jax.sharding import PartitionSpec as P

SPAN = 64


exact_matmul_setting = lax.Precision.HIGHEST


def from_partner(x, axis, bit):
    return lax.ppermute(x, axis, [(i, i ^ 1 << bit) for i in range(lax.axis_size(axis))])


def shifted(value, axis, steps):
    count = lax.axis_size(axis)
    first, last = (max(0, -steps), min(count, count - steps))
    return lax.ppermute(value, axis, [(source, source + steps) for source in range(first, last)])


def rms_norm(value, gain, epsilon):
    scale = lax.rsqrt(jnp.mean(value * value, axis=-1, keepdims=True) + epsilon)
    return value * scale * gain


def causal_conv(linear, taps):
    model_width = taps.shape[0]
    length = linear.shape[0]
    extended_by_zeroes = jnp.pad(linear, ((model_width - 1, 0), (0, 0)))
    total = extended_by_zeroes[0:length] * taps[0]
    for offset in range(1, model_width):
        total = total + extended_by_zeroes[offset : offset + length] * taps[offset]
    return total


def unit_rows(value, heads):
    shaped = value.reshape(value.shape[0], heads, -1)
    return shaped * lax.rsqrt(jnp.sum(shaped * shaped, axis=-1, keepdims=True) + 1e-06)


def delta_block(carried_memory_matrix, pieces):
    query_rows, lookup_vector_entries, values, betas = pieces
    size = lookup_vector_entries.shape[1]
    lower = jnp.tril(jnp.ones((size, size), jnp.float32), -1)
    identity = jnp.eye(size, dtype=jnp.float32)
    inner = jnp.einsum(
        "hck,hdk->hcd", lookup_vector_entries, lookup_vector_entries, precision=exact_matmul_setting
    )
    system = identity + betas[:, :, None] * inner * lower
    right = betas[:, :, None] * jnp.concatenate([values, lookup_vector_entries], axis=-1)
    triangular_result = jax.scipy.linalg.solve_triangular(
        system, right, lower=True, unit_diagonal=True
    )
    model_width = values.shape[-1]
    latest_content_vector = triangular_result[..., :model_width] - jnp.einsum(
        "ywj,yje->ywe",
        triangular_result[..., model_width:],
        carried_memory_matrix,
        precision=exact_matmul_setting,
    )
    scores = jnp.einsum(
        "hck,hdk->hcd", query_rows, lookup_vector_entries, precision=exact_matmul_setting
    ) * (lower + identity)
    outputs = jnp.einsum(
        "ywj,yje->ywe", query_rows, carried_memory_matrix, precision=exact_matmul_setting
    )
    outputs = outputs + jnp.einsum(
        "hcd,hdv->hcv", scores, latest_content_vector, precision=exact_matmul_setting
    )
    carried_memory_matrix = carried_memory_matrix + jnp.einsum(
        "elp,elk->epk", lookup_vector_entries, latest_content_vector, precision=exact_matmul_setting
    )
    return (carried_memory_matrix, outputs)


def arrange(value, block):
    length, heads = (value.shape[0], value.shape[1])
    return jnp.swapaxes(value.reshape(length // block, block, heads, -1), 1, 2)


def restore(value):
    count, heads, block = (value.shape[0], value.shape[1], value.shape[2])
    return jnp.swapaxes(value, 1, 2).reshape(count * block, heads, -1)


def rounded(value):
    return lax.optimization_barrier(value.astype(jnp.bfloat16)).astype(jnp.float32)


def activate(linear, beta_linear, taps):
    heads = beta_linear.shape[1]
    active = jax.nn.silu(jnp.stack([causal_conv(linear[which], taps[which]) for which in range(3)]))
    query_rows = unit_rows(active[0], heads)
    lookup_vector_entries = unit_rows(active[1], heads)
    values = active[2].reshape(active.shape[1], heads, -1)
    return (query_rows, lookup_vector_entries, values, jax.nn.sigmoid(beta_linear))


def head_norm(outputs, gain):
    return rms_norm(outputs, gain, 1e-05)


def swiglu(gate, expansion_branch_output):
    return jax.nn.silu(gate) * expansion_branch_output


def kernel_pieces(query_rows, lookup_vector_entries, values, betas, block):
    return (
        arrange(rounded(query_rows), block),
        arrange(rounded(lookup_vector_entries), block),
        arrange(rounded(values), block),
        arrange(betas[..., None], block)[..., 0],
    )


def delta_forward(pieces):
    heads, model_width = (pieces[0].shape[1], pieces[0].shape[3])

    def advance(carried_memory_matrix, piece):
        new_state, outputs = delta_block(carried_memory_matrix, piece)
        return (new_state, (outputs, carried_memory_matrix))

    final_state, (outputs, states) = lax.scan(
        advance, jnp.zeros((heads, model_width, model_width), jnp.float32), pieces
    )
    return (outputs, states)


def delta_backward(pieces, states, output_grads):

    def retreat(state_grad, item):
        piece, carried_memory_matrix, grad = item
        unused, pullback = jax.vjp(delta_block, carried_memory_matrix, piece)
        previous_grad, piece_grads = pullback((state_grad, grad))
        return (previous_grad, piece_grads)

    start = jnp.zeros_like(states[0])
    first_grad, piece_grads = lax.scan(retreat, start, (pieces, states, output_grads), reverse=True)
    return piece_grads


def contract_rows(left, right):
    return lax.dot_general(
        left, right, (((0,), (0,)), ((), ())), preferred_element_type=jnp.float32
    )


def contract_cols(left, right):
    return lax.dot_general(
        left, right, (((1,), (1,)), ((), ())), preferred_element_type=jnp.float32
    )


def mixer_front(stream, gain, w_qkv, w_beta, taps, out_gain, w_out, block):
    normed = rms_norm(stream, gain, 1e-06).astype(jnp.bfloat16)
    linear = jnp.einsum("td,idc->itc", normed, w_qkv, preferred_element_type=jnp.float32)
    beta_linear = jnp.dot(normed, w_beta, preferred_element_type=jnp.float32)
    query_rows, lookup_vector_entries, values, betas = activate(linear, beta_linear, taps)
    pieces = kernel_pieces(query_rows, lookup_vector_entries, values, betas, block)
    outputs, states = delta_forward(pieces)
    outputs = restore(outputs)
    normed_out = head_norm(outputs, out_gain).astype(jnp.bfloat16).reshape(stream.shape[0], -1)
    share = jnp.dot(normed_out, w_out, preferred_element_type=jnp.float32)
    return (share, states, outputs)


def mixer_back(stream, states, outputs, branch, gain, w_qkv, w_beta, taps, out_gain, w_out, block):
    length = stream.shape[0]
    normed = rms_norm(stream, gain, 1e-06).astype(jnp.bfloat16)
    linear = jnp.einsum("td,idc->itc", normed, w_qkv, preferred_element_type=jnp.float32)
    beta_linear = jnp.dot(normed, w_beta, preferred_element_type=jnp.float32)
    activated, activate_pull = jax.vjp(activate, linear, beta_linear, taps)
    pieces = kernel_pieces(activated[0], activated[1], activated[2], activated[3], block)
    head_value, head_pull = jax.vjp(head_norm, outputs, out_gain)
    normed_out = head_value.astype(jnp.bfloat16).reshape(length, -1)
    out_weight_grad = contract_rows(normed_out, branch)
    normed_out_grad = contract_cols(branch, w_out)
    outputs_grad, out_gain_grad = head_pull(normed_out_grad.reshape(outputs.shape))
    piece_grads = delta_backward(pieces, states, arrange(outputs_grad, block))
    query_grad = restore(piece_grads[0])
    key_grad = restore(piece_grads[1])
    value_grad = restore(piece_grads[2])
    beta_grad = restore(piece_grads[3][..., None])[..., 0]
    linear_grad, strength_projection_derivative, taps_grad = activate_pull(
        (query_grad, key_grad, value_grad, beta_grad)
    )
    linear_low = linear_grad.astype(jnp.bfloat16)
    beta_low = strength_projection_derivative.astype(jnp.bfloat16)
    qkv_grad = jnp.einsum("td,itc->idc", normed, linear_low, preferred_element_type=jnp.float32)
    beta_weight_grad = contract_rows(normed, beta_low)
    normed_grad = jnp.einsum("itc,idc->td", linear_low, w_qkv, preferred_element_type=jnp.float32)
    normed_grad = normed_grad + contract_cols(beta_low, w_beta)
    return (normed_grad, (qkv_grad, beta_weight_grad, taps_grad, out_weight_grad), out_gain_grad)


def feed_front(middle, gain, w_gate_up, w_down):
    normed = rms_norm(middle, gain, 1e-06).astype(jnp.bfloat16)
    lifted = jnp.einsum("td,idf->itf", normed, w_gate_up, preferred_element_type=jnp.float32)
    hidden = swiglu(lifted[0], lifted[1]).astype(jnp.bfloat16)
    return (jnp.dot(hidden, w_down, preferred_element_type=jnp.float32), lifted)


def feed_back(middle, lifted, branch, gain, w_gate_up, w_down):
    normed = rms_norm(middle, gain, 1e-06).astype(jnp.bfloat16)
    hidden_value, swiglu_pull = jax.vjp(swiglu, lifted[0], lifted[1])
    hidden = hidden_value.astype(jnp.bfloat16)
    down_grad = contract_rows(hidden, branch)
    inner_layer_derivative = contract_cols(branch, w_down)
    gate_grad, up_grad = swiglu_pull(inner_layer_derivative)
    lifted_low = jnp.stack([gate_grad, up_grad]).astype(jnp.bfloat16)
    gate_up_grad = jnp.einsum("td,itf->idf", normed, lifted_low, preferred_element_type=jnp.float32)
    normed_grad = jnp.einsum(
        "itf,idf->td", lifted_low, w_gate_up, preferred_element_type=jnp.float32
    )
    return (normed_grad, (gate_up_grad, down_grad))


def norm_back(stream, gain, normed_grad):
    unused, pullback = jax.vjp(partial(rms_norm, epsilon=1e-06), stream, gain)
    return pullback(normed_grad)


def when_valid(valid, function, *operands):

    def nothing(*ignored):
        return jax.tree.map(jnp.zeros_like, function(*ignored))

    return lax.cond(valid, function, nothing, *operands)


def store(buffer, value, index, valid):
    previous = lax.dynamic_index_in_dim(buffer, index, 0, keepdims=False)
    return lax.dynamic_update_index_in_dim(buffer, jnp.where(valid, value, previous), index, 0)


def pick(buffer, index):
    return lax.dynamic_index_in_dim(buffer, index, 0, keepdims=False)


def local(
    inputs, cotangent, w_qkv, w_beta, conv_taps, w_out, w_gate_up, w_down, norm_gains, out_gains
):
    batches = inputs.shape[0]
    length = inputs.shape[2]
    model_width = inputs.shape[3]
    block = SPAN
    heads = w_beta.shape[1]
    head_size = out_gains.shape[0] * 2
    place = lax.axis_index("section")
    rank = place // 2
    half = place % 2
    first = half == 0
    other_gains, other_out = from_partner((norm_gains, out_gains), "section", 0)
    gains = jnp.where(
        first,
        jnp.concatenate([norm_gains, other_gains], 1),
        jnp.concatenate([other_gains, norm_gains], 1),
    )
    out_gain = jnp.where(
        first, jnp.concatenate([out_gains, other_out]), jnp.concatenate([other_out, out_gains])
    )

    def own_half(vector):
        size = vector.shape[0] // 2
        return lax.dynamic_slice_in_dim(vector, half * size, size, 0)

    def pair_total(share):
        return share + from_partner(share, "section", 0)

    def mixer_part(stream):
        return mixer_front(stream, gains[0], w_qkv, w_beta, conv_taps, out_gain, w_out, block)

    def feed_part(middle):
        return feed_front(middle, gains[1], w_gate_up, w_down)

    def feed_piece(middle, lifted, branch):
        return feed_back(middle, lifted, branch, gains[1], w_gate_up, w_down)

    def mixer_piece(stream, states, outputs, branch):
        return mixer_back(
            stream,
            states,
            outputs,
            branch,
            gains[0],
            w_qkv,
            w_beta,
            conv_taps,
            out_gain,
            w_out,
            block,
        )

    count = length // block
    units = w_down.shape[0]
    kept_in = jnp.zeros((batches, length, model_width), jnp.float32)
    kept_mid = jnp.zeros((batches, length, model_width), jnp.float32)
    kept_states = jnp.zeros((batches, count, heads, head_size, head_size), jnp.float32)
    kept_out = jnp.zeros((batches, length, heads, head_size), jnp.float32)
    kept_lift = jnp.zeros((batches, 2, length, units), jnp.float32)
    results = jnp.zeros((batches, length, model_width), jnp.float32)
    arrived = jnp.zeros((length, model_width), jnp.bfloat16)
    ticks = batches + 1
    for tick in range(ticks):
        batch = tick - rank
        valid = (batch >= 0) & (batch < batches)
        index = jnp.clip(batch, 0, batches - 1)
        own = pick(inputs, index)[0]
        stream = jnp.where(rank == 0, own, arrived).astype(jnp.float32)
        share, states, outputs = when_valid(valid, mixer_part, stream)
        middle = stream + pair_total(share)
        share, lifted = when_valid(valid, feed_part, middle)
        result = middle + pair_total(share)
        kept_in = store(kept_in, stream, index, valid)
        kept_mid = store(kept_mid, middle, index, valid)
        kept_states = store(kept_states, states, index, valid)
        kept_out = store(kept_out, outputs, index, valid)
        kept_lift = store(kept_lift, lifted, index, valid)
        results = store(results, result, index, valid)
        if tick + 1 < ticks:
            arrived = shifted(result.astype(jnp.bfloat16), "section", 2)
    feed_acc = (jnp.zeros(w_gate_up.shape, jnp.float32), jnp.zeros(w_down.shape, jnp.float32))
    mixer_acc = (
        jnp.zeros(w_qkv.shape, jnp.float32),
        jnp.zeros(w_beta.shape, jnp.float32),
        jnp.zeros(conv_taps.shape, jnp.float32),
        jnp.zeros(w_out.shape, jnp.float32),
    )
    mix_gain_acc = jnp.zeros((model_width,), jnp.float32)
    feed_gain_acc = jnp.zeros((model_width,), jnp.float32)
    out_gain_acc = jnp.zeros((head_size,), jnp.float32)
    input_grads = jnp.zeros((batches, length, model_width), jnp.float32)
    returned = jnp.zeros((length, model_width), jnp.bfloat16)
    for tick in range(ticks):
        batch = tick - 1 + rank
        valid = (batch >= 0) & (batch < batches)
        index = jnp.clip(batch, 0, batches - 1)
        own_grad = pick(cotangent, index)[0]
        grad_out = jnp.where(rank == 1, own_grad, returned).astype(jnp.float32)
        stream = pick(kept_in, index)
        middle = pick(kept_mid, index)
        normed_share, feed_grads = when_valid(
            valid, feed_piece, middle, pick(kept_lift, index), grad_out.astype(jnp.bfloat16)
        )
        feed_acc = jax.tree.map(jnp.add, feed_acc, feed_grads)
        normed_grad = normed_share + from_partner(
            normed_share.astype(jnp.bfloat16), "section", 0
        ).astype(normed_share.dtype)
        middle_norm_grad, feed_gain_grad = norm_back(middle, gains[1], normed_grad)
        middle_grad = grad_out + middle_norm_grad
        feed_gain_acc = feed_gain_acc + jnp.where(valid, feed_gain_grad, 0.0)
        normed_share, mixer_grads, out_gain_share = when_valid(
            valid,
            mixer_piece,
            stream,
            pick(kept_states, index),
            pick(kept_out, index),
            middle_grad.astype(jnp.bfloat16),
        )
        mixer_acc = jax.tree.map(jnp.add, mixer_acc, mixer_grads)
        other_share, other_out_grad = (
            from_partner(normed_share.astype(jnp.bfloat16), "section", 0).astype(
                normed_share.dtype
            ),
            from_partner(out_gain_share.astype(jnp.bfloat16), "section", 0).astype(
                out_gain_share.dtype
            ),
        )
        normed_grad = normed_share + other_share
        out_gain_acc = out_gain_acc + out_gain_share + other_out_grad
        stream_norm_grad, mix_gain_grad = norm_back(stream, gains[0], normed_grad)
        mix_gain_acc = mix_gain_acc + jnp.where(valid, mix_gain_grad, 0.0)
        stream_grad = middle_grad + stream_norm_grad
        input_grads = store(input_grads, stream_grad, index, valid)
        if tick + 1 < ticks:
            returned = shifted(stream_grad.astype(jnp.bfloat16), "section", -2)
    summed = (
        lax.psum_scatter(mixer_acc[0], "dp", scatter_dimension=1, tiled=True),
        lax.psum_scatter(mixer_acc[1], "dp", scatter_dimension=0, tiled=True),
        lax.psum_scatter(mixer_acc[2], "dp", scatter_dimension=2, tiled=True),
        lax.psum_scatter(mixer_acc[3], "dp", scatter_dimension=0, tiled=True),
        lax.psum_scatter(feed_acc[0], "dp", scatter_dimension=1, tiled=True),
        lax.psum_scatter(feed_acc[1], "dp", scatter_dimension=0, tiled=True),
        lax.psum_scatter(
            jnp.stack([own_half(mix_gain_acc), own_half(feed_gain_acc)]),
            "dp",
            scatter_dimension=1,
            tiled=True,
        ),
        lax.psum_scatter(own_half(out_gain_acc), "dp", scatter_dimension=0, tiled=True),
    )
    (
        grad_qkv,
        grad_beta,
        grad_taps,
        grad_out,
        grad_gate_up,
        grad_down,
        grad_norm_gains,
        grad_out_gains,
    ) = summed
    held = jnp.where(rank == 1, results, input_grads).astype(jnp.bfloat16)
    quarter = model_width // lax.axis_size("section")
    partner = (place + 2) % 4
    sent = lax.dynamic_slice_in_dim(held, partner * quarter, quarter, 2)
    kept = lax.dynamic_slice_in_dim(held, place * quarter, quarter, 2)
    came = from_partner(sent, "section", 1)
    final_stream = jnp.where(rank == 1, kept, came)[:, None]
    final_grad = jnp.where(rank == 0, kept, came)[:, None]
    return (
        final_stream,
        final_grad,
        grad_qkv,
        grad_beta,
        grad_taps,
        grad_out,
        grad_gate_up,
        grad_down,
        grad_norm_gains,
        grad_out_gains,
    )


def solution(mesh):
    in_specs = (
        P(None, "dp", None, None),
        P(None, "dp", None, None),
        P(None, None, "section"),
        P(None, "section"),
        P(None, None, "section"),
        P("section", None),
        P(None, None, "section"),
        P("section", None),
        P(None, "section"),
        P("section"),
    )
    out_specs = (
        P(None, "dp", None, "section"),
        P(None, "dp", None, "section"),
        P(None, "dp", "section"),
        P("dp", "section"),
        P(None, None, ("section", "dp")),
        P(("section", "dp"), None),
        P(None, "dp", "section"),
        P(("section", "dp"), None),
        P(None, ("section", "dp")),
        P(("section", "dp")),
    )
    return jax.shard_map(local, mesh=mesh, in_specs=in_specs, out_specs=out_specs, check_vma=False)
```

profile of v0, /device:TPU:0, one launch (start us, length us, event | category | flops | bytes accessed | tf_op | source)
XLA Modules:
  0.0 3018.8 jit_solution(3894502078500136788)
XLA Ops:
  14.7 116.9 %conditional.20 = (f32[256,1024]{1,0:T(8,128)}, f32[4,4,128,128]{3,2,1,0:T(8,128)}, f32[256,4,128]{2,0,1:T(8,128)}) conditional(s32[]{:T(128)} %convert_element_type.839, () %tuple.360, (f32[256,1024]{1,0:T(8,128)S(1)}, f32[2,1024]{1,0:T(2,128)S(1)}, bf16[3,1024,512]{2,1,0:T(8,128)(2,1)}, f32[3,4,512]{2,1,0:T(4,128)S(1)}, ...), branch_computations={%region_0.1_spmd, %region_1.9_spmd} | conditional | flops 1362637056 | bytes 50303052 | solution.py:231
  26.6 99.9 %while.230 = (s32[]{:T(128)}, f32[4,128,128]{2,1,0:T(8,128)S(1)}, f32[4,4,64,128]{3,2,1,0:T(8,128)}, f32[4,4,128,128]{3,2,1,0:T(8,128)}, f32[4,4,64,128]{3,2,0,1...) while((s32[]{:T(128)}, f32[4,128,128]{2,1,0:T(8,128)S(1)}, ...), condition=%wide.region_6.7_spmd.clone, body=%wide.region_5.6_spmd.clone.sunk | while | flops 277487680 | bytes 5273993 | solution.py:126
  28.1 19.7 custom-call.75
  53.1 19.7 custom-call.75
  78.1 19.7 custom-call.75
  103.0 19.7 custom-call.75
  131.8 23.5 collective-permute-done.2
  167.8 22.1 collective-permute-done.3
  203.2 137.5 %conditional.22 = (f32[256,1024]{1,0:T(8,128)}, f32[4,4,128,128]{3,2,1,0:T(8,128)}, f32[256,4,128]{2,0,1:T(8,128)}) conditional(s32[]{:T(128)} %convert_element_type.842, () %tuple.364, (f32[256,1024]{1,0:T(8,128)S(1)}, f32[2,1024]{1,0:T(2,128)S(1)}, bf16[3,1024,512]{2,1,0:T(8,128)(2,1)}, f32[3,4,512]{2,1,0:T(4,128)S(1)}, ...), branch_computations={%region_11.13_spmd, %region_12.20_spmd} | conditional | flops 1362637056 | bytes 48189488 | solution.py:231
  217.7 107.4 %while.231 = (s32[]{:T(128)}, f32[4,128,128]{2,1,0:T(8,128)S(1)}, f32[4,4,64,128]{3,2,1,0:T(8,128)}, f32[4,4,128,128]{3,2,1,0:T(8,128)}, f32[4,4,64,128]{3,2,0,1...) while((s32[]{:T(128)}, f32[4,128,128]{2,1,0:T(8,128)S(1)}, ...), condition=%wide.region_17.18_spmd.clone, body=%wide.region_16.17_spmd.clone.sunk | while | flops 277487680 | bytes 5257609 | solution.py:126
  219.2 19.7 custom-call.74
  246.1 19.7 custom-call.74
  273.0 19.7 custom-call.74
  299.8 19.7 custom-call.74
  354.3 21.7 collective-permute-done.5
  393.4 18.6 collective-permute-done.6
  430.4 126.9 %conditional.24 = (f32[256,1024]{1,0:T(8,128)}, f32[4,4,128,128]{3,2,1,0:T(8,128)}, f32[256,4,128]{2,0,1:T(8,128)}) conditional(s32[]{:T(128)} %convert_element_type.845, () %tuple.368, (f32[256,1024]{1,0:T(8,128)S(1)}, f32[2,1024]{1,0:T(2,128)S(1)}, bf16[3,1024,512]{2,1,0:T(8,128)(2,1)}, f32[3,4,512]{2,1,0:T(4,128)S(1)}, ...), branch_computations={%region_22.24_spmd, %region_23.31_spmd} | conditional | flops 1362637056 | bytes 48189488 | solution.py:231
  444.9 107.4 %while.232 = (s32[]{:T(128)}, f32[4,128,128]{2,1,0:T(8,128)S(1)}, f32[4,4,64,128]{3,2,1,0:T(8,128)}, f32[4,4,128,128]{3,2,1,0:T(8,128)}, f32[4,4,64,128]{3,2,0,1...) while((s32[]{:T(128)}, f32[4,128,128]{2,1,0:T(8,128)S(1)}, ...), condition=%wide.region_28.29_spmd.clone, body=%wide.region_27.28_spmd.clone.sunk | while | flops 277487680 | bytes 5257609 | solution.py:126
  446.4 19.7 custom-call.73
  473.3 19.7 custom-call.73
  500.1 19.7 custom-call.73
  527.0 19.7 custom-call.73
  644.5 126.9 %conditional.26 = (f32[256,1024]{1,0:T(8,128)}, f32[4,4,128,128]{3,2,1,0:T(8,128)}, f32[256,4,128]{2,0,1:T(8,128)}) conditional(s32[]{:T(128)} %convert_element_type.848, () %tuple.372, (f32[256,1024]{1,0:T(8,128)S(1)}, f32[2,1024]{1,0:T(2,128)S(1)}, bf16[3,1024,512]{2,1,0:T(8,128)(2,1)}, f32[3,4,512]{2,1,0:T(4,128)S(1)}, ...), branch_computations={%region_33.35_spmd, %region_34.42_spmd} | conditional | flops 1362637056 | bytes 48189488 | solution.py:231
  659.0 107.4 %while.233 = (s32[]{:T(128)}, f32[4,128,128]{2,1,0:T(8,128)S(1)}, f32[4,4,64,128]{3,2,1,0:T(8,128)}, f32[4,4,128,128]{3,2,1,0:T(8,128)}, f32[4,4,64,128]{3,2,0,1...) while((s32[]{:T(128)}, f32[4,128,128]{2,1,0:T(8,128)S(1)}, ...), condition=%wide.region_39.40_spmd.clone, body=%wide.region_38.39_spmd.clone.sunk | while | flops 277487680 | bytes 5257609 | solution.py:126
  660.5 19.7 custom-call.72
  687.4 19.7 custom-call.72
  714.2 19.7 custom-call.72
  741.1 19.7 custom-call.72
  971.8 384.9 %collective-permute-done.18 = bf16[256,1024]{1,0:T(8,128)(2,1)} collective-permute-done((bf16[256,1024]{1,0:T(8,128)(2,1)}, bf16[256,1024]{1,0:T(8,128)(2,1)}, u32[]{:S(2)}, u32[]{:S(2)}) %collective-permute-start.18) | collective-permute-done | bytes 524320 | tf_op jit(solution)/shard_map/ppermute | solution.py:21
  1358.7 30.8 %conditional.32 = (f32[256,1024]{1,0:T(8,128)}, f32[1408,1024]{1,0:T(8,128)}, f32[2,1024,1408]{2,1,0:T(8,128)}) conditional(s32[]{:T(128)} %convert_element_type.862, () %tuple.384, (bf16[256,1024]{1,0:T(8,128)(2,1)}, bf16[1408,1024]{1,0:T(8,128)(2,1)}, f32[4,2,256,1408]{3,2,1,0:T(8,128)}, s32[]{:T(128)}, bf16[2,1024,1408]{2,1,0:T(8,128)(2,1)}, ...), branch_computations={%region_89.92_spmd, %region_90.94_spmd} | conditional | flops 4439146496 | bytes 88490600 | solution.py:231
  1409.6 236.2 %conditional.33 = (f32[256,1024]{1,0:T(8,128)}, f32[1024,4]{0,1:T(4,128)S(1)}, f32[3,4,512]{2,1,0:T(4,128)S(1)}, f32[512,1024]{1,0:T(8,128)}, f32[128]{0:T(128)}, /*index=5*/f32[3,1024,512]{2,1,0:T(8,128)}) conditional(s32[]{:T(128)} %convert_element_type.862, () %tuple.386, (f32[256,1024]{1,0:T(8,128)S(1)}, f32[2,1024]{1,0:T(2,128)S(1)}, ...), branch_computations={%region_94.97_spmd, %region_95.123_spmd} | conditional | flops 3702932480 | bytes 236043504 | solution.py:231
  1440.9 150.6 %while.236 = (s32[]{:T(128)}, f32[4,128,128]{2,1,0:T(8,128)S(1)}, f32[4,4,64,128]{3,2,1,0:T(8,128)}, f32[4,4,64,128]{3,2,1,0:T(8,128)}, f32[4,4,64,128]{3,2,1,0:...) while((s32[]{:T(128)}, f32[4,128,128]{2,1,0:T(8,128)S(1)}, ...), condition=%wide.region_104.106_spmd.clone, body=%wide.region_101.105_spmd.clone.sunk | while | flops 718643008 | bytes 15725556 | solution.py:141
  1444.2 19.7 custom-call.69
  1481.7 19.7 custom-call.69
  1519.3 19.7 custom-call.69
  1556.8 19.7 custom-call.69
  1666.3 24.8 collective-permute-done.21
  1693.1 29.6 conditional.34
  1740.7 236.0 %conditional.35 = (f32[256,1024]{1,0:T(8,128)}, f32[1024,4]{0,1:T(4,128)S(1)}, f32[3,4,512]{2,1,0:T(4,128)S(1)}, f32[512,1024]{1,0:T(8,128)}, f32[128]{0:T(128)}, /*index=5*/f32[3,1024,512]{2,1,0:T(8,128)}) conditional(s32[]{:T(128)} %convert_element_type.870, () %tuple.390, (f32[256,1024]{1,0:T(8,128)S(1)}, f32[2,1024]{1,0:T(2,128)S(1)}, ...), branch_computations={%region_128.131_spmd, %region_129.157_spmd} | conditional | flops 3702932480 | bytes 236043504 | solution.py:231
  1772.0 150.5 %while.237 = (s32[]{:T(128)}, f32[4,128,128]{2,1,0:T(8,128)S(1)}, f32[4,4,64,128]{3,2,1,0:T(8,128)}, f32[4,4,64,128]{3,2,1,0:T(8,128)}, f32[4,4,64,128]{3,2,1,0:...) while((s32[]{:T(128)}, f32[4,128,128]{2,1,0:T(8,128)S(1)}, ...), condition=%wide.region_138.140_spmd.clone, body=%wide.region_135.139_spmd.clone.sunk | while | flops 718643008 | bytes 15725556 | solution.py:141
  1775.2 19.7 custom-call.68
  1812.8 19.7 custom-call.68
  1850.3 19.7 custom-call.68
  1887.8 19.7 custom-call.68
  1997.0 24.5 collective-permute-done.24
  2023.4 29.6 conditional.36
  2071.0 234.1 %conditional.37 = (f32[256,1024]{1,0:T(8,128)}, f32[1024,4]{0,1:T(4,128)S(1)}, f32[3,4,512]{2,1,0:T(4,128)S(1)}, f32[512,1024]{1,0:T(8,128)}, f32[128]{0:T(128)}, /*index=5*/f32[3,1024,512]{2,1,0:T(8,128)}) conditional(s32[]{:T(128)} %convert_element_type.878, () %tuple.394, (f32[256,1024]{1,0:T(8,128)S(1)}, f32[2,1024]{1,0:T(2,128)S(1)}, ...), branch_computations={%region_162.165_spmd, %region_163.191_spmd} | conditional | flops 3702932480 | bytes 235947024 | solution.py:231
  2102.4 148.3 %while.238 = (s32[]{:T(128)}, f32[4,128,128]{2,1,0:T(8,128)S(1)}, f32[4,4,64,128]{3,2,1,0:T(8,128)}, f32[4,4,64,128]{3,2,1,0:T(8,128)}, f32[4,4,64,128]{3,2,1,0:...) while((s32[]{:T(128)}, f32[4,128,128]{2,1,0:T(8,128)S(1)}, ...), condition=%wide.region_172.174_spmd.clone, body=%wide.region_169.173_spmd.clone.sunk | while | flops 718643008 | bytes 15727604 | solution.py:141
  2105.7 19.7 custom-call.67
  2142.7 19.7 custom-call.67
  2179.6 19.7 custom-call.67
  2216.6 19.7 custom-call.67
  2325.2 24.3 collective-permute-done.27
  2351.4 29.7 conditional.38
  2400.8 236.7 %conditional.39 = (f32[256,1024]{1,0:T(8,128)S(1)}, f32[1024,4]{0,1:T(4,128)}, f32[3,4,512]{2,1,0:T(4,128)}, f32[512,1024]{1,0:T(8,128)}, f32[128]{0:T(128)}, /*index=5*/f32[3,1024,512]{2,1,0:T(8,128)}) conditional(s32[]{:T(128)} %convert_element_type.886, () %tuple.398, (f32[256,1024]{1,0:T(8,128)S(1)}, f32[2,1024]{1,0:T(2,128)S(1)}, ...), branch_computations={%region_196.199_spmd, %region_197.225_spmd} | conditional | flops 3702932480 | bytes 236289520 | solution.py:231
  2428.5 164.0 %while.239 = (s32[]{:T(128)}, f32[4,128,128]{2,1,0:T(8,128)}, f32[4,4,64,128]{3,2,1,0:T(8,128)}, f32[4,4,64,128]{3,2,1,0:T(8,128)}, f32[4,4,64,128]{3,2,1,0:T(8,...) while((s32[]{:T(128)}, f32[4,128,128]{2,1,0:T(8,128)}, ...), condition=%wide.region_206.208_spmd.clone, body=%wide.region_203.207_spmd.clone.sunk | while | flops 718643008 | bytes 11777124 | solution.py:141
  2434.4 19.6 custom-call.66
  2475.3 19.6 custom-call.66
  2516.2 19.6 custom-call.66
  2557.1 19.6 custom-call.66
  2690.1 23.1 add_add_fusion.15
  2792.0 62.9 %reduce-scatter.20.cloned.1.call-done = f32[176,1024]{1,0:T(8,128)} async-done(((f32[1408,1024]{1,0:T(8,128)}), f32[176,1024]{1,0:T(8,128)}) %reduce-scatter.20.cloned.1.call-update) | async-done | bytes 720912 | tf_op jit(solution)/shard_map/reduce_scatter | solution.py:386
  2854.9 66.0 %reduce-scatter.14.cloned.1.call-done = f32[3,128,512]{2,1,0:T(8,128)} async-done(((f32[3,1024,512]{2,1,0:T(8,128)}), f32[3,128,512]{2,1,0:T(8,128)}) %reduce-scatter.14.cloned.1.call-update) | async-done | bytes 786448 | tf_op jit(solution)/shard_map/reduce_scatter | solution.py:381
  2920.9 90.9 %reduce-scatter.18.cloned.1.call-done = f32[2,128,1408]{2,1,0:T(8,128)} async-done(((f32[2,1024,1408]{2,1,0:T(8,128)}), f32[2,128,1408]{2,1,0:T(8,128)}) %reduce-scatter.18.cloned.1.call-update) | async-done | bytes 1441808 | tf_op jit(solution)/shard_map/reduce_scatter | solution.py:385
  (2435 shorter events, 1612.9 us)
Async XLA Ops:
  7.2 2770.9 %reduce-scatter.22.cloned.1.call-start = ((), (), s32[]{:S(2)}) async-start(), calls=%async_computation.11 | async-start | bytes 589824
  7.3 7.4 collective-permute-start
  10.4 3.7 collective-permute-start.1
  131.5 23.7 collective-permute-start.2
  157.7 32.2 %copy-start.18 = (f32[256,1024]{1,0:T(8,128)}, f32[256,1024]{1,0:T(8,128)S(1)}, u32[]{:S(2)}) copy-start(f32[256,1024]{1,0:T(8,128)S(1)} %get-tuple-element.3866) | copy-start | bytes 3145732
  167.3 23.8 copy-start.54
  167.3 22.6 collective-permute-start.3
  191.0 9.8 collective-permute-start.4
  340.7 35.3 %collective-permute-start.5 = (f32[256,1024]{1,0:T(8,128)}, f32[256,1024]{1,0:T(8,128)S(1)}, u32[]{:S(2)}, u32[]{:S(2)}) collective-permute-start(f32[256,1024]{1,0:T(8,128)} %get-tuple-element.2363), channel_id=1, source_target_pairs={{0,8},{8,0},{16,24},{24,16},{1,9},{9,1},{17,25},{25,17},{2,10},{10... | collective-permute-start | bytes 3145736 | tf_op jit(solution)/shard_map/ppermute | solution.py:15
  354.3 24.4 copy-start.469
  378.7 33.4 %copy-start.20 = (f32[256,1024]{1,0:T(8,128)}, f32[256,1024]{1,0:T(8,128)S(1)}, u32[]{:S(2)}) copy-start(f32[256,1024]{1,0:T(8,128)S(1)} %get-tuple-element.3864) | copy-start | bytes 3145732
  387.9 24.2 copy-start.56
  387.9 24.2 collective-permute-start.6
  393.4 29.8 copy-start.13
  413.5 14.5 collective-permute-start.7
  557.3 35.4 %collective-permute-start.8 = (f32[256,1024]{1,0:T(8,128)}, f32[256,1024]{1,0:T(8,128)S(1)}, u32[]{:S(2)}, u32[]{:S(2)}) collective-permute-start(f32[256,1024]{1,0:T(8,128)} %get-tuple-element.2365), channel_id=1, source_target_pairs={{0,8},{8,0},{16,24},{24,16},{1,9},{9,1},{17,25},{25,17},{2,10},{10... | collective-permute-start | bytes 3145736 | tf_op jit(solution)/shard_map/ppermute | solution.py:15
  572.8 22.6 slice-start
  595.4 31.0 %copy-start.22 = (f32[256,1024]{1,0:T(8,128)}, f32[256,1024]{1,0:T(8,128)S(1)}, u32[]{:S(2)}) copy-start(f32[256,1024]{1,0:T(8,128)S(1)} %get-tuple-element.3862) | copy-start | bytes 3145732
  602.2 24.2 copy-start.58
  602.2 24.1 collective-permute-start.9
  627.4 14.7 collective-permute-start.10
  771.4 35.4 %collective-permute-start.11 = (f32[256,1024]{1,0:T(8,128)}, f32[256,1024]{1,0:T(8,128)S(1)}, u32[]{:S(2)}, u32[]{:S(2)}) collective-permute-start(f32[256,1024]{1,0:T(8,128)} %get-tuple-element.2367), channel_id=1, source_target_pairs={{0,8},{8,0},{16,24},{24,16},{1,9},{9,1},{17,25},{25,17},{2,10},{10... | collective-permute-start | bytes 3145736 | tf_op jit(solution)/shard_map/ppermute | solution.py:15
  809.5 30.8 %copy-start.24 = (f32[256,1024]{1,0:T(8,128)}, f32[256,1024]{1,0:T(8,128)S(1)}, u32[]{:S(2)}) copy-start(f32[256,1024]{1,0:T(8,128)S(1)} %get-tuple-element.3860) | copy-start | bytes 3145732
  816.2 24.1 copy-start.60
  816.2 24.1 collective-permute-start.12
  841.3 14.6 collective-permute-start.13
  861.9 35.5 %collective-permute-start.14 = (f32[256,1024]{1,0:T(8,128)}, f32[256,1024]{1,0:T(8,128)S(1)}, u32[]{:S(2)}, u32[]{:S(2)}) collective-permute-start(f32[256,1024]{1,0:T(8,128)} %get-tuple-element.2369), channel_id=1, source_target_pairs={{0,8},{8,0},{16,24},{24,16},{1,9},{9,1},{17,25},{25,17},{2,10},{10... | collective-permute-start | bytes 3145736 | tf_op jit(solution)/shard_map/ppermute | solution.py:15
  885.4 52.1 %copy-start.29 = (f32[256,1024]{1,0:T(8,128)}, f32[256,1024]{1,0:T(8,128)S(1)}, u32[]{:S(2)}) copy-start(f32[256,1024]{1,0:T(8,128)S(1)} %get-tuple-element.4244) | copy-start | bytes 3145732
  919.4 12.9 collective-permute-start.16
  953.5 12.0 collective-permute-start.17
  970.4 388.4 %copy-start.34 = (f32[256,1024]{1,0:T(8,128)S(1)}, f32[256,1024]{1,0:T(8,128)}, u32[]{:S(2)}) copy-start(f32[256,1024]{1,0:T(8,128)} %get-tuple-element.4250) | copy-start | bytes 3145732
  970.4 386.3 %collective-permute-start.18 = (bf16[256,1024]{1,0:T(8,128)(2,1)}, bf16[256,1024]{1,0:T(8,128)(2,1)}, u32[]{:S(2)}, u32[]{:S(2)}) collective-permute-start(bf16[256,1024]{1,0:T(8,128)(2,1)} %get-tuple-element.3841), channel_id=1, source_target_pairs={{16,0},{24,8},{17,1},{25,9},{18,2},{26,10},{19,3},{27,11},{20,4},{... | collective-permute-start | bytes 1572872 | tf_op jit(solution)/shard_map/ppermute | solution.py:21
  1390.9 13.8 collective-permute-start.19
  1647.1 12.9 collective-permute-start.20
  1664.9 28.1 copy-start.33
  1664.9 26.2 collective-permute-start.21
  1722.8 13.5 collective-permute-start.22
  1978.1 12.6 collective-permute-start.23
  1995.5 27.8 copy-start.32
  1995.5 25.9 collective-permute-start.24
  2053.1 13.5 collective-permute-start.25
  2071.6 20.8 copy-start.84
  2306.5 12.6 collective-permute-start.26
  2323.8 27.6 copy-start.31
  2323.8 25.7 collective-permute-start.27
  2382.1 13.7 collective-permute-start.28
  2433.0 21.5 copy-start.94
  2474.0 21.5 copy-start.94
  2514.9 21.5 copy-start.94
  2555.8 21.5 copy-start.94
  2638.5 12.8 collective-permute-start.29
  2640.6 139.0 %reduce-scatter.24.cloned.1.call-start = ((), (), s32[]{:S(2)}) async-start(), calls=%async_computation.12 | async-start | bytes 294912
  2643.1 138.1 %reduce-scatter.26.cloned.1.call-start = ((), (), s32[]{:S(2)}) async-start(), calls=%async_computation.13 | async-start | bytes 294912
  2653.8 138.2 %reduce-scatter.16.cloned.1.call-start = ((), (), s32[]{:S(2)}) async-start(), calls=%async_computation.8 | async-start | bytes 2359296 | tf_op jit(solution)/shard_map/reduce_scatter | solution.py:384
  2660.7 194.2 %reduce-scatter.20.cloned.1.call-start = ((), (), s32[]{:S(2)}) async-start(), calls=%async_computation.10 | async-start | bytes 6488064 | tf_op jit(solution)/shard_map/reduce_scatter | solution.py:386
  2674.9 246.0 %reduce-scatter.14.cloned.1.call-start = ((), (), s32[]{:S(2)}) async-start(), calls=%async_computation.7 | async-start | bytes 7077888 | tf_op jit(solution)/shard_map/reduce_scatter | solution.py:381
  2689.9 321.9 %reduce-scatter.18.cloned.1.call-start = ((), (), s32[]{:S(2)}) async-start(), calls=%async_computation.9 | async-start | bytes 12976128 | tf_op jit(solution)/shard_map/reduce_scatter | solution.py:385
  2719.0 22.8 collective-permute-start.15
  2751.8 30.8 %collective-permute-start.30 = (bf16[4,256,256]{2,1,0:T(8,128)(2,1)S(1)}, bf16[4,256,256]{2,1,0:T(8,128)(2,1)}, u32[]{:S(2)}, u32[]{:S(2)}) collective-permute-start(bf16[4,256,256]{2,1,0:T(8,128)(2,1)S(1)} %constant_dynamic-slice_fusion.10), channel_id=1, source_target_pairs={{0,16},{8,24},{16,0},{24,8},{1,17},{9,25},{17,1},{25,9},{2,18},{10... | collective-permute-start | bytes 1572872 | tf_op jit(solution)/shard_map/ppermute | solution.py:15
  2753.2 7.2 collective-permute-start.31
  2754.7 8.8 collective-permute-start.32
  2756.5 7.0 collective-permute-start.33
  2757.9 5.6 collective-permute-start.34
  2760.4 4.0 collective-permute-start.35
  (413 other events, 1522.0 us)
Sparse Core Ops, SparseCore 0:
  2640.7 31.6 reduce-scatter.21
  2675.7 33.5 reduce-scatter.23
  2713.0 33.6 reduce-scatter.25
  2750.7 41.2 reduce-scatter.15
  2795.8 59.0 reduce-scatter.19
  2859.1 61.7 reduce-scatter.13
  2925.0 86.7 reduce-scatter.17
where the time goes:
time: 3040 us; the launch traced here: 3020 us
  waiting for transfers between devices  990 us (33%)
  other arithmetic  966 us (32%)
  matrix products  503 us (17%)
  local copies, waits for them, and re-layouts  406 us (13%)
  starting transfers between devices  93.7 us (3%)
  loops' own time  30.8 us (1%)
    another operation x144, other arithmetic, delta_block(): jax.scipy.linalg.solve_triangular(system, right, lower=True, unit_diagona...  634 us
    ppermute x8, waiting for transfers between devices, shifted(): lax.ppermute(value, axis, [(source, source + steps) for source in range(f...  477 us
    ppermute x28, waiting for transfers between devices, from_partner(): lax.ppermute(x, axis, [(i, i ^ 1 << bit) for i in range(lax.axis_size(axi...  286 us
    reduce_scatter x1, waiting for transfers between devices, local(): lax.psum_scatter(feed_acc[0], 'dp', scatter_dimension=1, tiled=True)  90.9 us
    dot_general x48, matrix products, delta_block(): jnp.einsum('ywj,yje->ywe', query_rows, carried_memory_matrix, precision=e...  87.3 us
    cond x12, local copies, waits for them, and re-layouts, when_valid(): return lax.cond(valid, function, nothing, *operands)  77.4 us
    ppermute x28, starting transfers between devices, from_partner(): lax.ppermute(x, axis, [(i, i ^ 1 << bit) for i in range(lax.axis_size(axi...  70.6 us
    reduce_scatter x1, waiting for transfers between devices, local(): lax.psum_scatter(mixer_acc[0], 'dp', scatter_dimension=1, tiled=True)  66 us
  transfers between devices with their start and end apart: 43, of which 35 were waited for; matrix products, arithmetic and copies ran while one was open for 5% of the time, Pallas kernels for 0%

commit v1 on v0

v1 whole, which is shorter than its diff:
```python
import jax
import jax.numpy as jnp
from jax import lax
from jax.experimental import pallas as pl
from jax.experimental.pallas import tpu as pltpu
from jax.sharding import PartitionSpec as P

SPAN = 64
PAIR = 2 * SPAN
LANES = 128
TILE = 512
UNITS = 1408
LOW = jnp.bfloat16
WIDE = jnp.float32
VMEM = 56 * 1024 * 1024


def mm(left, right):
    return lax.dot_general(left, right, (((1,), (0,)), ((), ())), preferred_element_type=WIDE)


def mm_nt(left, right):
    return lax.dot_general(left, right, (((1,), (1,)), ((), ())), preferred_element_type=WIDE)


def mm_tn(left, right):
    return lax.dot_general(left, right, (((0,), (0,)), ((), ())), preferred_element_type=WIDE)


def low(value):
    return value.astype(LOW)


def sigmoid(value):
    return 0.5 * jnp.tanh(0.5 * value) + 0.5


def shift_down(value, steps):
    rows = lax.broadcasted_iota(jnp.int32, value.shape, 0)
    return jnp.where(rows >= steps, pltpu.roll(value, steps, 0), 0.0)


def shift_up(value, steps):
    size = value.shape[0]
    rows = lax.broadcasted_iota(jnp.int32, value.shape, 0)
    return jnp.where(rows < size - steps, pltpu.roll(value, size - steps, 0), 0.0)


def pick_lane(value, lane):
    lanes = lax.broadcasted_iota(jnp.int32, value.shape, 1)
    return jnp.sum(jnp.where(lanes == lane, value, 0.0), axis=1, keepdims=True)


def norm_scale(value, epsilon):
    return lax.rsqrt(jnp.mean(value * value, axis=-1, keepdims=True) + epsilon)


def norm_back(value, gain, grad, epsilon):
    scale = norm_scale(value, epsilon)
    scaled = gain * grad
    inner = jnp.mean(value * scaled, axis=-1, keepdims=True)
    value_grad = scale * (scaled - value * (scale * scale * inner))
    gain_grad = jnp.sum(grad * value * scale, axis=0, keepdims=True)
    return value_grad, gain_grad


def pair_masks():
    rows = lax.broadcasted_iota(jnp.int32, (PAIR, PAIR), 0)
    cols = lax.broadcasted_iota(jnp.int32, (PAIR, PAIR), 1)
    apart = rows ^ cols
    near = apart < SPAN
    return rows, cols, apart, near


def inverse(systems, apart):
    one = (apart == 0).astype(WIDE)
    found = [one - jnp.where(apart == 1, system, 0.0) for system in systems]
    lows = [low(system) for system in systems]
    size = 2
    while size < SPAN:
        level = (apart >= size) & (apart < 2 * size)
        parts = [jnp.where(level, system, jnp.zeros_like(system)) for system in lows]
        heads = [low(item) for item in found]
        steps = [low(mm(head, part)) for head, part in zip(heads, parts)]
        found = [item - mm(step, head) for item, step, head in zip(found, steps, heads)]
        size *= 2
    return found


def conv_silu(linear, taps):
    count = taps.shape[0]
    total = linear * taps[count - 1 : count]
    for back in range(1, count):
        total = total + shift_down(linear, back) * taps[count - 1 - back : count - back]
    return total


def mixer_forward_kernel(
    stream_ref,
    gain_ref,
    w_qkv_ref,
    w_beta_ref,
    taps_ref,
    out_gain_ref,
    w_out_ref,
    middle_ref,
    normed_ref,
    strengths_ref,
    linear_ref,
    out_ref,
    fresh_ref,
    solve_ref,
    states_ref,
    moves_ref,
):
    step = pl.program_id(0)
    length = stream_ref.shape[0]
    spans = length // SPAN
    heads = TILE // LANES

    @pl.when(step == 0)
    def first():
        stream = stream_ref[...].astype(WIDE)
        normed_ref[...] = low(stream * norm_scale(stream, 1e-6) * gain_ref[...])
        strengths_ref[...] = mm(normed_ref[...], w_beta_ref[...])
        middle_ref[...] = stream

    normed = normed_ref[...]
    active = []
    for which in range(3):
        linear = mm(normed, w_qkv_ref[which])
        linear_ref[which] = linear
        total = conv_silu(linear, taps_ref[which])
        active.append(total * sigmoid(total))
    rows, cols, apart, near = pair_masks()
    strict = (rows > cols) & near
    lower = (rows >= cols) & near
    queries, keys, values, betas = [], [], [], []
    for head in range(heads):
        lanes = slice(head * LANES, (head + 1) * LANES)
        query, key = active[0][:, lanes], active[1][:, lanes]
        queries.append(low(query * lax.rsqrt(jnp.sum(query * query, axis=1, keepdims=True) + 1e-6)))
        keys.append(low(key * lax.rsqrt(jnp.sum(key * key, axis=1, keepdims=True) + 1e-6)))
        values.append(low(active[2][:, lanes]))
        betas.append(sigmoid(pick_lane(strengths_ref[...], step * heads + head)))
    cells = [(head, pair) for head in range(heads) for pair in range(length // PAIR)]

    def part(array, pair):
        return array[pair * PAIR : (pair + 1) * PAIR]

    systems = []
    for head, pair in cells:
        key = part(keys[head], pair)
        systems.append(jnp.where(strict, mm_nt(key, key) * part(betas[head], pair), 0.0))
    solved = [low(item) for item in inverse(systems, apart)]
    both = {}
    scores = {}
    for (head, pair), solve in zip(cells, solved):
        solve_ref[head, pair] = solve
        beta = part(betas[head], pair)
        key = part(keys[head], pair)
        right = jnp.concatenate(
            [low(beta * key.astype(WIDE)), low(beta * part(values[head], pair).astype(WIDE))], axis=1
        )
        both[head, pair] = mm(solve, right)
        scores[head, pair] = low(jnp.where(lower, mm_nt(part(queries[head], pair), key), 0.0))

    def span_of(array, span):
        return array[span * SPAN : (span + 1) * SPAN]

    def both_of(head, span):
        return span_of(both[head, span // 2], span % 2)

    states = [[None] * spans for head in range(heads)]
    turns = {}
    for head in range(heads):
        for span in range(spans - 1):
            turns[head, span] = mm_tn(span_of(keys[head], span), low(both_of(head, span)))
    for span in range(1, spans):
        for head in range(heads):
            turn = turns[head, span - 1]
            if span == 1:
                states[head][span] = turn[:, LANES:]
            else:
                before = states[head][span - 1]
                move = low(turn[:, :LANES])
                moves_ref[head, span - 2] = move
                states[head][span] = before + turn[:, LANES:] - mm(move, low(before))
    fresh = {}
    carried = {}
    for head in range(heads):
        for span in range(spans):
            item = both_of(head, span)
            if span == 0:
                fresh[head, span] = low(item[:, LANES:])
                carried[head, span] = jnp.zeros((SPAN, LANES), WIDE)
            else:
                state = low(states[head][span])
                states_ref[head, span - 1] = state
                left = jnp.concatenate([low(item[:, :LANES]), span_of(queries[head], span)], axis=0)
                seen = mm(left, state)
                fresh[head, span] = low(item[:, LANES:] - seen[:SPAN])
                carried[head, span] = seen[SPAN:]
    normed_out = []
    for head in range(heads):
        lanes = slice(head * LANES, (head + 1) * LANES)
        pieces = []
        for pair in range(length // PAIR):
            piece = jnp.concatenate([fresh[head, 2 * pair], fresh[head, 2 * pair + 1]], axis=0)
            fresh_ref[pair * PAIR : (pair + 1) * PAIR, lanes] = piece
            base = jnp.concatenate([carried[head, 2 * pair], carried[head, 2 * pair + 1]], axis=0)
            pieces.append(base + mm(scores[head, pair], piece))
        output = jnp.concatenate(pieces, axis=0)
        out_ref[:, lanes] = output
        normed_out.append(low(output * norm_scale(output, 1e-5) * out_gain_ref[...]))
    middle_ref[...] += mm(jnp.concatenate(normed_out, axis=1), w_out_ref[...])


def whole(shape):
    return pl.BlockSpec(shape, lambda step: (0,) * len(shape))


def params(**extra):
    return pltpu.CompilerParams(dimension_semantics=("arbitrary",), vmem_limit_bytes=VMEM, **extra)


def mixer_forward(stream, gain, w_qkv, w_beta, taps, out_gain, w_out):
    length, width = stream.shape
    inner = w_qkv.shape[2]
    heads = inner // LANES
    spans = length // SPAN
    pairs = length // PAIR
    here = TILE // LANES
    out = jax.ShapeDtypeStruct
    flops = 2 * length * width * inner * 4 + 2 * heads * length * (10 * 128 * 2 + 8 * 128 * 2)
    return pl.pallas_call(
        mixer_forward_kernel,
        name="mixer_forward",
        grid=(inner // TILE,),
        in_specs=[
            whole((length, width)),
            whole((1, width)),
            pl.BlockSpec((3, width, TILE), lambda step: (0, 0, step)),
            whole((width, LANES)),
            pl.BlockSpec((3, taps.shape[1], TILE), lambda step: (0, 0, step)),
            whole((1, LANES)),
            pl.BlockSpec((TILE, width), lambda step: (step, 0)),
        ],
        out_specs=[
            whole((length, width)),
            whole((length, width)),
            whole((length, LANES)),
            pl.BlockSpec((3, length, TILE), lambda step: (0, 0, step)),
            pl.BlockSpec((length, TILE), lambda step: (0, step)),
            pl.BlockSpec((length, TILE), lambda step: (0, step)),
            pl.BlockSpec((here, pairs, PAIR, PAIR), lambda step: (step, 0, 0, 0)),
            pl.BlockSpec((here, spans - 1, LANES, LANES), lambda step: (step, 0, 0, 0)),
            pl.BlockSpec((here, spans - 2, LANES, LANES), lambda step: (step, 0, 0, 0)),
        ],
        out_shape=[
            out((length, width), WIDE),
            out((length, width), LOW),
            out((length, LANES), WIDE),
            out((3, length, inner), WIDE),
            out((length, inner), WIDE),
            out((length, inner), LOW),
            out((heads, pairs, PAIR, PAIR), LOW),
            out((heads, spans - 1, LANES, LANES), LOW),
            out((heads, spans - 2, LANES, LANES), LOW),
        ],
        compiler_params=params(),
        cost_estimate=pl.CostEstimate(flops=flops * 2, bytes_accessed=18 * 2**20, transcendentals=0),
    )(stream, gain, w_qkv, w_beta, taps, out_gain, w_out)


def mixer_backward_kernel(
    stream_ref,
    branch_ref,
    strengths_ref,
    linear_ref,
    out_ref,
    fresh_ref,
    solve_ref,
    states_ref,
    moves_ref,
    gain_ref,
    w_qkv_ref,
    w_beta_ref,
    taps_ref,
    out_gain_ref,
    w_out_ref,
    stream_grad_ref,
    gain_grad_ref,
    branch_low_ref,
    linear_grad_ref,
    strengths_grad_ref,
    normed_out_ref,
    taps_grad_ref,
    out_gain_grad_ref,
    normed_grad_ref,
    strengths_sum_ref,
):
    step = pl.program_id(0)
    steps = pl.num_programs(0)
    length = stream_ref.shape[0]
    spans = length // SPAN
    pairs = length // PAIR
    heads = TILE // LANES

    @pl.when(step == 0)
    def first():
        branch_low_ref[...] = low(branch_ref[...])
        out_gain_grad_ref[...] = jnp.zeros_like(out_gain_grad_ref)
        strengths_sum_ref[...] = jnp.zeros_like(strengths_sum_ref)
        normed_grad_ref[...] = jnp.zeros_like(normed_grad_ref)

    rows, cols, apart, near = pair_masks()
    strict = (rows > cols) & near
    lower = (rows >= cols) & near
    upper_strict = (rows < cols) & near
    upper = (rows <= cols) & near
    cells = [(head, pair) for head in range(heads) for pair in range(pairs)]

    def part(array, pair):
        return array[pair * PAIR : (pair + 1) * PAIR]

    def span_of(array, span):
        return array[span * SPAN : (span + 1) * SPAN]

    normed_out_grad = mm_nt(branch_low_ref[...], w_out_ref[...])
    totals, gates, active = [], [], []
    for which in range(3):
        total = conv_silu(linear_ref[which], taps_ref[which])
        gate = sigmoid(total)
        totals.append(total)
        gates.append(gate)
        active.append(total * gate)
    query_scales, key_scales = [], []
    queries, keys, values, betas, output_grads = [], [], [], [], []
    for head in range(heads):
        lanes = slice(head * LANES, (head + 1) * LANES)
        query, key = active[0][:, lanes], active[1][:, lanes]
        query_scales.append(lax.rsqrt(jnp.sum(query * query, axis=1, keepdims=True) + 1e-6))
        key_scales.append(lax.rsqrt(jnp.sum(key * key, axis=1, keepdims=True) + 1e-6))
        queries.append(low(query * query_scales[head]))
        keys.append(low(key * key_scales[head]))
        values.append(low(active[2][:, lanes]))
        betas.append(sigmoid(pick_lane(strengths_ref[...], step * heads + head)))
        output = out_ref[:, lanes]
        scale = norm_scale(output, 1e-5)
        grad = normed_out_grad[:, lanes]
        normed_out_ref[:, lanes] = low(output * scale * out_gain_ref[...])
        scaled = out_gain_ref[...] * grad
        inner = jnp.mean(output * scaled, axis=1, keepdims=True)
        output_grads.append(low(scale * (scaled - output * (scale * scale * inner))))
        out_gain_grad_ref[...] += jnp.sum(grad * output * scale, axis=0, keepdims=True)
    fresh = [fresh_ref[:, head * LANES : (head + 1) * LANES] for head in range(heads)]

    scores_back, score_grads, score_grads_back = {}, {}, {}
    for head, pair in cells:
        query, key = part(queries[head], pair), part(keys[head], pair)
        grad, new = part(output_grads[head], pair), part(fresh[head], pair)
        scores_back[head, pair] = low(jnp.where(upper, mm_nt(key, query), 0.0))
        score_grads[head, pair] = low(jnp.where(lower, mm_nt(grad, new), 0.0))
        score_grads_back[head, pair] = low(jnp.where(upper, mm_nt(new, grad), 0.0))
    inside, early = {}, {}
    for head, pair in cells:
        inside[head, pair] = mm(scores_back[head, pair], part(output_grads[head], pair))
    for head, pair in cells:
        early[head, pair] = mm_tn(solve_ref[head, pair], low(inside[head, pair]))
    returns = {}
    for head in range(heads):
        for span in range(1, spans):
            beta = span_of(betas[head], span)
            back = low(-beta * span_of(early[head, span // 2], span % 2))
            left = jnp.concatenate([span_of(queries[head], span), span_of(keys[head], span)], axis=0)
            right = jnp.concatenate([span_of(output_grads[head], span), back], axis=0)
            returns[head, span] = mm_tn(left, right)
    state_grads = {}
    for span in range(spans - 2, -1, -1):
        for head in range(heads):
            if span == spans - 2:
                state_grads[head, span] = returns[head, span + 1]
            else:
                after = state_grads[head, span + 1]
                state_grads[head, span] = (
                    after + returns[head, span + 1] - mm_tn(moves_ref[head, span], low(after))
                )
    fresh_add = {}
    for head, pair in cells:
        pieces = []
        for span in (2 * pair, 2 * pair + 1):
            if span == spans - 1:
                pieces.append(jnp.zeros((SPAN, LANES), WIDE))
            else:
                pieces.append(mm(span_of(keys[head], span), low(state_grads[head, span])))
        fresh_add[head, pair] = low(jnp.concatenate(pieces, axis=0))
    lasts, backs = {}, {}
    for head, pair in cells:
        last = early[head, pair] + mm_tn(solve_ref[head, pair], fresh_add[head, pair])
        lasts[head, pair] = last
        backs[head, pair] = part(betas[head], pair) * last
    system_grads, system_grads_back = {}, {}
    for head, pair in cells:
        last, new = low(lasts[head, pair]), part(fresh[head], pair)
        system_grads[head, pair] = low(jnp.where(strict, -mm_nt(last, new), 0.0))
        system_grads_back[head, pair] = low(jnp.where(upper_strict, -mm_nt(new, last), 0.0))
    query_grads, key_grads, beta_grads = [], [], []
    for head in range(heads):
        query_pieces, key_pieces, beta_pieces = [], [], []
        for pair in range(pairs):
            query, key = part(queries[head], pair), part(keys[head], pair)
            beta, new = part(betas[head], pair), part(fresh[head], pair)
            grad = part(output_grads[head], pair)
            stacked = jnp.concatenate(
                [score_grads[head, pair], system_grads[head, pair]], axis=0
            )
            through = mm(stacked, key)
            query_grad = through[:PAIR]
            key_grad = beta * through[PAIR:]
            wide = jnp.concatenate(
                [score_grads_back[head, pair], system_grads_back[head, pair]], axis=1
            )
            tall = jnp.concatenate([query, low(beta * key.astype(WIDE))], axis=0)
            key_grad = key_grad + mm(wide, tall)
            inner = low(jnp.where(strict, mm_nt(key, key), 0.0))
            residual = part(values[head], pair).astype(WIDE) - mm(inner, new)
            back = low(backs[head, pair])
            more_query, more_key, seen = [], [], []
            for local_span in range(2):
                span = 2 * pair + local_span
                new_span = span_of(new, local_span)
                if span == 0:
                    more_query.append(jnp.zeros((SPAN, LANES), WIDE))
                    seen.append(jnp.zeros((SPAN, LANES), WIDE))
                    more_key.append(mm_nt(new_span, low(state_grads[head, span])))
                    continue
                state = states_ref[head, span - 1]
                more_query.append(mm_nt(span_of(grad, local_span), state))
                seen.append(mm(span_of(key, local_span), state))
                taken = -span_of(back, local_span)
                if span == spans - 1:
                    more_key.append(mm_nt(taken, state))
                else:
                    left = jnp.concatenate([new_span, taken], axis=1)
                    right = jnp.concatenate([low(state_grads[head, span]), state], axis=1)
                    more_key.append(mm_nt(left, right))
            residual = residual - jnp.concatenate(seen, axis=0)
            query_pieces.append(query_grad + jnp.concatenate(more_query, axis=0))
            key_pieces.append(key_grad + jnp.concatenate(more_key, axis=0))
            beta_pieces.append(jnp.sum(lasts[head, pair] * residual, axis=1, keepdims=True))
        query_grads.append(jnp.concatenate(query_pieces, axis=0))
        key_grads.append(jnp.concatenate(key_pieces, axis=0))
        beta_grads.append(jnp.concatenate(beta_pieces, axis=0))
    lane_ids = lax.broadcasted_iota(jnp.int32, (length, LANES), 1)
    strengths_sum = strengths_sum_ref[...]
    for head in range(heads):
        beta = betas[head]
        strengths_sum = strengths_sum + jnp.where(
            lane_ids == step * heads + head, beta_grads[head] * beta * (1.0 - beta), 0.0
        )
    strengths_sum_ref[...] = strengths_sum

    active_grads = []
    for grads, scales, source in ((query_grads, query_scales, active[0]), (key_grads, key_scales, active[1])):
        pieces = []
        for head in range(heads):
            lanes = slice(head * LANES, (head + 1) * LANES)
            value, scale, grad = source[:, lanes], scales[head], grads[head]
            inner = jnp.sum(value * grad, axis=1, keepdims=True)
            pieces.append(scale * (grad - value * (scale * scale * inner)))
        active_grads.append(jnp.concatenate(pieces, axis=1))
    active_grads.append(
        jnp.concatenate(
            [jnp.concatenate([backs[head, pair] for pair in range(pairs)], axis=0) for head in range(heads)],
            axis=1,
        )
    )
    normed_grad = normed_grad_ref[...]
    for which in range(3):
        total, gate = totals[which], gates[which]
        total_grad = active_grads[which] * (gate * (1.0 + total * (1.0 - gate)))
        taps = taps_ref[which]
        linear = linear_ref[which]
        count = taps.shape[0]
        linear_grad = total_grad * taps[count - 1 : count]
        taps_grad_ref[which, count - 1 : count] = jnp.sum(total_grad * linear, axis=0, keepdims=True)
        for ahead in range(1, count):
            moved = shift_up(total_grad, ahead)
            place = slice(count - 1 - ahead, count - ahead)
            linear_grad = linear_grad + moved * taps[place]
            taps_grad_ref[which, place] = jnp.sum(moved * linear, axis=0, keepdims=True)
        linear_low = low(linear_grad)
        linear_grad_ref[which] = linear_low
        normed_grad = normed_grad + mm_nt(linear_low, w_qkv_ref[which])
    normed_grad_ref[...] = normed_grad

    @pl.when(step == steps - 1)
    def last_step():
        strengths_low = low(strengths_sum_ref[...])
        strengths_grad_ref[...] = strengths_low
        total = normed_grad_ref[...] + mm_nt(strengths_low, w_beta_ref[...])
        value_grad, gain_grad = norm_back(stream_ref[...].astype(WIDE), gain_ref[...], total, 1e-6)
        stream_grad_ref[...] = low(branch_ref[...] + value_grad)
        gain_grad_ref[...] = gain_grad


def mixer_backward(stream, branch, kept, gain, w_qkv, w_beta, taps, out_gain, w_out):
    strengths, linear, output, fresh, solve, states, moves = kept
    length, width = stream.shape
    inner = w_qkv.shape[2]
    spans = length // SPAN
    pairs = length // PAIR
    here = TILE // LANES
    out = jax.ShapeDtypeStruct
    count = taps.shape[1]
    flops = 2 * length * width * inner * 4 + 4 * inner * length * 128 * 40
    return pl.pallas_call(
        mixer_backward_kernel,
        name="mixer_backward",
        grid=(inner // TILE,),
        in_specs=[
            whole((length, width)),
            whole((length, width)),
            whole((length, LANES)),
            pl.BlockSpec((3, length, TILE), lambda step: (0, 0, step)),
            pl.BlockSpec((length, TILE), lambda step: (0, step)),
            pl.BlockSpec((length, TILE), lambda step: (0, step)),
            pl.BlockSpec((here, pairs, PAIR, PAIR), lambda step: (step, 0, 0, 0)),
            pl.BlockSpec((here, spans - 1, LANES, LANES), lambda step: (step, 0, 0, 0)),
            pl.BlockSpec((here, spans - 2, LANES, LANES), lambda step: (step, 0, 0, 0)),
            whole((1, width)),
            pl.BlockSpec((3, width, TILE), lambda step: (0, 0, step)),
            whole((width, LANES)),
            pl.BlockSpec((3, count, TILE), lambda step: (0, 0, step)),
            whole((1, LANES)),
            pl.BlockSpec((TILE, width), lambda step: (step, 0)),
        ],
        out_specs=[
            whole((length, width)),
            whole((1, width)),
            whole((length, width)),
            pl.BlockSpec((3, length, TILE), lambda step: (0, 0, step)),
            whole((length, LANES)),
            pl.BlockSpec((length, TILE), lambda step: (0, step)),
            pl.BlockSpec((3, count, TILE), lambda step: (0, 0, step)),
            whole((1, LANES)),
        ],
        out_shape=[
            out((length, width), LOW),
            out((1, width), WIDE),
            out((length, width), LOW),
            out((3, length, inner), LOW),
            out((length, LANES), LOW),
            out((length, inner), LOW),
            out((3, count, inner), WIDE),
            out((1, LANES), WIDE),
        ],
        scratch_shapes=[
            pltpu.VMEM((length, width), WIDE),
            pltpu.VMEM((length, LANES), WIDE),
        ],
        compiler_params=params(),
        cost_estimate=pl.CostEstimate(flops=flops * 2, bytes_accessed=20 * 2**20, transcendentals=0),
    )(stream, branch, strengths, linear, output, fresh, solve, states, moves, gain, w_qkv, w_beta, taps, out_gain, w_out)


def feed_forward_kernel(
    middle_ref, gain_ref, w_gate_up_ref, w_down_ref, result_ref, normed_ref, lifted_ref, total_ref
):
    step = pl.program_id(0)

    @pl.when(step == 0)
    def first():
        middle = middle_ref[...]
        normed_ref[...] = low(middle * norm_scale(middle, 1e-6) * gain_ref[...])
        total_ref[...] = middle

    normed = normed_ref[...]
    gate = mm(normed, w_gate_up_ref[0])
    up = mm(normed, w_gate_up_ref[1])
    lifted_ref[0] = low(gate)
    lifted_ref[1] = low(up)
    hidden = low(gate * sigmoid(gate) * up)
    total_ref[...] += mm(hidden, w_down_ref[...])

    @pl.when(step == pl.num_programs(0) - 1)
    def last():
        result_ref[...] = low(total_ref[...])


def feed_forward(middle, gain, w_gate_up, w_down):
    length, width = middle.shape
    units = w_down.shape[0]
    out = jax.ShapeDtypeStruct
    return pl.pallas_call(
        feed_forward_kernel,
        name="feed_forward",
        grid=(units // UNITS,),
        in_specs=[
            whole((length, width)),
            whole((1, width)),
            pl.BlockSpec((2, width, UNITS), lambda step: (0, 0, step)),
            pl.BlockSpec((UNITS, width), lambda step: (step, 0)),
        ],
        out_specs=[
            whole((length, width)),
            whole((length, width)),
            pl.BlockSpec((2, length, UNITS), lambda step: (0, 0, step)),
        ],
        out_shape=[
            out((length, width), LOW),
            out((length, width), LOW),
            out((2, length, units), LOW),
        ],
        scratch_shapes=[pltpu.VMEM((length, width), WIDE)],
        compiler_params=params(),
        cost_estimate=pl.CostEstimate(
            flops=2 * length * width * units * 3, bytes_accessed=24 * 2**20, transcendentals=0
        ),
    )(middle, gain, w_gate_up, w_down)


def feed_backward_kernel(
    middle_ref,
    grad_ref,
    lifted_ref,
    gain_ref,
    w_gate_up_ref,
    w_down_ref,
    middle_grad_ref,
    gain_grad_ref,
    lifted_grad_ref,
    hidden_ref,
    normed_grad_ref,
):
    step = pl.program_id(0)

    @pl.when(step == 0)
    def first():
        normed_grad_ref[...] = jnp.zeros_like(normed_grad_ref)

    hidden_grad = mm_nt(grad_ref[...], w_down_ref[...])
    gate = lifted_ref[0].astype(WIDE)
    up = lifted_ref[1].astype(WIDE)
    open_ = sigmoid(gate)
    silu = gate * open_
    hidden_ref[...] = low(silu * up)
    up_grad = low(hidden_grad * silu)
    gate_grad = low(hidden_grad * up * (open_ + silu * (1.0 - open_)))
    lifted_grad_ref[0] = gate_grad
    lifted_grad_ref[1] = up_grad
    normed_grad_ref[...] += mm_nt(gate_grad, w_gate_up_ref[0]) + mm_nt(up_grad, w_gate_up_ref[1])

    @pl.when(step == pl.num_programs(0) - 1)
    def last():
        value_grad, gain_grad = norm_back(middle_ref[...], gain_ref[...], normed_grad_ref[...], 1e-6)
        middle_grad_ref[...] = grad_ref[...].astype(WIDE) + value_grad
        gain_grad_ref[...] = gain_grad


def feed_backward(middle, grad, lifted, gain, w_gate_up, w_down):
    length, width = middle.shape
    units = w_down.shape[0]
    out = jax.ShapeDtypeStruct
    return pl.pallas_call(
        feed_backward_kernel,
        name="feed_backward",
        grid=(units // UNITS,),
        in_specs=[
            whole((length, width)),
            whole((length, width)),
            pl.BlockSpec((2, length, UNITS), lambda step: (0, 0, step)),
            whole((1, width)),
            pl.BlockSpec((2, width, UNITS), lambda step: (0, 0, step)),
            pl.BlockSpec((UNITS, width), lambda step: (step, 0)),
        ],
        out_specs=[
            whole((length, width)),
            whole((1, width)),
            pl.BlockSpec((2, length, UNITS), lambda step: (0, 0, step)),
            pl.BlockSpec((length, UNITS), lambda step: (0, step)),
        ],
        out_shape=[
            out((length, width), WIDE),
            out((1, width), WIDE),
            out((2, length, units), LOW),
            out((length, units), LOW),
        ],
        scratch_shapes=[pltpu.VMEM((length, width), WIDE)],
        compiler_params=params(),
        cost_estimate=pl.CostEstimate(
            flops=2 * length * width * units * 3, bytes_accessed=28 * 2**20, transcendentals=0
        ),
    )(middle, grad, lifted, gain, w_gate_up, w_down)


def rows_times(left, right):
    return lax.dot_general(left, right, (((0,), (0,)), ((), ())), preferred_element_type=WIDE)


def weight_grads(normed, linear_grad, strengths_grad, normed_out, branch, normed2, lifted_grad, hidden, grad):
    tall = lambda items: jnp.concatenate(items, axis=-2)
    normed, normed2 = tall(normed), tall(normed2)
    linear_grad, lifted_grad = tall(linear_grad), tall(lifted_grad)
    qkv = jnp.stack([rows_times(normed, linear_grad[i]) for i in range(3)])
    gate_up = jnp.stack([rows_times(normed2, lifted_grad[i]) for i in range(2)])
    return (
        low(qkv),
        rows_times(normed, tall(strengths_grad)),
        low(rows_times(tall(normed_out), tall(branch))),
        low(gate_up),
        low(rows_times(tall(hidden), tall(grad))),
    )


def local(
    inputs, cotangent, w_qkv, w_beta, conv_taps, w_out, w_gate_up, w_down, norm_gains, out_gains
):
    batches, unused, length, width = inputs.shape
    place = lax.axis_index("section")
    rank, half = place // 2, place % 2
    me, copies = lax.axis_index("dp"), lax.axis_size("dp")
    per = batches // 2
    layers = lax.axis_size("section") // 2

    def across(value, bit):
        return lax.ppermute(value, "section", [(i, i ^ bit) for i in range(2 * layers)])

    def by_half(own, other, axis):
        return jnp.where(
            half == 0, jnp.concatenate([own, other], axis), jnp.concatenate([other, own], axis)
        )

    def of_partner(value, axis):
        size = value.shape[axis] // copies
        mine = lax.dynamic_slice_in_dim(value, me * size, size, axis)
        return lax.all_gather(across(mine, 1), "dp", axis=axis, tiled=True)

    smalls = [conv_taps, w_beta.astype(WIDE), norm_gains, out_gains]
    packed = across(jnp.concatenate([item.reshape(-1) for item in smalls]), 1)
    others, start = [], 0
    for item in smalls:
        others.append(packed[start : start + item.size].reshape(item.shape))
        start += item.size
    taps = jnp.concatenate([conv_taps, others[0]], 2)
    heads = w_beta.shape[1]
    w_beta = jnp.concatenate([w_beta, low(others[1])], 1)
    w_beta = jnp.pad(w_beta, ((0, 0), (0, LANES - 2 * heads)))
    gains = by_half(norm_gains, others[2], 1)
    out_gain = by_half(out_gains, others[3], 0)[None]
    inner, units = w_out.shape[0], w_down.shape[0]
    w_qkv = jnp.concatenate([w_qkv, of_partner(w_qkv, 1)], 2)
    w_out = jnp.concatenate([w_out, of_partner(w_out, 0)], 0)
    w_gate_up = jnp.concatenate([w_gate_up, of_partner(w_gate_up, 1)], 2)
    w_down = jnp.concatenate([w_down, of_partner(w_down, 0)], 0)

    def forward(stream):
        middle, normed, *kept = mixer_forward(stream, gains[0:1], w_qkv, w_beta, taps, out_gain, w_out)
        result, normed2, lifted = feed_forward(middle, gains[1:2], w_gate_up, w_down)
        return result, (stream, middle, normed, kept, normed2, lifted)

    def backward(grad, saved):
        stream, middle, normed, kept, normed2, lifted = saved
        middle_grad, feed_gain, lifted_grad, hidden = feed_backward(
            middle, grad, lifted, gains[1:2], w_gate_up, w_down
        )
        stream_grad, mix_gain, branch, linear_grad, strengths_grad, normed_out, taps_grad, out_gain_grad = (
            mixer_backward(
                stream, middle_grad, kept, gains[0:1], w_qkv, w_beta, taps, out_gain, w_out
            )
        )
        big = (normed, linear_grad, strengths_grad, normed_out, branch, normed2, lifted_grad, hidden, grad)
        return stream_grad, big, (taps_grad, mix_gain, feed_gain, out_gain_grad)

    def own(value):
        items = lax.dynamic_slice_in_dim(value, half * per, per, 0)
        return [items[i, 0] for i in range(per)]

    up = [(i, i + 2) for i in range(2)]
    down = [(i + 2, i) for i in range(2)]
    saved0, arrived = [], []
    for stream in own(inputs):
        result, saved = forward(stream)
        saved0.append(saved)
        arrived.append(lax.ppermute(result, "section", up))
    saved1, results = [], []
    for stream in arrived:
        result, saved = forward(stream)
        saved1.append(saved)
        results.append(result)
    big1, small1, returned = [], [], []
    for grad, saved in zip(own(cotangent), saved1):
        stream_grad, big, small = backward(grad, saved)
        big1.append(big)
        small1.append(small)
        returned.append(lax.ppermute(stream_grad, "section", down))
    big0, small0, input_grads = [], [], []
    for grad, saved in zip(returned, saved0):
        stream_grad, big, small = backward(grad, saved)
        big0.append(big)
        small0.append(small)
        input_grads.append(stream_grad)

    turned = lambda items: [list(item) for item in zip(*items)]
    grads = lax.cond(
        rank == 0,
        lambda first, second: weight_grads(*first),
        lambda first, second: weight_grads(*second),
        turned(big0),
        turned(big1),
    )
    smalls = [
        sum(jnp.where(rank == 0, a, b) for a, b in zip(first, second))
        for first, second in zip(turned(small0), turned(small1))
    ]
    d_qkv, d_beta, d_out, d_gate_up, d_down = grads
    d_taps, d_mix, d_feed, d_out_gain = smalls

    def total(value, axis, split):
        value = lax.psum_scatter(value, "dp", scatter_dimension=axis, tiled=True)
        size = value.shape[split] // 2
        mine = lax.slice_in_dim(value, 0, size, axis=split)
        theirs = lax.slice_in_dim(value, size, 2 * size, axis=split)
        return mine.astype(WIDE) + across(theirs, 1).astype(WIDE)

    grad_qkv = total(d_qkv, 1, 2)
    grad_gate_up = total(d_gate_up, 1, 2)
    grad_out = total(d_out.reshape(2, inner, width), 1, 0)[0]
    grad_down = total(d_down.reshape(2, units, width), 1, 0)[0]

    d_gains = jnp.concatenate([d_mix, d_feed], 0)
    d_beta = d_beta[:, : 2 * heads]
    flat = [d_taps, d_beta, d_gains, d_out_gain]
    packed = lax.psum(jnp.concatenate([item.reshape(-1) for item in flat]), "dp")
    sums, start = [], 0
    for item in flat:
        sums.append(packed[start : start + item.size].reshape(item.shape))
        start += item.size

    def part(value, axis, size):
        return lax.dynamic_slice_in_dim(value, me * size, size, axis)

    def halves(value, axis):
        size = value.shape[axis] // 2
        return [
            lax.dynamic_slice_in_dim(value, which * size, size, axis) for which in (half, 1 - half)
        ]

    t_size = d_taps.shape[2] // 2 // copies
    pieces = [
        [part(sums[0][:, :, i * inner : (i + 1) * inner], 2, t_size) for i in range(2)],
        [part(sums[1][:, i * heads : (i + 1) * heads], 0, width // copies) for i in range(2)],
        [part(item, 1, width // 2 // copies) for item in halves(sums[2], 1)],
        [part(item, 1, LANES // 2 // copies) for item in halves(sums[3], 1)],
    ]
    sent = across(jnp.concatenate([theirs.reshape(-1) for mine, theirs in pieces]), 1)
    ends, start = [], 0
    for mine, theirs in pieces:
        ends.append(mine + sent[start : start + mine.size].reshape(mine.shape))
        start += mine.size
    grad_taps, grad_beta, grad_gains, grad_out_gains = ends

    held = jnp.stack([jnp.where(rank == 1, a, b) for a, b in zip(results, input_grads)])
    quarter = width // (2 * layers)

    def quarter_of(index):
        return lax.dynamic_slice_in_dim(held, index * quarter, quarter, 2)

    came = [across(quarter_of(place ^ bit), bit) for bit in (1, 2, 3)]
    same = by_half(quarter_of(place), came[0], 0)
    other = by_half(came[1], came[2], 0)
    final_stream = jnp.where(rank == 1, same, other)[:, None]
    final_grad = jnp.where(rank == 0, same, other)[:, None]
    return (
        final_stream,
        final_grad,
        grad_qkv,
        grad_beta,
        grad_taps,
        grad_out,
        grad_gate_up,
        grad_down,
        grad_gains,
        grad_out_gains[0],
    )


def solution(mesh):
    in_specs = (
        P(None, "dp", None, None),
        P(None, "dp", None, None),
        P(None, None, "section"),
        P(None, "section"),
        P(None, None, "section"),
        P("section", None),
        P(None, None, "section"),
        P("section", None),
        P(None, "section"),
        P("section"),
    )
    out_specs = (
        P(None, "dp", None, "section"),
        P(None, "dp", None, "section"),
        P(None, "dp", "section"),
        P("dp", "section"),
        P(None, None, ("section", "dp")),
        P(("section", "dp"), None),
        P(None, "dp", "section"),
        P(("section", "dp"), None),
        P(None, ("section", "dp")),
        P(("section", "dp")),
    )
    return jax.shard_map(local, mesh=mesh, in_specs=in_specs, out_specs=out_specs, check_vma=False)
```

time: 3040 us -> 786 us (0.26)
  other arithmetic: 966 us -> 23.5 us
  waiting for transfers between devices: 990 us -> 393 us
  matrix products: 503 us -> 20.5 us
  local copies, waits for them, and re-layouts: 406 us -> 59.9 us
  Pallas kernels: 0 us -> 235 us
  starting transfers between devices: 93.7 us -> 29.8 us
    ppermute x36 -> x17, waiting for transfers between devices: 763 us -> 46.5 us  [the longest x13 46.5 us: across(): lax.ppermute(value, 'section', [(i, i ^ bit) for i in range(2 * layers)])]
    another operation x169 -> x4, other arithmetic: 639 us -> 9.45 us  [the longest x1 5.36 us: weight_grads(): gate_up = jnp.stack([rows_times(normed2, lifted_grad[i]) for i in range(2)])]
    dot_general x420 -> x7, matrix products: 474 us -> 20 us  [rows_times(): lax.dot_general(left, right, (((0,), (0,)), ((), ())), preferred_element_...]
    pallas_call x0 -> x16, Pallas kernels: none -> 235 us  [the longest x4 78.1 us: mixer_backward(): pl.pallas_call(mixer_backward_kernel, name='mixer_backward', grid=(inner...]
    cond x578 -> x0, local copies, waits for them, and re-layouts: 107 us -> none  [the longest x12 77.4 us: when_valid(): return lax.cond(valid, function, nothing, *operands)]
    dynamic_update_slice x67 -> x0, other arithmetic: 80.7 us -> none  [the longest x35 62.1 us: store(): lax.dynamic_update_index_in_dim(buffer, jnp.where(valid, value, previous)...]
    ppermute x36 -> x17, starting transfers between devices: 93.2 us -> 29.2 us  [the longest x13 20.5 us: across(): lax.ppermute(value, 'section', [(i, i ^ bit) for i in range(2 * layers)])]
    add x40 -> x7, other arithmetic: 66.1 us -> 4.87 us  [the longest x2 2.25 us: total(): return mine.astype(WIDE) + across(theirs, 1).astype(WIDE)]
  transfers between devices with their start and end apart: 43 -> 26, of which waited for: 35 -> 12; matrix products, arithmetic and copies ran while one was open for 5% -> 6% of each run, Pallas kernels for 0% -> 24%
where the time goes in v1:
time: 786 us; the launch traced here: 777 us
  waiting for transfers between devices  393 us (50%)
  Pallas kernels  235 us (30%)
  local copies, waits for them, and re-layouts  59.9 us (8%)
  starting transfers between devices  29.8 us (4%)
  other arithmetic  23.5 us (3%)
  matrix products  20.5 us (3%)
  between operations  15 us (2%)
    reduce_scatter x4, waiting for transfers between devices, total(): value = lax.psum_scatter(value, 'dp', scatter_dimension=axis, tiled=True)  240 us
    pallas_call x4, Pallas kernels, mixer_backward(): pl.pallas_call(mixer_backward_kernel, name='mixer_backward', grid=(inner...  78.1 us
    all_gather x4, waiting for transfers between devices, of_partner(): return lax.all_gather(across(mine, 1), 'dp', axis=axis, tiled=True)  57.9 us
    pallas_call x4, Pallas kernels, feed_backward(): pl.pallas_call(feed_backward_kernel, name='feed_backward', grid=(units //...  56.8 us
    pallas_call x4, Pallas kernels, mixer_forward(): pl.pallas_call(mixer_forward_kernel, name='mixer_forward', grid=(inner //...  56.5 us
    psum x1, waiting for transfers between devices, local(): lax.psum(jnp.concatenate([item.reshape(-1) for item in flat]), 'dp')  46.6 us
    ppermute x13, waiting for transfers between devices, across(): lax.ppermute(value, 'section', [(i, i ^ bit) for i in range(2 * layers)])  46.5 us
    pallas_call x4, Pallas kernels, feed_forward(): pl.pallas_call(feed_forward_kernel, name='feed_forward', grid=(units // U...  43.1 us
  transfers between devices with their start and end apart: 26, of which 12 were waited for; matrix products, arithmetic and copies ran while one was open for 6% of the time, Pallas kernels for 24%

profile of v1, /device:TPU:0, one launch (start us, length us, event | category | flops | bytes accessed | tf_op | source)
XLA Modules:
  0.0 776.7 jit_solution(2537206277947609267)
XLA Ops:
  8.3 3.1 collective-permute-start.2
  11.4 3.5 collective-permute-done.2
  16.6 1.8 collective-permute-start.4
  18.4 7.9 %collective-permute-done.4 = bf16[176,1024]{1,0:T(8,128)(2,1)S(1)} collective-permute-done((bf16[176,1024]{1,0:T(8,128)(2,1)S(1)}, bf16[176,1024]{1,0:T(8,128)(2,1)S(1)}, u32[]{:S(2)}, u32[]{:S(2)}) %collective-permute-start.4) | collective-permute-done | bytes 360480 | tf_op jit(solution)/shard_map/ppermute | solution.py:728
  28.1 1.5 collective-permute-start.1
  29.6 8.0 %collective-permute-done.1 = bf16[3,128,512]{2,1,0:T(8,128)(2,1)S(1)} collective-permute-done((bf16[3,128,512]{2,1,0:T(8,128)(2,1)S(1)}, bf16[3,128,512]{2,1,0:T(8,128)(2,1)S(1)}, u32[]{:S(2)}, u32[]{:S(2)}) %collective-permute-start.1) | collective-permute-done | bytes 393248 | tf_op jit(solution)/shard_map/ppermute | solution.py:728
  40.7 14.4 %collective-permute-done.3 = bf16[2,128,1408]{2,1,0:T(8,128)(2,1)S(1)} collective-permute-done((bf16[2,128,1408]{2,1,0:T(8,128)(2,1)S(1)}, bf16[2,128,1408]{2,1,0:T(8,128)(2,1)S(1)}, u32[]{:S(2)}, u32[]{:S(2)}) %collective-permute-start.3) | collective-permute-done | bytes 720928 | tf_op jit(solution)/shard_map/ppermute | solution.py:728
  58.5 2.5 dynamic-slice_bitcast_fusion.1
  61.0 2.2 dynamic-slice_bitcast_fusion
  63.2 1.9 constant_dynamic-update-slice_fusion.17
  65.2 1.9 constant_dynamic-update-slice_fusion.25
  67.1 3.0 constant_dynamic-update-slice_fusion.23
  73.0 1.3 constant_dynamic-update-slice_fusion.20.w_out_ref
  74.4 4.5 constant_dynamic-update-slice_fusion.24.w_down_ref
  78.9 30.2 %all-gather.5.cloned.1.call-done = bf16[3,1024,512]{2,1,0:T(8,128)(2,1)} async-done(((bf16[3,128,512]{2,1,0:T(8,128)(2,1)}), bf16[3,1024,512]{2,1,0:T(8,128)(2,1)}) %all-gather.5.cloned.1.call-update) | async-done | bytes 3145744 | tf_op jit(solution)/shard_map/all_gather | solution.py:738
  109.1 3.8 constant_dynamic-update-slice_fusion.16.w_qkv_ref
  113.0 14.1 %mixer_forward.4 = (f32[256,1024]{1,0:T(8,128)}, bf16[256,1024]{1,0:T(8,128)(2,1)}, f32[256,128]{1,0:T(8,128)}, f32[3,256,1024]{2,1,0:T(8,128)}, f32[256,1024]{1...) custom-call(bf16[256,1024]{1,0:T(8,128)(2,1)} %get-tuple-element.377, ...), custom_call_target="tpu_custom_call" | custom-call | flops 4332716032 | bytes 18874368 | tf_op jit(solution)/shard_map/mixer_forward/pallas_call | solution.py:236
  127.1 27.7 %all-gather.9.cloned.1.call-done = bf16[2,1024,1408]{2,1,0:T(8,128)(2,1)} async-done(((bf16[2,128,1408]{2,1,0:T(8,128)(2,1)}), bf16[2,1024,1408]{2,1,0:T(8,128)(2,1)}) %all-gather.9.cloned.1.call-update) | async-done | bytes 5767184 | tf_op jit(solution)/shard_map/all_gather | solution.py:738
  154.8 5.6 constant_dynamic-update-slice_fusion.22.w_gate_up_ref
  160.4 10.8 %feed_forward.4 = (bf16[256,1024]{1,0:T(8,128)(2,1)}, bf16[256,1024]{1,0:T(8,128)(2,1)}, bf16[2,256,2816]{2,1,0:T(8,128)(2,1)}) custom-call(f32[256,1024]{1,0:T(8,128)} %get-tuple-element.229.middle_ref, f32[1,1024]{1,0:T(1,128)} %get-tuple-element.388.gain_ref, bf16[2,1024,2816]{2,1,0:T(8,128)(2,1)} %constant_dynamic-update-slice_fusion.22.w_gate_up_ref, ...), custom_call_target="tpu_custom_call" | custom-call | flops 4429185024 | bytes 25165824 | tf_op jit(solution)/shard_map/feed_forward/pallas_call | solution.py:596
  171.2 4.5 collective-permute-start.5
  175.7 14.1 %mixer_forward.6 = (f32[256,1024]{1,0:T(8,128)}, bf16[256,1024]{1,0:T(8,128)(2,1)}, f32[256,128]{1,0:T(8,128)}, f32[3,256,1024]{2,1,0:T(8,128)}, f32[256,1024]{1...) custom-call(bf16[256,1024]{1,0:T(8,128)(2,1)} %get-tuple-element.376, ...), custom_call_target="tpu_custom_call" | custom-call | flops 4332716032 | bytes 18874368 | tf_op jit(solution)/shard_map/mixer_forward/pallas_call | solution.py:236
  189.8 10.8 %feed_forward.6 = (bf16[256,1024]{1,0:T(8,128)(2,1)}, bf16[256,1024]{1,0:T(8,128)(2,1)}, bf16[2,256,2816]{2,1,0:T(8,128)(2,1)}) custom-call(f32[256,1024]{1,0:T(8,128)} %get-tuple-element.253.middle_ref, f32[1,1024]{1,0:T(1,128)} %get-tuple-element.388.gain_ref, bf16[2,1024,2816]{2,1,0:T(8,128)(2,1)} %constant_dynamic-update-slice_fusion.22.w_gate_up_ref, ...), custom_call_target="tpu_custom_call" | custom-call | flops 4429185024 | bytes 25165824 | tf_op jit(solution)/shard_map/feed_forward/pallas_call | solution.py:596
  200.6 1.6 collective-permute-start.7
  203.0 14.0 %mixer_forward.5 = (f32[256,1024]{1,0:T(8,128)}, bf16[256,1024]{1,0:T(8,128)(2,1)S(1)}, f32[256,128]{1,0:T(8,128)}, f32[3,256,1024]{2,1,0:T(8,128)}, f32[256,102...) custom-call(bf16[256,1024]{1,0:T(8,128)(2,1)} %copy-done.60, ...), custom_call_target="tpu_custom_call" | custom-call | flops 4332716032 | bytes 18874368 | tf_op jit(solution)/shard_map/mixer_forward/pallas_call | solution.py:236
  217.1 10.7 %feed_forward.5 = (bf16[256,1024]{1,0:T(8,128)(2,1)}, bf16[256,1024]{1,0:T(8,128)(2,1)S(1)}, bf16[2,256,2816]{2,1,0:T(8,128)(2,1)}) custom-call(f32[256,1024]{1,0:T(8,128)} %get-tuple-element.231.middle_ref, f32[1,1024]{1,0:T(1,128)} %get-tuple-element.388.gain_ref, bf16[2,1024,2816]{2,1,0:T(8,128)(2,1)} %constant_dynamic-update-slice_fusion.22.w_gate_up_ref, ...), custom_call_target="tpu_custom_call" | custom-call | flops 4429185024 | bytes 25165824 | tf_op jit(solution)/shard_map/feed_forward/pallas_call | solution.py:596
  227.8 13.8 %feed_backward.4 = (f32[256,1024]{1,0:T(8,128)}, f32[1,1024]{1,0:T(1,128)}, bf16[2,256,2816]{2,1,0:T(8,128)(2,1)S(1)}, bf16[256,2816]{1,0:T(8,128)(2,1)}) custom-call(f32[256,1024]{1,0:T(8,128)} %get-tuple-element.231.middle_ref, bf16[256,1024]{1,0:T(8,128)(2,1)S(1)} %copy-done.7, bf16[2,256,2816]{2,1,0:T(8,128)(2,1)} %get-tuple-element.233.lifted_ref, ...), custom_call_target="tpu_custom_call" | custom-call | flops 4429185024 | bytes 29360128 | tf_op jit(solution)/shard_map/feed_backward/pallas_call | solution.py:666
  241.5 19.8 %mixer_backward.4 = (bf16[256,1024]{1,0:T(8,128)(2,1)}, f32[1,1024]{1,0:T(1,128)}, bf16[256,1024]{1,0:T(8,128)(2,1)}, bf16[3,256,1024]{2,1,0:T(8,128)(2,1)}, bf1...) custom-call(bf16[256,1024]{1,0:T(8,128)(2,1)} %copy-done.60, ...), custom_call_target="tpu_custom_call" | custom-call | flops 15032385536 | bytes 20971520 | tf_op jit(solution)/shard_map/mixer_backward/pallas_call | solution.py:518
  263.5 14.2 %mixer_forward.7 = (f32[256,1024]{1,0:T(8,128)}, bf16[256,1024]{1,0:T(8,128)(2,1)S(1)}, f32[256,128]{1,0:T(8,128)}, f32[3,256,1024]{2,1,0:T(8,128)}, f32[256,102...) custom-call(bf16[256,1024]{1,0:T(8,128)(2,1)} %copy-done.59, ...), custom_call_target="tpu_custom_call" | custom-call | flops 4332716032 | bytes 18874368 | tf_op jit(solution)/shard_map/mixer_forward/pallas_call | solution.py:236
  277.7 10.8 %feed_forward.7 = (bf16[256,1024]{1,0:T(8,128)(2,1)}, bf16[256,1024]{1,0:T(8,128)(2,1)S(1)}, bf16[2,256,2816]{2,1,0:T(8,128)(2,1)}) custom-call(f32[256,1024]{1,0:T(8,128)} %get-tuple-element.255.middle_ref, f32[1,1024]{1,0:T(1,128)} %get-tuple-element.388.gain_ref, bf16[2,1024,2816]{2,1,0:T(8,128)(2,1)} %constant_dynamic-update-slice_fusion.22.w_gate_up_ref, ...), custom_call_target="tpu_custom_call" | custom-call | flops 4429185024 | bytes 25165824 | tf_op jit(solution)/shard_map/feed_forward/pallas_call | solution.py:596
  288.5 14.1 %feed_backward.6 = (f32[256,1024]{1,0:T(8,128)}, f32[1,1024]{1,0:T(1,128)}, bf16[2,256,2816]{2,1,0:T(8,128)(2,1)}, bf16[256,2816]{1,0:T(8,128)(2,1)}) custom-call(f32[256,1024]{1,0:T(8,128)} %get-tuple-element.255.middle_ref, bf16[256,1024]{1,0:T(8,128)(2,1)S(1)} %get-tuple-element.374.grad_ref, bf16[2,256,2816]{2,1,0:T(8,128)(2,1)} %get-tuple-element.257.lifted_ref, ...), custom_call_target="tpu_custom_call" | custom-call | flops 4429185024 | bytes 29360128 | tf_op jit(solution)/shard_map/feed_backward/pallas_call | solution.py:666
  302.6 19.6 %mixer_backward.6 = (bf16[256,1024]{1,0:T(8,128)(2,1)}, f32[1,1024]{1,0:T(1,128)}, bf16[256,1024]{1,0:T(8,128)(2,1)}, bf16[3,256,1024]{2,1,0:T(8,128)(2,1)}, bf1...) custom-call(bf16[256,1024]{1,0:T(8,128)(2,1)} %copy-done.59, ...), custom_call_target="tpu_custom_call" | custom-call | flops 15032385536 | bytes 20971520 | tf_op jit(solution)/shard_map/mixer_backward/pallas_call | solution.py:518
  323.5 14.7 %feed_backward.5 = (f32[256,1024]{1,0:T(8,128)}, f32[1,1024]{1,0:T(1,128)}, bf16[2,256,2816]{2,1,0:T(8,128)(2,1)}, bf16[256,2816]{1,0:T(8,128)(2,1)}) custom-call(f32[256,1024]{1,0:T(8,128)} %get-tuple-element.229.middle_ref, bf16[256,1024]{1,0:T(8,128)(2,1)S(1)} %collective-permute-done.6.grad_ref, bf16[2,256,2816]{2,1,0:T(8,128)(2,1)} %get-tuple-element.243.lifted_ref, ...), custom_call_target="tpu_custom_call" | custom-call | flops 4429185024 | bytes 29360128 | tf_op jit(solution)/shard_map/feed_backward/pallas_call | solution.py:666
  338.2 19.4 %mixer_backward.5 = (bf16[256,1024]{1,0:T(8,128)(2,1)}, f32[1,1024]{1,0:T(1,128)}, bf16[256,1024]{1,0:T(8,128)(2,1)}, bf16[3,256,1024]{2,1,0:T(8,128)(2,1)}, bf1...) custom-call(bf16[256,1024]{1,0:T(8,128)(2,1)} %get-tuple-element.377.stream_ref, ...), custom_call_target="tpu_custom_call" | custom-call | flops 15032385536 | bytes 20971520 | tf_op jit(solution)/shard_map/mixer_backward/pallas_call | solution.py:518
  357.6 14.3 %feed_backward.7 = (f32[256,1024]{1,0:T(8,128)}, f32[1,1024]{1,0:T(1,128)}, bf16[2,256,2816]{2,1,0:T(8,128)(2,1)}, bf16[256,2816]{1,0:T(8,128)(2,1)}) custom-call(f32[256,1024]{1,0:T(8,128)} %get-tuple-element.253.middle_ref, bf16[256,1024]{1,0:T(8,128)(2,1)S(1)} %collective-permute-done.8.grad_ref, bf16[2,256,2816]{2,1,0:T(8,128)(2,1)} %get-tuple-element.267.lifted_ref, ...), custom_call_target="tpu_custom_call" | custom-call | flops 4429185024 | bytes 29360128 | tf_op jit(solution)/shard_map/feed_backward/pallas_call | solution.py:666
  372.0 19.3 %mixer_backward.7 = (bf16[256,1024]{1,0:T(8,128)(2,1)}, f32[1,1024]{1,0:T(1,128)}, bf16[256,1024]{1,0:T(8,128)(2,1)}, bf16[3,256,1024]{2,1,0:T(8,128)(2,1)}, bf1...) custom-call(bf16[256,1024]{1,0:T(8,128)(2,1)} %get-tuple-element.376.stream_ref, ...), custom_call_target="tpu_custom_call" | custom-call | flops 15032385536 | bytes 20971520 | tf_op jit(solution)/shard_map/mixer_backward/pallas_call | solution.py:518
  393.6 39.2 %conditional.2 = (bf16[3,1024,1024]{2,1,0:T(8,128)(2,1)}, bf16[1024,1024]{1,0:T(8,128)(2,1)}, bf16[2,1024,2816]{2,1,0:T(8,128)(2,1)}, bf16[2816,1024]{1,0:T(8,128)(2,1)}, f32[8192]{0:T(1024)S(1)}) conditional(s32[]{:T(128)} %convert_element_type.55, (bf16[256,1024]{1,0:T(8,128)(2,1)S(1)}, bf16[256,1024]{1,0:T(8,128)(2,1)S(1)}, ...), branch_computations={%region_0.1_spmd, %region_1.2_spmd} | conditional | flops 13185859584 | bytes 173507072
  393.9 1.5 constant_dynamic-update-slice_fusion.9
  399.4 4.0 fusion.23
  405.0 1.3 convolution_bitcast_fusion.7
  406.3 1.3 convolution_bitcast_fusion.8
  408.9 3.1 pad_maximum_fusion.5
  412.3 1.6 copy-done.4
  415.2 3.5 convolution_bitcast_fusion.5
  418.7 3.5 convolution_bitcast_fusion.6
  422.3 5.4 pad_maximum_fusion.4
  427.7 5.1 fusion.19
  433.4 1.3 pad_maximum_fusion.8
  438.8 46.6 %all-reduce.3.cloned.1.call-done = f32[22656]{0:T(1024)} async-done(((f32[22656]{0:T(1024)}), f32[22656]{0:T(1024)}) %all-reduce.3.cloned.1.call-update) | async-done | bytes 90640 | tf_op jit(solution)/shard_map/psum | solution.py:835
  489.4 1.5 collective-permute-start.13
  492.3 2.4 collective-permute-start.10
  494.7 1.4 collective-permute-start.11
  499.0 31.9 %reduce-scatter.7.cloned.1.call-done = bf16[2,64,1024]{2,1,0:T(8,128)(2,1)} async-done(((bf16[2,512,1024]{2,1,0:T(8,128)(2,1)}), bf16[2,64,1024]{2,1,0:T(8,128)(2,1)}) %reduce-scatter.7.cloned.1.call-update) | async-done | bytes 262160 | tf_op jit(solution)/shard_map/reduce_scatter | solution.py:821
  530.9 1.6 slice.227
  532.5 1.5 collective-permute-start.14
  533.9 59.5 %reduce-scatter.11.cloned.1.call-done = bf16[2,176,1024]{2,1,0:T(8,128)(2,1)} async-done(((bf16[2,1408,1024]{2,1,0:T(8,128)(2,1)}), bf16[2,176,1024]{2,1,0:T(8,128)(2,1)}) %reduce-scatter.11.cloned.1.call-update) | async-done | bytes 720912 | tf_op jit(solution)/shard_map/reduce_scatter | solution.py:821
  594.5 1.6 collective-permute-start.16
  596.1 2.2 select_bitcast_fusion
  598.3 60.7 %reduce-scatter.5.cloned.1.call-done = bf16[3,128,1024]{2,1,0:T(8,128)(2,1)} async-done(((bf16[3,1024,1024]{2,1,0:T(8,128)(2,1)}), bf16[3,128,1024]{2,1,0:T(8,128)(2,1)}) %reduce-scatter.5.cloned.1.call-update) | async-done | bytes 786448 | tf_op jit(solution)/shard_map/reduce_scatter | solution.py:821
  660.0 1.6 collective-permute-start.12
  661.6 87.6 %reduce-scatter.9.cloned.1.call-done = bf16[2,128,2816]{2,1,0:T(8,128)(2,1)} async-done(((bf16[2,1024,2816]{2,1,0:T(8,128)(2,1)}), bf16[2,128,2816]{2,1,0:T(8,128)(2,1)}) %reduce-scatter.9.cloned.1.call-update) | async-done | bytes 1441808 | tf_op jit(solution)/shard_map/reduce_scatter | solution.py:821
  750.5 1.6 collective-permute-start.15
  752.1 1.6 add_bitcast_fusion.1
  755.7 12.8 %collective-permute-done.15 = bf16[2,128,1408]{2,1,0:T(8,128)(2,1)S(1)} collective-permute-done((bf16[2,128,1408]{2,1,0:T(8,128)(2,1)S(1)}, bf16[2,128,1408]{2,1,0:T(8,128)(2,1)S(1)}, u32[]{:S(2)}, u32[]{:S(2)}) %collective-permute-start.15) | collective-permute-done | bytes 720928 | tf_op jit(solution)/shard_map/ppermute | solution.py:728
  (218 shorter events, 48.3 us)
Async XLA Ops:
  7.2 50.3 %copy-start.15 = (bf16[512,1024]{1,0:T(8,128)(2,1)S(1)}, bf16[512,1024]{1,0:T(8,128)(2,1)}, u32[]{:S(2)}) copy-start(bf16[512,1024]{1,0:T(8,128)(2,1)} %param.17) | copy-start | bytes 3145732
  7.2 48.9 %copy-start.45 = (f32[2,512]{1,0:T(2,128)S(1)}, f32[2,512]{1,0:T(2,128)}, u32[]{:S(2)}) copy-start(f32[2,512]{1,0:T(2,128)} %param.20) | copy-start | bytes 12292
  7.2 48.9 %copy-start.37 = (f32[3,4,512]{2,1,0:T(4,128)S(1)}, f32[3,4,512]{2,1,0:T(4,128)}, u32[]{:S(2)}) copy-start(f32[3,4,512]{2,1,0:T(4,128)} %param.16) | copy-start | bytes 73732
  7.2 48.9 %copy-start.44 = (bf16[1024,4]{0,1:T(4,128)(2,1)S(1)}, bf16[1024,4]{0,1:T(4,128)(2,1)}, u32[]{:S(2)}) copy-start(bf16[1024,4]{0,1:T(4,128)(2,1)} %param.15) | copy-start | bytes 24580
  7.2 49.3 %copy-start.54 = (f32[64]{0:T(128)S(1)}, f32[64]{0:T(128)}, u32[]{:S(2)}) copy-start(f32[64]{0:T(128)} %param.21) | copy-start | bytes 772
  7.2 65.8 %all-gather.7.cloned.1.call-start = ((), (), s32[]{:S(2)}) async-start(), calls=%async_computation.5 | async-start | bytes 1179648 | tf_op jit(solution)/shard_map/all_gather | solution.py:738
  8.3 6.6 collective-permute-start.2
  15.5 58.9 %all-gather.11.cloned.1.call-start = ((), (), s32[]{:S(2)}) async-start(), calls=%async_computation.7 | async-start | bytes 3244032 | tf_op jit(solution)/shard_map/all_gather | solution.py:738
  16.6 9.7 %collective-permute-start.4 = (bf16[176,1024]{1,0:T(8,128)(2,1)S(1)}, bf16[176,1024]{1,0:T(8,128)(2,1)S(1)}, u32[]{:S(2)}, u32[]{:S(2)}) collective-permute-start(bf16[176,1024]{1,0:T(8,128)(2,1)S(1)} %constant_dynamic-slice_fusion.4), channel_id=1, source_target_pairs={{0,8},{8,0},{16,24},{24,16},{1,9},{9,1},{17,25},{25,17},{2,10},{10... | collective-permute-start | bytes 1081352 | tf_op jit(solution)/shard_map/ppermute | solution.py:728
  27.0 82.1 %all-gather.5.cloned.1.call-start = ((), (), s32[]{:S(2)}) async-start(), calls=%async_computation.4 | async-start | bytes 3538944 | tf_op jit(solution)/shard_map/all_gather | solution.py:738
  28.1 9.4 %collective-permute-start.1 = (bf16[3,128,512]{2,1,0:T(8,128)(2,1)S(1)}, bf16[3,128,512]{2,1,0:T(8,128)(2,1)S(1)}, u32[]{:S(2)}, u32[]{:S(2)}) collective-permute-start(bf16[3,128,512]{2,1,0:T(8,128)(2,1)S(1)} %constant_dynamic-slice_fusion.7), channel_id=1, source_target_pairs={{0,8},{8,0},{16,24},{24,16},{1,9},{9,1},{17,25},{25,17},{2,10},{10... | collective-permute-start | bytes 1179656 | tf_op jit(solution)/shard_map/ppermute | solution.py:728
  38.3 116.5 %all-gather.9.cloned.1.call-start = ((), (), s32[]{:S(2)}) async-start(), calls=%async_computation.6 | async-start | bytes 6488064 | tf_op jit(solution)/shard_map/all_gather | solution.py:738
  39.6 15.5 %collective-permute-start.3 = (bf16[2,128,1408]{2,1,0:T(8,128)(2,1)S(1)}, bf16[2,128,1408]{2,1,0:T(8,128)(2,1)S(1)}, u32[]{:S(2)}, u32[]{:S(2)}) collective-permute-start(bf16[2,128,1408]{2,1,0:T(8,128)(2,1)S(1)} %constant_dynamic-slice_fusion.5), channel_id=1, source_target_pairs={{0,8},{8,0},{16,24},{24,16},{1,9},{9,1},{17,25},{25,17},{2,10},{10... | collective-permute-start | bytes 2162696 | tf_op jit(solution)/shard_map/ppermute | solution.py:728
  56.0 429.4 %all-reduce.3.cloned.1.call-start = ((), (), s32[]{:S(2)}) async-start(), calls=%async_computation.9 | async-start | bytes 188416 | tf_op jit(solution)/shard_map/psum | solution.py:835
  56.6 13.7 %collective-permute-start = (f32[11328]{0:T(1024)S(1)}, f32[11328]{0:T(1024)S(1)}, u32[]{:S(2)}, u32[]{:S(2)}) collective-permute-start(f32[11328]{0:T(1024)S(1)} %pad_maximum_fusion.9), channel_id=1, source_target_pairs={{0,8},{8,0},{16,24},{24,16},{1,9},{9,1},{17,25},{25,17},{2,10},{10... | collective-permute-start | bytes 135944 | tf_op jit(solution)/shard_map/ppermute | solution.py:728
  57.5 5.8 copy-start
  61.0 4.2 copy-start.1
  61.0 6.1 slice-start
  63.2 3.8 slice-start.1
  67.1 6.0 copy-start.23
  71.5 7.4 copy-start.46
  74.4 38.6 %copy-start.24 = (bf16[1024,1024]{1,0:T(8,128)(2,1)}, bf16[1024,1024]{1,0:T(8,128)(2,1)S(1)}, u32[]{:S(2)}) copy-start(bf16[1024,1024]{1,0:T(8,128)(2,1)S(1)} %constant_dynamic-update-slice_fusion.20.w_out_ref) | copy-start | bytes 6291460
  171.2 31.0 %collective-permute-start.5 = (bf16[256,1024]{1,0:T(8,128)(2,1)}, bf16[256,1024]{1,0:T(8,128)(2,1)S(1)}, u32[]{:S(2)}, u32[]{:S(2)}) collective-permute-start(bf16[256,1024]{1,0:T(8,128)(2,1)} %get-tuple-element.230), channel_id=1, source_target_pairs={{0,16},{8,24},{1,17},{9,25},{2,18},{10,26},{3,19},{11,27},{4,20},{... | collective-permute-start | bytes 1572872 | tf_op jit(solution)/shard_map/ppermute | solution.py:786
  200.6 62.0 %collective-permute-start.7 = (bf16[256,1024]{1,0:T(8,128)(2,1)}, bf16[256,1024]{1,0:T(8,128)(2,1)S(1)}, u32[]{:S(2)}, u32[]{:S(2)}) collective-permute-start(bf16[256,1024]{1,0:T(8,128)(2,1)} %get-tuple-element.254), channel_id=1, source_target_pairs={{0,16},{8,24},{1,17},{9,25},{2,18},{10,26},{3,19},{11,27},{4,20},{... | collective-permute-start | bytes 1572872 | tf_op jit(solution)/shard_map/ppermute | solution.py:786
  217.1 10.7 %copy-start.7 = (bf16[256,1024]{1,0:T(8,128)(2,1)S(1)}, bf16[256,1024]{1,0:T(8,128)(2,1)}, u32[]{:S(2)}) copy-start(bf16[256,1024]{1,0:T(8,128)(2,1)} %get-tuple-element.375.grad_ref) | copy-start | bytes 1572868
  261.4 62.1 %collective-permute-start.6 = (bf16[256,1024]{1,0:T(8,128)(2,1)}, bf16[256,1024]{1,0:T(8,128)(2,1)S(1)}, u32[]{:S(2)}, u32[]{:S(2)}) collective-permute-start(bf16[256,1024]{1,0:T(8,128)(2,1)} %get-tuple-element.242), channel_id=1, source_target_pairs={{16,0},{24,8},{17,1},{25,9},{18,2},{26,10},{19,3},{27,11},{20,4},{... | collective-permute-start | bytes 1572872 | tf_op jit(solution)/shard_map/ppermute | solution.py:797
  322.2 35.4 %collective-permute-start.8 = (bf16[256,1024]{1,0:T(8,128)(2,1)}, bf16[256,1024]{1,0:T(8,128)(2,1)S(1)}, u32[]{:S(2)}, u32[]{:S(2)}) collective-permute-start(bf16[256,1024]{1,0:T(8,128)(2,1)} %get-tuple-element.266), channel_id=1, source_target_pairs={{16,0},{24,8},{17,1},{25,9},{18,2},{26,10},{19,3},{27,11},{20,4},{... | collective-permute-start | bytes 1572872 | tf_op jit(solution)/shard_map/ppermute | solution.py:797
  371.9 19.4 %copy-start.47 = (f32[1,1024]{1,0:T(1,128)S(1)}, f32[1,1024]{1,0:T(1,128)}, u32[]{:S(2)}) copy-start(f32[1,1024]{1,0:T(1,128)} %get-tuple-element.320) | copy-start | bytes 12292
  371.9 19.4 %copy-start.48 = (f32[1,1024]{1,0:T(1,128)S(1)}, f32[1,1024]{1,0:T(1,128)}, u32[]{:S(2)}) copy-start(f32[1,1024]{1,0:T(1,128)} %get-tuple-element.316) | copy-start | bytes 12292
  371.9 19.4 %copy-start.49 = (f32[1,1024]{1,0:T(1,128)S(1)}, f32[1,1024]{1,0:T(1,128)}, u32[]{:S(2)}) copy-start(f32[1,1024]{1,0:T(1,128)} %get-tuple-element.322) | copy-start | bytes 12292
  371.9 19.4 %copy-start.50 = (f32[1,1024]{1,0:T(1,128)S(1)}, f32[1,1024]{1,0:T(1,128)}, u32[]{:S(2)}) copy-start(f32[1,1024]{1,0:T(1,128)} %get-tuple-element.318) | copy-start | bytes 12292
  371.9 19.4 %copy-start.51 = (f32[1,1024]{1,0:T(1,128)S(1)}, f32[1,1024]{1,0:T(1,128)}, u32[]{:S(2)}) copy-start(f32[1,1024]{1,0:T(1,128)} %get-tuple-element.319) | copy-start | bytes 12292
  371.9 19.4 %copy-start.52 = (f32[1,1024]{1,0:T(1,128)S(1)}, f32[1,1024]{1,0:T(1,128)}, u32[]{:S(2)}) copy-start(f32[1,1024]{1,0:T(1,128)} %get-tuple-element.315) | copy-start | bytes 12292
  372.0 19.4 %copy-start.53 = (f32[1,1024]{1,0:T(1,128)S(1)}, f32[1,1024]{1,0:T(1,128)}, u32[]{:S(2)}) copy-start(f32[1,1024]{1,0:T(1,128)} %get-tuple-element.321) | copy-start | bytes 12292
  372.0 20.7 %copy-start.41 = (f32[3,4,1024]{2,1,0:T(4,128)S(1)}, f32[3,4,1024]{2,1,0:T(4,128)}, u32[]{:S(2)}) copy-start(f32[3,4,1024]{2,1,0:T(4,128)} %get-tuple-element.311) | copy-start | bytes 147460
  372.0 20.7 %copy-start.42 = (f32[3,4,1024]{2,1,0:T(4,128)S(1)}, f32[3,4,1024]{2,1,0:T(4,128)}, u32[]{:S(2)}) copy-start(f32[3,4,1024]{2,1,0:T(4,128)} %get-tuple-element.313) | copy-start | bytes 147460
  372.0 20.7 %copy-start.43 = (f32[3,4,1024]{2,1,0:T(4,128)S(1)}, f32[3,4,1024]{2,1,0:T(4,128)}, u32[]{:S(2)}) copy-start(f32[3,4,1024]{2,1,0:T(4,128)} %get-tuple-element.310) | copy-start | bytes 147460
  393.8 3.9 copy-start.19
  393.8 3.9 copy-start.21
  393.8 4.9 copy-start.39
  393.8 4.9 copy-start.40
  393.8 5.6 copy-start.61
  393.8 5.6 copy-start.62
  399.4 4.0 copy-start.12
  422.2 5.4 copy-start.20
  422.3 5.4 copy-start.22
  422.3 5.4 copy-start.57
  422.3 5.4 copy-start.58
  434.8 96.1 %reduce-scatter.7.cloned.1.call-start = ((), (), s32[]{:S(2)}) async-start(), calls=%async_computation.10 | async-start | bytes 2359296 | tf_op jit(solution)/shard_map/reduce_scatter | solution.py:821
  435.4 158.0 %reduce-scatter.11.cloned.1.call-start = ((), (), s32[]{:S(2)}) async-start(), calls=%async_computation.12 | async-start | bytes 6488064 | tf_op jit(solution)/shard_map/reduce_scatter | solution.py:821
  436.1 222.8 %reduce-scatter.5.cloned.1.call-start = ((), (), s32[]{:S(2)}) async-start(), calls=%async_computation.8 | async-start | bytes 7077888 | tf_op jit(solution)/shard_map/reduce_scatter | solution.py:821
  436.9 312.4 %reduce-scatter.9.cloned.1.call-start = ((), (), s32[]{:S(2)}) async-start(), calls=%async_computation.11 | async-start | bytes 12976128 | tf_op jit(solution)/shard_map/reduce_scatter | solution.py:821
  489.4 6.7 collective-permute-start.13
  491.7 104.3 %collective-permute-start.9 = (bf16[2,256,256]{2,1,0:T(8,128)(2,1)}, bf16[2,256,256]{2,1,0:T(8,128)(2,1)S(1)}, u32[]{:S(2)}, u32[]{:S(2)}) collective-permute-start(bf16[2,256,256]{2,1,0:T(8,128)(2,1)} %get-tuple-element.380), channel_id=1, source_target_pairs={{0,8},{8,0},{16,24},{24,16},{1,9},{9,1},{17,25},{25,17},{2,10},{10... | collective-permute-start | bytes 786440 | tf_op jit(solution)/shard_map/ppermute | solution.py:728
  492.3 103.8 %collective-permute-start.10 = (bf16[2,256,256]{2,1,0:T(8,128)(2,1)S(1)}, bf16[2,256,256]{2,1,0:T(8,128)(2,1)S(1)}, u32[]{:S(2)}, u32[]{:S(2)}) collective-permute-start(bf16[2,256,256]{2,1,0:T(8,128)(2,1)S(1)} %get-tuple-element.382), channel_id=1, source_target_pairs={{0,16},{8,24},{16,0},{24,8},{1,17},{9,25},{17,1},{25,9},{2,18},{10... | collective-permute-start | bytes 786440 | tf_op jit(solution)/shard_map/ppermute | solution.py:728
  494.7 101.4 %collective-permute-start.11 = (bf16[2,256,256]{2,1,0:T(8,128)(2,1)S(1)}, bf16[2,256,256]{2,1,0:T(8,128)(2,1)}, u32[]{:S(2)}, u32[]{:S(2)}) collective-permute-start(bf16[2,256,256]{2,1,0:T(8,128)(2,1)S(1)} %get-tuple-element.383), channel_id=1, source_target_pairs={{0,24},{8,16},{16,8},{24,0},{1,25},{9,17},{17,9},{25,1},{2,26},{10... | collective-permute-start | bytes 786440 | tf_op jit(solution)/shard_map/ppermute | solution.py:728
  532.5 219.6 %collective-permute-start.14 = (bf16[1,64,1024]{2,1,0:T(8,128)(2,1)}, bf16[1,64,1024]{2,1,0:T(8,128)(2,1)}, u32[]{:S(2)}, u32[]{:S(2)}) collective-permute-start(bf16[1,64,1024]{2,1,0:T(8,128)(2,1)} %slice.227), channel_id=1, source_target_pairs={{0,8},{8,0},{16,24},{24,16},{1,9},{9,1},{17,25},{25,17},{2,10},{10... | collective-permute-start | bytes 393224 | tf_op jit(solution)/shard_map/ppermute | solution.py:728
  593.4 160.3 %copy-start.18 = (bf16[2,176,1024]{2,1,0:T(8,128)(2,1)S(1)}, bf16[2,176,1024]{2,1,0:T(8,128)(2,1)}, u32[]{:S(2)}) copy-start(bf16[2,176,1024]{2,1,0:T(8,128)(2,1)} %reduce-scatter.11.cloned.1.call-done) | copy-start | bytes 2162692
  594.5 159.2 %collective-permute-start.16 = (bf16[1,176,1024]{2,1,0:T(8,128)(2,1)S(1)}, bf16[1,176,1024]{2,1,0:T(8,128)(2,1)S(1)}, u32[]{:S(2)}, u32[]{:S(2)}) collective-permute-start(bf16[1,176,1024]{2,1,0:T(8,128)(2,1)S(1)} %slice.231), channel_id=1, source_target_pairs={{0,8},{8,0},{16,24},{24,16},{1,9},{9,1},{17,25},{25,17},{2,10},{10... | collective-permute-start | bytes 1081352 | tf_op jit(solution)/shard_map/ppermute | solution.py:728
  596.0 156.0 %copy-start.35 = (bf16[2,64,1024]{2,1,0:T(8,128)(2,1)S(1)}, bf16[2,64,1024]{2,1,0:T(8,128)(2,1)}, u32[]{:S(2)}) copy-start(bf16[2,64,1024]{2,1,0:T(8,128)(2,1)} %reduce-scatter.7.cloned.1.call-done) | copy-start | bytes 786436
  658.9 95.7 %copy-start.16 = (bf16[3,128,1024]{2,1,0:T(8,128)(2,1)S(1)}, bf16[3,128,1024]{2,1,0:T(8,128)(2,1)}, u32[]{:S(2)}) copy-start(bf16[3,128,1024]{2,1,0:T(8,128)(2,1)} %reduce-scatter.5.cloned.1.call-done) | copy-start | bytes 2359300
  660.0 94.6 %collective-permute-start.12 = (bf16[3,128,512]{2,1,0:T(8,128)(2,1)S(1)}, bf16[3,128,512]{2,1,0:T(8,128)(2,1)S(1)}, u32[]{:S(2)}, u32[]{:S(2)}) collective-permute-start(bf16[3,128,512]{2,1,0:T(8,128)(2,1)S(1)} %slice.215), channel_id=1, source_target_pairs={{0,8},{8,0},{16,24},{24,16},{1,9},{9,1},{17,25},{25,17},{2,10},{10... | collective-permute-start | bytes 1179656 | tf_op jit(solution)/shard_map/ppermute | solution.py:728
  749.2 19.2 %copy-start.14 = (bf16[2,128,2816]{2,1,0:T(8,128)(2,1)S(1)}, bf16[2,128,2816]{2,1,0:T(8,128)(2,1)}, u32[]{:S(2)}) copy-start(bf16[2,128,2816]{2,1,0:T(8,128)(2,1)} %reduce-scatter.9.cloned.1.call-done) | copy-start | bytes 4325380
  750.5 18.0 %collective-permute-start.15 = (bf16[2,128,1408]{2,1,0:T(8,128)(2,1)S(1)}, bf16[2,128,1408]{2,1,0:T(8,128)(2,1)S(1)}, u32[]{:S(2)}, u32[]{:S(2)}) collective-permute-start(bf16[2,128,1408]{2,1,0:T(8,128)(2,1)S(1)} %slice.229), channel_id=1, source_target_pairs={{0,8},{8,0},{16,24},{24,16},{1,9},{9,1},{17,25},{25,17},{2,10},{10... | collective-permute-start | bytes 2162696 | tf_op jit(solution)/shard_map/ppermute | solution.py:728
  (15 other events, 18.4 us)
Sparse Core Ops, SparseCore 0:
  15.7 24.8 all-gather.6
  43.1 31.1 all-gather.10
  76.8 32.3 all-gather.4
  111.5 43.3 all-gather.8
  434.9 50.4 all-reduce.2
  488.8 41.9 reduce-scatter.6
  534.3 59.0 reduce-scatter.10
  597.1 61.7 reduce-scatter.4
  662.4 86.7 reduce-scatter.8

commit v2 on v1

v2 whole, which is shorter than its diff:
```python
import jax
import jax.numpy as jnp
from jax import lax
from jax.experimental import pallas as pl
from jax.experimental.pallas import tpu as pltpu
from jax.sharding import PartitionSpec as P

SPAN = 64
PAIR = 2 * SPAN
LANES = 128
LOW = jnp.bfloat16
WIDE = jnp.float32
VMEM = 56 * 1024 * 1024


def mm(left, right):
    return lax.dot_general(left, right, (((1,), (0,)), ((), ())), preferred_element_type=WIDE)


def mm_nt(left, right):
    return lax.dot_general(left, right, (((1,), (1,)), ((), ())), preferred_element_type=WIDE)


def mm_tn(left, right):
    return lax.dot_general(left, right, (((0,), (0,)), ((), ())), preferred_element_type=WIDE)


def low(value):
    return value.astype(LOW)


def sigmoid(value):
    return 0.5 * jnp.tanh(0.5 * value) + 0.5


def shift_down(value, steps):
    rows = lax.broadcasted_iota(jnp.int32, value.shape, 0)
    return jnp.where(rows >= steps, pltpu.roll(value, steps, 0), 0.0)


def shift_up(value, steps):
    size = value.shape[0]
    rows = lax.broadcasted_iota(jnp.int32, value.shape, 0)
    return jnp.where(rows < size - steps, pltpu.roll(value, size - steps, 0), 0.0)


def pick_lane(value, lane):
    lanes = lax.broadcasted_iota(jnp.int32, value.shape, 1)
    return jnp.sum(jnp.where(lanes == lane, value, 0.0), axis=1, keepdims=True)


def norm_scale(value, epsilon):
    return lax.rsqrt(jnp.mean(value * value, axis=-1, keepdims=True) + epsilon)


def norm_back(value, gain, grad, epsilon):
    scale = norm_scale(value, epsilon)
    scaled = gain * grad
    inner = jnp.mean(value * scaled, axis=-1, keepdims=True)
    value_grad = scale * (scaled - value * (scale * scale * inner))
    gain_grad = jnp.sum(grad * value * scale, axis=0, keepdims=True)
    return value_grad, gain_grad


def pair_masks():
    rows = lax.broadcasted_iota(jnp.int32, (PAIR, PAIR), 0)
    cols = lax.broadcasted_iota(jnp.int32, (PAIR, PAIR), 1)
    apart = rows ^ cols
    near = apart < SPAN
    return rows, cols, apart, near


def inverse(systems, apart):
    one = (apart == 0).astype(WIDE)
    found = [one - jnp.where(apart == 1, system, 0.0) for system in systems]
    lows = [low(system) for system in systems]
    size = 2
    while size < SPAN:
        level = (apart >= size) & (apart < 2 * size)
        parts = [jnp.where(level, system, jnp.zeros_like(system)) for system in lows]
        heads = [low(item) for item in found]
        steps = [low(mm(head, part)) for head, part in zip(heads, parts)]
        found = [item - mm(step, head) for item, step, head in zip(found, steps, heads)]
        size *= 2
    return found


def conv_silu(linear, taps):
    count = taps.shape[0]
    total = linear * taps[count - 1 : count]
    for back in range(1, count):
        total = total + shift_down(linear, back) * taps[count - 1 - back : count - back]
    return total


def whole(shape):
    return pl.BlockSpec(shape, lambda step, *scalars: (0,) * len(shape))


def tiled(shape, axis):
    return pl.BlockSpec(
        shape, lambda step, *scalars: tuple(step if i == axis else 0 for i in range(len(shape)))
    )


def tiled_old(shape, axis):
    return pl.BlockSpec(
        shape,
        lambda step, info: tuple(step * (1 - info[8]) if i == axis else 0 for i in range(len(shape))),
    )


ANYWHERE = pl.BlockSpec(memory_space=pl.ANY)

DOWN, OUT = 9, 17


def mixer_copies(info_ref, refs, into_qkv, into_out, sems):
    qkv_ref, out_ref, qkv_came, qkv_twin, out_came, out_twin = refs
    rows = qkv_came.shape[1]
    first, second = pl.ds(0, rows), pl.ds(rows, rows)
    pairs = [
        (qkv_ref, into_qkv.at[0]),
        (out_ref, into_out.at[0]),
        (qkv_came, into_qkv.at[1, :, first]),
        (qkv_twin, into_qkv.at[1, :, second]),
    ]
    rows = out_came.shape[0]
    for index, source in enumerate((out_came, out_twin)):
        place = pl.multiple_of(info_ref[OUT + index] * rows, rows)
        pairs.append((source, into_out.at[1, pl.ds(place, rows)]))
    copies = [pltpu.make_async_copy(*pair, sems.at[i]) for i, pair in enumerate(pairs)]
    return copies[0], copies[1], copies[2:4], copies[4:]


def apart_order(info_ref, value_ref, into_ref, first=0):
    size = value_ref.shape[1] // 8
    for index in range(8):
        place = pl.multiple_of(info_ref[first + index] * size, size)
        into_ref[:, index * size : (index + 1) * size] = value_ref[:, pl.ds(place, size)]


def add_from_apart(info_ref, value_ref, into_ref, first=0):
    size = value_ref.shape[1] // 8
    for index in range(8):
        place = pl.ds(pl.multiple_of(info_ref[first + index] * size, size), size)
        into_ref[:, place] += value_ref[:, index * size : (index + 1) * size]


def start_all(step, copies):
    @pl.when(step == 0)
    def begin():
        for copy in copies:
            copy.start()


def wait_all(step, at, copies):
    @pl.when(step == at)
    def wait():
        for copy in copies:
            copy.wait()


def mixer_forward_kernel(
    info_ref,
    after_ref,
    stream_ref,
    gain_ref,
    w_beta_ref,
    taps_ref,
    out_gain_ref,
    qkv_own_ref,
    out_own_ref,
    qkv_came_ref,
    qkv_twin_ref,
    out_came_ref,
    out_twin_ref,
    middle_ref,
    strengths_ref,
    linear_ref,
    out_ref,
    fresh_ref,
    solve_ref,
    states_ref,
    moves_ref,
    normed_ref,
    w_qkv_ref,
    w_out_ref,
    sems,
):
    step = pl.program_id(0)
    length = stream_ref.shape[0]
    spans = length // SPAN
    heads = linear_ref.shape[2] // LANES
    refs = (qkv_own_ref, out_own_ref, qkv_came_ref, qkv_twin_ref, out_came_ref, out_twin_ref)
    own_qkv, own_out, qkv, out = mixer_copies(info_ref, refs, w_qkv_ref, w_out_ref, sems)
    start_all(step, [own_qkv, own_out])

    @pl.when(step == 0)
    def first():
        stream = stream_ref[...].astype(WIDE)
        normed_ref[0] = low(stream * norm_scale(stream, 1e-6) * gain_ref[...])
        apart_order(info_ref, normed_ref.at[0], normed_ref.at[1])
        strengths_ref[...] = mm(normed_ref[0], w_beta_ref[...])
        middle_ref[...] = stream

    normed = normed_ref[step]
    wait_all(step, 0, [own_qkv, own_out])
    wait_all(step, 1, qkv + out)
    start_all(step, qkv + out)
    active = []
    for which in range(3):
        linear = mm(normed, w_qkv_ref[step, which])
        linear_ref[which] = low(linear)
        total = conv_silu(linear, taps_ref[which])
        active.append(total * sigmoid(total))
    rows, cols, apart, near = pair_masks()
    strict = (rows > cols) & near
    lower = (rows >= cols) & near
    queries, keys, values, betas = [], [], [], []
    for head in range(heads):
        lanes = slice(head * LANES, (head + 1) * LANES)
        query, key = active[0][:, lanes], active[1][:, lanes]
        queries.append(low(query * lax.rsqrt(jnp.sum(query * query, axis=1, keepdims=True) + 1e-6)))
        keys.append(low(key * lax.rsqrt(jnp.sum(key * key, axis=1, keepdims=True) + 1e-6)))
        values.append(low(active[2][:, lanes]))
        betas.append(sigmoid(pick_lane(strengths_ref[...], step * heads + head)))
    cells = [(head, pair) for head in range(heads) for pair in range(length // PAIR)]

    def part(array, pair):
        return array[pair * PAIR : (pair + 1) * PAIR]

    systems = []
    for head, pair in cells:
        key = part(keys[head], pair)
        systems.append(jnp.where(strict, mm_nt(key, key) * part(betas[head], pair), 0.0))
    solved = [low(item) for item in inverse(systems, apart)]
    both = {}
    scores = {}
    for (head, pair), solve in zip(cells, solved):
        solve_ref[head, pair] = solve
        beta = part(betas[head], pair)
        key = part(keys[head], pair)
        right = jnp.concatenate(
            [low(beta * key.astype(WIDE)), low(beta * part(values[head], pair).astype(WIDE))], axis=1
        )
        both[head, pair] = mm(solve, right)
        scores[head, pair] = low(jnp.where(lower, mm_nt(part(queries[head], pair), key), 0.0))

    def span_of(array, span):
        return array[span * SPAN : (span + 1) * SPAN]

    def both_of(head, span):
        return span_of(both[head, span // 2], span % 2)

    states = [[None] * spans for head in range(heads)]
    turns = {}
    for head in range(heads):
        for span in range(spans - 1):
            turns[head, span] = mm_tn(span_of(keys[head], span), low(both_of(head, span)))
    for span in range(1, spans):
        for head in range(heads):
            turn = turns[head, span - 1]
            if span == 1:
                states[head][span] = turn[:, LANES:]
            else:
                before = states[head][span - 1]
                move = low(turn[:, :LANES])
                moves_ref[head, span - 2] = move
                states[head][span] = before + turn[:, LANES:] - mm(move, low(before))
    fresh = {}
    carried = {}
    for head in range(heads):
        for span in range(spans):
            item = both_of(head, span)
            if span == 0:
                fresh[head, span] = low(item[:, LANES:])
                carried[head, span] = jnp.zeros((SPAN, LANES), WIDE)
            else:
                state = low(states[head][span])
                states_ref[head, span - 1] = state
                left = jnp.concatenate([low(item[:, :LANES]), span_of(queries[head], span)], axis=0)
                seen = mm(left, state)
                fresh[head, span] = low(item[:, LANES:] - seen[:SPAN])
                carried[head, span] = seen[SPAN:]
    normed_out = []
    for head in range(heads):
        lanes = slice(head * LANES, (head + 1) * LANES)
        pieces = []
        for pair in range(length // PAIR):
            piece = jnp.concatenate([fresh[head, 2 * pair], fresh[head, 2 * pair + 1]], axis=0)
            fresh_ref[pair * PAIR : (pair + 1) * PAIR, lanes] = piece
            base = jnp.concatenate([carried[head, 2 * pair], carried[head, 2 * pair + 1]], axis=0)
            pieces.append(base + mm(scores[head, pair], piece))
        output = jnp.concatenate(pieces, axis=0)
        out_ref[:, lanes] = low(output)
        normed_out.append(low(output * norm_scale(output, 1e-5) * out_gain_ref[...]))
    middle_ref[...] += mm(jnp.concatenate(normed_out, axis=1), w_out_ref[step])


def cost(micros):
    return pl.CostEstimate(flops=int(micros * 1.1e9), bytes_accessed=2**20, transcendentals=0)


def params(**extra):
    return pltpu.CompilerParams(dimension_semantics=("arbitrary",), vmem_limit_bytes=VMEM, **extra)


def mixer_forward(info, after, stream, gain, weights, w_beta, taps, out_gain):
    length, width = stream.shape
    tile = weights[0].shape[2]
    inner = 2 * tile
    heads = inner // LANES
    spans = length // SPAN
    pairs = length // PAIR
    here = tile // LANES
    out = jax.ShapeDtypeStruct
    return pl.pallas_call(
        mixer_forward_kernel,
        name="mixer_forward",
        grid_spec=pltpu.PrefetchScalarGridSpec(
            num_scalar_prefetch=1,
            grid=(2,),
            in_specs=[
                ANYWHERE,
                whole((length, width)),
                whole((1, width)),
                whole((width, LANES)),
                tiled((3, taps.shape[1], tile), 2),
                whole((1, LANES)),
            ]
            + [ANYWHERE] * 6,
            out_specs=[
                whole((length, width)),
                whole((length, LANES)),
                tiled((3, length, tile), 2),
                tiled((length, tile), 1),
                tiled((length, tile), 1),
                tiled((here, pairs, PAIR, PAIR), 0),
                tiled((here, spans - 1, LANES, LANES), 0),
                tiled((here, spans - 2, LANES, LANES), 0),
            ],
            scratch_shapes=[
                pltpu.VMEM((2, length, width), LOW),
                pltpu.VMEM((2, 3, width, tile), LOW),
                pltpu.VMEM((2, tile, width), LOW),
                pltpu.SemaphoreType.DMA((6,)),
            ],
        ),
        out_shape=[
            out((length, width), WIDE),
            out((length, LANES), WIDE),
            out((3, length, inner), LOW),
            out((length, inner), LOW),
            out((length, inner), LOW),
            out((heads, pairs, PAIR, PAIR), LOW),
            out((heads, spans - 1, LANES, LANES), LOW),
            out((heads, spans - 2, LANES, LANES), LOW),
        ],
        compiler_params=params(),
        cost_estimate=cost(14),
    )(info, after, stream, gain, w_beta, taps, out_gain, *weights)


def or_keep(kernel, inputs, outputs, first_kept, in_place=0):
    def either(*refs):
        start = 1 + inputs
        old = refs[start : start + outputs - first_kept]
        rest = refs[start + len(old) :]

        @pl.when(refs[0][8] == 1)
        def compute():
            kernel(*refs[:start], *rest)

        @pl.when(refs[0][8] == 0)
        def keep():
            for source, target in zip(old[: len(old) - in_place], rest[first_kept:outputs]):
                target[...] = source[...]

    return either


def mixer_backward_kernel(
    info_ref,
    after_ref,
    also_ref,
    stream_ref,
    branch_ref,
    strengths_ref,
    linear_ref,
    out_ref,
    fresh_ref,
    solve_ref,
    states_ref,
    moves_ref,
    gain_ref,
    w_beta_ref,
    taps_ref,
    out_gain_ref,
    qkv_own_ref,
    out_own_ref,
    qkv_came_ref,
    qkv_twin_ref,
    out_came_ref,
    out_twin_ref,
    stream_grad_ref,
    gain_grad_ref,
    stack_ref,
    strengths_grad_ref,
    taps_grad_ref,
    out_gain_grad_ref,
    normed_grad_ref,
    strengths_sum_ref,
    branch_low_ref,
    normed_ref,
    w_qkv_ref,
    w_out_ref,
    sems,
):
    step = pl.program_id(0)
    steps = pl.num_programs(0)
    length = stream_ref.shape[0]
    spans = length // SPAN
    pairs = length // PAIR
    tile = stack_ref.shape[2]
    heads = tile // LANES
    refs = (qkv_own_ref, out_own_ref, qkv_came_ref, qkv_twin_ref, out_came_ref, out_twin_ref)
    own_qkv, own_out, qkv, out = mixer_copies(info_ref, refs, w_qkv_ref, w_out_ref, sems)
    start_all(step, [own_out, own_qkv])

    @pl.when(step == 0)
    def first():
        branch_low_ref[...] = low(branch_ref[...])
        stream = stream_ref[...].astype(WIDE)
        normed_ref[...] = low(stream * norm_scale(stream, 1e-6) * gain_ref[...])
        out_gain_grad_ref[...] = jnp.zeros_like(out_gain_grad_ref)
        strengths_sum_ref[...] = jnp.zeros_like(strengths_sum_ref)
        normed_grad_ref[...] = jnp.zeros_like(normed_grad_ref)

    columns = pl.ds(pl.multiple_of(step * tile, tile), tile)
    stack_ref[4] = branch_low_ref[:, columns]
    stack_ref[5] = normed_ref[:, columns]
    rows, cols, apart, near = pair_masks()
    strict = (rows > cols) & near
    lower = (rows >= cols) & near
    upper_strict = (rows < cols) & near
    upper = (rows <= cols) & near
    cells = [(head, pair) for head in range(heads) for pair in range(pairs)]

    def part(array, pair):
        return array[pair * PAIR : (pair + 1) * PAIR]

    def span_of(array, span):
        return array[span * SPAN : (span + 1) * SPAN]

    wait_all(step, 0, [own_out, own_qkv])
    wait_all(step, 1, out + qkv)
    start_all(step, out + qkv)
    normed_out_grad = mm_nt(branch_low_ref[...], w_out_ref[step])
    totals, gates, active = [], [], []
    for which in range(3):
        total = conv_silu(linear_ref[which].astype(WIDE), taps_ref[which])
        gate = sigmoid(total)
        totals.append(total)
        gates.append(gate)
        active.append(total * gate)
    query_scales, key_scales = [], []
    queries, keys, values, betas, output_grads = [], [], [], [], []
    for head in range(heads):
        lanes = slice(head * LANES, (head + 1) * LANES)
        query, key = active[0][:, lanes], active[1][:, lanes]
        query_scales.append(lax.rsqrt(jnp.sum(query * query, axis=1, keepdims=True) + 1e-6))
        key_scales.append(lax.rsqrt(jnp.sum(key * key, axis=1, keepdims=True) + 1e-6))
        queries.append(low(query * query_scales[head]))
        keys.append(low(key * key_scales[head]))
        values.append(low(active[2][:, lanes]))
        betas.append(sigmoid(pick_lane(strengths_ref[...], step * heads + head)))
        output = out_ref[:, lanes].astype(WIDE)
        scale = norm_scale(output, 1e-5)
        grad = normed_out_grad[:, lanes]
        stack_ref[3, :, lanes] = low(output * scale * out_gain_ref[...])
        scaled = out_gain_ref[...] * grad
        inner = jnp.mean(output * scaled, axis=1, keepdims=True)
        output_grads.append(low(scale * (scaled - output * (scale * scale * inner))))
        out_gain_grad_ref[...] += jnp.sum(grad * output * scale, axis=0, keepdims=True)
    fresh = [fresh_ref[:, head * LANES : (head + 1) * LANES] for head in range(heads)]

    scores_back, score_grads, score_grads_back = {}, {}, {}
    for head, pair in cells:
        query, key = part(queries[head], pair), part(keys[head], pair)
        grad, new = part(output_grads[head], pair), part(fresh[head], pair)
        scores_back[head, pair] = low(jnp.where(upper, mm_nt(key, query), 0.0))
        score_grads[head, pair] = low(jnp.where(lower, mm_nt(grad, new), 0.0))
        score_grads_back[head, pair] = low(jnp.where(upper, mm_nt(new, grad), 0.0))
    inside, early = {}, {}
    for head, pair in cells:
        inside[head, pair] = mm(scores_back[head, pair], part(output_grads[head], pair))
    for head, pair in cells:
        early[head, pair] = mm_tn(solve_ref[head, pair], low(inside[head, pair]))
    returns = {}
    for head in range(heads):
        for span in range(1, spans):
            beta = span_of(betas[head], span)
            back = low(-beta * span_of(early[head, span // 2], span % 2))
            left = jnp.concatenate([span_of(queries[head], span), span_of(keys[head], span)], axis=0)
            right = jnp.concatenate([span_of(output_grads[head], span), back], axis=0)
            returns[head, span] = mm_tn(left, right)
    state_grads = {}
    for span in range(spans - 2, -1, -1):
        for head in range(heads):
            if span == spans - 2:
                state_grads[head, span] = returns[head, span + 1]
            else:
                after = state_grads[head, span + 1]
                state_grads[head, span] = (
                    after + returns[head, span + 1] - mm_tn(moves_ref[head, span], low(after))
                )
    fresh_add = {}
    for head, pair in cells:
        pieces = []
        for span in (2 * pair, 2 * pair + 1):
            if span == spans - 1:
                pieces.append(jnp.zeros((SPAN, LANES), WIDE))
            else:
                pieces.append(mm(span_of(keys[head], span), low(state_grads[head, span])))
        fresh_add[head, pair] = low(jnp.concatenate(pieces, axis=0))
    lasts, backs = {}, {}
    for head, pair in cells:
        last = early[head, pair] + mm_tn(solve_ref[head, pair], fresh_add[head, pair])
        lasts[head, pair] = last
        backs[head, pair] = part(betas[head], pair) * last
    system_grads, system_grads_back = {}, {}
    for head, pair in cells:
        last, new = low(lasts[head, pair]), part(fresh[head], pair)
        system_grads[head, pair] = low(jnp.where(strict, -mm_nt(last, new), 0.0))
        system_grads_back[head, pair] = low(jnp.where(upper_strict, -mm_nt(new, last), 0.0))
    query_grads, key_grads, beta_grads = [], [], []
    for head in range(heads):
        query_pieces, key_pieces, beta_pieces = [], [], []
        for pair in range(pairs):
            query, key = part(queries[head], pair), part(keys[head], pair)
            beta, new = part(betas[head], pair), part(fresh[head], pair)
            grad = part(output_grads[head], pair)
            stacked = jnp.concatenate(
                [score_grads[head, pair], system_grads[head, pair]], axis=0
            )
            through = mm(stacked, key)
            query_grad = through[:PAIR]
            key_grad = beta * through[PAIR:]
            wide = jnp.concatenate(
                [score_grads_back[head, pair], system_grads_back[head, pair]], axis=1
            )
            tall = jnp.concatenate([query, low(beta * key.astype(WIDE))], axis=0)
            key_grad = key_grad + mm(wide, tall)
            inner = low(jnp.where(strict, mm_nt(key, key), 0.0))
            residual = part(values[head], pair).astype(WIDE) - mm(inner, new)
            back = low(backs[head, pair])
            more_query, more_key, seen = [], [], []
            for local_span in range(2):
                span = 2 * pair + local_span
                new_span = span_of(new, local_span)
                if span == 0:
                    more_query.append(jnp.zeros((SPAN, LANES), WIDE))
                    seen.append(jnp.zeros((SPAN, LANES), WIDE))
                    more_key.append(mm_nt(new_span, low(state_grads[head, span])))
                    continue
                state = states_ref[head, span - 1]
                more_query.append(mm_nt(span_of(grad, local_span), state))
                seen.append(mm(span_of(key, local_span), state))
                taken = -span_of(back, local_span)
                if span == spans - 1:
                    more_key.append(mm_nt(taken, state))
                else:
                    left = jnp.concatenate([new_span, taken], axis=1)
                    right = jnp.concatenate([low(state_grads[head, span]), state], axis=1)
                    more_key.append(mm_nt(left, right))
            residual = residual - jnp.concatenate(seen, axis=0)
            query_pieces.append(query_grad + jnp.concatenate(more_query, axis=0))
            key_pieces.append(key_grad + jnp.concatenate(more_key, axis=0))
            beta_pieces.append(jnp.sum(lasts[head, pair] * residual, axis=1, keepdims=True))
        query_grads.append(jnp.concatenate(query_pieces, axis=0))
        key_grads.append(jnp.concatenate(key_pieces, axis=0))
        beta_grads.append(jnp.concatenate(beta_pieces, axis=0))
    lane_ids = lax.broadcasted_iota(jnp.int32, (length, LANES), 1)
    strengths_sum = strengths_sum_ref[...]
    for head in range(heads):
        beta = betas[head]
        strengths_sum = strengths_sum + jnp.where(
            lane_ids == step * heads + head, beta_grads[head] * beta * (1.0 - beta), 0.0
        )
    strengths_sum_ref[...] = strengths_sum

    active_grads = []
    for grads, scales, source in ((query_grads, query_scales, active[0]), (key_grads, key_scales, active[1])):
        pieces = []
        for head in range(heads):
            lanes = slice(head * LANES, (head + 1) * LANES)
            value, scale, grad = source[:, lanes], scales[head], grads[head]
            inner = jnp.sum(value * grad, axis=1, keepdims=True)
            pieces.append(scale * (grad - value * (scale * scale * inner)))
        active_grads.append(jnp.concatenate(pieces, axis=1))
    active_grads.append(
        jnp.concatenate(
            [jnp.concatenate([backs[head, pair] for pair in range(pairs)], axis=0) for head in range(heads)],
            axis=1,
        )
    )
    normed_grad = normed_grad_ref[step]
    for which in range(3):
        total, gate = totals[which], gates[which]
        total_grad = active_grads[which] * (gate * (1.0 + total * (1.0 - gate)))
        taps = taps_ref[which]
        linear = linear_ref[which].astype(WIDE)
        count = taps.shape[0]
        linear_grad = total_grad * taps[count - 1 : count]
        taps_grad_ref[which, count - 1 : count] = jnp.sum(total_grad * linear, axis=0, keepdims=True)
        for ahead in range(1, count):
            moved = shift_up(total_grad, ahead)
            place = slice(count - 1 - ahead, count - ahead)
            linear_grad = linear_grad + moved * taps[place]
            taps_grad_ref[which, place] = jnp.sum(moved * linear, axis=0, keepdims=True)
        linear_low = low(linear_grad)
        stack_ref[which] = linear_low
        normed_grad = normed_grad + mm_nt(linear_low, w_qkv_ref[step, which])
    normed_grad_ref[step] = normed_grad

    @pl.when(step == steps - 1)
    def last_step():
        strengths_low = low(strengths_sum_ref[...])
        strengths_grad_ref[...] = strengths_low
        add_from_apart(info_ref, normed_grad_ref.at[1], normed_grad_ref.at[0])
        total = normed_grad_ref[0] + mm_nt(strengths_low, w_beta_ref[...])
        value_grad, gain_grad = norm_back(stream_ref[...].astype(WIDE), gain_ref[...], total, 1e-6)
        stream_grad_ref[...] = low(branch_ref[...] + value_grad)
        gain_grad_ref[...] = gain_grad


def mixer_backward(info, after, stream, branch, kept, gain, weights, w_beta, taps, out_gain, old=None):
    strengths, linear, output, fresh, solve, states, moves = kept
    length, width = stream.shape
    tile = weights[0].shape[2]
    inner = 2 * tile
    spans = length // SPAN
    pairs = length // PAIR
    here = tile // LANES
    out = jax.ShapeDtypeStruct
    count = taps.shape[1]
    in_specs = [
        ANYWHERE,
        ANYWHERE,
        whole((length, width)),
        whole((length, width)),
        whole((length, LANES)),
        tiled((3, length, tile), 2),
        tiled((length, tile), 1),
        tiled((length, tile), 1),
        tiled((here, pairs, PAIR, PAIR), 0),
        tiled((here, spans - 1, LANES, LANES), 0),
        tiled((here, spans - 2, LANES, LANES), 0),
        whole((1, width)),
        whole((width, LANES)),
        tiled((3, count, tile), 2),
        whole((1, LANES)),
    ] + [ANYWHERE] * 6
    kernel, more = mixer_backward_kernel, []
    if old is not None:
        more = old[1:]
        kernel = or_keep(kernel, len(in_specs), 6, 1)
        in_specs = in_specs + [
            whole((1, width)),
            tiled_old((6, length, tile), 2),
            whole((length, LANES)),
            tiled_old((3, count, tile), 2),
            whole((1, LANES)),
        ]
    return pl.pallas_call(
        kernel,
        name="mixer_backward",
        grid_spec=pltpu.PrefetchScalarGridSpec(
            num_scalar_prefetch=1,
            grid=(2,),
            in_specs=in_specs,
            out_specs=[
                whole((length, width)),
                whole((1, width)),
                tiled((6, length, tile), 2),
                whole((length, LANES)),
                tiled((3, count, tile), 2),
                whole((1, LANES)),
            ],
            scratch_shapes=[
                pltpu.VMEM((2, length, width), WIDE),
                pltpu.VMEM((length, LANES), WIDE),
                pltpu.VMEM((length, width), LOW),
                pltpu.VMEM((length, width), LOW),
                pltpu.VMEM((2, 3, width, tile), LOW),
                pltpu.VMEM((2, tile, width), LOW),
                pltpu.SemaphoreType.DMA((6,)),
            ],
        ),
        out_shape=[
            out((length, width), LOW),
            out((1, width), WIDE),
            out((6, length, inner), LOW),
            out((length, LANES), LOW),
            out((3, count, inner), WIDE),
            out((1, LANES), WIDE),
        ],
        compiler_params=params(),
        cost_estimate=cost(20),
    )(
        info, *after, stream, branch, strengths, linear, output, fresh, solve, states, moves,
        gain, w_beta, taps, out_gain, *weights, *more,
    )


def unit_tiles(units):
    count = -(-units // 512)
    size = -(-units // count // LANES) * LANES
    return [(start, min(size, units - start)) for start in range(0, units, size)]


def feed_tiles(refs, into_lift, into_down, sems):
    lift_ref, down_ref, lift_came, lift_twin, down_came, down_twin = refs
    tiles, at = [], 0
    for which in range(2):
        for start, size in unit_tiles(down_ref.shape[0]):
            span = pl.ds(start, size)
            if which == 0:
                lift = [(lift_ref.at[:, :, span], into_lift.at[0, :, :, span])]
                down = [(down_ref.at[span], into_down.at[0, span])]
            else:
                rows, columns = lift_came.shape[1], down_came.shape[1]
                lift = [
                    (lift_came.at[:, :, span], into_lift.at[1, :, pl.ds(0, rows), span]),
                    (lift_twin.at[:, :, span], into_lift.at[1, :, pl.ds(rows, rows), span]),
                ]
                down = [
                    (down_came.at[span], into_down.at[1, span, pl.ds(0, columns)]),
                    (down_twin.at[span], into_down.at[1, span, pl.ds(columns, columns)]),
                ]
            copies = []
            for group in (lift, down):
                copies.append([pltpu.make_async_copy(*pair, sems.at[at + i]) for i, pair in enumerate(group)])
                at += len(group)
            tiles.append((which, start, size, copies[0], copies[1]))
    return tiles


def start_each(copies):
    for copy in copies:
        copy.start()


def wait_each(copies):
    for copy in copies:
        copy.wait()


AHEAD = 3


def feed_forward_kernel(
    info_ref,
    middle_ref,
    gain_ref,
    lift_own_ref,
    down_own_ref,
    lift_came_ref,
    lift_twin_ref,
    down_came_ref,
    down_twin_ref,
    result_ref,
    lifted_ref,
    total_ref,
    normed_ref,
    w_gate_up_ref,
    w_down_ref,
    kept_ref,
    sems,
    out_sems,
):
    units = down_own_ref.shape[0]
    refs = (lift_own_ref, down_own_ref, lift_came_ref, lift_twin_ref, down_came_ref, down_twin_ref)
    tiles = feed_tiles(refs, w_gate_up_ref, w_down_ref, sems)
    for tile in tiles[:AHEAD]:
        start_each(tile[3] + tile[4])
    middle = middle_ref[...]
    normed_ref[0] = low(middle * norm_scale(middle, 1e-6) * gain_ref[...])
    apart_order(info_ref, normed_ref.at[0], normed_ref.at[1])
    outs = []
    lifted = []
    for index in range(len(tiles) + 1):
        if index < len(tiles):
            which, start, size, lift, down = tiles[index]
            wait_each(lift)
        if index:
            wait_each(tiles[index - 1][4])
        if 0 < index <= len(tiles) - AHEAD:
            start_each(tiles[index + AHEAD - 1][3] + tiles[index + AHEAD - 1][4])
        if index < len(tiles):
            span = pl.ds(start, size)
            normed = normed_ref[which]
            gate = mm(normed, w_gate_up_ref[which, 0, :, span])
            up = mm(normed, w_gate_up_ref[which, 1, :, span])
            place = pl.ds(which * units + start, size)
            kept_ref[0, :, place] = low(gate)
            kept_ref[1, :, place] = low(up)
            lifted.append((gate, up))
        if index:
            which, start, size, lift, down = tiles[index - 1]
            span = pl.ds(start, size)
            place = pl.ds(which * units + start, size)
            outs.append(
                pltpu.make_async_copy(
                    kept_ref.at[:, :, place], lifted_ref.at[:, :, place], out_sems.at[index - 1]
                )
            )
            outs[-1].start()
            gate, up = lifted[index - 1]
            hidden = low(gate * sigmoid(gate) * up)
            part = mm(hidden, w_down_ref[which, span, :])
            if start:
                total_ref[which] += part
            else:
                total_ref[which] = part + middle if which == 0 else part
    add_from_apart(info_ref, total_ref.at[1], total_ref.at[0], DOWN)
    result_ref[...] = low(total_ref[0])
    wait_each(outs)


def feed_forward(info, middle, gain, weights):
    length, width = middle.shape
    units = weights[1].shape[0]
    count = 2 * len(unit_tiles(units))
    out = jax.ShapeDtypeStruct
    return pl.pallas_call(
        feed_forward_kernel,
        name="feed_forward",
        grid_spec=pltpu.PrefetchScalarGridSpec(
            num_scalar_prefetch=1,
            grid=(1,),
            in_specs=[whole((length, width)), whole((1, width))] + [ANYWHERE] * 6,
            out_specs=[whole((length, width)), ANYWHERE],
            scratch_shapes=[
                pltpu.VMEM((2, length, width), WIDE),
                pltpu.VMEM((2, length, width), LOW),
                pltpu.VMEM((2, 2, width, units), LOW),
                pltpu.VMEM((2, units, width), LOW),
                pltpu.VMEM((2, length, 2 * units), LOW),
                pltpu.SemaphoreType.DMA((3 * count,)),
                pltpu.SemaphoreType.DMA((count,)),
            ],
        ),
        out_shape=[out((length, width), LOW), out((2, length, 2 * units), LOW)],
        compiler_params=params(),
        cost_estimate=cost(10),
    )(info, middle, gain, *weights)


def feed_backward_kernel(
    info_ref,
    after_ref,
    middle_ref,
    grad_ref,
    gain_ref,
    lifted_ref,
    lift_own_ref,
    down_own_ref,
    lift_came_ref,
    lift_twin_ref,
    down_came_ref,
    down_twin_ref,
    middle_grad_ref,
    gain_grad_ref,
    stack_ref,
    normed_grad_ref,
    grads_ref,
    w_gate_up_ref,
    w_down_ref,
    kept_ref,
    made_ref,
    sems,
    in_sems,
    out_sems,
):
    width = middle_ref.shape[1]
    units = down_own_ref.shape[0]
    refs = (lift_own_ref, down_own_ref, lift_came_ref, lift_twin_ref, down_came_ref, down_twin_ref)
    tiles = feed_tiles(refs, w_gate_up_ref, w_down_ref, sems)
    ins, outs = [], []
    for index, (which, start, size, lift, down) in enumerate(tiles):
        place = pl.ds(which * units + start, size)
        ins.append(pltpu.make_async_copy(lifted_ref.at[:, :, place], kept_ref.at[:, :, place], in_sems.at[index]))
        outs.append(
            pltpu.make_async_copy(
                made_ref.at[pl.ds(0, 3), :, place], stack_ref.at[pl.ds(0, 3), :, place], out_sems.at[index]
            )
        )
    for index in range(AHEAD):
        start_each(tiles[index][4] + [ins[index]] + tiles[index][3])
    middle = middle_ref[...]
    made_ref[3] = jnp.zeros(made_ref.shape[1:], LOW)
    made_ref[3, :, :width] = low(middle * norm_scale(middle, 1e-6) * gain_ref[...])
    made_ref[3, :, units : units + width] = grad_ref[...]
    ends = pltpu.make_async_copy(made_ref.at[3], stack_ref.at[3], out_sems.at[len(tiles)])
    ends.start()
    grads_ref[0] = grad_ref[...]
    apart_order(info_ref, grads_ref.at[0], grads_ref.at[1], DOWN)
    hidden_grads = []
    for index in range(len(tiles) + 1):
        if index < len(tiles):
            which, start, size, lift, down = tiles[index]
            wait_each(down)
        if index:
            ins[index - 1].wait()
            wait_each(tiles[index - 1][3])
        if 0 < index <= len(tiles) - AHEAD:
            more = index + AHEAD - 1
            start_each(tiles[more][4] + [ins[more]] + tiles[more][3])
        if index < len(tiles):
            span = pl.ds(start, size)
            hidden_grads.append(mm_nt(grads_ref[which], w_down_ref[which, span, :]))
        if index:
            which, start, size, lift, down = tiles[index - 1]
            span = pl.ds(start, size)
            place = pl.ds(which * units + start, size)
            hidden_grad = hidden_grads[index - 1]
            gate = kept_ref[0, :, place].astype(WIDE)
            up = kept_ref[1, :, place].astype(WIDE)
            open_ = sigmoid(gate)
            silu = gate * open_
            up_grad = low(hidden_grad * silu)
            gate_grad = low(hidden_grad * up * (open_ + silu * (1.0 - open_)))
            made_ref[0, :, place] = gate_grad
            made_ref[1, :, place] = up_grad
            made_ref[2, :, place] = low(silu * up)
            outs[index - 1].start()
            part = mm_nt(gate_grad, w_gate_up_ref[which, 0, :, span]) + mm_nt(
                up_grad, w_gate_up_ref[which, 1, :, span]
            )
            if start:
                normed_grad_ref[which] += part
            else:
                normed_grad_ref[which] = part
    add_from_apart(info_ref, normed_grad_ref.at[1], normed_grad_ref.at[0])
    value_grad, gain_grad = norm_back(middle, gain_ref[...], normed_grad_ref[0], 1e-6)
    middle_grad_ref[...] = grad_ref[...].astype(WIDE) + value_grad
    gain_grad_ref[...] = gain_grad
    wait_each(outs)
    ends.wait()


def feed_backward(info, after, middle, grad, lifted, gain, weights, old=None):
    length, width = middle.shape
    units = weights[1].shape[0]
    count = 2 * len(unit_tiles(units))
    out = jax.ShapeDtypeStruct
    in_specs = [ANYWHERE, whole((length, width)), whole((length, width)), whole((1, width))] + [ANYWHERE] * 7
    kernel, more, aliases = feed_backward_kernel, [], {}
    if old is not None:
        more = old[1:]
        kernel = or_keep(kernel, len(in_specs), 3, 1, 1)
        in_specs = in_specs + [whole((1, width)), ANYWHERE]
        aliases = {len(in_specs): 2}
    return pl.pallas_call(
        kernel,
        name="feed_backward",
        grid_spec=pltpu.PrefetchScalarGridSpec(
            num_scalar_prefetch=1,
            grid=(1,),
            in_specs=in_specs,
            out_specs=[whole((length, width)), whole((1, width)), ANYWHERE],
            scratch_shapes=[
                pltpu.VMEM((2, length, width), WIDE),
                pltpu.VMEM((2, length, width), LOW),
                pltpu.VMEM((2, 2, width, units), LOW),
                pltpu.VMEM((2, units, width), LOW),
                pltpu.VMEM((2, length, 2 * units), LOW),
                pltpu.VMEM((4, length, 2 * units), LOW),
                pltpu.SemaphoreType.DMA((3 * count,)),
                pltpu.SemaphoreType.DMA((count,)),
                pltpu.SemaphoreType.DMA((count + 1,)),
            ],
        ),
        out_shape=[
            out((length, width), WIDE),
            out((1, width), WIDE),
            out((4, length, 2 * units), LOW),
        ],
        input_output_aliases=aliases,
        compiler_params=params(),
        cost_estimate=cost(13),
    )(info, after, middle, grad, gain, lifted, *weights, *more)


def rows_kernel(halves, width, count, info_ref, after_ref, *refs):
    lefts, rights = refs[:count], refs[count : 2 * count]
    keep_ref, send_ref, turned_ref, rows_ref = refs[2 * count :]
    size = width // halves // 8

    @pl.when((pl.program_id(0) == 0) & (pl.program_id(1) == 0))
    def first():
        for item in range(count):
            turned_ref[item] = lefts[item][:, :width].T
            place = 0
            for which in range(halves):
                for index in (0, 2, 1, 3):
                    start = which * (width // halves) + info_ref[index] * size
                    source = pl.ds(pl.multiple_of(start, size), size)
                    rows_ref[item, place : place + size, :] = turned_ref[item, source, :]
                    place += size

    tile = keep_ref.shape[1]
    if rights[0].shape[1] == tile:
        pieces = [right[...] for right in rights]
    else:
        columns = pl.ds(pl.multiple_of(pl.program_id(1) * tile, tile), tile)
        pieces = [right[:, columns] for right in rights]
    total = mm(rows_ref[0], pieces[0])
    for item in range(1, count):
        total = total + mm(rows_ref[item], pieces[item])
    half = keep_ref.shape[0]
    keep_ref[...] = low(total[:half])
    send_ref[...] = low(total[half:])


def rows_grads(info, after, items, left, right, groups, halves, tile, tiles):
    length = items[0].shape[1]
    count = len(items)
    rows = left[3] // 2
    spread = 1 if right[1] == tile else 0
    half = pl.BlockSpec((None, rows // 2, tile), lambda g, t, info: (g, 0, t))
    shape = jax.ShapeDtypeStruct((groups, rows // 2, tile * tiles), LOW)
    return pl.pallas_call(
        lambda *refs: rows_kernel(halves, left[3], count, *refs),
        name="rows_grads",
        grid_spec=pltpu.PrefetchScalarGridSpec(
            num_scalar_prefetch=1,
            grid=(groups, tiles),
            in_specs=[ANYWHERE]
            + [pl.BlockSpec((None, length, left[1]), lambda g, t, info: (left[0], 0, left[2]))] * count
            + [pl.BlockSpec((None, length, right[1]), lambda g, t, info: (right[0] + g, 0, right[2] + spread * t))]
            * count,
            out_specs=[half, half],
            scratch_shapes=[pltpu.VMEM((count, left[3], length), LOW), pltpu.VMEM((count, rows, length), LOW)],
        ),
        out_shape=[shape, shape],
        compiler_params=pltpu.CompilerParams(
            dimension_semantics=("arbitrary", "arbitrary"), vmem_limit_bytes=VMEM
        ),
        cost_estimate=cost(1),
    )(info, after, *items, *items)


def halve(after, keep, came, axis):
    def kernel(after_ref, keep_ref, came_ref, *outs):
        total = keep_ref[...].astype(WIDE) + came_ref[...].astype(WIDE)
        if axis is None:
            outs[0][...] = total
        else:
            size = total.shape[axis - 1] // 2
            for i in range(2):
                at = slice(i * size, (i + 1) * size)
                outs[i][...] = low(total[at] if axis == 1 else total[:, at])

    groups, rows, columns = keep.shape
    shape = {None: (rows, columns), 1: (rows // 2, columns), 2: (rows, columns // 2)}[axis]
    count, dtype = (1, WIDE) if axis is None else (2, LOW)
    block = pl.BlockSpec((None, rows, columns), lambda g: (g, 0, 0))
    return pl.pallas_call(
        kernel,
        name="halve",
        grid=(groups,),
        in_specs=[ANYWHERE, block, block],
        out_specs=[pl.BlockSpec((None, *shape), lambda g: (g, 0, 0))] * count,
        out_shape=[jax.ShapeDtypeStruct((groups, *shape), dtype)] * count,
        compiler_params=params(),
        cost_estimate=cost(0.01),
    )(after, keep, came)


def tied(*values):
    return lax.optimization_barrier(values)


def exchange(value, axis, apart):
    return lax.ppermute(value, axis, [(i, i ^ apart(i)) for i in range(lax.axis_size(axis))])


def unpack(packed, like):
    found, start = [], 0
    for item in like:
        found.append(packed[start : start + item.size].reshape(item.shape))
        start += item.size
    return found


def pack(items):
    return jnp.concatenate([item.reshape(-1) for item in items])


def local(
    inputs, cotangent, w_qkv, w_beta, conv_taps, w_out, w_gate_up, w_down, norm_gains, out_gains
):
    batches, unused, length, width = inputs.shape
    place = lax.axis_index("section")
    rank, half = place // 2, place % 2
    me, copies = lax.axis_index("dp"), lax.axis_size("dp")
    per = batches // 2
    cube = copies == 8

    def across(value, bits=1):
        return exchange(value, "section", lambda i: bits)

    def flip(value, even, odd):
        return exchange(value, "dp", lambda i: odd if i % 2 else even)

    def by_half(own, other, axis):
        return jnp.where(
            half == 0, jnp.concatenate([own, other], axis), jnp.concatenate([other, own], axis)
        )

    first_apart = 2 + 2 * (me % 2)

    def mine_of(value, axis):
        size = value.shape[axis] // copies
        return lax.dynamic_slice_in_dim(value, me * size, size, axis)

    def collect(came, axis):
        came = jnp.concatenate([came, flip(came, 2, 4)], axis)
        came = jnp.concatenate([came, flip(came, 4, 2)], axis)
        return came, flip(came, 1, 1)

    smalls = [conv_taps, w_beta.astype(WIDE), norm_gains, out_gains]
    others = unpack(across(pack(smalls)), smalls)
    taps = jnp.concatenate([conv_taps, others[0]], 2)
    heads = w_beta.shape[1]
    w_beta = jnp.concatenate([w_beta, low(others[1])], 1)
    w_beta = jnp.pad(w_beta, ((0, 0), (0, LANES - 2 * heads)))
    gains = by_half(norm_gains, others[2], 1)
    out_gain = by_half(out_gains, others[3], 0)[None]
    inner, units = w_out.shape[0], w_down.shape[0]
    tile = w_qkv.shape[2]

    if cube:
        block = width // copies
        core = me % 2
        corner = 2 * ((me // 2 + me // 4) % 2) + core
        quarter, rows = width // 4, inner // 2
        came = across(mine_of(w_qkv, 1))
        came, lift = tied(came, mine_of(w_gate_up, 1))
        lift = across(lift)
        lift, out = tied(lift, lax.dynamic_slice_in_dim(w_out, core * rows, rows, 0))
        out = across(out)
        out, down = tied(out, lax.dynamic_slice_in_dim(w_down, corner * quarter, quarter, 1))
        down = across(down)
        mixer_weights = (w_qkv, w_out, *collect(came, 1), out, flip(out, 1, 1))
        near = flip(lift, 2, 4)
        lift = jnp.concatenate([lift, near], 1)
        far = flip(lift, 4, 2)
        apart = [0, first_apart, 6 - first_apart, 6, 1, 7 - first_apart, 1 + first_apart, 7]
        places = [me ^ bits for bits in apart]
        down_places = [2 * (corner ^ bits) + i for bits in (0, 2, 1, 3) for i in range(2)]
    else:

        def gathered(value):
            return lax.all_gather(across(mine_of(value, 1)), "dp", axis=1, tiled=True)

        def halves_of(value):
            return jnp.split(gathered(value), 2, 1)

        out = lax.all_gather(across(mine_of(w_out, 0)), "dp", axis=0, tiled=True)
        mixer_weights = (w_qkv, w_out, *halves_of(w_qkv), *jnp.split(out, 2, 0))
        feed_weights = (w_gate_up, w_down, *halves_of(w_gate_up), *halves_of(w_down))
        places = down_places = list(range(8))
        core, near = 0, taps
    info = jnp.stack([jnp.asarray(item, jnp.int32) for item in places + [rank == 0] + down_places + [core, 1 - core]])

    def mixer_part(after, stream):
        return mixer_forward(info, after, stream, gains[0:1], mixer_weights, w_beta, taps, out_gain)

    def feed_back(after, grad, saved, old=None):
        stream, middle, kept, lifted = saved
        return feed_backward(info, after, middle, grad, lifted, gains[1:2], feed_weights, old)

    def mixer_back(after, middle_grad, saved, old=None):
        stream, middle, kept, lifted = saved
        return mixer_backward(
            info, after, stream, middle_grad, kept, gains[0:1], mixer_weights, w_beta, taps, out_gain, old
        )

    def own(value):
        items = lax.dynamic_slice_in_dim(value, half * per, per, 0)
        return [items[i, 0] for i in range(per)]

    up = [(0, 2), (1, 3)]
    streams = own(inputs)
    saved0 = []
    for stream in streams:
        near, *kept = mixer_part(near, stream)
        saved0.append([stream, near, kept])
    if cube:
        far, down, saved0[0][1] = tied(far, down, saved0[0][1])
        lift = jnp.concatenate([lift, far], 1)
        lift_twin = flip(lift, 1, 1)
        down = jnp.concatenate([down, flip(down, 2, 4)], 1)
        down, saved0[-1][1] = tied(down, saved0[-1][1])
        feed_weights = (w_gate_up, w_down, lift, lift_twin, down, flip(down, 1, 1))
    firsts = []
    for saved in saved0:
        result, lifted = feed_forward(info, saved[1], gains[1:2], feed_weights)
        saved.append(lifted)
        firsts.append(result)
    saved1, results = [], []
    for index in range(per):
        stream = lax.ppermute(firsts[index], "section", up)
        middle, *kept = mixer_part(taps, stream)
        if index + 1 < per:
            firsts[index + 1], middle = tied(firsts[index + 1], middle)
        result, lifted = feed_forward(info, middle, gains[1:2], feed_weights)
        saved1.append([stream, middle, kept, lifted])
        results.append(result)
    returned, feeds, mixes = [], [], []
    for grad, saved in zip(own(cotangent), saved1):
        feeds.append(feed_back(taps, grad, saved))
        mixes.append(mixer_back((taps, taps), feeds[-1][0], saved))
        returned.append(lax.ppermute(mixes[-1][0], "section", [(2, 0), (3, 1)]))
    feed_twins, mix_twins = [], []
    waited = mixes[-1][0]
    for index, (grad, saved) in enumerate(zip(returned, saved0)):
        feeds[index] = feed_back(waited, grad, saved, feeds[index])
        after = (taps, taps)
        if cube:
            feed_twins.append(flip(feeds[index][2], 1, 1))
            if index:
                after = (feed_twins[index - 1], mix_twins[index - 1])
        mixes[index] = mixer_back(after, feeds[index][0], saved, mixes[index])
        if cube:
            mix_twins.append(flip(mixes[index][2], 1, 1))
    feed_all = [feed[2] for feed in feeds] + feed_twins
    if cube:
        lifts = rows_grads(info, mixes[-1][1], feed_all, (3, units, 0, width), (0, units, 0), 2, 1, units, 2)
        lift_came = flip(lifts[1], 2, 4)
        downs = rows_grads(
            info, lifts[0], feed_all, (2, 2 * units, 0, 2 * units), (3, units, 1), 1, 2, width // 2, 2
        )
        down_came = across(downs[1])
    mix_all = [mix[2] for mix in mixes]
    if cube:
        mix_all = mix_all + mix_twins
        qkvs = rows_grads(info, downs[0], mix_all, (5, width, 0, width), (0, width, 0), 3, 1, width, 1)
        qkv_came = flip(qkvs[1], 2, 4)
        outs = rows_grads(info, qkvs[0], mix_all, (3, width, 0, width), (4, width, 0), 1, 2, width, 1)
        out_came = across(outs[1])
        lifts = halve(outs[0], lifts[0], lift_came, 1)
        lift_came = flip(lifts[1], 4, 2)
        downs = halve(lifts[0], downs[0], down_came, 1)
        down_came = flip(downs[1], 2, 4)
        outs = halve(downs[0], outs[0], out_came, 1)
        out_came = flip(outs[1], 2, 4)
        qkvs = halve(outs[0], qkvs[0], qkv_came, 1)
        qkv_came = flip(qkvs[1], 4, 2)
        marks = [qkvs[0]]
        lifts = halve(qkvs[0], lifts[0], lift_came, 2)
        lift_came = across(lifts[1])
        marks.append(lifts[0])
        downs = halve(lifts[0], downs[0], down_came, 1)
        down_came = flip(downs[1], 4, 2)
        outs = halve(downs[0], outs[0], out_came, 1)
        out_came = flip(outs[1], 4, 2)
        qkvs = halve(outs[0], qkvs[0], qkv_came, 2)
        qkv_came = across(qkvs[1])
        marks.append(qkvs[0])
        grad_down = halve(qkvs[0], downs[0], down_came, None)[0]
        marks.append(grad_down)
        grad_out = halve(grad_down, outs[0], out_came, None)[0]
        grad_gate_up = halve(grad_out, lifts[0], lift_came, None)[0]
        grad_qkv = halve(grad_gate_up, qkvs[0], qkv_came, None)[0]
        grad_down, grad_out = grad_down[0], grad_out[0]
    else:

        def tall(items, index):
            return jnp.concatenate([item[index] for item in items], 0)

        def total(value, axis, split):
            value = lax.psum_scatter(low(value), "dp", scatter_dimension=axis, tiled=True)
            size = value.shape[split] // 2
            mine = lax.slice_in_dim(value, 0, size, axis=split)
            theirs = lax.slice_in_dim(value, size, 2 * size, axis=split)
            return mine.astype(WIDE) + across(theirs).astype(WIDE)

        ends = tall(feed_all, 3)
        normed2, grad, normed = ends[:, :width], ends[:, units : units + width], tall(mix_all, 5)
        grad_gate_up = total(jnp.stack([mm_tn(normed2, tall(feed_all, i)) for i in range(2)]), 1, 2)
        grad_qkv = total(jnp.stack([mm_tn(normed, tall(mix_all, i)) for i in range(3)]), 1, 2)
        down = mm_tn(tall(feed_all, 2), grad).reshape(2, units, width)
        out = mm_tn(tall(mix_all, 3), tall(mix_all, 4)).reshape(2, inner, width)
        grad_down, grad_out = total(down, 1, 0)[0], total(out, 1, 0)[0]

    strengths = [mix[3] for mix in mixes]
    if cube:
        strengths[0] = tied(strengths[0], marks[0])[0]
    d_beta = sum(mm_tn(mix[5], item) for mix, item in zip(mix_all, strengths))[:, : 2 * heads]
    d_taps = sum(mix[4] for mix in mixes)
    d_gains = jnp.concatenate([sum(mix[1] for mix in mixes), sum(feed[1] for feed in feeds)], 0)
    d_out_gain = sum(mix[5] for mix in mixes)

    flat = [d_taps, d_beta, d_gains, d_out_gain]
    packed = pack(flat)
    if cube:
        for bits, mark in zip((1, 2, 4), marks[1:]):
            packed = packed + tied(flip(packed, bits, bits), mark)[0]
    else:
        packed = lax.psum(packed, "dp")
    d_taps, d_beta, d_gains, d_out_gain = unpack(packed, flat)

    def part(value, axis, size):
        return lax.dynamic_slice_in_dim(value, me * size, size, axis)

    def halves(value, axis):
        size = value.shape[axis] // 2
        return [
            lax.dynamic_slice_in_dim(value, which * size, size, axis) for which in (half, 1 - half)
        ]

    pieces = [
        [part(d_taps[:, :, i * inner : (i + 1) * inner], 2, inner // copies) for i in range(2)],
        [part(d_beta[:, i * heads : (i + 1) * heads], 0, width // copies) for i in range(2)],
        [part(item, 1, width // 2 // copies) for item in halves(d_gains, 1)],
        [part(item, 1, LANES // 2 // copies) for item in halves(d_out_gain, 1)],
    ]
    mine = [item[0] for item in pieces]
    came = unpack(across(pack([item[1] for item in pieces])), mine)
    grad_taps, grad_beta, grad_gains, grad_out_gains = [a + b for a, b in zip(mine, came)]

    held = jnp.stack([jnp.where(rank == 1, a, mix[0]) for a, mix in zip(results, mixes)])
    if cube:
        held = tied(held, marks[0])[0]
    quarter = width // 4

    def quarter_of(index):
        return lax.dynamic_slice_in_dim(held, index * quarter, quarter, 2)

    came = [across(quarter_of(place ^ bits), bits) for bits in (1, 2, 3)]
    same = by_half(quarter_of(place), came[0], 0)
    other = by_half(came[1], came[2], 0)
    final_stream = jnp.where(rank == 1, same, other)[:, None]
    final_grad = jnp.where(rank == 0, same, other)[:, None]
    return (
        final_stream,
        final_grad,
        grad_qkv,
        grad_beta,
        grad_taps,
        grad_out,
        grad_gate_up,
        grad_down,
        grad_gains,
        grad_out_gains[0],
    )


def solution(mesh):
    in_specs = (
        P(None, "dp", None, None),
        P(None, "dp", None, None),
        P(None, None, "section"),
        P(None, "section"),
        P(None, None, "section"),
        P("section", None),
        P(None, None, "section"),
        P("section", None),
        P(None, "section"),
        P("section"),
    )
    out_specs = (
        P(None, "dp", None, "section"),
        P(None, "dp", None, "section"),
        P(None, "dp", "section"),
        P("dp", "section"),
        P(None, None, ("section", "dp")),
        P(("section", "dp"), None),
        P(None, "dp", "section"),
        P(("section", "dp"), None),
        P(None, ("section", "dp")),
        P(("section", "dp")),
    )
    return jax.shard_map(local, mesh=mesh, in_specs=in_specs, out_specs=out_specs, check_vma=False)
```

time: 786 us -> 520 us (0.66)
  waiting for transfers between devices: 393 us -> 84.1 us
  Pallas kernels: 235 us -> 320 us
  starting transfers between devices: 29.8 us -> 59.2 us
  local copies, waits for them, and re-layouts: 59.9 us -> 40.3 us
  matrix products: 20.5 us -> 2.65 us
  other arithmetic: 23.5 us -> 7.21 us
  between operations: 15 us -> 1.79 us
    reduce_scatter x4 -> x0, waiting for transfers between devices: 240 us -> none  [total(): value = lax.psum_scatter(value, 'dp', scatter_dimension=axis, tiled=True)]
    pallas_call x16 -> x32, Pallas kernels: 235 us -> 320 us  [the longest x4 86.4 us: mixer_backward(): pl.pallas_call(kernel, name='mixer_backward', grid_spec=pltpu.PrefetchSca...]
    all_gather x4 -> x0, waiting for transfers between devices: 57.9 us -> none  [of_partner(): return lax.all_gather(across(mine, 1), 'dp', axis=axis, tiled=True)]
    psum x1 -> x0, waiting for transfers between devices: 46.6 us -> none  [local(): lax.psum(jnp.concatenate([item.reshape(-1) for item in flat]), 'dp')]
    ppermute x17 -> x41, waiting for transfers between devices: 46.5 us -> 84.1 us  [the longest x37 79.2 us: exchange(): lax.ppermute(value, axis, [(i, i ^ apart(i)) for i in range(lax.axis_size...]
    ppermute x17 -> x41, starting transfers between devices: 29.2 us -> 59.2 us  [the longest x37 46.4 us: exchange(): lax.ppermute(value, axis, [(i, i ^ apart(i)) for i in range(lax.axis_size...]
    dot_general x7 -> x2, matrix products: 20 us -> 2.65 us  [mm_tn(): lax.dot_general(left, right, (((0,), (0,)), ((), ())), preferred_element_...]
    concatenate x7 -> x2, local copies, waits for them, and re-layouts: 16.8 us -> 2.18 us  [the longest x1 1.21 us: local(): lift = jnp.concatenate([lift, far], 1)]
  transfers between devices with their start and end apart: 26 -> 41, of which waited for: 12 -> 15; matrix products, arithmetic and copies ran while one was open for 6% -> 6% of each run, Pallas kernels for 24% -> 54%
where the time goes in v2:
time: 520 us; the launch traced here: 515 us
  Pallas kernels  320 us (62%)
  waiting for transfers between devices  84.1 us (16%)
  starting transfers between devices  59.2 us (11%)
  local copies, waits for them, and re-layouts  40.3 us (8%)
  other arithmetic  7.21 us (1%)
    pallas_call x4, Pallas kernels, mixer_backward(): pl.pallas_call(kernel, name='mixer_backward', grid_spec=pltpu.PrefetchSca...  86.4 us
    ppermute x37, waiting for transfers between devices, exchange(): lax.ppermute(value, axis, [(i, i ^ apart(i)) for i in range(lax.axis_size...  79.2 us
    pallas_call x4, Pallas kernels, mixer_forward(): pl.pallas_call(mixer_forward_kernel, name='mixer_forward', grid_spec=pltp...  62.4 us
    pallas_call x4, Pallas kernels, feed_backward(): pl.pallas_call(kernel, name='feed_backward', grid_spec=pltpu.PrefetchScal...  55.1 us
    pallas_call x4, Pallas kernels, feed_forward(): pl.pallas_call(feed_forward_kernel, name='feed_forward', grid_spec=pltpu....  46.9 us
    ppermute x37, starting transfers between devices, exchange(): lax.ppermute(value, axis, [(i, i ^ apart(i)) for i in range(lax.axis_size...  46.4 us
    pallas_call x4, Pallas kernels, rows_grads(): pl.pallas_call(lambda *refs: rows_kernel(halves, left[3], count, *refs),...  37.7 us
    pallas_call x12, Pallas kernels, halve(): pl.pallas_call(kernel, name='halve', grid=(groups,), in_specs=[ANYWHERE,...  31.6 us
  transfers between devices with their start and end apart: 41, of which 15 were waited for; matrix products, arithmetic and copies ran while one was open for 6% of the time, Pallas kernels for 54%

profile of v2, /device:TPU:0, one launch (start us, length us, event | category | flops | bytes accessed | tf_op | source)
XLA Modules:
  0.0 515.3 jit_solution(10422353322269899324)
XLA Ops:
  1.7 3.1 collective-permute-start
  4.8 2.0 constant_dynamic-slice_fusion.9
  6.8 7.1 %collective-permute-done = bf16[3,128,512]{2,1,0:T(8,128)(2,1)S(1)} collective-permute-done((bf16[3,128,512]{2,1,0:T(8,128)(2,1)S(1)}, bf16[3,128,512]{2,1,0:T(8,128)(2,1)S(1)}, u32[]{:S(2)}, u32[]{:S(2)}) %collective-permute-start) | collective-permute-done | bytes 393248 | tf_op jit(solution)/shard_map/ppermute | solution.py:1088
  13.9 1.7 collective-permute-start.7
  16.8 1.6 collective-permute-start.6
  18.4 3.3 collective-permute-done.7
  21.8 1.7 collective-permute-start.8
  23.5 1.9 constant_dynamic-slice_fusion.8
  25.4 2.2 dynamic-slice_bitcast_fusion.2
  27.6 2.0 constant_dynamic-slice_fusion.7
  29.6 1.6 collective-permute-start.1
  34.8 10.8 %collective-permute-done.1 = bf16[2,128,1408]{2,1,0:T(8,128)(2,1)S(1)} collective-permute-done((bf16[2,128,1408]{2,1,0:T(8,128)(2,1)}, bf16[2,128,1408]{2,1,0:T(8,128)(2,1)S(1)}, u32[]{:S(2)}, u32[]{:S(2)}) %collective-permute-start.1) | collective-permute-done | bytes 720928 | tf_op jit(solution)/shard_map/ppermute | solution.py:1088
  51.4 9.1 %collective-permute-done.4.out_came_ref.refs_20_ = bf16[256,1024]{1,0:T(8,128)(2,1)S(1)} collective-permute-done((bf16[256,1024]{1,0:T(8,128)(2,1)}, bf16[256,1024]{1,0:T(8,128)(2,1)S(1)}, u32[]{:S(2)}, u32[]{:S(2)}) %collective-permute-start.4) | collective-permute-done | bytes 524320 | tf_op jit(solution)/shard_map/ppermute | solution.py:1088
  60.5 1.5 collective-permute-start.5
  64.2 15.8 %mixer_forward.4 = (f32[256,1024]{1,0:T(8,128)}, f32[256,128]{1,0:T(8,128)}, bf16[3,256,1024]{2,1,0:T(8,128)(2,1)}, bf16[256,1024]{1,0:T(8,128)(2,1)}, bf16[256,...) custom-call(s32[19]{0:T(128)} %stack.92.info_ref.refs_0_, ...), custom_call_target="tpu_custom_call" | custom-call | flops 15399999488 | bytes 1048576 | tf_op jit(solution)/shard_map/mixer_forward/pallas_call | solution.py:318
  82.8 15.5 %mixer_forward.5 = (f32[256,1024]{1,0:T(8,128)}, f32[256,128]{1,0:T(8,128)}, bf16[3,256,1024]{2,1,0:T(8,128)(2,1)}, bf16[256,1024]{1,0:T(8,128)(2,1)}, bf16[256,...) custom-call(s32[19]{0:T(128)} %stack.92.info_ref.refs_0_, ...), custom_call_target="tpu_custom_call" | custom-call | flops 15399999488 | bytes 1048576 | tf_op jit(solution)/shard_map/mixer_forward/pallas_call | solution.py:318
  98.9 1.6 copy-done.10
  103.8 11.7 %feed_forward.5 = (bf16[256,1024]{1,0:T(8,128)(2,1)}, bf16[2,256,2816]{2,1,0:T(8,128)(2,1)}) custom-call(s32[19]{0:T(128)} %stack.92.info_ref.refs_0_, f32[256,1024]{1,0:T(8,128)} %get-tuple-element.141.after_ref.middle_ref.refs_2_, f32[1,1024]{1,0:T(1,128)} %get-tuple-element.300.gain_ref.refs_4_, bf16[2,1024,1408]{2,1,0:T(8,128)(2,1)} %refs_6_.3, ...), custom_call_target="tpu_custom_call" | custom-call | flops 11000000512 | bytes 1048576 | tf_op jit(solution)/shard_map/feed_forward/pallas_call | solution.py:837
  115.5 4.5 collective-permute-start.14
  120.0 11.7 %feed_forward.4 = (bf16[256,1024]{1,0:T(8,128)(2,1)}, bf16[2,256,2816]{2,1,0:T(8,128)(2,1)}) custom-call(s32[19]{0:T(128)} %stack.92.info_ref.refs_0_, f32[256,1024]{1,0:T(8,128)} %get-tuple-element.137.middle_ref.refs_2_, f32[1,1024]{1,0:T(1,128)} %get-tuple-element.300.gain_ref.refs_4_, bf16[2,1024,1408]{2,1,0:T(8,128)(2,1)} %refs_6_.3, ...), custom_call_target="tpu_custom_call" | custom-call | flops 11000000512 | bytes 1048576 | tf_op jit(solution)/shard_map/feed_forward/pallas_call | solution.py:837
  132.8 15.4 %mixer_forward.6 = (f32[256,1024]{1,0:T(8,128)}, f32[256,128]{1,0:T(8,128)}, bf16[3,256,1024]{2,1,0:T(8,128)(2,1)}, bf16[256,1024]{1,0:T(8,128)(2,1)}, bf16[256,...) custom-call(s32[19]{0:T(128)} %stack.92.info_ref.refs_0_, ...), custom_call_target="tpu_custom_call" | custom-call | flops 15399999488 | bytes 1048576 | tf_op jit(solution)/shard_map/mixer_forward/pallas_call | solution.py:318
  148.2 5.7 %collective-permute-start.15 = (bf16[256,1024]{1,0:T(8,128)(2,1)S(1)}, bf16[256,1024]{1,0:T(8,128)(2,1)S(1)}, u32[]{:S(2)}, u32[]{:S(2)}) collective-permute-start(bf16[256,1024]{1,0:T(8,128)(2,1)S(1)} %copy-done.34), channel_id=1, source_target_pairs={{0,16},{8,24},{1,17},{9,25},{2,18},{10,26},{3,19},{11,27},{4,20},{... | collective-permute-start | bytes 1572872 | tf_op jit(solution)/shard_map/ppermute | solution.py:1217
  153.9 11.7 %feed_forward.6 = (bf16[256,1024]{1,0:T(8,128)(2,1)}, bf16[2,256,2816]{2,1,0:T(8,128)(2,1)}) custom-call(s32[19]{0:T(128)} %stack.92.info_ref.refs_0_, f32[256,1024]{1,0:T(8,128)} %get-tuple-element.144.middle_ref, f32[1,1024]{1,0:T(1,128)} %get-tuple-element.300.gain_ref.refs_4_, bf16[2,1024,1408]{2,1,0:T(8,128)(2,1)} %refs_6_.3, ...), custom_call_target="tpu_custom_call" | custom-call | flops 11000000512 | bytes 1048576 | tf_op jit(solution)/shard_map/feed_forward/pallas_call | solution.py:837
  165.6 13.4 %feed_backward.5 = (f32[256,1024]{1,0:T(8,128)}, f32[1,1024]{1,0:T(1,128)}, bf16[4,256,2816]{2,1,0:T(8,128)(2,1)}) custom-call(s32[19]{0:T(128)} %stack.92.info_ref.refs_0_, f32[3,4,1024]{2,1,0:T(4,128)} %copy-done.22, f32[256,1024]{1,0:T(8,128)} %get-tuple-element.144.middle_ref, bf16[256,1024]{1,0:T(8,128)(2,1)} %get-tuple-element.286.grad_ref, ...), custom_call_target="tpu_custom_call" | custom-call | flops 14300000256 | bytes 1048576 | tf_op jit(solution)/shard_map/feed_backward/pallas_call | solution.py:966
  179.1 21.4 %mixer_backward.5 = (bf16[256,1024]{1,0:T(8,128)(2,1)}, f32[1,1024]{1,0:T(1,128)}, bf16[6,256,1024]{2,1,0:T(8,128)(2,1)}, bf16[256,128]{1,0:T(8,128)(2,1)}, f32[3,4,1024]{2,1,0:T(4,128)}, /*index=5*/f32[1,128]{1,0:T(1,128)}) custom-call(s32[19]{0:T(128)} %stack.92.info_ref.refs_0_, f32[3,4,1024]{2,1,0:T(4,128)} %copy-done.22, f32[3,4,1024]{2,1,0:T(4,128)} %copy-done.22, ...), custom_call_target="tpu_custom_call" | custom-call | flops 22000001024 | bytes 1048576 | tf_op jit(solution)/shard_map/mixer_backward/pallas_call | solution.py:676
  202.6 15.7 %mixer_forward.7 = (f32[256,1024]{1,0:T(8,128)}, f32[256,128]{1,0:T(8,128)}, bf16[3,256,1024]{2,1,0:T(8,128)(2,1)}, bf16[256,1024]{1,0:T(8,128)(2,1)}, bf16[256,...) custom-call(s32[19]{0:T(128)} %stack.92.info_ref.refs_0_, ...), custom_call_target="tpu_custom_call" | custom-call | flops 15399999488 | bytes 1048576 | tf_op jit(solution)/shard_map/mixer_forward/pallas_call | solution.py:318
  218.3 11.7 %feed_forward.7 = (bf16[256,1024]{1,0:T(8,128)(2,1)}, bf16[2,256,2816]{2,1,0:T(8,128)(2,1)}) custom-call(s32[19]{0:T(128)} %stack.92.info_ref.refs_0_, f32[256,1024]{1,0:T(8,128)} %get-tuple-element.147.middle_ref, f32[1,1024]{1,0:T(1,128)} %get-tuple-element.300.gain_ref.refs_4_, bf16[2,1024,1408]{2,1,0:T(8,128)(2,1)} %refs_6_.3, ...), custom_call_target="tpu_custom_call" | custom-call | flops 11000000512 | bytes 1048576 | tf_op jit(solution)/shard_map/feed_forward/pallas_call | solution.py:837
  230.1 13.5 %feed_backward.4 = (f32[256,1024]{1,0:T(8,128)}, f32[1,1024]{1,0:T(1,128)}, bf16[4,256,2816]{2,1,0:T(8,128)(2,1)}) custom-call(s32[19]{0:T(128)} %stack.92.info_ref.refs_0_, f32[3,4,1024]{2,1,0:T(4,128)} %copy-done.22, f32[256,1024]{1,0:T(8,128)} %get-tuple-element.147.middle_ref, bf16[256,1024]{1,0:T(8,128)(2,1)} %get-tuple-element.287.grad_ref, ...), custom_call_target="tpu_custom_call" | custom-call | flops 14300000256 | bytes 1048576 | tf_op jit(solution)/shard_map/feed_backward/pallas_call | solution.py:966
  243.6 21.4 %mixer_backward.4 = (bf16[256,1024]{1,0:T(8,128)(2,1)}, f32[1,1024]{1,0:T(1,128)}, bf16[6,256,1024]{2,1,0:T(8,128)(2,1)}, bf16[256,128]{1,0:T(8,128)(2,1)}, f32[3,4,1024]{2,1,0:T(4,128)}, /*index=5*/f32[1,128]{1,0:T(1,128)}) custom-call(s32[19]{0:T(128)} %stack.92.info_ref.refs_0_, f32[3,4,1024]{2,1,0:T(4,128)} %copy-done.22, f32[3,4,1024]{2,1,0:T(4,128)} %copy-done.22, ...), custom_call_target="tpu_custom_call" | custom-call | flops 22000001024 | bytes 1048576 | tf_op jit(solution)/shard_map/mixer_backward/pallas_call | solution.py:676
  265.7 14.0 %feed_backward.6 = (f32[256,1024]{1,0:T(8,128)}, f32[1,1024]{1,0:T(1,128)}, bf16[4,256,2816]{2,1,0:T(8,128)(2,1)}) custom-call(s32[19]{0:T(128)} %stack.92.info_ref.refs_0_, bf16[256,1024]{1,0:T(8,128)(2,1)} %get-tuple-element.157.refs_1_, f32[256,1024]{1,0:T(8,128)} %get-tuple-element.141.after_ref.middle_ref.refs_2_, ...), custom_call_target="tpu_custom_call", output_to_operand_aliasing={{2}: (13, {})} | custom-call | flops 14300000256 | bytes 1048576 | tf_op jit(solution)/shard_map/feed_backward/pallas_call | solution.py:966
  281.2 21.9 %mixer_backward.6 = (bf16[256,1024]{1,0:T(8,128)(2,1)}, f32[1,1024]{1,0:T(1,128)}, bf16[6,256,1024]{2,1,0:T(8,128)(2,1)}, bf16[256,128]{1,0:T(8,128)(2,1)}, f32[3,4,1024]{2,1,0:T(4,128)}, /*index=5*/f32[1,128]{1,0:T(1,128)}) custom-call(s32[19]{0:T(128)} %stack.92.info_ref.refs_0_, f32[3,4,1024]{2,1,0:T(4,128)} %copy-done.22, f32[3,4,1024]{2,1,0:T(4,128)} %copy-done.22, ...), custom_call_target="tpu_custom_call" | custom-call | flops 22000001024 | bytes 1048576 | tf_op jit(solution)/shard_map/mixer_backward/pallas_call | solution.py:676
  303.6 4.6 collective-permute-done.19.refs_3_
  309.0 14.1 %feed_backward.7 = (f32[256,1024]{1,0:T(8,128)}, f32[1,1024]{1,0:T(1,128)}, bf16[4,256,2816]{2,1,0:T(8,128)(2,1)}) custom-call(s32[19]{0:T(128)} %stack.92.info_ref.refs_0_, bf16[256,1024]{1,0:T(8,128)(2,1)} %get-tuple-element.157.refs_1_, f32[256,1024]{1,0:T(8,128)} %get-tuple-element.137.middle_ref.refs_2_, ...), custom_call_target="tpu_custom_call", output_to_operand_aliasing={{2}: (13, {})} | custom-call | flops 14300000256 | bytes 1048576 | tf_op jit(solution)/shard_map/feed_backward/pallas_call | solution.py:966
  323.2 2.4 copy-done
  325.7 21.8 %mixer_backward.7 = (bf16[256,1024]{1,0:T(8,128)(2,1)}, f32[1,1024]{1,0:T(1,128)}, bf16[6,256,1024]{2,1,0:T(8,128)(2,1)}, bf16[256,128]{1,0:T(8,128)(2,1)}, f32[3,4,1024]{2,1,0:T(4,128)}, /*index=5*/f32[1,128]{1,0:T(1,128)}) custom-call(s32[19]{0:T(128)} %stack.92.info_ref.refs_0_, bf16[4,256,2816]{2,1,0:T(8,128)(2,1)} %copy-done, ...), custom_call_target="tpu_custom_call" | custom-call | flops 22000001024 | bytes 1048576 | tf_op jit(solution)/shard_map/mixer_backward/pallas_call | solution.py:676
  348.0 13.0 %rows_grads.4 = (bf16[2,256,2816]{2,1,0:T(8,128)(2,1)}, bf16[2,256,2816]{2,1,0:T(8,128)(2,1)}) custom-call(s32[19]{0:T(128)} %stack.92.info_ref.refs_0_, f32[1,1024]{1,0:T(1,128)} %get-tuple-element.205.refs_1_, bf16[4,256,2816]{2,1,0:T(8,128)(2,1)} %get-tuple-element.186.refs_2_.refs_6_, bf16[4,256,2816]{2,1,0:T(8,128)(2,1)} %get-tuple-element.206.refs_3_.refs_7_, ...), custom_call_target="tpu_custom_call" | custom-call | flops 1100000000 | bytes 1048576 | tf_op jit(solution)/shard_map/rows_grads/pallas_call | solution.py:1035
  362.3 10.3 %rows_grads.5 = (bf16[1,704,1024]{2,1,0:T(8,128)(2,1)}, bf16[1,704,1024]{2,1,0:T(8,128)(2,1)}) custom-call(s32[19]{0:T(128)} %stack.92.info_ref.refs_0_, bf16[2,256,2816]{2,1,0:T(8,128)(2,1)} %get-tuple-element.207.refs_1_.keep_ref, bf16[4,256,2816]{2,1,0:T(8,128)(2,1)} %get-tuple-element.186.refs_2_.refs_6_, ...), custom_call_target="tpu_custom_call" | custom-call | flops 1100000000 | bytes 1048576 | tf_op jit(solution)/shard_map/rows_grads/pallas_call | solution.py:1035
  372.7 1.8 copy-done.1
  374.5 9.0 %rows_grads.6 = (bf16[3,256,1024]{2,1,0:T(8,128)(2,1)}, bf16[3,256,1024]{2,1,0:T(8,128)(2,1)}) custom-call(s32[19]{0:T(128)} %stack.92.info_ref.refs_0_, bf16[1,704,1024]{2,1,0:T(8,128)(2,1)} %get-tuple-element.208.refs_1_.keep_ref, bf16[6,256,1024]{2,1,0:T(8,128)(2,1)} %get-tuple-element.187.refs_2_.refs_6_, ...), custom_call_target="tpu_custom_call" | custom-call | flops 1100000000 | bytes 1048576 | tf_op jit(solution)/shard_map/rows_grads/pallas_call | solution.py:1035
  384.2 7.0 %collective-permute-start.23 = (bf16[1,704,1024]{2,1,0:T(8,128)(2,1)}, bf16[1,704,1024]{2,1,0:T(8,128)(2,1)}, u32[]{:S(2)}, u32[]{:S(2)}) collective-permute-start(bf16[1,704,1024]{2,1,0:T(8,128)(2,1)} %get-tuple-element.214), channel_id=1, source_target_pairs={{0,8},{8,0},{16,24},{24,16},{1,9},{9,1},{17,25},{25,17},{2,10},{10... | collective-permute-start | bytes 4325384 | tf_op jit(solution)/shard_map/ppermute | solution.py:1088
  392.4 5.4 %rows_grads.7 = (bf16[1,256,1024]{2,1,0:T(8,128)(2,1)}, bf16[1,256,1024]{2,1,0:T(8,128)(2,1)}) custom-call(s32[19]{0:T(128)} %stack.92.info_ref.refs_0_, bf16[3,256,1024]{2,1,0:T(8,128)(2,1)} %get-tuple-element.210.refs_1_.keep_ref, bf16[6,256,1024]{2,1,0:T(8,128)(2,1)} %get-tuple-element.187.refs_2_.refs_6_, ...), custom_call_target="tpu_custom_call" | custom-call | flops 1100000000 | bytes 1048576 | tf_op jit(solution)/shard_map/rows_grads/pallas_call | solution.py:1035
  397.8 4.1 halve.12
  404.7 19.3 %collective-permute-done.23.came_ref = bf16[1,704,1024]{2,1,0:T(8,128)(2,1)} collective-permute-done((bf16[1,704,1024]{2,1,0:T(8,128)(2,1)}, bf16[1,704,1024]{2,1,0:T(8,128)(2,1)}, u32[]{:S(2)}, u32[]{:S(2)}) %collective-permute-start.23) | collective-permute-done | bytes 1441824 | tf_op jit(solution)/shard_map/ppermute | solution.py:1088
  423.9 3.1 halve.13
  428.3 5.6 %collective-permute-done.24.came_ref = bf16[1,256,1024]{2,1,0:T(8,128)(2,1)S(1)} collective-permute-done((bf16[1,256,1024]{2,1,0:T(8,128)(2,1)}, bf16[1,256,1024]{2,1,0:T(8,128)(2,1)S(1)}, u32[]{:S(2)}, u32[]{:S(2)}) %collective-permute-start.24) | collective-permute-done | bytes 524320 | tf_op jit(solution)/shard_map/ppermute | solution.py:1088
  434.7 2.0 halve.14
  437.9 3.8 halve.15
  446.6 2.7 halve.16
  450.2 2.3 halve.17
  452.5 1.5 collective-permute-start.33
  455.6 1.8 halve.18
  457.4 1.7 collective-permute-done.32.came_ref
  460.0 3.0 halve.19
  463.0 1.5 collective-permute-start.39
  465.4 1.7 collective-permute-start.26
  467.1 2.6 collective-permute-start.28
  470.5 2.0 halve.20.after_ref
  475.8 12.4 %collective-permute-done.27 = bf16[2,256,256]{2,1,0:T(8,128)(2,1)S(1)} collective-permute-done((bf16[2,256,256]{2,1,0:T(8,128)(2,1)S(1)}, bf16[2,256,256]{2,1,0:T(8,128)(2,1)S(1)}, u32[]{:S(2)}, u32[]{:S(2)}) %collective-permute-start.27) | collective-permute-done | bytes 262176 | tf_op jit(solution)/shard_map/ppermute | solution.py:1088
  489.3 6.1 %collective-permute-start.36 = (bf16[3,128,512]{2,1,0:T(8,128)(2,1)}, bf16[3,128,512]{2,1,0:T(8,128)(2,1)S(1)}, u32[]{:S(2)}, u32[]{:S(2)}) collective-permute-start(bf16[3,128,512]{2,1,0:T(8,128)(2,1)} %get-tuple-element.232), channel_id=1, source_target_pairs={{0,8},{8,0},{16,24},{24,16},{1,9},{9,1},{17,25},{25,17},{2,10},{10... | collective-permute-start | bytes 1179656 | tf_op jit(solution)/shard_map/ppermute | solution.py:1088
  495.5 1.7 halve.21.after_ref
  497.2 5.6 %collective-permute-done.35.came_ref = bf16[2,128,1408]{2,1,0:T(8,128)(2,1)S(1)} collective-permute-done((bf16[2,128,1408]{2,1,0:T(8,128)(2,1)}, bf16[2,128,1408]{2,1,0:T(8,128)(2,1)S(1)}, u32[]{:S(2)}, u32[]{:S(2)}) %collective-permute-start.35) | collective-permute-done | bytes 720928 | tf_op jit(solution)/shard_map/ppermute | solution.py:1088
  503.6 2.3 halve.22.after_ref
  508.8 2.6 collective-permute-done.36.came_ref
  512.1 2.9 halve.23
  (214 shorter events, 55.5 us)
Async XLA Ops:
  0.6 16.1 %copy-start.14 = (f32[3,4,512]{2,1,0:T(4,128)S(1)}, f32[3,4,512]{2,1,0:T(4,128)}, u32[]{:S(2)}) copy-start(f32[3,4,512]{2,1,0:T(4,128)} %param.14) | copy-start | bytes 73732
  0.7 16.1 %copy-start.21 = (f32[2,512]{1,0:T(2,128)S(1)}, f32[2,512]{1,0:T(2,128)}, u32[]{:S(2)}) copy-start(f32[2,512]{1,0:T(2,128)} %param.18) | copy-start | bytes 12292
  0.7 16.1 %copy-start.26 = (f32[64]{0:T(128)S(1)}, f32[64]{0:T(128)}, u32[]{:S(2)}) copy-start(f32[64]{0:T(128)} %param.19) | copy-start | bytes 772
  1.7 12.2 %collective-permute-start = (bf16[3,128,512]{2,1,0:T(8,128)(2,1)S(1)}, bf16[3,128,512]{2,1,0:T(8,128)(2,1)S(1)}, u32[]{:S(2)}, u32[]{:S(2)}) collective-permute-start(bf16[3,128,512]{2,1,0:T(8,128)(2,1)S(1)} %constant_dynamic-slice_fusion.10), channel_id=1, source_target_pairs={{0,8},{8,0},{16,24},{24,16},{1,9},{9,1},{17,25},{25,17},{2,10},{10... | collective-permute-start | bytes 1179656 | tf_op jit(solution)/shard_map/ppermute | solution.py:1088
  13.9 7.8 %collective-permute-start.7 = (bf16[3,128,512]{2,1,0:T(8,128)(2,1)S(1)}, bf16[3,128,512]{2,1,0:T(8,128)(2,1)S(1)}, u32[]{:S(2)}, u32[]{:S(2)}) collective-permute-start(bf16[3,128,512]{2,1,0:T(8,128)(2,1)S(1)} %collective-permute-done), channel_id=1, source_target_pairs={{0,2},{1,5},{2,0},{3,7},{4,6},{5,1},{6,4},{7,3},{8,10},{9,13},{10,... | collective-permute-start | bytes 1179656 | tf_op jit(solution)/shard_map/ppermute | solution.py:1088
  16.8 15.3 %collective-permute-start.6 = (f32[11328]{0:T(1024)S(1)}, f32[11328]{0:T(1024)S(1)}, u32[]{:S(2)}, u32[]{:S(2)}) collective-permute-start(f32[11328]{0:T(1024)S(1)} %pad_maximum_fusion.5), channel_id=1, source_target_pairs={{0,8},{8,0},{16,24},{24,16},{1,9},{9,1},{17,25},{25,17},{2,10},{10... | collective-permute-start | bytes 135944 | tf_op jit(solution)/shard_map/ppermute | solution.py:1088
  18.4 12.8 %copy-start.19 = (bf16[1024,4]{0,1:T(4,128)(2,1)S(1)}, bf16[1024,4]{0,1:T(4,128)(2,1)}, u32[]{:S(2)}) copy-start(bf16[1024,4]{0,1:T(4,128)(2,1)} %param.13) | copy-start | bytes 24580
  21.8 12.1 %collective-permute-start.8 = (bf16[3,256,512]{2,1,0:T(8,128)(2,1)S(1)}, bf16[3,256,512]{2,1,0:T(8,128)(2,1)S(1)}, u32[]{:S(2)}, u32[]{:S(2)}) collective-permute-start(bf16[3,256,512]{2,1,0:T(8,128)(2,1)S(1)} %pad_maximum_fusion.3), channel_id=1, source_target_pairs={{0,4},{1,3},{2,6},{3,1},{4,0},{5,7},{6,2},{7,5},{8,12},{9,11},{10,... | collective-permute-start | bytes 2359304 | tf_op jit(solution)/shard_map/ppermute | solution.py:1088
  29.6 16.1 %collective-permute-start.1 = (bf16[2,128,1408]{2,1,0:T(8,128)(2,1)}, bf16[2,128,1408]{2,1,0:T(8,128)(2,1)S(1)}, u32[]{:S(2)}, u32[]{:S(2)}) collective-permute-start(bf16[2,128,1408]{2,1,0:T(8,128)(2,1)} %constant_dynamic-slice_fusion.9), channel_id=1, source_target_pairs={{0,8},{8,0},{16,24},{24,16},{1,9},{9,1},{17,25},{25,17},{2,10},{10... | collective-permute-start | bytes 2162696 | tf_op jit(solution)/shard_map/ppermute | solution.py:1088
  33.8 26.7 %copy-start.7 = (bf16[1408,256]{1,0:T(8,128)(2,1)S(1)}, bf16[1408,256]{1,0:T(8,128)(2,1)}, u32[]{:S(2)}) copy-start(bf16[1408,256]{1,0:T(8,128)(2,1)} %constant_dynamic-slice_fusion.7) | copy-start | bytes 2162692
  34.8 28.6 %collective-permute-start.9 = (bf16[3,512,512]{2,1,0:T(8,128)(2,1)}, bf16[3,512,512]{2,1,0:T(8,128)(2,1)}, u32[]{:S(2)}, u32[]{:S(2)}) collective-permute-start(bf16[3,512,512]{2,1,0:T(8,128)(2,1)} %constant_dynamic-update-slice_fusion.2.qkv_came_ref.refs_18_), channel_id=1, source_target_pairs={{0,1},{1,0},{2,3},{3,2},{4,5},{5,4},{6,7},{7,6},{8,9},{9,8},{10,11... | collective-permute-start | bytes 4718600 | tf_op jit(solution)/shard_map/ppermute | solution.py:1088
  34.8 28.6 %copy-start.22 = (f32[3,4,1024]{2,1,0:T(4,128)}, f32[3,4,1024]{2,1,0:T(4,128)S(1)}, u32[]{:S(2)}) copy-start(f32[3,4,1024]{2,1,0:T(4,128)S(1)} %constant_dynamic-update-slice_fusion.taps_ref.after_ref.also_ref.refs_1_.refs_2_.refs_14_) | copy-start | bytes 147460
  45.7 16.3 %collective-permute-start.2 = (bf16[2,128,1408]{2,1,0:T(8,128)(2,1)S(1)}, bf16[2,128,1408]{2,1,0:T(8,128)(2,1)S(1)}, u32[]{:S(2)}, u32[]{:S(2)}) collective-permute-start(bf16[2,128,1408]{2,1,0:T(8,128)(2,1)S(1)} %collective-permute-done.1), channel_id=1, source_target_pairs={{0,2},{1,5},{2,0},{3,7},{4,6},{5,1},{6,4},{7,3},{8,10},{9,13},{10,... | collective-permute-start | bytes 2162696 | tf_op jit(solution)/shard_map/ppermute | solution.py:1088
  47.8 12.6 %collective-permute-start.4 = (bf16[256,1024]{1,0:T(8,128)(2,1)}, bf16[256,1024]{1,0:T(8,128)(2,1)S(1)}, u32[]{:S(2)}, u32[]{:S(2)}) collective-permute-start(bf16[256,1024]{1,0:T(8,128)(2,1)} %constant_dynamic-slice_fusion.8), channel_id=1, source_target_pairs={{0,8},{8,0},{16,24},{24,16},{1,9},{9,1},{17,25},{25,17},{2,10},{10... | collective-permute-start | bytes 1572872 | tf_op jit(solution)/shard_map/ppermute | solution.py:1088
  60.5 2.9 copy-start.29
  60.5 2.9 collective-permute-start.10
  60.5 19.5 %collective-permute-start.5 = (bf16[1408,256]{1,0:T(8,128)(2,1)S(1)}, bf16[1408,256]{1,0:T(8,128)(2,1)S(1)}, u32[]{:S(2)}, u32[]{:S(2)}) collective-permute-start(bf16[1408,256]{1,0:T(8,128)(2,1)S(1)} %copy-done.7), channel_id=1, source_target_pairs={{0,8},{8,0},{16,24},{24,16},{1,9},{9,1},{17,25},{25,17},{2,10},{10... | collective-permute-start | bytes 2162696 | tf_op jit(solution)/shard_map/ppermute | solution.py:1088
  62.1 19.1 %collective-permute-start.3 = (bf16[2,256,1408]{2,1,0:T(8,128)(2,1)S(1)}, bf16[2,256,1408]{2,1,0:T(8,128)(2,1)S(1)}, u32[]{:S(2)}, u32[]{:S(2)}) collective-permute-start(bf16[2,256,1408]{2,1,0:T(8,128)(2,1)S(1)} %pad_maximum_fusion), channel_id=1, source_target_pairs={{0,4},{1,3},{2,6},{3,1},{4,0},{5,7},{6,2},{7,5},{8,12},{9,11},{10,... | collective-permute-start | bytes 4325384 | tf_op jit(solution)/shard_map/ppermute | solution.py:1088
  82.4 19.4 %collective-permute-start.12 = (bf16[2,512,1408]{2,1,0:T(8,128)(2,1)}, bf16[2,512,1408]{2,1,0:T(8,128)(2,1)S(1)}, u32[]{:S(2)}, u32[]{:S(2)}) collective-permute-start(bf16[2,512,1408]{2,1,0:T(8,128)(2,1)} %constant_dynamic-update-slice_fusion.5.lift_came_ref.refs_8_), channel_id=1, source_target_pairs={{0,1},{1,0},{2,3},{3,2},{4,5},{5,4},{6,7},{7,6},{8,9},{9,8},{10,11... | collective-permute-start | bytes 8650760 | tf_op jit(solution)/shard_map/ppermute | solution.py:1088
  82.4 15.9 %collective-permute-start.11 = (bf16[1408,256]{1,0:T(8,128)(2,1)S(1)}, bf16[1408,256]{1,0:T(8,128)(2,1)S(1)}, u32[]{:S(2)}, u32[]{:S(2)}) collective-permute-start(bf16[1408,256]{1,0:T(8,128)(2,1)S(1)} %collective-permute-done.5), channel_id=1, source_target_pairs={{0,2},{1,5},{2,0},{3,7},{4,6},{5,1},{6,4},{7,3},{8,10},{9,13},{10,... | collective-permute-start | bytes 2162696 | tf_op jit(solution)/shard_map/ppermute | solution.py:1088
  98.3 2.1 copy-start.10
  98.4 3.3 copy-start.4
  98.5 3.3 collective-permute-start.13
  115.5 16.5 %collective-permute-start.14 = (bf16[256,1024]{1,0:T(8,128)(2,1)}, bf16[256,1024]{1,0:T(8,128)(2,1)S(1)}, u32[]{:S(2)}, u32[]{:S(2)}) collective-permute-start(bf16[256,1024]{1,0:T(8,128)(2,1)} %get-tuple-element.142), channel_id=1, source_target_pairs={{0,16},{8,24},{1,17},{9,25},{2,18},{10,26},{3,19},{11,27},{4,20},{... | collective-permute-start | bytes 1572872 | tf_op jit(solution)/shard_map/ppermute | solution.py:1217
  131.7 16.5 %copy-start.34 = (bf16[256,1024]{1,0:T(8,128)(2,1)S(1)}, bf16[256,1024]{1,0:T(8,128)(2,1)}, u32[]{:S(2)}) copy-start(bf16[256,1024]{1,0:T(8,128)(2,1)} %get-tuple-element.146) | copy-start | bytes 1572868
  148.2 53.6 %collective-permute-start.15 = (bf16[256,1024]{1,0:T(8,128)(2,1)S(1)}, bf16[256,1024]{1,0:T(8,128)(2,1)S(1)}, u32[]{:S(2)}, u32[]{:S(2)}) collective-permute-start(bf16[256,1024]{1,0:T(8,128)(2,1)S(1)} %copy-done.34), channel_id=1, source_target_pairs={{0,16},{8,24},{1,17},{9,25},{2,18},{10,26},{3,19},{11,27},{4,20},{... | collective-permute-start | bytes 1572872 | tf_op jit(solution)/shard_map/ppermute | solution.py:1217
  200.5 64.5 %collective-permute-start.16 = (bf16[256,1024]{1,0:T(8,128)(2,1)}, bf16[256,1024]{1,0:T(8,128)(2,1)S(1)}, u32[]{:S(2)}, u32[]{:S(2)}) collective-permute-start(bf16[256,1024]{1,0:T(8,128)(2,1)} %get-tuple-element.167), channel_id=1, source_target_pairs={{16,0},{24,8},{17,1},{25,9},{18,2},{26,10},{19,3},{27,11},{20,4},{... | collective-permute-start | bytes 1572872 | tf_op jit(solution)/shard_map/ppermute | solution.py:1228
  265.7 14.1 %copy-start.31 = (bf16[256,1024]{1,0:T(8,128)(2,1)S(1)}, bf16[256,1024]{1,0:T(8,128)(2,1)}, u32[]{:S(2)}) copy-start(bf16[256,1024]{1,0:T(8,128)(2,1)} %get-tuple-element.157.refs_1_) | copy-start | bytes 1572868
  279.8 43.5 %collective-permute-start.17 = (bf16[4,256,2816]{2,1,0:T(8,128)(2,1)}, bf16[4,256,2816]{2,1,0:T(8,128)(2,1)S(1)}, u32[]{:S(2)}, u32[]{:S(2)}) collective-permute-start(bf16[4,256,2816]{2,1,0:T(8,128)(2,1)} %get-tuple-element.186.refs_2_.refs_6_), channel_id=1, source_target_pairs={{0,1},{1,0},{2,3},{3,2},{4,5},{5,4},{6,7},{7,6},{8,9},{9,8},{10,11... | collective-permute-start | bytes 17301512 | tf_op jit(solution)/shard_map/ppermute | solution.py:1088
  279.9 28.3 %collective-permute-start.19 = (bf16[256,1024]{1,0:T(8,128)(2,1)S(1)}, bf16[256,1024]{1,0:T(8,128)(2,1)S(1)}, u32[]{:S(2)}, u32[]{:S(2)}) collective-permute-start(bf16[256,1024]{1,0:T(8,128)(2,1)S(1)} %copy-done.31), channel_id=1, source_target_pairs={{16,0},{24,8},{17,1},{25,9},{18,2},{26,10},{19,3},{27,11},{20,4},{... | collective-permute-start | bytes 1572872 | tf_op jit(solution)/shard_map/ppermute | solution.py:1228
  303.0 20.2 %collective-permute-start.18 = (bf16[6,256,1024]{2,1,0:T(8,128)(2,1)}, bf16[6,256,1024]{2,1,0:T(8,128)(2,1)}, u32[]{:S(2)}, u32[]{:S(2)}) collective-permute-start(bf16[6,256,1024]{2,1,0:T(8,128)(2,1)} %get-tuple-element.187.refs_2_.refs_6_), channel_id=1, source_target_pairs={{0,1},{1,0},{2,3},{3,2},{4,5},{5,4},{6,7},{7,6},{8,9},{9,8},{10,11... | collective-permute-start | bytes 9437192 | tf_op jit(solution)/shard_map/ppermute | solution.py:1088
  323.1 24.9 %collective-permute-start.20 = (bf16[4,256,2816]{2,1,0:T(8,128)(2,1)}, bf16[4,256,2816]{2,1,0:T(8,128)(2,1)}, u32[]{:S(2)}, u32[]{:S(2)}) collective-permute-start(bf16[4,256,2816]{2,1,0:T(8,128)(2,1)} %get-tuple-element.206.refs_3_.refs_7_), channel_id=1, source_target_pairs={{0,1},{1,0},{2,3},{3,2},{4,5},{5,4},{6,7},{7,6},{8,9},{9,8},{10,11... | collective-permute-start | bytes 17301512 | tf_op jit(solution)/shard_map/ppermute | solution.py:1088
  323.2 2.5 copy-start
  347.5 25.2 %collective-permute-start.21 = (bf16[6,256,1024]{2,1,0:T(8,128)(2,1)}, bf16[6,256,1024]{2,1,0:T(8,128)(2,1)S(1)}, u32[]{:S(2)}, u32[]{:S(2)}) collective-permute-start(bf16[6,256,1024]{2,1,0:T(8,128)(2,1)} %get-tuple-element.209.refs_3_.refs_7_), channel_id=1, source_target_pairs={{0,1},{1,0},{2,3},{3,2},{4,5},{5,4},{6,7},{7,6},{8,9},{9,8},{10,11... | collective-permute-start | bytes 9437192 | tf_op jit(solution)/shard_map/ppermute | solution.py:1088
  361.0 36.8 %collective-permute-start.22 = (bf16[2,256,2816]{2,1,0:T(8,128)(2,1)}, bf16[2,256,2816]{2,1,0:T(8,128)(2,1)}, u32[]{:S(2)}, u32[]{:S(2)}) collective-permute-start(bf16[2,256,2816]{2,1,0:T(8,128)(2,1)} %get-tuple-element.212), channel_id=1, source_target_pairs={{0,2},{1,5},{2,0},{3,7},{4,6},{5,1},{6,4},{7,3},{8,10},{9,13},{10,... | collective-permute-start | bytes 8650760 | tf_op jit(solution)/shard_map/ppermute | solution.py:1088
  374.4 17.9 %copy-start.23 = (f32[1,1024]{1,0:T(1,128)S(1)}, f32[1,1024]{1,0:T(1,128)}, u32[]{:S(2)}) copy-start(f32[1,1024]{1,0:T(1,128)} %get-tuple-element.239) | copy-start | bytes 12292
  374.4 17.9 %copy-start.25 = (f32[1,1024]{1,0:T(1,128)S(1)}, f32[1,1024]{1,0:T(1,128)}, u32[]{:S(2)}) copy-start(f32[1,1024]{1,0:T(1,128)} %get-tuple-element.240) | copy-start | bytes 12292
  374.4 17.9 %copy-start.17 = (f32[3,4,1024]{2,1,0:T(4,128)S(1)}, f32[3,4,1024]{2,1,0:T(4,128)}, u32[]{:S(2)}) copy-start(f32[3,4,1024]{2,1,0:T(4,128)} %get-tuple-element.233) | copy-start | bytes 147460
  374.4 17.9 %copy-start.18 = (f32[3,4,1024]{2,1,0:T(4,128)S(1)}, f32[3,4,1024]{2,1,0:T(4,128)}, u32[]{:S(2)}) copy-start(f32[3,4,1024]{2,1,0:T(4,128)} %get-tuple-element.234) | copy-start | bytes 147460
  374.4 17.9 %copy-start.20 = (f32[1,1024]{1,0:T(1,128)S(1)}, f32[1,1024]{1,0:T(1,128)}, u32[]{:S(2)}) copy-start(f32[1,1024]{1,0:T(1,128)} %get-tuple-element.205.refs_1_) | copy-start | bytes 12292
  374.4 17.9 %copy-start.24 = (f32[1,1024]{1,0:T(1,128)S(1)}, f32[1,1024]{1,0:T(1,128)}, u32[]{:S(2)}) copy-start(f32[1,1024]{1,0:T(1,128)} %get-tuple-element.238) | copy-start | bytes 12292
  383.5 53.3 %collective-permute-start.25 = (bf16[3,256,1024]{2,1,0:T(8,128)(2,1)}, bf16[3,256,1024]{2,1,0:T(8,128)(2,1)S(1)}, u32[]{:S(2)}, u32[]{:S(2)}) collective-permute-start(bf16[3,256,1024]{2,1,0:T(8,128)(2,1)} %get-tuple-element.218), channel_id=1, source_target_pairs={{0,2},{1,5},{2,0},{3,7},{4,6},{5,1},{6,4},{7,3},{8,10},{9,13},{10,... | collective-permute-start | bytes 4718600 | tf_op jit(solution)/shard_map/ppermute | solution.py:1088
  384.2 39.7 %collective-permute-start.23 = (bf16[1,704,1024]{2,1,0:T(8,128)(2,1)}, bf16[1,704,1024]{2,1,0:T(8,128)(2,1)}, u32[]{:S(2)}, u32[]{:S(2)}) collective-permute-start(bf16[1,704,1024]{2,1,0:T(8,128)(2,1)} %get-tuple-element.214), channel_id=1, source_target_pairs={{0,8},{8,0},{16,24},{24,16},{1,9},{9,1},{17,25},{25,17},{2,10},{10... | collective-permute-start | bytes 4325384 | tf_op jit(solution)/shard_map/ppermute | solution.py:1088
  392.4 5.4 %copy-start.38 = (f32[1,128]{1,0:T(1,128)S(1)}, f32[1,128]{1,0:T(1,128)}, u32[]{:S(2)}) copy-start(f32[1,128]{1,0:T(1,128)} %get-tuple-element.241) | copy-start | bytes 1540
  392.4 5.4 %copy-start.39 = (f32[1,128]{1,0:T(1,128)S(1)}, f32[1,128]{1,0:T(1,128)}, u32[]{:S(2)}) copy-start(f32[1,128]{1,0:T(1,128)} %get-tuple-element.242) | copy-start | bytes 1540
  397.8 36.1 %collective-permute-start.24 = (bf16[1,256,1024]{2,1,0:T(8,128)(2,1)}, bf16[1,256,1024]{2,1,0:T(8,128)(2,1)S(1)}, u32[]{:S(2)}, u32[]{:S(2)}) collective-permute-start(bf16[1,256,1024]{2,1,0:T(8,128)(2,1)} %get-tuple-element.216), channel_id=1, source_target_pairs={{0,8},{8,0},{16,24},{24,16},{1,9},{9,1},{17,25},{25,17},{2,10},{10... | collective-permute-start | bytes 1572872 | tf_op jit(solution)/shard_map/ppermute | solution.py:1088
  397.8 5.5 %copy-start.16 = (bf16[256,128]{1,0:T(8,128)(2,1)S(1)}, bf16[256,128]{1,0:T(8,128)(2,1)}, u32[]{:S(2)}) copy-start(bf16[256,128]{1,0:T(8,128)(2,1)} %get-tuple-element.237) | copy-start | bytes 196612
  401.9 44.7 %collective-permute-start.29 = (bf16[2,128,2816]{2,1,0:T(8,128)(2,1)}, bf16[2,128,2816]{2,1,0:T(8,128)(2,1)}, u32[]{:S(2)}, u32[]{:S(2)}) collective-permute-start(bf16[2,128,2816]{2,1,0:T(8,128)(2,1)} %get-tuple-element.221), channel_id=1, source_target_pairs={{0,4},{1,3},{2,6},{3,1},{4,0},{5,7},{6,2},{7,5},{8,12},{9,11},{10,... | collective-permute-start | bytes 4325384 | tf_op jit(solution)/shard_map/ppermute | solution.py:1088
  427.0 14.7 %copy-start.15 = (bf16[256,128]{1,0:T(8,128)(2,1)S(1)}, bf16[256,128]{1,0:T(8,128)(2,1)}, u32[]{:S(2)}) copy-start(bf16[256,128]{1,0:T(8,128)(2,1)} %get-tuple-element.236) | copy-start | bytes 196612
  427.0 22.4 %collective-permute-start.30 = (bf16[1,352,1024]{2,1,0:T(8,128)(2,1)}, bf16[1,352,1024]{2,1,0:T(8,128)(2,1)S(1)}, u32[]{:S(2)}, u32[]{:S(2)}) collective-permute-start(bf16[1,352,1024]{2,1,0:T(8,128)(2,1)} %get-tuple-element.223), channel_id=1, source_target_pairs={{0,2},{1,5},{2,0},{3,7},{4,6},{5,1},{6,4},{7,3},{8,10},{9,13},{10,... | collective-permute-start | bytes 2162696 | tf_op jit(solution)/shard_map/ppermute | solution.py:1088
  441.7 3.0 copy-start.37
  443.5 5.8 %collective-permute-start.37 = (f32[22656]{0:T(1024)S(1)}, f32[22656]{0:T(1024)S(1)}, u32[]{:S(2)}, u32[]{:S(2)}) collective-permute-start(f32[22656]{0:T(1024)S(1)} %pad_maximum_fusion.4), channel_id=1, source_target_pairs={{0,1},{1,0},{2,3},{3,2},{4,5},{5,4},{6,7},{7,6},{8,9},{9,8},{10,11... | collective-permute-start | bytes 271880 | tf_op jit(solution)/shard_map/ppermute | solution.py:1088
  444.7 10.2 %collective-permute-start.31 = (bf16[1,128,1024]{2,1,0:T(8,128)(2,1)S(1)}, bf16[1,128,1024]{2,1,0:T(8,128)(2,1)S(1)}, u32[]{:S(2)}, u32[]{:S(2)}) collective-permute-start(bf16[1,128,1024]{2,1,0:T(8,128)(2,1)S(1)} %copy-done.37), channel_id=1, source_target_pairs={{0,2},{1,5},{2,0},{3,7},{4,6},{5,1},{6,4},{7,3},{8,10},{9,13},{10,... | collective-permute-start | bytes 786440 | tf_op jit(solution)/shard_map/ppermute | solution.py:1088
  446.0 13.0 %collective-permute-start.32 = (bf16[3,128,1024]{2,1,0:T(8,128)(2,1)}, bf16[3,128,1024]{2,1,0:T(8,128)(2,1)S(1)}, u32[]{:S(2)}, u32[]{:S(2)}) collective-permute-start(bf16[3,128,1024]{2,1,0:T(8,128)(2,1)} %get-tuple-element.227), channel_id=1, source_target_pairs={{0,4},{1,3},{2,6},{3,1},{4,0},{5,7},{6,2},{7,5},{8,12},{9,11},{10,... | collective-permute-start | bytes 2359304 | tf_op jit(solution)/shard_map/ppermute | solution.py:1088
  452.5 17.3 %collective-permute-start.33 = (bf16[1,176,1024]{2,1,0:T(8,128)(2,1)}, bf16[1,176,1024]{2,1,0:T(8,128)(2,1)S(1)}, u32[]{:S(2)}, u32[]{:S(2)}) collective-permute-start(bf16[1,176,1024]{2,1,0:T(8,128)(2,1)} %get-tuple-element.229), channel_id=1, source_target_pairs={{0,4},{1,3},{2,6},{3,1},{4,0},{5,7},{6,2},{7,5},{8,12},{9,11},{10,... | collective-permute-start | bytes 1081352 | tf_op jit(solution)/shard_map/ppermute | solution.py:1088
  454.0 9.1 %collective-permute-start.38 = (f32[22656]{0:T(1024)S(1)}, f32[22656]{0:T(1024)S(1)}, u32[]{:S(2)}, u32[]{:S(2)}) collective-permute-start(f32[22656]{0:T(1024)S(1)} %fusion.10), channel_id=1, source_target_pairs={{0,2},{1,3},{2,0},{3,1},{4,6},{5,7},{6,4},{7,5},{8,10},{9,11},{10,... | collective-permute-start | bytes 271880 | tf_op jit(solution)/shard_map/ppermute | solution.py:1088
  463.0 9.5 %collective-permute-start.39 = (f32[22656]{0:T(1024)S(1)}, f32[22656]{0:T(1024)S(1)}, u32[]{:S(2)}, u32[]{:S(2)}) collective-permute-start(f32[22656]{0:T(1024)S(1)} %add.164), channel_id=1, source_target_pairs={{0,4},{1,5},{2,6},{3,7},{4,0},{5,1},{6,2},{7,3},{8,12},{9,13},{10,... | collective-permute-start | bytes 271880 | tf_op jit(solution)/shard_map/ppermute | solution.py:1088
  465.4 9.1 %collective-permute-start.26 = (bf16[2,256,256]{2,1,0:T(8,128)(2,1)}, bf16[2,256,256]{2,1,0:T(8,128)(2,1)S(1)}, u32[]{:S(2)}, u32[]{:S(2)}) collective-permute-start(bf16[2,256,256]{2,1,0:T(8,128)(2,1)} %get-tuple-element.292), channel_id=1, source_target_pairs={{0,8},{8,0},{16,24},{24,16},{1,9},{9,1},{17,25},{25,17},{2,10},{10... | collective-permute-start | bytes 786440 | tf_op jit(solution)/shard_map/ppermute | solution.py:1088
  467.1 21.1 %collective-permute-start.27 = (bf16[2,256,256]{2,1,0:T(8,128)(2,1)S(1)}, bf16[2,256,256]{2,1,0:T(8,128)(2,1)S(1)}, u32[]{:S(2)}, u32[]{:S(2)}) collective-permute-start(bf16[2,256,256]{2,1,0:T(8,128)(2,1)S(1)} %get-tuple-element.294), channel_id=1, source_target_pairs={{0,16},{8,24},{16,0},{24,8},{1,17},{9,25},{17,1},{25,9},{2,18},{10... | collective-permute-start | bytes 786440 | tf_op jit(solution)/shard_map/ppermute | solution.py:1088
  467.1 21.1 %collective-permute-start.28 = (bf16[2,256,256]{2,1,0:T(8,128)(2,1)S(1)}, bf16[2,256,256]{2,1,0:T(8,128)(2,1)S(1)}, u32[]{:S(2)}, u32[]{:S(2)}) collective-permute-start(bf16[2,256,256]{2,1,0:T(8,128)(2,1)S(1)} %get-tuple-element.293), channel_id=1, source_target_pairs={{0,24},{8,16},{16,8},{24,0},{1,25},{9,17},{17,9},{25,1},{2,26},{10... | collective-permute-start | bytes 786440 | tf_op jit(solution)/shard_map/ppermute | solution.py:1088
  469.8 25.7 %collective-permute-start.34 = (bf16[1,64,1024]{2,1,0:T(8,128)(2,1)}, bf16[1,64,1024]{2,1,0:T(8,128)(2,1)}, u32[]{:S(2)}, u32[]{:S(2)}) collective-permute-start(bf16[1,64,1024]{2,1,0:T(8,128)(2,1)} %get-tuple-element.230), channel_id=1, source_target_pairs={{0,4},{1,3},{2,6},{3,1},{4,0},{5,7},{6,2},{7,5},{8,12},{9,11},{10,... | collective-permute-start | bytes 393224 | tf_op jit(solution)/shard_map/ppermute | solution.py:1088
  472.5 30.3 %collective-permute-start.35 = (bf16[2,128,1408]{2,1,0:T(8,128)(2,1)}, bf16[2,128,1408]{2,1,0:T(8,128)(2,1)S(1)}, u32[]{:S(2)}, u32[]{:S(2)}) collective-permute-start(bf16[2,128,1408]{2,1,0:T(8,128)(2,1)} %get-tuple-element.231), channel_id=1, source_target_pairs={{0,8},{8,0},{16,24},{24,16},{1,9},{9,1},{17,25},{25,17},{2,10},{10... | collective-permute-start | bytes 2162696 | tf_op jit(solution)/shard_map/ppermute | solution.py:1088
  474.5 31.4 %collective-permute-start.40 = (f32[1416]{0:T(1024)S(1)}, f32[1416]{0:T(1024)S(1)}, u32[]{:S(2)}, u32[]{:S(2)}) collective-permute-start(f32[1416]{0:T(1024)S(1)} %pad_maximum_fusion.6), channel_id=1, source_target_pairs={{0,8},{8,0},{16,24},{24,16},{1,9},{9,1},{17,25},{25,17},{2,10},{10... | collective-permute-start | bytes 17000 | tf_op jit(solution)/shard_map/ppermute | solution.py:1088
  489.3 22.1 %collective-permute-start.36 = (bf16[3,128,512]{2,1,0:T(8,128)(2,1)}, bf16[3,128,512]{2,1,0:T(8,128)(2,1)S(1)}, u32[]{:S(2)}, u32[]{:S(2)}) collective-permute-start(bf16[3,128,512]{2,1,0:T(8,128)(2,1)} %get-tuple-element.232), channel_id=1, source_target_pairs={{0,8},{8,0},{16,24},{24,16},{1,9},{9,1},{17,25},{25,17},{2,10},{10... | collective-permute-start | bytes 1179656 | tf_op jit(solution)/shard_map/ppermute | solution.py:1088
  (17 other events, 17.1 us)

commit v3 on v2

--- a/solution.py
+++ b/solution.py
@@ -106,13 +106,13 @@
 def tiled_old(shape, axis):
     return pl.BlockSpec(
         shape,
-        lambda step, info: tuple(step * (1 - info[8]) if i == axis else 0 for i in range(len(shape))),
+        lambda step, info: tuple(step * (1 - info[FIRST]) if i == axis else 0 for i in range(len(shape))),
     )
 
 
 ANYWHERE = pl.BlockSpec(memory_space=pl.ANY)
 
-DOWN, OUT = 9, 17
+FIRST, DOWN, OUT, SECOND = 8, 9, 17, 19
 
 
 def mixer_copies(info_ref, refs, into_qkv, into_out, sems):
@@ -159,6 +159,33 @@
     def wait():
         for copy in copies:
             copy.wait()
+
+
+def or_keep(kernel, inputs, outputs, first_kept, in_place=0):
+    def either(*refs):
+        start = 1 + inputs
+        old = refs[start : start + outputs - first_kept]
+        rest = refs[start + len(old) :]
+
+        @pl.when(refs[0][FIRST] == 1)
+        def compute():
+            kernel(*refs[:start], *rest)
+
+        @pl.when(refs[0][FIRST] == 0)
+        def keep():
+            for source, target in zip(old[: len(old) - in_place], rest[first_kept:outputs]):
+                target[...] = source[...]
+
+    return either
+
+
+def only_second(kernel):
+    def either(info_ref, *refs):
+        @pl.when(info_ref[SECOND] == 1)
+        def compute():
+            kernel(info_ref, *refs)
+
+    return either
 
 
 def mixer_forward_kernel(
@@ -302,11 +329,11 @@
     return pl.CostEstimate(flops=int(micros * 1.1e9), bytes_accessed=2**20, transcendentals=0)
 
 
-def params(**extra):
-    return pltpu.CompilerParams(dimension_semantics=("arbitrary",), vmem_limit_bytes=VMEM, **extra)
-
-
-def mixer_forward(info, after, stream, gain, weights, w_beta, taps, out_gain):
+def params(limit=VMEM, **extra):
+    return pltpu.CompilerParams(dimension_semantics=("arbitrary",), vmem_limit_bytes=limit, **extra)
+
+
+def mixer_forward(info, after, stream, gain, weights, w_beta, taps, out_gain, wrap=lambda kernel: kernel):
     length, width = stream.shape
     tile = weights[0].shape[2]
     inner = 2 * tile
@@ -316,7 +343,7 @@
     here = tile // LANES
     out = jax.ShapeDtypeStruct
     return pl.pallas_call(
-        mixer_forward_kernel,
+        wrap(mixer_forward_kernel),
         name="mixer_forward",
         grid_spec=pltpu.PrefetchScalarGridSpec(
             num_scalar_prefetch=1,
@@ -362,28 +389,11 @@
     )(info, after, stream, gain, w_beta, taps, out_gain, *weights)
 
 
-def or_keep(kernel, inputs, outputs, first_kept, in_place=0):
-    def either(*refs):
-        start = 1 + inputs
-        old = refs[start : start + outputs - first_kept]
-        rest = refs[start + len(old) :]
-
-        @pl.when(refs[0][8] == 1)
-        def compute():
-            kernel(*refs[:start], *rest)
-
-        @pl.when(refs[0][8] == 0)
-        def keep():
-            for source, target in zip(old[: len(old) - in_place], rest[first_kept:outputs]):
-                target[...] = source[...]
-
-    return either
-
-
 def mixer_backward_kernel(
     info_ref,
     after_ref,
     also_ref,
+    third_ref,
     stream_ref,
     branch_ref,
     strengths_ref,
@@ -648,6 +658,7 @@
     in_specs = [
         ANYWHERE,
         ANYWHERE,
+        ANYWHERE,
         whole((length, width)),
         whole((length, width)),
         whole((length, LANES)),
@@ -662,10 +673,10 @@
         tiled((3, count, tile), 2),
         whole((1, LANES)),
     ] + [ANYWHERE] * 6
-    kernel, more = mixer_backward_kernel, []
+    kernel, more = only_second(mixer_backward_kernel), []
     if old is not None:
         more = old[1:]
-        kernel = or_keep(kernel, len(in_specs), 6, 1)
+        kernel = or_keep(mixer_backward_kernel, len(in_specs), 6, 1)
         in_specs = in_specs + [
             whole((1, width)),
             tiled_old((6, length, tile), 2),
@@ -829,13 +840,13 @@
     wait_each(outs)
 
 
-def feed_forward(info, middle, gain, weights):
+def feed_forward(info, middle, gain, weights, wrap=lambda kernel: kernel):
     length, width = middle.shape
     units = weights[1].shape[0]
     count = 2 * len(unit_tiles(units))
     out = jax.ShapeDtypeStruct
     return pl.pallas_call(
-        feed_forward_kernel,
+        wrap(feed_forward_kernel),
         name="feed_forward",
         grid_spec=pltpu.PrefetchScalarGridSpec(
             num_scalar_prefetch=1,
@@ -860,7 +871,6 @@
 
 def feed_backward_kernel(
     info_ref,
-    after_ref,
     middle_ref,
     grad_ref,
     gain_ref,
@@ -956,11 +966,13 @@
     units = weights[1].shape[0]
     count = 2 * len(unit_tiles(units))
     out = jax.ShapeDtypeStruct
-    in_specs = [ANYWHERE, whole((length, width)), whole((length, width)), whole((1, width))] + [ANYWHERE] * 7
-    kernel, more, aliases = feed_backward_kernel, [], {}
+    waits = len(after)
+    in_specs = [ANYWHERE] * waits + [whole((length, width)), whole((length, width)), whole((1, width))] + [ANYWHERE] * 7
+    body = lambda info_ref, *refs: feed_backward_kernel(info_ref, *refs[waits:])
+    kernel, more, aliases = only_second(body), [], {}
     if old is not None:
         more = old[1:]
-        kernel = or_keep(kernel, len(in_specs), 3, 1, 1)
+        kernel = or_keep(body, len(in_specs), 3, 1, 1)
         in_specs = in_specs + [whole((1, width)), ANYWHERE]
         aliases = {len(in_specs): 2}
     return pl.pallas_call(
@@ -991,10 +1003,10 @@
         input_output_aliases=aliases,
         compiler_params=params(),
         cost_estimate=cost(13),
-    )(info, after, middle, grad, gain, lifted, *weights, *more)
-
-
-def rows_kernel(halves, width, count, info_ref, after_ref, *refs):
+    )(info, *after, middle, grad, gain, lifted, *weights, *more)
+
+
+def rows_kernel(halves, width, count, info_ref, *refs):
     lefts, rights = refs[:count], refs[count : 2 * count]
     keep_ref, send_ref, turned_ref, rows_ref = refs[2 * count :]
     size = width // halves // 8
@@ -1033,12 +1045,12 @@
     half = pl.BlockSpec((None, rows // 2, tile), lambda g, t, info: (g, 0, t))
     shape = jax.ShapeDtypeStruct((groups, rows // 2, tile * tiles), LOW)
     return pl.pallas_call(
-        lambda *refs: rows_kernel(halves, left[3], count, *refs),
+        lambda info_ref, *refs: rows_kernel(halves, left[3], count, info_ref, *refs[len(after) :]),
         name="rows_grads",
         grid_spec=pltpu.PrefetchScalarGridSpec(
             num_scalar_prefetch=1,
             grid=(groups, tiles),
-            in_specs=[ANYWHERE]
+            in_specs=[ANYWHERE] * len(after)
             + [pl.BlockSpec((None, length, left[1]), lambda g, t, info: (left[0], 0, left[2]))] * count
             + [pl.BlockSpec((None, length, right[1]), lambda g, t, info: (right[0] + g, 0, right[2] + spread * t))]
             * count,
@@ -1047,10 +1059,10 @@
         ),
         out_shape=[shape, shape],
         compiler_params=pltpu.CompilerParams(
-            dimension_semantics=("arbitrary", "arbitrary"), vmem_limit_bytes=VMEM
+            dimension_semantics=("arbitrary", "arbitrary"), vmem_limit_bytes=40 * 2**20
         ),
-        cost_estimate=cost(1),
-    )(info, after, *items, *items)
+        cost_estimate=cost(10),
+    )(info, *after, *items, *items)
 
 
 def halve(after, keep, came, axis):
@@ -1075,8 +1087,8 @@
         in_specs=[ANYWHERE, block, block],
         out_specs=[pl.BlockSpec((None, *shape), lambda g: (g, 0, 0))] * count,
         out_shape=[jax.ShapeDtypeStruct((groups, *shape), dtype)] * count,
-        compiler_params=params(),
-        cost_estimate=cost(0.01),
+        compiler_params=params(16 * 2**20),
+        cost_estimate=cost(2),
     )(after, keep, came)
 
 
@@ -1175,10 +1187,10 @@
         feed_weights = (w_gate_up, w_down, *halves_of(w_gate_up), *halves_of(w_down))
         places = down_places = list(range(8))
         core, near = 0, taps
-    info = jnp.stack([jnp.asarray(item, jnp.int32) for item in places + [rank == 0] + down_places + [core, 1 - core]])
-
-    def mixer_part(after, stream):
-        return mixer_forward(info, after, stream, gains[0:1], mixer_weights, w_beta, taps, out_gain)
+    info = jnp.stack([jnp.asarray(item, jnp.int32) for item in places + [rank == 0] + down_places + [core, 1 - core, rank == 1]])
+
+    def mixer_part(after, stream, *wrap):
+        return mixer_forward(info, after, stream, gains[0:1], mixer_weights, w_beta, taps, out_gain, *wrap)
 
     def feed_back(after, grad, saved, old=None):
         stream, middle, kept, lifted = saved
@@ -1212,72 +1224,90 @@
         result, lifted = feed_forward(info, saved[1], gains[1:2], feed_weights)
         saved.append(lifted)
         firsts.append(result)
-    saved1, results = [], []
+    grads = own(cotangent)
+    results, returned, feeds, mixes = [], [], [], []
+    after = taps
     for index in range(per):
         stream = lax.ppermute(firsts[index], "section", up)
-        middle, *kept = mixer_part(taps, stream)
+        middle, *kept = mixer_part(after, stream, *([only_second] if index else []))
         if index + 1 < per:
             firsts[index + 1], middle = tied(firsts[index + 1], middle)
-        result, lifted = feed_forward(info, middle, gains[1:2], feed_weights)
-        saved1.append([stream, middle, kept, lifted])
+        result, lifted = feed_forward(info, middle, gains[1:2], feed_weights, only_second)
         results.append(result)
-    returned, feeds, mixes = [], [], []
-    for grad, saved in zip(own(cotangent), saved1):
-        feeds.append(feed_back(taps, grad, saved))
-        mixes.append(mixer_back((taps, taps), feeds[-1][0], saved))
-        returned.append(lax.ppermute(mixes[-1][0], "section", [(2, 0), (3, 1)]))
+        saved = [stream, middle, kept, lifted]
+        feeds.append(feed_back([taps], grads[index], saved))
+        mixes.append(mixer_back((taps, taps, taps), feeds[-1][0], saved))
+        after = mixes[-1][0]
+        returned.append(lax.ppermute(after, "section", [(2, 0), (3, 1)]))
     feed_twins, mix_twins = [], []
-    waited = mixes[-1][0]
+    waited = [mixes[-1][0]]
     for index, (grad, saved) in enumerate(zip(returned, saved0)):
         feeds[index] = feed_back(waited, grad, saved, feeds[index])
-        after = (taps, taps)
+        after = (taps, taps, taps)
         if cube:
             feed_twins.append(flip(feeds[index][2], 1, 1))
             if index:
-                after = (feed_twins[index - 1], mix_twins[index - 1])
+                after = (feed_twins[index - 1], mix_twins[index - 1], taps)
         mixes[index] = mixer_back(after, feeds[index][0], saved, mixes[index])
+        waited = [mixes[index][0]]
         if cube:
             mix_twins.append(flip(mixes[index][2], 1, 1))
     feed_all = [feed[2] for feed in feeds] + feed_twins
-    if cube:
-        lifts = rows_grads(info, mixes[-1][1], feed_all, (3, units, 0, width), (0, units, 0), 2, 1, units, 2)
-        lift_came = flip(lifts[1], 2, 4)
-        downs = rows_grads(
-            info, lifts[0], feed_all, (2, 2 * units, 0, 2 * units), (3, units, 1), 1, 2, width // 2, 2
-        )
-        down_came = across(downs[1])
+    held = jnp.stack([jnp.where(rank == 1, result, mix[0]) for result, mix in zip(results, mixes)])
+    column = width // 2
+    moved = across(lax.dynamic_slice_in_dim(held, (1 - rank) * column, column, 2), 2)
+    held = lax.dynamic_slice_in_dim(held, rank * column, column, 2)
     mix_all = [mix[2] for mix in mixes]
     if cube:
         mix_all = mix_all + mix_twins
-        qkvs = rows_grads(info, downs[0], mix_all, (5, width, 0, width), (0, width, 0), 3, 1, width, 1)
-        qkv_came = flip(qkvs[1], 2, 4)
-        outs = rows_grads(info, qkvs[0], mix_all, (3, width, 0, width), (4, width, 0), 1, 2, width, 1)
-        out_came = across(outs[1])
-        lifts = halve(outs[0], lifts[0], lift_came, 1)
-        lift_came = flip(lifts[1], 4, 2)
-        downs = halve(lifts[0], downs[0], down_came, 1)
-        down_came = flip(downs[1], 2, 4)
-        outs = halve(downs[0], outs[0], out_came, 1)
-        out_came = flip(outs[1], 2, 4)
-        qkvs = halve(outs[0], qkvs[0], qkv_came, 1)
-        qkv_came = flip(qkvs[1], 4, 2)
-        marks = [qkvs[0]]
-        lifts = halve(qkvs[0], lifts[0], lift_came, 2)
-        lift_came = across(lifts[1])
-        marks.append(lifts[0])
-        downs = halve(lifts[0], downs[0], down_came, 1)
-        down_came = flip(downs[1], 4, 2)
-        outs = halve(downs[0], outs[0], out_came, 1)
-        out_came = flip(outs[1], 4, 2)
-        qkvs = halve(outs[0], qkvs[0], qkv_came, 2)
-        qkv_came = across(qkvs[1])
-        marks.append(qkvs[0])
-        grad_down = halve(qkvs[0], downs[0], down_came, None)[0]
-        marks.append(grad_down)
-        grad_out = halve(grad_down, outs[0], out_came, None)[0]
-        grad_gate_up = halve(grad_out, lifts[0], lift_came, None)[0]
-        grad_qkv = halve(grad_gate_up, qkvs[0], qkv_came, None)[0]
-        grad_down, grad_out = grad_down[0], grad_out[0]
+        plans = (
+            (feed_all, (3, units, 0, width), (0, units, 0), 2, 1, units, 2),
+            (feed_all, (2, 2 * units, 0, 2 * units), (3, units, 1), 1, 2, width // 2, 2),
+            (mix_all, (5, width, 0, width), (0, width, 0), 3, 1, width, 1),
+            (mix_all, (3, width, 0, width), (4, width, 0), 1, 2, width, 1),
+        )
+        after, kept, came = [mixes[-1][1]], [], []
+        for index, plan in enumerate(plans):
+            keep, send = rows_grads(info, after, *plan)
+            after = [keep]
+            kept.append(keep)
+            came.append(across(send) if index % 2 else flip(send, 2, 4))
+        after = kept[-1]
+        lifts, downs, qkvs, outs = range(4)
+
+        def turn(which, axis, onward=None):
+            nonlocal after
+            parts = halve(after, kept[which], came[which], axis)
+            after = kept[which] = parts[0]
+            if axis is not None:
+                came[which] = onward(parts[1])
+
+        def far(value):
+            return flip(value, 4, 2)
+
+        def near_flip(value):
+            return flip(value, 2, 4)
+
+        marks = [kept[downs]]
+        turn(lifts, 1, far)
+        turn(downs, 1, near_flip)
+        marks.append(after)
+        turn(outs, 1, near_flip)
+        turn(qkvs, 1, far)
+        marks.append(after)
+        turn(lifts, 2, across)
+        marks.append(after)
+        turn(downs, 1, far)
+        turn(outs, 1, far)
+        marks.append(after)
+        turn(qkvs, 2, across)
+        marks.append(after)
+        turn(lifts, None)
+        marks.append(after)
+        turn(downs, None)
+        turn(outs, None)
+        turn(qkvs, None)
+        grad_gate_up, grad_down, grad_qkv, grad_out = kept[0], kept[1][0], kept[2], kept[3][0]
     else:
 
         def tall(items, index):
@@ -1300,7 +1330,8 @@
 
     strengths = [mix[3] for mix in mixes]
     if cube:
-        strengths[0] = tied(strengths[0], marks[0])[0]
+        strengths[0] = tied(strengths[0], marks[3])[0]
+        moved = tied(moved, marks[1])[0]
     d_beta = sum(mm_tn(mix[5], item) for mix, item in zip(mix_all, strengths))[:, : 2 * heads]
     d_taps = sum(mix[4] for mix in mixes)
     d_gains = jnp.concatenate([sum(mix[1] for mix in mixes), sum(feed[1] for feed in feeds)], 0)
@@ -1309,7 +1340,7 @@
     flat = [d_taps, d_beta, d_gains, d_out_gain]
     packed = pack(flat)
     if cube:
-        for bits, mark in zip((1, 2, 4), marks[1:]):
+        for bits, mark in zip((1, 2, 4), marks[4:]):
             packed = packed + tied(flip(packed, bits, bits), mark)[0]
     else:
         packed = lax.psum(packed, "dp")
@@ -1334,19 +1365,11 @@
     came = unpack(across(pack([item[1] for item in pieces])), mine)
     grad_taps, grad_beta, grad_gains, grad_out_gains = [a + b for a, b in zip(mine, came)]
 
-    held = jnp.stack([jnp.where(rank == 1, a, mix[0]) for a, mix in zip(results, mixes)])
-    if cube:
-        held = tied(held, marks[0])[0]
-    quarter = width // 4
-
-    def quarter_of(index):
-        return lax.dynamic_slice_in_dim(held, index * quarter, quarter, 2)
-
-    came = [across(quarter_of(place ^ bits), bits) for bits in (1, 2, 3)]
-    same = by_half(quarter_of(place), came[0], 0)
-    other = by_half(came[1], came[2], 0)
-    final_stream = jnp.where(rank == 1, same, other)[:, None]
-    final_grad = jnp.where(rank == 0, same, other)[:, None]
+    kinds = jnp.stack([jnp.where(rank == 1, held, moved), jnp.where(rank == 1, moved, held)])
+    mine, theirs = [
+        lax.dynamic_slice_in_dim(kinds, which * column // 2, column // 2, 3) for which in (half, 1 - half)
+    ]
+    final_stream, final_grad = by_half(mine, across(theirs), 1)[:, :, None]
     return (
         final_stream,
         final_grad,

time: 520 us -> 464 us (0.89)
  Pallas kernels: 320 us -> 232 us
  waiting for transfers between devices: 84.1 us -> 133 us
  starting transfers between devices: 59.2 us -> 45.4 us
    ppermute x2, waiting for transfers between devices: 4.62 us -> 61 us  [local(): returned.append(lax.ppermute(after, 'section', [(2, 0), (3, 1)]))]
    pallas_call x4, Pallas kernels: 86.4 us -> 54.9 us  [mixer_backward(): pl.pallas_call(kernel, name='mixer_backward', grid_spec=pltpu.PrefetchSca...]
    pallas_call x12, Pallas kernels: 147 us -> 123 us  [the longest x4 62.1 us: mixer_forward(): pl.pallas_call(wrap(mixer_forward_kernel), name='mixer_forward', grid_spe...]
    pallas_call x12, Pallas kernels: 31.6 us -> 12.5 us  [halve(): pl.pallas_call(kernel, name='halve', grid=(groups,), in_specs=[ANYWHERE,...]
    ppermute x37 -> x36, starting transfers between devices: 46.4 us -> 32.6 us  [exchange(): lax.ppermute(value, axis, [(i, i ^ apart(i)) for i in range(lax.axis_size...]
    pallas_call x4, Pallas kernels: 55.1 us -> 41.4 us  [feed_backward(): pl.pallas_call(kernel, name='feed_backward', grid_spec=pltpu.PrefetchScal...]
    ppermute x37 -> x36, waiting for transfers between devices: 79.2 us -> 71.8 us  [exchange(): lax.ppermute(value, axis, [(i, i ^ apart(i)) for i in range(lax.axis_size...]
    unnamed x91 -> x120, local copies, waits for them, and re-layouts: 22.3 us -> 22.6 us
  transfers between devices with their start and end apart: 41 -> 40, of which waited for: 15 -> 21; matrix products, arithmetic and copies ran while one was open for 6% -> 7% of each run, Pallas kernels for 54% -> 41%
where the time goes in v3:
time: 464 us; the launch traced here: 463 us
  Pallas kernels  232 us (50%)
  waiting for transfers between devices  133 us (29%)
  starting transfers between devices  45.4 us (10%)
  local copies, waits for them, and re-layouts  41.6 us (9%)
  other arithmetic  8.85 us (2%)
    ppermute x36, waiting for transfers between devices, exchange(): lax.ppermute(value, axis, [(i, i ^ apart(i)) for i in range(lax.axis_size...  71.8 us
    pallas_call x4, Pallas kernels, mixer_forward(): pl.pallas_call(wrap(mixer_forward_kernel), name='mixer_forward', grid_spe...  62.1 us
    ppermute x2, waiting for transfers between devices, local(): returned.append(lax.ppermute(after, 'section', [(2, 0), (3, 1)]))  61 us
    pallas_call x4, Pallas kernels, mixer_backward(): pl.pallas_call(kernel, name='mixer_backward', grid_spec=pltpu.PrefetchSca...  54.9 us
    pallas_call x4, Pallas kernels, feed_backward(): pl.pallas_call(kernel, name='feed_backward', grid_spec=pltpu.PrefetchScal...  41.4 us
    ppermute x36, starting transfers between devices, exchange(): lax.ppermute(value, axis, [(i, i ^ apart(i)) for i in range(lax.axis_size...  32.6 us
    pallas_call x4, Pallas kernels, rows_grads(): pl.pallas_call(lambda info_ref, *refs: rows_kernel(halves, left[3], count...  31.8 us
    pallas_call x4, Pallas kernels, feed_forward(): pl.pallas_call(wrap(feed_forward_kernel), name='feed_forward', grid_spec=...  29.1 us
  transfers between devices with their start and end apart: 40, of which 21 were waited for; matrix products, arithmetic and copies ran while one was open for 7% of the time, Pallas kernels for 41%

profile of v3, /device:TPU:0, one launch (start us, length us, event | category | flops | bytes accessed | tf_op | source)
XLA Modules:
  0.0 463.3 jit_solution(4656258948095802921)
XLA Ops:
  1.7 3.1 collective-permute-start
  4.8 2.0 constant_dynamic-slice_fusion.6
  6.8 7.1 %collective-permute-done = bf16[3,128,512]{2,1,0:T(8,128)(2,1)S(1)} collective-permute-done((bf16[3,128,512]{2,1,0:T(8,128)(2,1)S(1)}, bf16[3,128,512]{2,1,0:T(8,128)(2,1)S(1)}, u32[]{:S(2)}, u32[]{:S(2)}) %collective-permute-start) | collective-permute-done | bytes 393248 | tf_op jit(solution)/shard_map/ppermute | solution.py:1100
  13.9 1.7 collective-permute-start.7
  16.8 1.6 collective-permute-start.6
  18.4 3.3 collective-permute-done.7
  21.8 1.7 collective-permute-start.8
  23.5 1.9 constant_dynamic-slice_fusion.5
  25.4 2.2 dynamic-slice_bitcast_fusion.2
  27.6 2.0 constant_dynamic-slice_fusion.4
  29.6 1.6 collective-permute-start.1
  34.8 10.9 %collective-permute-done.1 = bf16[2,128,1408]{2,1,0:T(8,128)(2,1)S(1)} collective-permute-done((bf16[2,128,1408]{2,1,0:T(8,128)(2,1)}, bf16[2,128,1408]{2,1,0:T(8,128)(2,1)S(1)}, u32[]{:S(2)}, u32[]{:S(2)}) %collective-permute-start.1) | collective-permute-done | bytes 720928 | tf_op jit(solution)/shard_map/ppermute | solution.py:1100
  47.8 1.4 collective-permute-start.4
  51.4 9.1 %collective-permute-done.4.out_came_ref.refs_20_.refs_10_.refs_21_ = bf16[256,1024]{1,0:T(8,128)(2,1)S(1)} collective-permute-done((bf16[256,1024]{1,0:T(8,128)(2,1)}, bf16[256,1024]{1,0:T(8,128)(2,1)S(1)}, u32[]{:S(2)}, u32[]{:S(2)}) %collective-permute-start.4) | collective-permute-done | bytes 524320 | tf_op jit(solution)/shard_map/ppermute | solution.py:1100
  60.5 1.5 collective-permute-start.5
  64.2 15.5 %mixer_forward.4 = (f32[256,1024]{1,0:T(8,128)}, f32[256,128]{1,0:T(8,128)}, bf16[3,256,1024]{2,1,0:T(8,128)(2,1)}, bf16[256,1024]{1,0:T(8,128)(2,1)}, bf16[256,...) custom-call(s32[20]{0:T(128)} %stack.109.info_ref.refs_0_, ...), custom_call_target="tpu_custom_call" | custom-call | flops 15399999488 | bytes 1048576 | tf_op jit(solution)/shard_map/mixer_forward/pallas_call | solution.py:345
  79.7 1.5 collective-permute-done.3
  82.5 15.7 %mixer_forward.5 = (f32[256,1024]{1,0:T(8,128)}, f32[256,128]{1,0:T(8,128)}, bf16[3,256,1024]{2,1,0:T(8,128)(2,1)}, bf16[256,1024]{1,0:T(8,128)(2,1)}, bf16[256,...) custom-call(s32[20]{0:T(128)} %stack.109.info_ref.refs_0_, ...), custom_call_target="tpu_custom_call" | custom-call | flops 15399999488 | bytes 1048576 | tf_op jit(solution)/shard_map/mixer_forward/pallas_call | solution.py:345
  98.8 1.5 copy-done.30
  102.8 11.7 %feed_forward.5 = (bf16[256,1024]{1,0:T(8,128)(2,1)}, bf16[2,256,2816]{2,1,0:T(8,128)(2,1)}) custom-call(s32[20]{0:T(128)} %stack.109.info_ref.refs_0_, f32[256,1024]{1,0:T(8,128)} %get-tuple-element.141.after_ref.middle_ref.refs_2_, f32[1,1024]{1,0:T(1,128)} %get-tuple-element.300.gain_ref.refs_1_.refs_3_.refs_4_, bf16[2,1024,1408]{2,1,0:T(8,128)(2,1)} %refs_6_.9, ...), custom_call_target="tpu_custom_call" | custom-call | flops 11000000512 | bytes 1048576 | tf_op jit(solution)/shard_map/feed_forward/pallas_call | solution.py:848
  114.5 4.5 collective-permute-start.14
  119.0 11.7 %feed_forward.4 = (bf16[256,1024]{1,0:T(8,128)(2,1)}, bf16[2,256,2816]{2,1,0:T(8,128)(2,1)}) custom-call(s32[20]{0:T(128)} %stack.109.info_ref.refs_0_, f32[256,1024]{1,0:T(8,128)} %get-tuple-element.137.middle_ref.refs_2_, f32[1,1024]{1,0:T(1,128)} %get-tuple-element.300.gain_ref.refs_1_.refs_3_.refs_4_, bf16[2,1024,1408]{2,1,0:T(8,128)(2,1)} %refs_6_.9, ...), custom_call_target="tpu_custom_call" | custom-call | flops 11000000512 | bytes 1048576 | tf_op jit(solution)/shard_map/feed_forward/pallas_call | solution.py:848
  131.8 26.5 %mixer_forward.6 = (f32[256,1024]{1,0:T(8,128)}, f32[256,128]{1,0:T(8,128)}, bf16[3,256,1024]{2,1,0:T(8,128)(2,1)}, bf16[256,1024]{1,0:T(8,128)(2,1)}, bf16[256,...) custom-call(s32[20]{0:T(128)} %stack.109.info_ref.refs_0_, ...), custom_call_target="tpu_custom_call" | custom-call | flops 15399999488 | bytes 1048576 | tf_op jit(solution)/shard_map/mixer_forward/pallas_call | solution.py:345
  158.3 5.3 %collective-permute-start.15 = (bf16[256,1024]{1,0:T(8,128)(2,1)S(1)}, bf16[256,1024]{1,0:T(8,128)(2,1)S(1)}, u32[]{:S(2)}, u32[]{:S(2)}) collective-permute-start(bf16[256,1024]{1,0:T(8,128)(2,1)S(1)} %copy-done.48), channel_id=1, source_target_pairs={{0,16},{8,24},{1,17},{9,25},{2,18},{10,26},{3,19},{11,27},{4,20},{... | collective-permute-start | bytes 1572872 | tf_op jit(solution)/shard_map/ppermute | solution.py:1231
  163.6 2.9 feed_forward.6
  166.5 3.6 feed_backward.4
  170.1 5.1 %mixer_backward.4 = (bf16[256,1024]{1,0:T(8,128)(2,1)}, f32[1,1024]{1,0:T(1,128)}, bf16[6,256,1024]{2,1,0:T(8,128)(2,1)}, bf16[256,128]{1,0:T(8,128)(2,1)}, f32[3,4,1024]{2,1,0:T(4,128)}, /*index=5*/f32[1,128]{1,0:T(1,128)}) custom-call(s32[20]{0:T(128)} %stack.109.info_ref.refs_0_, f32[3,4,1024]{2,1,0:T(4,128)} %copy-done.37, f32[3,4,1024]{2,1,0:T(4,128)} %copy-done.37, ...), custom_call_target="tpu_custom_call" | custom-call | flops 22000001024 | bytes 1048576 | tf_op jit(solution)/shard_map/mixer_backward/pallas_call | solution.py:687
  175.2 1.7 collective-permute-start.16
  177.7 4.4 mixer_forward.7
  182.1 2.9 feed_forward.7
  185.1 9.3 %feed_backward.5 = (f32[256,1024]{1,0:T(8,128)}, f32[1,1024]{1,0:T(1,128)}, bf16[4,256,2816]{2,1,0:T(8,128)(2,1)}) custom-call(s32[20]{0:T(128)} %stack.109.info_ref.refs_0_, f32[3,4,1024]{2,1,0:T(4,128)} %copy-done.37, f32[256,1024]{1,0:T(8,128)} %get-tuple-element.157.refs_0_.refs_1_, bf16[256,1024]{1,0:T(8,128)(2,1)} %get-tuple-element.286.refs_2_, ...), custom_call_target="tpu_custom_call" | custom-call | flops 14300000256 | bytes 1048576 | tf_op jit(solution)/shard_map/feed_backward/pallas_call | solution.py:978
  194.4 5.2 %mixer_backward.5 = (bf16[256,1024]{1,0:T(8,128)(2,1)}, f32[1,1024]{1,0:T(1,128)}, bf16[6,256,1024]{2,1,0:T(8,128)(2,1)}, bf16[256,128]{1,0:T(8,128)(2,1)}, f32[3,4,1024]{2,1,0:T(4,128)}, /*index=5*/f32[1,128]{1,0:T(1,128)}) custom-call(s32[20]{0:T(128)} %stack.109.info_ref.refs_0_, f32[3,4,1024]{2,1,0:T(4,128)} %copy-done.37, f32[3,4,1024]{2,1,0:T(4,128)} %copy-done.37, ...), custom_call_target="tpu_custom_call" | custom-call | flops 22000001024 | bytes 1048576 | tf_op jit(solution)/shard_map/mixer_backward/pallas_call | solution.py:687
  200.9 33.2 %collective-permute-done.16.refs_3_ = bf16[256,1024]{1,0:T(8,128)(2,1)S(1)} collective-permute-done((bf16[256,1024]{1,0:T(8,128)(2,1)}, bf16[256,1024]{1,0:T(8,128)(2,1)S(1)}, u32[]{:S(2)}, u32[]{:S(2)}) %collective-permute-start.16) | collective-permute-done | bytes 524320 | tf_op jit(solution)/shard_map/ppermute | solution.py:1241
  234.9 14.2 %feed_backward.6 = (f32[256,1024]{1,0:T(8,128)}, f32[1,1024]{1,0:T(1,128)}, bf16[4,256,2816]{2,1,0:T(8,128)(2,1)}) custom-call(s32[20]{0:T(128)} %stack.109.info_ref.refs_0_, bf16[256,1024]{1,0:T(8,128)(2,1)} %get-tuple-element.167.refs_1_, f32[256,1024]{1,0:T(8,128)} %get-tuple-element.141.after_ref.middle_ref.refs_2_, ...), custom_call_target="tpu_custom_call", output_to_operand_aliasing={{2}: (13, {})} | custom-call | flops 14300000256 | bytes 1048576 | tf_op jit(solution)/shard_map/feed_backward/pallas_call | solution.py:978
  249.1 21.8 %mixer_backward.6 = (bf16[256,1024]{1,0:T(8,128)(2,1)}, f32[1,1024]{1,0:T(1,128)}, bf16[6,256,1024]{2,1,0:T(8,128)(2,1)}, bf16[256,128]{1,0:T(8,128)(2,1)}, f32[3,4,1024]{2,1,0:T(4,128)}, /*index=5*/f32[1,128]{1,0:T(1,128)}) custom-call(s32[20]{0:T(128)} %stack.109.info_ref.refs_0_, f32[3,4,1024]{2,1,0:T(4,128)} %copy-done.37, f32[3,4,1024]{2,1,0:T(4,128)} %copy-done.37, ...), custom_call_target="tpu_custom_call" | custom-call | flops 22000001024 | bytes 1048576 | tf_op jit(solution)/shard_map/mixer_backward/pallas_call | solution.py:687
  271.4 27.8 %collective-permute-done.19.refs_3_ = bf16[256,1024]{1,0:T(8,128)(2,1)S(1)} collective-permute-done((bf16[256,1024]{1,0:T(8,128)(2,1)}, bf16[256,1024]{1,0:T(8,128)(2,1)S(1)}, u32[]{:S(2)}, u32[]{:S(2)}) %collective-permute-start.19) | collective-permute-done | bytes 524320 | tf_op jit(solution)/shard_map/ppermute | solution.py:1241
  300.0 14.3 %feed_backward.7 = (f32[256,1024]{1,0:T(8,128)}, f32[1,1024]{1,0:T(1,128)}, bf16[4,256,2816]{2,1,0:T(8,128)(2,1)}) custom-call(s32[20]{0:T(128)} %stack.109.info_ref.refs_0_, bf16[256,1024]{1,0:T(8,128)(2,1)} %get-tuple-element.184.refs_1_, f32[256,1024]{1,0:T(8,128)} %get-tuple-element.137.middle_ref.refs_2_, ...), custom_call_target="tpu_custom_call", output_to_operand_aliasing={{2}: (13, {})} | custom-call | flops 14300000256 | bytes 1048576 | tf_op jit(solution)/shard_map/feed_backward/pallas_call | solution.py:978
  314.5 1.6 copy-done.7
  316.2 22.8 %mixer_backward.7 = (bf16[256,1024]{1,0:T(8,128)(2,1)}, f32[1,1024]{1,0:T(1,128)}, bf16[6,256,1024]{2,1,0:T(8,128)(2,1)}, bf16[256,128]{1,0:T(8,128)(2,1)}, f32[3,4,1024]{2,1,0:T(4,128)}, /*index=5*/f32[1,128]{1,0:T(1,128)}) custom-call(s32[20]{0:T(128)} %stack.109.info_ref.refs_0_, bf16[4,256,2816]{2,1,0:T(8,128)(2,1)} %collective-permute-done.17.refs_1_.refs_3_.refs_7_, ...), custom_call_target="tpu_custom_call" | custom-call | flops 22000001024 | bytes 1048576 | tf_op jit(solution)/shard_map/mixer_backward/pallas_call | solution.py:687
  342.5 12.0 %rows_grads.4 = (bf16[2,256,2816]{2,1,0:T(8,128)(2,1)S(1)}, bf16[2,256,2816]{2,1,0:T(8,128)(2,1)}) custom-call(s32[20]{0:T(128)S(1)} %copy-done.6, f32[1,1024]{1,0:T(1,128)S(1)} %copy-done.5, bf16[4,256,2816]{2,1,0:T(8,128)(2,1)S(1)} %bitcast.72, bf16[4,256,2816]{2,1,0:T(8,128)(2,1)} %get-tuple-element.206.refs_2_.refs_6_, ...), custom_call_target="tpu_custom_call" | custom-call | flops 11000000512 | bytes 1048576 | tf_op jit(solution)/shard_map/rows_grads/pallas_call | solution.py:1047
  354.5 1.3 collective-permute-start.23
  355.9 9.7 %rows_grads.5 = (bf16[1,704,1024]{2,1,0:T(8,128)(2,1)S(1)}, bf16[1,704,1024]{2,1,0:T(8,128)(2,1)}) custom-call(s32[20]{0:T(128)S(1)} %copy-done.6, bf16[2,256,2816]{2,1,0:T(8,128)(2,1)S(1)} %get-tuple-element.207.refs_0_.keep_ref, bf16[4,256,2816]{2,1,0:T(8,128)(2,1)S(1)} %bitcast.72, bf16[4,256,2816]{2,1,0:T(8,128)(2,1)} %get-tuple-element.206.refs_2_.refs_6_, ...), custom_call_target="tpu_custom_call" | custom-call | flops 11000000512 | bytes 1048576 | tf_op jit(solution)/shard_map/rows_grads/pallas_call | solution.py:1047
  366.1 1.9 copy-done.3
  368.0 1.9 copy-done.8
  369.9 6.4 %rows_grads.6 = (bf16[3,256,1024]{2,1,0:T(8,128)(2,1)S(1)}, bf16[3,256,1024]{2,1,0:T(8,128)(2,1)S(1)}) custom-call(s32[20]{0:T(128)S(1)} %copy-done.6, bf16[1,704,1024]{2,1,0:T(8,128)(2,1)S(1)} %get-tuple-element.208.refs_0_.keep_ref, bf16[6,256,1024]{2,1,0:T(8,128)(2,1)S(1)} %copy-done.2, bf16[6,256,1024]{2,1,0:T(8,128)(2,1)S(1)} %copy-done.3, ...), custom_call_target="tpu_custom_call" | custom-call | flops 11000000512 | bytes 1048576 | tf_op jit(solution)/shard_map/rows_grads/pallas_call | solution.py:1047
  376.4 3.6 rows_grads.7
  380.0 1.6 collective-permute-start.26
  382.6 6.7 %collective-permute-done.23.came_ref = bf16[2,256,2816]{2,1,0:T(8,128)(2,1)} collective-permute-done((bf16[2,256,2816]{2,1,0:T(8,128)(2,1)}, bf16[2,256,2816]{2,1,0:T(8,128)(2,1)}, u32[]{:S(2)}, u32[]{:S(2)}) %collective-permute-start.23) | collective-permute-done | bytes 2883616 | tf_op jit(solution)/shard_map/ppermute | solution.py:1100
  389.3 2.3 halve.12
  391.6 1.8 collective-permute-start.28
  393.4 6.9 %collective-permute-done.24.came_ref = bf16[1,704,1024]{2,1,0:T(8,128)(2,1)} collective-permute-done((bf16[1,704,1024]{2,1,0:T(8,128)(2,1)}, bf16[1,704,1024]{2,1,0:T(8,128)(2,1)}, u32[]{:S(2)}, u32[]{:S(2)}) %collective-permute-start.24) | collective-permute-done | bytes 1441824 | tf_op jit(solution)/shard_map/ppermute | solution.py:1100
  400.3 1.7 halve.13
  402.0 1.5 select_bitcast_fusion
  406.2 5.3 %collective-permute-done.26.came_ref = bf16[1,256,1024]{2,1,0:T(8,128)(2,1)S(1)} collective-permute-done((bf16[1,256,1024]{2,1,0:T(8,128)(2,1)S(1)}, bf16[1,256,1024]{2,1,0:T(8,128)(2,1)S(1)}, u32[]{:S(2)}, u32[]{:S(2)}) %collective-permute-start.26) | collective-permute-done | bytes 524320 | tf_op jit(solution)/shard_map/ppermute | solution.py:1100
  413.2 8.9 %collective-permute-done.25 = bf16[2,2,256,256]{3,2,1,0:T(8,128)(2,1)S(1)} collective-permute-done((bf16[2,2,256,256]{3,2,1,0:T(8,128)(2,1)S(1)}, bf16[2,2,256,256]{3,2,1,0:T(8,128)(2,1)S(1)}, u32[]{:S(2)}, u32[]{:S(2)}) %collective-permute-start.25) | collective-permute-done | bytes 524320 | tf_op jit(solution)/shard_map/ppermute | solution.py:1100
  423.7 1.8 collective-permute-start.31
  430.4 2.0 collective-permute-done.29.came_ref
  434.7 1.3 halve.17
  436.0 1.7 collective-permute-start.33
  439.2 1.7 collective-permute-start.34
  441.2 5.4 %collective-permute-done.37 = f32[22656]{0:T(1024)S(1)} collective-permute-done((f32[22656]{0:T(1024)S(1)}, f32[22656]{0:T(1024)S(1)}, u32[]{:S(2)}, u32[]{:S(2)}) %collective-permute-start.37) | collective-permute-done | bytes 90656 | tf_op jit(solution)/shard_map/ppermute | solution.py:1100
  449.6 1.4 copy-done.12
  455.0 2.9 collective-permute-done.39
  461.7 1.5 halve.23
  (243 shorter events, 52.6 us)
Async XLA Ops:
  0.6 16.1 %copy-start.31 = (f32[3,4,512]{2,1,0:T(4,128)S(1)}, f32[3,4,512]{2,1,0:T(4,128)}, u32[]{:S(2)}) copy-start(f32[3,4,512]{2,1,0:T(4,128)} %param.14) | copy-start | bytes 73732
  0.7 16.1 %copy-start.36 = (f32[2,512]{1,0:T(2,128)S(1)}, f32[2,512]{1,0:T(2,128)}, u32[]{:S(2)}) copy-start(f32[2,512]{1,0:T(2,128)} %param.18) | copy-start | bytes 12292
  0.7 16.1 %copy-start.41 = (f32[64]{0:T(128)S(1)}, f32[64]{0:T(128)}, u32[]{:S(2)}) copy-start(f32[64]{0:T(128)} %param.19) | copy-start | bytes 772
  1.7 12.2 %collective-permute-start = (bf16[3,128,512]{2,1,0:T(8,128)(2,1)S(1)}, bf16[3,128,512]{2,1,0:T(8,128)(2,1)S(1)}, u32[]{:S(2)}, u32[]{:S(2)}) collective-permute-start(bf16[3,128,512]{2,1,0:T(8,128)(2,1)S(1)} %constant_dynamic-slice_fusion.7), channel_id=1, source_target_pairs={{0,8},{8,0},{16,24},{24,16},{1,9},{9,1},{17,25},{25,17},{2,10},{10... | collective-permute-start | bytes 1179656 | tf_op jit(solution)/shard_map/ppermute | solution.py:1100
  13.9 7.8 %collective-permute-start.7 = (bf16[3,128,512]{2,1,0:T(8,128)(2,1)S(1)}, bf16[3,128,512]{2,1,0:T(8,128)(2,1)S(1)}, u32[]{:S(2)}, u32[]{:S(2)}) collective-permute-start(bf16[3,128,512]{2,1,0:T(8,128)(2,1)S(1)} %collective-permute-done), channel_id=1, source_target_pairs={{0,2},{1,5},{2,0},{3,7},{4,6},{5,1},{6,4},{7,3},{8,10},{9,13},{10,... | collective-permute-start | bytes 1179656 | tf_op jit(solution)/shard_map/ppermute | solution.py:1100
  16.8 15.3 %collective-permute-start.6 = (f32[11328]{0:T(1024)S(1)}, f32[11328]{0:T(1024)S(1)}, u32[]{:S(2)}, u32[]{:S(2)}) collective-permute-start(f32[11328]{0:T(1024)S(1)} %pad_maximum_fusion.4), channel_id=1, source_target_pairs={{0,8},{8,0},{16,24},{24,16},{1,9},{9,1},{17,25},{25,17},{2,10},{10... | collective-permute-start | bytes 135944 | tf_op jit(solution)/shard_map/ppermute | solution.py:1100
  18.4 12.8 %copy-start.35 = (bf16[1024,4]{0,1:T(4,128)(2,1)S(1)}, bf16[1024,4]{0,1:T(4,128)(2,1)}, u32[]{:S(2)}) copy-start(bf16[1024,4]{0,1:T(4,128)(2,1)} %param.13) | copy-start | bytes 24580
  21.8 12.1 %collective-permute-start.8 = (bf16[3,256,512]{2,1,0:T(8,128)(2,1)S(1)}, bf16[3,256,512]{2,1,0:T(8,128)(2,1)S(1)}, u32[]{:S(2)}, u32[]{:S(2)}) collective-permute-start(bf16[3,256,512]{2,1,0:T(8,128)(2,1)S(1)} %pad_maximum_fusion.2), channel_id=1, source_target_pairs={{0,4},{1,3},{2,6},{3,1},{4,0},{5,7},{6,2},{7,5},{8,12},{9,11},{10,... | collective-permute-start | bytes 2359304 | tf_op jit(solution)/shard_map/ppermute | solution.py:1100
  29.6 16.1 %collective-permute-start.1 = (bf16[2,128,1408]{2,1,0:T(8,128)(2,1)}, bf16[2,128,1408]{2,1,0:T(8,128)(2,1)S(1)}, u32[]{:S(2)}, u32[]{:S(2)}) collective-permute-start(bf16[2,128,1408]{2,1,0:T(8,128)(2,1)} %constant_dynamic-slice_fusion.6), channel_id=1, source_target_pairs={{0,8},{8,0},{16,24},{24,16},{1,9},{9,1},{17,25},{25,17},{2,10},{10... | collective-permute-start | bytes 2162696 | tf_op jit(solution)/shard_map/ppermute | solution.py:1100
  33.8 26.7 %copy-start.26 = (bf16[1408,256]{1,0:T(8,128)(2,1)S(1)}, bf16[1408,256]{1,0:T(8,128)(2,1)}, u32[]{:S(2)}) copy-start(bf16[1408,256]{1,0:T(8,128)(2,1)} %constant_dynamic-slice_fusion.4) | copy-start | bytes 2162692
  34.8 28.6 %collective-permute-start.9 = (bf16[3,512,512]{2,1,0:T(8,128)(2,1)}, bf16[3,512,512]{2,1,0:T(8,128)(2,1)}, u32[]{:S(2)}, u32[]{:S(2)}) collective-permute-start(bf16[3,512,512]{2,1,0:T(8,128)(2,1)} %constant_dynamic-update-slice_fusion.2.qkv_came_ref.refs_18_.refs_8_.refs_19_), channel_id=1, source_target_pairs={{0,1},{1,0},{2,3},{3,2},{4,5},{5,4},{6,7},{7,6},{8,9},{9,8},{10,11... | collective-permute-start | bytes 4718600 | tf_op jit(solution)/shard_map/ppermute | solution.py:1100
  34.8 28.6 %copy-start.37 = (f32[3,4,1024]{2,1,0:T(4,128)}, f32[3,4,1024]{2,1,0:T(4,128)S(1)}, u32[]{:S(2)}) copy-start(f32[3,4,1024]{2,1,0:T(4,128)S(1)} %constant_dynamic-update-slice_fusion.taps_ref.after_ref.refs_0_.refs_1_.refs_2_.refs_14_.refs_4_.refs_3_.refs_15_) | copy-start | bytes 147460
  45.7 16.3 %collective-permute-start.2 = (bf16[2,128,1408]{2,1,0:T(8,128)(2,1)S(1)}, bf16[2,128,1408]{2,1,0:T(8,128)(2,1)S(1)}, u32[]{:S(2)}, u32[]{:S(2)}) collective-permute-start(bf16[2,128,1408]{2,1,0:T(8,128)(2,1)S(1)} %collective-permute-done.1), channel_id=1, source_target_pairs={{0,2},{1,5},{2,0},{3,7},{4,6},{5,1},{6,4},{7,3},{8,10},{9,13},{10,... | collective-permute-start | bytes 2162696 | tf_op jit(solution)/shard_map/ppermute | solution.py:1100
  47.8 12.6 %collective-permute-start.4 = (bf16[256,1024]{1,0:T(8,128)(2,1)}, bf16[256,1024]{1,0:T(8,128)(2,1)S(1)}, u32[]{:S(2)}, u32[]{:S(2)}) collective-permute-start(bf16[256,1024]{1,0:T(8,128)(2,1)} %constant_dynamic-slice_fusion.5), channel_id=1, source_target_pairs={{0,8},{8,0},{16,24},{24,16},{1,9},{9,1},{17,25},{25,17},{2,10},{10... | collective-permute-start | bytes 1572872 | tf_op jit(solution)/shard_map/ppermute | solution.py:1100
  60.5 2.9 collective-permute-start.10
  60.5 19.2 %collective-permute-start.5 = (bf16[1408,256]{1,0:T(8,128)(2,1)S(1)}, bf16[1408,256]{1,0:T(8,128)(2,1)S(1)}, u32[]{:S(2)}, u32[]{:S(2)}) collective-permute-start(bf16[1408,256]{1,0:T(8,128)(2,1)S(1)} %copy-done.26), channel_id=1, source_target_pairs={{0,8},{8,0},{16,24},{24,16},{1,9},{9,1},{17,25},{25,17},{2,10},{10... | collective-permute-start | bytes 2162696 | tf_op jit(solution)/shard_map/ppermute | solution.py:1100
  62.1 19.1 %collective-permute-start.3 = (bf16[2,256,1408]{2,1,0:T(8,128)(2,1)S(1)}, bf16[2,256,1408]{2,1,0:T(8,128)(2,1)S(1)}, u32[]{:S(2)}, u32[]{:S(2)}) collective-permute-start(bf16[2,256,1408]{2,1,0:T(8,128)(2,1)S(1)} %pad_maximum_fusion), channel_id=1, source_target_pairs={{0,4},{1,3},{2,6},{3,1},{4,0},{5,7},{6,2},{7,5},{8,12},{9,11},{10,... | collective-permute-start | bytes 4325384 | tf_op jit(solution)/shard_map/ppermute | solution.py:1100
  82.3 19.3 %collective-permute-start.12 = (bf16[2,512,1408]{2,1,0:T(8,128)(2,1)}, bf16[2,512,1408]{2,1,0:T(8,128)(2,1)}, u32[]{:S(2)}, u32[]{:S(2)}) collective-permute-start(bf16[2,512,1408]{2,1,0:T(8,128)(2,1)} %constant_dynamic-update-slice_fusion.5.lift_came_ref.refs_4_.refs_7_.refs_8_), channel_id=1, source_target_pairs={{0,1},{1,0},{2,3},{3,2},{4,5},{5,4},{6,7},{7,6},{8,9},{9,8},{10,11... | collective-permute-start | bytes 8650760 | tf_op jit(solution)/shard_map/ppermute | solution.py:1100
  82.3 15.9 %collective-permute-start.11 = (bf16[1408,256]{1,0:T(8,128)(2,1)S(1)}, bf16[1408,256]{1,0:T(8,128)(2,1)S(1)}, u32[]{:S(2)}, u32[]{:S(2)}) collective-permute-start(bf16[1408,256]{1,0:T(8,128)(2,1)S(1)} %collective-permute-done.5), channel_id=1, source_target_pairs={{0,2},{1,5},{2,0},{3,7},{4,6},{5,1},{6,4},{7,3},{8,10},{9,13},{10,... | collective-permute-start | bytes 2162696 | tf_op jit(solution)/shard_map/ppermute | solution.py:1100
  98.4 3.3 collective-permute-start.13
  114.5 16.5 %collective-permute-start.14 = (bf16[256,1024]{1,0:T(8,128)(2,1)}, bf16[256,1024]{1,0:T(8,128)(2,1)S(1)}, u32[]{:S(2)}, u32[]{:S(2)}) collective-permute-start(bf16[256,1024]{1,0:T(8,128)(2,1)} %get-tuple-element.142), channel_id=1, source_target_pairs={{0,16},{8,24},{1,17},{9,25},{2,18},{10,26},{3,19},{11,27},{4,20},{... | collective-permute-start | bytes 1572872 | tf_op jit(solution)/shard_map/ppermute | solution.py:1231
  130.7 27.6 %copy-start.48 = (bf16[256,1024]{1,0:T(8,128)(2,1)S(1)}, bf16[256,1024]{1,0:T(8,128)(2,1)}, u32[]{:S(2)}) copy-start(bf16[256,1024]{1,0:T(8,128)(2,1)} %get-tuple-element.146) | copy-start | bytes 1572868
  158.3 18.6 %collective-permute-start.15 = (bf16[256,1024]{1,0:T(8,128)(2,1)S(1)}, bf16[256,1024]{1,0:T(8,128)(2,1)S(1)}, u32[]{:S(2)}, u32[]{:S(2)}) collective-permute-start(bf16[256,1024]{1,0:T(8,128)(2,1)S(1)} %copy-done.48), channel_id=1, source_target_pairs={{0,16},{8,24},{1,17},{9,25},{2,18},{10,26},{3,19},{11,27},{4,20},{... | collective-permute-start | bytes 1572872 | tf_op jit(solution)/shard_map/ppermute | solution.py:1231
  175.2 58.8 %collective-permute-start.16 = (bf16[256,1024]{1,0:T(8,128)(2,1)}, bf16[256,1024]{1,0:T(8,128)(2,1)S(1)}, u32[]{:S(2)}, u32[]{:S(2)}) collective-permute-start(bf16[256,1024]{1,0:T(8,128)(2,1)} %get-tuple-element.156.refs_0_), channel_id=1, source_target_pairs={{16,0},{24,8},{17,1},{25,9},{18,2},{26,10},{19,3},{27,11},{20,4},{... | collective-permute-start | bytes 1572872 | tf_op jit(solution)/shard_map/ppermute | solution.py:1241
  199.6 99.6 %collective-permute-start.19 = (bf16[256,1024]{1,0:T(8,128)(2,1)}, bf16[256,1024]{1,0:T(8,128)(2,1)S(1)}, u32[]{:S(2)}, u32[]{:S(2)}) collective-permute-start(bf16[256,1024]{1,0:T(8,128)(2,1)} %get-tuple-element.167.refs_1_), channel_id=1, source_target_pairs={{16,0},{24,8},{17,1},{25,9},{18,2},{26,10},{19,3},{27,11},{20,4},{... | collective-permute-start | bytes 1572872 | tf_op jit(solution)/shard_map/ppermute | solution.py:1241
  249.0 65.5 %collective-permute-start.17 = (bf16[4,256,2816]{2,1,0:T(8,128)(2,1)}, bf16[4,256,2816]{2,1,0:T(8,128)(2,1)}, u32[]{:S(2)}, u32[]{:S(2)}) collective-permute-start(bf16[4,256,2816]{2,1,0:T(8,128)(2,1)} %get-tuple-element.186.refs_1_.refs_5_), channel_id=1, source_target_pairs={{0,1},{1,0},{2,3},{3,2},{4,5},{5,4},{6,7},{7,6},{8,9},{9,8},{10,11... | collective-permute-start | bytes 17301512 | tf_op jit(solution)/shard_map/ppermute | solution.py:1100
  270.9 43.6 %collective-permute-start.18 = (bf16[6,256,1024]{2,1,0:T(8,128)(2,1)}, bf16[6,256,1024]{2,1,0:T(8,128)(2,1)S(1)}, u32[]{:S(2)}, u32[]{:S(2)}) collective-permute-start(bf16[6,256,1024]{2,1,0:T(8,128)(2,1)} %get-tuple-element.187.refs_1_.refs_5_), channel_id=1, source_target_pairs={{0,1},{1,0},{2,3},{3,2},{4,5},{5,4},{6,7},{7,6},{8,9},{9,8},{10,11... | collective-permute-start | bytes 9437192 | tf_op jit(solution)/shard_map/ppermute | solution.py:1100
  314.3 28.1 %collective-permute-start.21 = (bf16[4,256,2816]{2,1,0:T(8,128)(2,1)}, bf16[4,256,2816]{2,1,0:T(8,128)(2,1)}, u32[]{:S(2)}, u32[]{:S(2)}) collective-permute-start(bf16[4,256,2816]{2,1,0:T(8,128)(2,1)} %get-tuple-element.206.refs_2_.refs_6_), channel_id=1, source_target_pairs={{0,1},{1,0},{2,3},{3,2},{4,5},{5,4},{6,7},{7,6},{8,9},{9,8},{10,11... | collective-permute-start | bytes 17301512 | tf_op jit(solution)/shard_map/ppermute | solution.py:1100
  316.2 26.3 %slice-start = ((s8[5767168]{0:T(1024)(128)(4,1)}), s8[4194304]{0:T(1024)(128)(4,1)S(1)}, s32[]{:S(2)}) async-start(s8[5767168]{0:T(1024)(128)(4,1)} %bitcast.71), calls=%async_computation | async-start | bytes 8388608
  316.2 23.3 %copy-start.27 = (bf16[256,1024]{1,0:T(8,128)(2,1)S(1)}, bf16[256,1024]{1,0:T(8,128)(2,1)}, u32[]{:S(2)}) copy-start(bf16[256,1024]{1,0:T(8,128)(2,1)} %get-tuple-element.145) | copy-start | bytes 1572868
  316.2 23.3 %copy-start.29 = (bf16[256,1024]{1,0:T(8,128)(2,1)S(1)}, bf16[256,1024]{1,0:T(8,128)(2,1)}, u32[]{:S(2)}) copy-start(bf16[256,1024]{1,0:T(8,128)(2,1)} %get-tuple-element.184.refs_1_) | copy-start | bytes 1572868
  316.2 23.4 %copy-start.39 = (f32[1,1024]{1,0:T(1,128)S(1)}, f32[1,1024]{1,0:T(1,128)}, u32[]{:S(2)}) copy-start(f32[1,1024]{1,0:T(1,128)} %get-tuple-element.239) | copy-start | bytes 12292
  316.2 23.4 %copy-start.40 = (f32[1,1024]{1,0:T(1,128)S(1)}, f32[1,1024]{1,0:T(1,128)}, u32[]{:S(2)}) copy-start(f32[1,1024]{1,0:T(1,128)} %get-tuple-element.240) | copy-start | bytes 12292
  316.2 23.4 %copy-start.34 = (f32[3,4,1024]{2,1,0:T(4,128)S(1)}, f32[3,4,1024]{2,1,0:T(4,128)}, u32[]{:S(2)}) copy-start(f32[3,4,1024]{2,1,0:T(4,128)} %get-tuple-element.233) | copy-start | bytes 147460
  316.2 24.3 %copy-start.28 = (bf16[256,1024]{1,0:T(8,128)(2,1)S(1)}, bf16[256,1024]{1,0:T(8,128)(2,1)}, u32[]{:S(2)}) copy-start(bf16[256,1024]{1,0:T(8,128)(2,1)} %get-tuple-element.185) | copy-start | bytes 1572868
  316.2 26.3 %slice-start.1 = ((s8[5767168]{0:T(1024)(128)(4,1)}), s8[1572864]{0:T(1024)(128)(4,1)S(1)}, s32[]{:S(2)}) async-start(s8[5767168]{0:T(1024)(128)(4,1)} %bitcast.71), calls=%async_computation.1 | async-start | bytes 3145728
  339.1 27.0 %collective-permute-start.22 = (bf16[6,256,1024]{2,1,0:T(8,128)(2,1)}, bf16[6,256,1024]{2,1,0:T(8,128)(2,1)}, u32[]{:S(2)}, u32[]{:S(2)}) collective-permute-start(bf16[6,256,1024]{2,1,0:T(8,128)(2,1)} %get-tuple-element.209.refs_2_.refs_6_), channel_id=1, source_target_pairs={{0,1},{1,0},{2,3},{3,2},{4,5},{5,4},{6,7},{7,6},{8,9},{9,8},{10,11... | collective-permute-start | bytes 9437192 | tf_op jit(solution)/shard_map/ppermute | solution.py:1100
  342.4 59.6 %collective-permute-start.20 = (bf16[2,256,512]{2,1,0:T(8,128)(2,1)}, bf16[2,256,512]{2,1,0:T(8,128)(2,1)}, u32[]{:S(2)}, u32[]{:S(2)}) collective-permute-start(bf16[2,256,512]{2,1,0:T(8,128)(2,1)} %fusion.2), channel_id=1, source_target_pairs={{0,16},{8,24},{16,0},{24,8},{1,17},{9,25},{17,1},{25,9},{2,18},{10... | collective-permute-start | bytes 1572872 | tf_op jit(solution)/shard_map/ppermute | solution.py:1100
  354.5 11.1 %copy-start = (bf16[2,256,2816]{2,1,0:T(8,128)(2,1)}, bf16[2,256,2816]{2,1,0:T(8,128)(2,1)S(1)}, u32[]{:S(2)}) copy-start(bf16[2,256,2816]{2,1,0:T(8,128)(2,1)S(1)} %get-tuple-element.207.refs_0_.keep_ref) | copy-start | bytes 8650756
  354.5 34.8 %collective-permute-start.23 = (bf16[2,256,2816]{2,1,0:T(8,128)(2,1)}, bf16[2,256,2816]{2,1,0:T(8,128)(2,1)}, u32[]{:S(2)}, u32[]{:S(2)}) collective-permute-start(bf16[2,256,2816]{2,1,0:T(8,128)(2,1)} %get-tuple-element.212), channel_id=1, source_target_pairs={{0,2},{1,5},{2,0},{3,7},{4,6},{5,1},{6,4},{7,3},{8,10},{9,13},{10,... | collective-permute-start | bytes 8650760 | tf_op jit(solution)/shard_map/ppermute | solution.py:1100
  355.9 10.2 %copy-start.2 = (bf16[6,256,1024]{2,1,0:T(8,128)(2,1)S(1)}, bf16[6,256,1024]{2,1,0:T(8,128)(2,1)}, u32[]{:S(2)}) copy-start(bf16[6,256,1024]{2,1,0:T(8,128)(2,1)} %get-tuple-element.187.refs_1_.refs_5_) | copy-start | bytes 9437188
  365.6 10.8 %copy-start.10 = (bf16[1,704,1024]{2,1,0:T(8,128)(2,1)}, bf16[1,704,1024]{2,1,0:T(8,128)(2,1)S(1)}, u32[]{:S(2)}) copy-start(bf16[1,704,1024]{2,1,0:T(8,128)(2,1)S(1)} %get-tuple-element.208.refs_0_.keep_ref) | copy-start | bytes 4325380
  365.6 34.7 %collective-permute-start.24 = (bf16[1,704,1024]{2,1,0:T(8,128)(2,1)}, bf16[1,704,1024]{2,1,0:T(8,128)(2,1)}, u32[]{:S(2)}, u32[]{:S(2)}) collective-permute-start(bf16[1,704,1024]{2,1,0:T(8,128)(2,1)} %get-tuple-element.214), channel_id=1, source_target_pairs={{0,8},{8,0},{16,24},{24,16},{1,9},{9,1},{17,25},{25,17},{2,10},{10... | collective-permute-start | bytes 4325384 | tf_op jit(solution)/shard_map/ppermute | solution.py:1100
  369.9 6.5 %copy-start.9 = (bf16[6,256,1024]{2,1,0:T(8,128)(2,1)S(1)}, bf16[6,256,1024]{2,1,0:T(8,128)(2,1)}, u32[]{:S(2)}) copy-start(bf16[6,256,1024]{2,1,0:T(8,128)(2,1)} %copy-done.7) | copy-start | bytes 9437188
  376.4 12.9 %copy-start.1 = (bf16[2,256,2816]{2,1,0:T(8,128)(2,1)S(1)}, bf16[2,256,2816]{2,1,0:T(8,128)(2,1)}, u32[]{:S(2)}) copy-start(bf16[2,256,2816]{2,1,0:T(8,128)(2,1)} %copy-done) | copy-start | bytes 8650756
  380.0 31.4 %collective-permute-start.26 = (bf16[1,256,1024]{2,1,0:T(8,128)(2,1)S(1)}, bf16[1,256,1024]{2,1,0:T(8,128)(2,1)S(1)}, u32[]{:S(2)}, u32[]{:S(2)}) collective-permute-start(bf16[1,256,1024]{2,1,0:T(8,128)(2,1)S(1)} %get-tuple-element.217), channel_id=1, source_target_pairs={{0,8},{8,0},{16,24},{24,16},{1,9},{9,1},{17,25},{25,17},{2,10},{10... | collective-permute-start | bytes 1572872 | tf_op jit(solution)/shard_map/ppermute | solution.py:1100
  381.6 41.7 %collective-permute-start.27 = (bf16[3,256,1024]{2,1,0:T(8,128)(2,1)S(1)}, bf16[3,256,1024]{2,1,0:T(8,128)(2,1)S(1)}, u32[]{:S(2)}, u32[]{:S(2)}) collective-permute-start(bf16[3,256,1024]{2,1,0:T(8,128)(2,1)S(1)} %get-tuple-element.219), channel_id=1, source_target_pairs={{0,2},{1,5},{2,0},{3,7},{4,6},{5,1},{6,4},{7,3},{8,10},{9,13},{10,... | collective-permute-start | bytes 4718600 | tf_op jit(solution)/shard_map/ppermute | solution.py:1100
  389.3 11.0 %copy-start.11 = (bf16[1,704,1024]{2,1,0:T(8,128)(2,1)S(1)}, bf16[1,704,1024]{2,1,0:T(8,128)(2,1)}, u32[]{:S(2)}) copy-start(bf16[1,704,1024]{2,1,0:T(8,128)(2,1)} %copy-done.10) | copy-start | bytes 4325380
  391.6 34.6 %collective-permute-start.28 = (bf16[2,128,2816]{2,1,0:T(8,128)(2,1)S(1)}, bf16[2,128,2816]{2,1,0:T(8,128)(2,1)S(1)}, u32[]{:S(2)}, u32[]{:S(2)}) collective-permute-start(bf16[2,128,2816]{2,1,0:T(8,128)(2,1)S(1)} %get-tuple-element.221), channel_id=1, source_target_pairs={{0,4},{1,3},{2,6},{3,1},{4,0},{5,7},{6,2},{7,5},{8,12},{9,11},{10,... | collective-permute-start | bytes 4325384 | tf_op jit(solution)/shard_map/ppermute | solution.py:1100
  402.0 9.4 %copy-start.15 = (bf16[1,352,1024]{2,1,0:T(8,128)(2,1)}, bf16[1,352,1024]{2,1,0:T(8,128)(2,1)S(1)}, u32[]{:S(2)}) copy-start(bf16[1,352,1024]{2,1,0:T(8,128)(2,1)S(1)} %get-tuple-element.215.after_ref.keep_ref) | copy-start | bytes 2162692
  404.2 17.9 %collective-permute-start.25 = (bf16[2,2,256,256]{3,2,1,0:T(8,128)(2,1)S(1)}, bf16[2,2,256,256]{3,2,1,0:T(8,128)(2,1)S(1)}, u32[]{:S(2)}, u32[]{:S(2)}) collective-permute-start(bf16[2,2,256,256]{3,2,1,0:T(8,128)(2,1)S(1)} %get-tuple-element.295), channel_id=1, source_target_pairs={{0,8},{8,0},{16,24},{24,16},{1,9},{9,1},{17,25},{25,17},{2,10},{10... | collective-permute-start | bytes 1572872 | tf_op jit(solution)/shard_map/ppermute | solution.py:1100
  405.1 27.4 %collective-permute-start.29 = (bf16[1,352,1024]{2,1,0:T(8,128)(2,1)S(1)}, bf16[1,352,1024]{2,1,0:T(8,128)(2,1)}, u32[]{:S(2)}, u32[]{:S(2)}) collective-permute-start(bf16[1,352,1024]{2,1,0:T(8,128)(2,1)S(1)} %get-tuple-element.223), channel_id=1, source_target_pairs={{0,2},{1,5},{2,0},{3,7},{4,6},{5,1},{6,4},{7,3},{8,10},{9,13},{10,... | collective-permute-start | bytes 2162696 | tf_op jit(solution)/shard_map/ppermute | solution.py:1100
  412.2 11.5 %copy-start.22 = (bf16[1,128,1024]{2,1,0:T(8,128)(2,1)}, bf16[1,128,1024]{2,1,0:T(8,128)(2,1)S(1)}, u32[]{:S(2)}) copy-start(bf16[1,128,1024]{2,1,0:T(8,128)(2,1)S(1)} %get-tuple-element.218.after_ref.keep_ref) | copy-start | bytes 786436
  412.2 25.9 %collective-permute-start.30 = (bf16[1,128,1024]{2,1,0:T(8,128)(2,1)}, bf16[1,128,1024]{2,1,0:T(8,128)(2,1)}, u32[]{:S(2)}, u32[]{:S(2)}) collective-permute-start(bf16[1,128,1024]{2,1,0:T(8,128)(2,1)} %get-tuple-element.225), channel_id=1, source_target_pairs={{0,2},{1,5},{2,0},{3,7},{4,6},{5,1},{6,4},{7,3},{8,10},{9,13},{10,... | collective-permute-start | bytes 786440 | tf_op jit(solution)/shard_map/ppermute | solution.py:1100
  423.7 17.2 %collective-permute-start.31 = (bf16[3,128,1024]{2,1,0:T(8,128)(2,1)S(1)}, bf16[3,128,1024]{2,1,0:T(8,128)(2,1)S(1)}, u32[]{:S(2)}, u32[]{:S(2)}) collective-permute-start(bf16[3,128,1024]{2,1,0:T(8,128)(2,1)S(1)} %get-tuple-element.227), channel_id=1, source_target_pairs={{0,4},{1,3},{2,6},{3,1},{4,0},{5,7},{6,2},{7,5},{8,12},{9,11},{10,... | collective-permute-start | bytes 2359304 | tf_op jit(solution)/shard_map/ppermute | solution.py:1100
  429.8 11.1 %collective-permute-start.36 = (f32[22656]{0:T(1024)S(1)}, f32[22656]{0:T(1024)S(1)}, u32[]{:S(2)}, u32[]{:S(2)}) collective-permute-start(f32[22656]{0:T(1024)S(1)} %pad_maximum_fusion.3), channel_id=1, source_target_pairs={{0,1},{1,0},{2,3},{3,2},{4,5},{5,4},{6,7},{7,6},{8,9},{9,8},{10,11... | collective-permute-start | bytes 271880 | tf_op jit(solution)/shard_map/ppermute | solution.py:1100
  429.9 18.6 %collective-permute-start.32 = (bf16[2,128,1408]{2,1,0:T(8,128)(2,1)S(1)}, bf16[2,128,1408]{2,1,0:T(8,128)(2,1)S(1)}, u32[]{:S(2)}, u32[]{:S(2)}) collective-permute-start(bf16[2,128,1408]{2,1,0:T(8,128)(2,1)S(1)} %get-tuple-element.229), channel_id=1, source_target_pairs={{0,8},{8,0},{16,24},{24,16},{1,9},{9,1},{17,25},{25,17},{2,10},{10... | collective-permute-start | bytes 2162696 | tf_op jit(solution)/shard_map/ppermute | solution.py:1100
  436.0 13.6 %collective-permute-start.33 = (bf16[1,176,1024]{2,1,0:T(8,128)(2,1)S(1)}, bf16[1,176,1024]{2,1,0:T(8,128)(2,1)S(1)}, u32[]{:S(2)}, u32[]{:S(2)}) collective-permute-start(bf16[1,176,1024]{2,1,0:T(8,128)(2,1)S(1)} %get-tuple-element.230), channel_id=1, source_target_pairs={{0,4},{1,3},{2,6},{3,1},{4,0},{5,7},{6,2},{7,5},{8,12},{9,11},{10,... | collective-permute-start | bytes 1081352 | tf_op jit(solution)/shard_map/ppermute | solution.py:1100
  439.2 15.1 %collective-permute-start.34 = (bf16[1,64,1024]{2,1,0:T(8,128)(2,1)S(1)}, bf16[1,64,1024]{2,1,0:T(8,128)(2,1)S(1)}, u32[]{:S(2)}, u32[]{:S(2)}) collective-permute-start(bf16[1,64,1024]{2,1,0:T(8,128)(2,1)S(1)} %get-tuple-element.231), channel_id=1, source_target_pairs={{0,4},{1,3},{2,6},{3,1},{4,0},{5,7},{6,2},{7,5},{8,12},{9,11},{10,... | collective-permute-start | bytes 393224 | tf_op jit(solution)/shard_map/ppermute | solution.py:1100
  440.9 7.5 %copy-start.21 = (bf16[2,128,1408]{2,1,0:T(8,128)(2,1)S(1)}, bf16[2,128,1408]{2,1,0:T(8,128)(2,1)}, u32[]{:S(2)}) copy-start(bf16[2,128,1408]{2,1,0:T(8,128)(2,1)} %copy-done.19) | copy-start | bytes 2162692
  440.9 5.7 %collective-permute-start.37 = (f32[22656]{0:T(1024)S(1)}, f32[22656]{0:T(1024)S(1)}, u32[]{:S(2)}, u32[]{:S(2)}) collective-permute-start(f32[22656]{0:T(1024)S(1)} %fusion.14), channel_id=1, source_target_pairs={{0,2},{1,3},{2,0},{3,1},{4,6},{5,7},{6,4},{7,5},{8,10},{9,11},{10,... | collective-permute-start | bytes 271880 | tf_op jit(solution)/shard_map/ppermute | solution.py:1100
  446.6 5.3 %collective-permute-start.38 = (f32[22656]{0:T(1024)S(1)}, f32[22656]{0:T(1024)S(1)}, u32[]{:S(2)}, u32[]{:S(2)}) collective-permute-start(f32[22656]{0:T(1024)S(1)} %add.166), channel_id=1, source_target_pairs={{0,4},{1,5},{2,6},{3,7},{4,0},{5,1},{6,2},{7,3},{8,12},{9,13},{10,... | collective-permute-start | bytes 271880 | tf_op jit(solution)/shard_map/ppermute | solution.py:1100
  447.1 13.6 %collective-permute-start.35 = (bf16[3,128,512]{2,1,0:T(8,128)(2,1)S(1)}, bf16[3,128,512]{2,1,0:T(8,128)(2,1)S(1)}, u32[]{:S(2)}, u32[]{:S(2)}) collective-permute-start(bf16[3,128,512]{2,1,0:T(8,128)(2,1)S(1)} %get-tuple-element.232), channel_id=1, source_target_pairs={{0,8},{8,0},{16,24},{24,16},{1,9},{9,1},{17,25},{25,17},{2,10},{10... | collective-permute-start | bytes 1179656 | tf_op jit(solution)/shard_map/ppermute | solution.py:1100
  453.1 4.8 %collective-permute-start.39 = (f32[1416]{0:T(1024)S(1)}, f32[1416]{0:T(1024)S(1)}, u32[]{:S(2)}, u32[]{:S(2)}) collective-permute-start(f32[1416]{0:T(1024)S(1)} %pad_maximum_fusion.5), channel_id=1, source_target_pairs={{0,8},{8,0},{16,24},{24,16},{1,9},{9,1},{17,25},{25,17},{2,10},{10... | collective-permute-start | bytes 17000 | tf_op jit(solution)/shard_map/ppermute | solution.py:1100
  (30 other events, 64.3 us)

commit v4 on v3

--- a/solution.py
+++ b/solution.py
@@ -189,8 +189,8 @@
 
 
 def mixer_forward_kernel(
+    step,
     info_ref,
-    after_ref,
     stream_ref,
     gain_ref,
     w_beta_ref,
@@ -215,7 +215,6 @@
     w_out_ref,
     sems,
 ):
-    step = pl.program_id(0)
     length = stream_ref.shape[0]
     spans = length // SPAN
     heads = linear_ref.shape[2] // LANES
@@ -343,7 +342,7 @@
     here = tile // LANES
     out = jax.ShapeDtypeStruct
     return pl.pallas_call(
-        wrap(mixer_forward_kernel),
+        wrap(lambda info_ref, after_ref, *refs: mixer_forward_kernel(pl.program_id(0), info_ref, *refs)),
         name="mixer_forward",
         grid_spec=pltpu.PrefetchScalarGridSpec(
             num_scalar_prefetch=1,
@@ -390,10 +389,9 @@
 
 
 def mixer_backward_kernel(
+    step,
+    load,
     info_ref,
-    after_ref,
-    also_ref,
-    third_ref,
     stream_ref,
     branch_ref,
     strengths_ref,
@@ -427,16 +425,15 @@
     w_out_ref,
     sems,
 ):
-    step = pl.program_id(0)
-    steps = pl.num_programs(0)
     length = stream_ref.shape[0]
     spans = length // SPAN
     pairs = length // PAIR
     tile = stack_ref.shape[2]
     heads = tile // LANES
-    refs = (qkv_own_ref, out_own_ref, qkv_came_ref, qkv_twin_ref, out_came_ref, out_twin_ref)
-    own_qkv, own_out, qkv, out = mixer_copies(info_ref, refs, w_qkv_ref, w_out_ref, sems)
-    start_all(step, [own_out, own_qkv])
+    if load:
+        refs = (qkv_own_ref, out_own_ref, qkv_came_ref, qkv_twin_ref, out_came_ref, out_twin_ref)
+        own_qkv, own_out, qkv, out = mixer_copies(info_ref, refs, w_qkv_ref, w_out_ref, sems)
+        start_all(step, [own_out, own_qkv])
 
     @pl.when(step == 0)
     def first():
@@ -463,9 +460,10 @@
     def span_of(array, span):
         return array[span * SPAN : (span + 1) * SPAN]
 
-    wait_all(step, 0, [own_out, own_qkv])
-    wait_all(step, 1, out + qkv)
-    start_all(step, out + qkv)
+    if load:
+        wait_all(step, 0, [own_out, own_qkv])
+        wait_all(step, 1, out + qkv)
+        start_all(step, out + qkv)
     normed_out_grad = mm_nt(branch_low_ref[...], w_out_ref[step])
     totals, gates, active = [], [], []
     for which in range(3):
@@ -634,7 +632,7 @@
         normed_grad = normed_grad + mm_nt(linear_low, w_qkv_ref[step, which])
     normed_grad_ref[step] = normed_grad
 
-    @pl.when(step == steps - 1)
+    @pl.when(step == 1)
     def last_step():
         strengths_low = low(strengths_sum_ref[...])
         strengths_grad_ref[...] = strengths_low
@@ -645,7 +643,7 @@
         gain_grad_ref[...] = gain_grad
 
 
-def mixer_backward(info, after, stream, branch, kept, gain, weights, w_beta, taps, out_gain, old=None):
+def mixer_backward(info, after, stream, branch, kept, gain, weights, w_beta, taps, out_gain, old):
     strengths, linear, output, fresh, solve, states, moves = kept
     length, width = stream.shape
     tile = weights[0].shape[2]
@@ -673,17 +671,16 @@
         tiled((3, count, tile), 2),
         whole((1, LANES)),
     ] + [ANYWHERE] * 6
-    kernel, more = only_second(mixer_backward_kernel), []
-    if old is not None:
-        more = old[1:]
-        kernel = or_keep(mixer_backward_kernel, len(in_specs), 6, 1)
-        in_specs = in_specs + [
-            whole((1, width)),
-            tiled_old((6, length, tile), 2),
-            whole((length, LANES)),
-            tiled_old((3, count, tile), 2),
-            whole((1, LANES)),
-        ]
+    body = lambda info_ref, *refs: mixer_backward_kernel(pl.program_id(0), True, info_ref, *refs[3:])
+    kernel = or_keep(body, len(in_specs), 6, 1)
+    more = old[1:]
+    in_specs = in_specs + [
+        whole((1, width)),
+        tiled_old((6, length, tile), 2),
+        whole((length, LANES)),
+        tiled_old((3, count, tile), 2),
+        whole((1, LANES)),
+    ]
     return pl.pallas_call(
         kernel,
         name="mixer_backward",
@@ -772,6 +769,7 @@
 
 
 def feed_forward_kernel(
+    alone,
     info_ref,
     middle_ref,
     gain_ref,
@@ -794,8 +792,9 @@
     units = down_own_ref.shape[0]
     refs = (lift_own_ref, down_own_ref, lift_came_ref, lift_twin_ref, down_came_ref, down_twin_ref)
     tiles = feed_tiles(refs, w_gate_up_ref, w_down_ref, sems)
-    for tile in tiles[:AHEAD]:
-        start_each(tile[3] + tile[4])
+    if alone:
+        for tile in tiles[:AHEAD]:
+            start_each(tile[3] + tile[4])
     middle = middle_ref[...]
     normed_ref[0] = low(middle * norm_scale(middle, 1e-6) * gain_ref[...])
     apart_order(info_ref, normed_ref.at[0], normed_ref.at[1])
@@ -822,12 +821,13 @@
             which, start, size, lift, down = tiles[index - 1]
             span = pl.ds(start, size)
             place = pl.ds(which * units + start, size)
-            outs.append(
-                pltpu.make_async_copy(
-                    kept_ref.at[:, :, place], lifted_ref.at[:, :, place], out_sems.at[index - 1]
+            if alone:
+                outs.append(
+                    pltpu.make_async_copy(
+                        kept_ref.at[:, :, place], lifted_ref.at[:, :, place], out_sems.at[index - 1]
+                    )
                 )
-            )
-            outs[-1].start()
+                outs[-1].start()
             gate, up = lifted[index - 1]
             hidden = low(gate * sigmoid(gate) * up)
             part = mm(hidden, w_down_ref[which, span, :])
@@ -846,7 +846,7 @@
     count = 2 * len(unit_tiles(units))
     out = jax.ShapeDtypeStruct
     return pl.pallas_call(
-        wrap(feed_forward_kernel),
+        wrap(lambda *refs: feed_forward_kernel(True, *refs)),
         name="feed_forward",
         grid_spec=pltpu.PrefetchScalarGridSpec(
             num_scalar_prefetch=1,
@@ -870,6 +870,7 @@
 
 
 def feed_backward_kernel(
+    alone,
     info_ref,
     middle_ref,
     grad_ref,
@@ -901,19 +902,24 @@
     ins, outs = [], []
     for index, (which, start, size, lift, down) in enumerate(tiles):
         place = pl.ds(which * units + start, size)
-        ins.append(pltpu.make_async_copy(lifted_ref.at[:, :, place], kept_ref.at[:, :, place], in_sems.at[index]))
+        if alone:
+            ins.append(
+                pltpu.make_async_copy(lifted_ref.at[:, :, place], kept_ref.at[:, :, place], in_sems.at[index])
+            )
+        first, at = pl.ds(0, 2), out_sems.at
         outs.append(
-            pltpu.make_async_copy(
-                made_ref.at[pl.ds(0, 3), :, place], stack_ref.at[pl.ds(0, 3), :, place], out_sems.at[index]
-            )
+            [
+                pltpu.make_async_copy(kept_ref.at[:, :, place], stack_ref.at[first, :, place], at[2 * index]),
+                pltpu.make_async_copy(made_ref.at[0, :, place], stack_ref.at[2, :, place], at[2 * index + 1]),
+            ]
         )
-    for index in range(AHEAD):
+    for index in range(AHEAD if alone else 0):
         start_each(tiles[index][4] + [ins[index]] + tiles[index][3])
     middle = middle_ref[...]
-    made_ref[3] = jnp.zeros(made_ref.shape[1:], LOW)
-    made_ref[3, :, :width] = low(middle * norm_scale(middle, 1e-6) * gain_ref[...])
-    made_ref[3, :, units : units + width] = grad_ref[...]
-    ends = pltpu.make_async_copy(made_ref.at[3], stack_ref.at[3], out_sems.at[len(tiles)])
+    made_ref[1] = jnp.zeros(made_ref.shape[1:], LOW)
+    made_ref[1, :, :width] = low(middle * norm_scale(middle, 1e-6) * gain_ref[...])
+    made_ref[1, :, units : units + width] = grad_ref[...]
+    ends = pltpu.make_async_copy(made_ref.at[1], stack_ref.at[3], out_sems.at[2 * len(tiles)])
     ends.start()
     grads_ref[0] = grad_ref[...]
     apart_order(info_ref, grads_ref.at[0], grads_ref.at[1], DOWN)
@@ -921,11 +927,12 @@
     for index in range(len(tiles) + 1):
         if index < len(tiles):
             which, start, size, lift, down = tiles[index]
-            wait_each(down)
-        if index:
+            if alone:
+                wait_each(down)
+        if index and alone:
             ins[index - 1].wait()
             wait_each(tiles[index - 1][3])
-        if 0 < index <= len(tiles) - AHEAD:
+        if alone and 0 < index <= len(tiles) - AHEAD:
             more = index + AHEAD - 1
             start_each(tiles[more][4] + [ins[more]] + tiles[more][3])
         if index < len(tiles):
@@ -942,10 +949,10 @@
             silu = gate * open_
             up_grad = low(hidden_grad * silu)
             gate_grad = low(hidden_grad * up * (open_ + silu * (1.0 - open_)))
-            made_ref[0, :, place] = gate_grad
-            made_ref[1, :, place] = up_grad
-            made_ref[2, :, place] = low(silu * up)
-            outs[index - 1].start()
+            kept_ref[0, :, place] = gate_grad
+            kept_ref[1, :, place] = up_grad
+            made_ref[0, :, place] = low(silu * up)
+            start_each(outs[index - 1])
             part = mm_nt(gate_grad, w_gate_up_ref[which, 0, :, span]) + mm_nt(
                 up_grad, w_gate_up_ref[which, 1, :, span]
             )
@@ -957,24 +964,22 @@
     value_grad, gain_grad = norm_back(middle, gain_ref[...], normed_grad_ref[0], 1e-6)
     middle_grad_ref[...] = grad_ref[...].astype(WIDE) + value_grad
     gain_grad_ref[...] = gain_grad
-    wait_each(outs)
+    for copies in outs:
+        wait_each(copies)
     ends.wait()
 
 
-def feed_backward(info, after, middle, grad, lifted, gain, weights, old=None):
+def feed_backward(info, after, middle, grad, lifted, gain, weights, old):
     length, width = middle.shape
     units = weights[1].shape[0]
     count = 2 * len(unit_tiles(units))
     out = jax.ShapeDtypeStruct
     waits = len(after)
     in_specs = [ANYWHERE] * waits + [whole((length, width)), whole((length, width)), whole((1, width))] + [ANYWHERE] * 7
-    body = lambda info_ref, *refs: feed_backward_kernel(info_ref, *refs[waits:])
-    kernel, more, aliases = only_second(body), [], {}
-    if old is not None:
-        more = old[1:]
-        kernel = or_keep(body, len(in_specs), 3, 1, 1)
-        in_specs = in_specs + [whole((1, width)), ANYWHERE]
-        aliases = {len(in_specs): 2}
+    body = lambda info_ref, *refs: feed_backward_kernel(True, info_ref, *refs[waits:])
+    kernel = or_keep(body, len(in_specs), 3, 1, 1)
+    in_specs = in_specs + [whole((1, width)), ANYWHERE]
+    more, aliases = old[1:], {len(in_specs): 2}
     return pl.pallas_call(
         kernel,
         name="feed_backward",
@@ -989,10 +994,10 @@
                 pltpu.VMEM((2, 2, width, units), LOW),
                 pltpu.VMEM((2, units, width), LOW),
                 pltpu.VMEM((2, length, 2 * units), LOW),
-                pltpu.VMEM((4, length, 2 * units), LOW),
+                pltpu.VMEM((2, length, 2 * units), LOW),
                 pltpu.SemaphoreType.DMA((3 * count,)),
                 pltpu.SemaphoreType.DMA((count,)),
-                pltpu.SemaphoreType.DMA((count + 1,)),
+                pltpu.SemaphoreType.DMA((2 * count + 1,)),
             ],
         ),
         out_shape=[
@@ -1004,6 +1009,276 @@
         compiler_params=params(),
         cost_estimate=cost(13),
     )(info, *after, middle, grad, gain, lifted, *weights, *more)
+
+
+def second_layer_kernel(
+    info_ref,
+    after_ref,
+    stream_ref,
+    grad_ref,
+    gain_ref,
+    feed_gain_ref,
+    w_beta_ref,
+    taps_ref,
+    out_gain_ref,
+    qkv_own_ref,
+    out_own_ref,
+    qkv_came_ref,
+    qkv_twin_ref,
+    out_came_ref,
+    out_twin_ref,
+    lift_own_ref,
+    down_own_ref,
+    lift_came_ref,
+    lift_twin_ref,
+    down_came_ref,
+    down_twin_ref,
+    result_ref,
+    stream_grad_ref,
+    feed_gain_grad_ref,
+    gain_grad_ref,
+    strengths_grad_ref,
+    taps_grad_ref,
+    out_gain_grad_ref,
+    feed_stack_ref,
+    stack_ref,
+    middle_ref,
+    branch_ref,
+    strengths_ref,
+    linear_ref,
+    out_ref,
+    fresh_ref,
+    solve_ref,
+    states_ref,
+    moves_ref,
+    normed_ref,
+    w_qkv_ref,
+    w_out_ref,
+    totals_ref,
+    lows_ref,
+    w_gate_up_ref,
+    w_down_ref,
+    kept_ref,
+    made_ref,
+    strengths_sum_ref,
+    branch_low_ref,
+    again_ref,
+    stacks_ref,
+    sems,
+    feed_sems,
+    out_sems,
+    stack_sems,
+):
+    turn = pl.program_id(0)
+    tile = taps_ref.shape[3]
+    mixer_weights = (qkv_own_ref, out_own_ref, qkv_came_ref, qkv_twin_ref, out_came_ref, out_twin_ref)
+    feed_weights = (lift_own_ref, down_own_ref, lift_came_ref, lift_twin_ref, down_came_ref, down_twin_ref)
+    tiles = feed_tiles(feed_weights, w_gate_up_ref, w_down_ref, feed_sems)
+
+    def leave(which):
+        columns = pl.ds(which * tile, tile)
+        return pltpu.make_async_copy(stacks_ref.at[which], stack_ref.at[:, :, columns], stack_sems.at[which])
+
+    @pl.when(turn < 2)
+    def forward():
+        mixer_forward_kernel(
+            turn,
+            info_ref,
+            stream_ref,
+            gain_ref,
+            w_beta_ref,
+            taps_ref.at[turn],
+            out_gain_ref,
+            *mixer_weights,
+            middle_ref,
+            strengths_ref,
+            linear_ref.at[turn],
+            out_ref.at[turn],
+            fresh_ref.at[turn],
+            solve_ref.at[turn],
+            states_ref.at[turn],
+            moves_ref.at[turn],
+            normed_ref,
+            w_qkv_ref,
+            w_out_ref,
+            sems,
+        )
+
+    @pl.when(turn == 0)
+    def ahead():
+        for item in tiles[:AHEAD]:
+            start_each(item[3] + item[4])
+
+    @pl.when(turn == 1)
+    def feed():
+        feed_forward_kernel(
+            False,
+            info_ref,
+            middle_ref,
+            feed_gain_ref,
+            *feed_weights,
+            result_ref,
+            None,
+            totals_ref,
+            lows_ref,
+            w_gate_up_ref,
+            w_down_ref,
+            kept_ref,
+            feed_sems,
+            None,
+        )
+        feed_backward_kernel(
+            False,
+            info_ref,
+            middle_ref,
+            grad_ref,
+            feed_gain_ref,
+            None,
+            *feed_weights,
+            branch_ref,
+            feed_gain_grad_ref,
+            feed_stack_ref,
+            totals_ref,
+            lows_ref,
+            w_gate_up_ref,
+            w_down_ref,
+            kept_ref,
+            made_ref,
+            feed_sems,
+            None,
+            out_sems,
+        )
+
+    @pl.when(turn >= 2)
+    def backward():
+        half = turn - 2
+        mixer_backward_kernel(
+            half,
+            False,
+            info_ref,
+            stream_ref,
+            branch_ref,
+            strengths_ref,
+            linear_ref.at[half],
+            out_ref.at[half],
+            fresh_ref.at[half],
+            solve_ref.at[half],
+            states_ref.at[half],
+            moves_ref.at[half],
+            gain_ref,
+            w_beta_ref,
+            taps_ref.at[half],
+            out_gain_ref,
+            *mixer_weights,
+            stream_grad_ref,
+            gain_grad_ref,
+            stacks_ref.at[half],
+            strengths_grad_ref,
+            taps_grad_ref.at[half],
+            out_gain_grad_ref,
+            totals_ref,
+            strengths_sum_ref,
+            branch_low_ref,
+            again_ref,
+            w_qkv_ref,
+            w_out_ref,
+            None,
+        )
+
+    for which in range(2):
+
+        @pl.when(turn == 2 + which)
+        def start_leaving():
+            leave(which).start()
+
+    @pl.when(turn == 3)
+    def wait_leaving():
+        leave(0).wait()
+        leave(1).wait()
+
+
+def second_layer(info, after, stream, grad, gains, w_beta, taps, out_gain, mixer_weights, feed_weights):
+    length, width = stream.shape
+    tile, units = mixer_weights[0].shape[2], feed_weights[1].shape[0]
+    inner, spans, pairs, here = 2 * tile, length // SPAN, length // PAIR, tile // LANES
+    taps_count = taps.shape[1]
+    count = 2 * len(unit_tiles(units))
+    out = jax.ShapeDtypeStruct
+    taps = jnp.moveaxis(taps.reshape(3, taps_count, 2, tile), 2, 0)
+    results = pl.pallas_call(
+        only_second(second_layer_kernel),
+        name="second_layer",
+        grid_spec=pltpu.PrefetchScalarGridSpec(
+            num_scalar_prefetch=1,
+            grid=(4,),
+            in_specs=[
+                ANYWHERE,
+                whole((length, width)),
+                whole((length, width)),
+                whole((1, width)),
+                whole((1, width)),
+                whole((width, LANES)),
+                whole((2, 3, taps_count, tile)),
+                whole((1, LANES)),
+            ]
+            + [ANYWHERE] * 12,
+            out_specs=[
+                whole((length, width)),
+                whole((length, width)),
+                whole((1, width)),
+                whole((1, width)),
+                whole((length, LANES)),
+                whole((2, 3, taps_count, tile)),
+                whole((1, LANES)),
+                ANYWHERE,
+                ANYWHERE,
+            ],
+            scratch_shapes=[
+                pltpu.VMEM((length, width), WIDE),
+                pltpu.VMEM((length, width), WIDE),
+                pltpu.VMEM((length, LANES), WIDE),
+                pltpu.VMEM((2, 3, length, tile), LOW),
+                pltpu.VMEM((2, length, tile), LOW),
+                pltpu.VMEM((2, length, tile), LOW),
+                pltpu.VMEM((2, here, pairs, PAIR, PAIR), LOW),
+                pltpu.VMEM((2, here, spans - 1, LANES, LANES), LOW),
+                pltpu.VMEM((2, here, spans - 2, LANES, LANES), LOW),
+                pltpu.VMEM((2, length, width), LOW),
+                pltpu.VMEM((2, 3, width, tile), LOW),
+                pltpu.VMEM((2, tile, width), LOW),
+                pltpu.VMEM((2, length, width), WIDE),
+                pltpu.VMEM((2, length, width), LOW),
+                pltpu.VMEM((2, 2, width, units), LOW),
+                pltpu.VMEM((2, units, width), LOW),
+                pltpu.VMEM((2, length, 2 * units), LOW),
+                pltpu.VMEM((2, length, 2 * units), LOW),
+                pltpu.VMEM((length, LANES), WIDE),
+                pltpu.VMEM((length, width), LOW),
+                pltpu.VMEM((length, width), LOW),
+                pltpu.VMEM((2, 6, length, tile), LOW),
+                pltpu.SemaphoreType.DMA((6,)),
+                pltpu.SemaphoreType.DMA((3 * count,)),
+                pltpu.SemaphoreType.DMA((2 * count + 1,)),
+                pltpu.SemaphoreType.DMA((2,)),
+            ],
+        ),
+        out_shape=[
+            out((length, width), LOW),
+            out((length, width), LOW),
+            out((1, width), WIDE),
+            out((1, width), WIDE),
+            out((length, LANES), LOW),
+            out((2, 3, taps_count, tile), WIDE),
+            out((1, LANES), WIDE),
+            out((4, length, 2 * units), LOW),
+            out((6, length, inner), LOW),
+        ],
+        compiler_params=pltpu.CompilerParams(dimension_semantics=("arbitrary",), vmem_limit_bytes=60 * 2**20),
+        cost_estimate=cost(50),
+    )(info, after, stream, grad, gains[0:1], gains[1:2], w_beta, taps, out_gain, *mixer_weights, *feed_weights)
+    result, stream_grad, feed_gain, gain, strengths, taps_grad, out_gain_grad, feed_stack, stack = results
+    taps_grad = jnp.moveaxis(taps_grad, 0, 2).reshape(3, taps_count, inner)
+    return result, (None, feed_gain, feed_stack), (stream_grad, gain, stack, strengths, taps_grad, out_gain_grad)
 
 
 def rows_kernel(halves, width, count, info_ref, *refs):
@@ -1192,11 +1467,11 @@
     def mixer_part(after, stream, *wrap):
         return mixer_forward(info, after, stream, gains[0:1], mixer_weights, w_beta, taps, out_gain, *wrap)
 
-    def feed_back(after, grad, saved, old=None):
+    def feed_back(after, grad, saved, old):
         stream, middle, kept, lifted = saved
         return feed_backward(info, after, middle, grad, lifted, gains[1:2], feed_weights, old)
 
-    def mixer_back(after, middle_grad, saved, old=None):
+    def mixer_back(after, middle_grad, saved, old):
         stream, middle, kept, lifted = saved
         return mixer_backward(
             info, after, stream, middle_grad, kept, gains[0:1], mixer_weights, w_beta, taps, out_gain, old
@@ -1225,19 +1500,23 @@
         saved.append(lifted)
         firsts.append(result)
     grads = own(cotangent)
+    streams = [lax.ppermute(firsts[0], "section", up)]
+    after = taps
+    if per > 1:
+        through, streams[0], firsts[1] = tied(info.astype(WIDE), streams[0], firsts[1])
+        after = lax.ppermute(through, "section", [(0, 1), (1, 0)])
+        for index in range(1, per):
+            firsts[index], after = tied(firsts[index], after)
+            streams.append(lax.ppermute(firsts[index], "section", up))
     results, returned, feeds, mixes = [], [], [], []
-    after = taps
     for index in range(per):
-        stream = lax.ppermute(firsts[index], "section", up)
-        middle, *kept = mixer_part(after, stream, *([only_second] if index else []))
-        if index + 1 < per:
-            firsts[index + 1], middle = tied(firsts[index + 1], middle)
-        result, lifted = feed_forward(info, middle, gains[1:2], feed_weights, only_second)
+        result, feed, mix = second_layer(
+            info, after, streams[index], grads[index], gains, w_beta, taps, out_gain, mixer_weights, feed_weights
+        )
         results.append(result)
-        saved = [stream, middle, kept, lifted]
-        feeds.append(feed_back([taps], grads[index], saved))
-        mixes.append(mixer_back((taps, taps, taps), feeds[-1][0], saved))
-        after = mixes[-1][0]
+        feeds.append(feed)
+        mixes.append(mix)
+        after = mix[0]
         returned.append(lax.ppermute(after, "section", [(2, 0), (3, 1)]))
     feed_twins, mix_twins = [], []
     waited = [mixes[-1][0]]

time: 464 us -> 440 us (0.948)
  Pallas kernels: 232 us -> 196 us
  starting transfers between devices: 45.4 us -> 53.4 us
    pallas_call x4 -> x2, Pallas kernels: 41.4 us -> 27.4 us  [feed_backward(): pl.pallas_call(kernel, name='feed_backward', grid_spec=pltpu.PrefetchScal...]
    pallas_call x8 -> x6, Pallas kernels: 91.2 us -> 79.7 us  [the longest x2 31.2 us: mixer_forward(): pl.pallas_call(wrap(lambda info_ref, after_ref, *refs: mixer_forward_kern...]
    pallas_call x4 -> x2, Pallas kernels: 54.9 us -> 44.8 us  [mixer_backward(): pl.pallas_call(kernel, name='mixer_backward', grid_spec=pltpu.PrefetchSca...]
    ppermute x2 -> x3, starting transfers between devices: 9.8 us -> 19.4 us  [the longest x1 13.5 us: local(): after = lax.ppermute(through, 'section', [(0, 1), (1, 0)])]
    ppermute x2, waiting for transfers between devices: 61 us -> 52.4 us  [local(): returned.append(lax.ppermute(after, 'section', [(2, 0), (3, 1)]))]
    ppermute x2 -> x3, waiting for transfers between devices: 0.33 us -> 5.43 us  [the longest x1 4.2 us: local(): streams.append(lax.ppermute(firsts[index], 'section', up))]
    unnamed x120 -> x122, local copies, waits for them, and re-layouts: 22.6 us -> 20.5 us
  transfers between devices with their start and end apart: 40 -> 41, of which waited for: 21 -> 22; matrix products, arithmetic and copies ran while one was open for 7% -> 8% of each run, Pallas kernels for 41% -> 42%
where the time goes in v4:
time: 440 us; the launch traced here: 436 us
  Pallas kernels  196 us (45%)
  waiting for transfers between devices  132 us (30%)
  starting transfers between devices  53.4 us (12%)
  local copies, waits for them, and re-layouts  41.6 us (9%)
  other arithmetic  9.49 us (2%)
    ppermute x36, waiting for transfers between devices, exchange(): lax.ppermute(value, axis, [(i, i ^ apart(i)) for i in range(lax.axis_size...  74.5 us
    ppermute x2, waiting for transfers between devices, local(): returned.append(lax.ppermute(after, 'section', [(2, 0), (3, 1)]))  52.4 us
    pallas_call x2, Pallas kernels, mixer_backward(): pl.pallas_call(kernel, name='mixer_backward', grid_spec=pltpu.PrefetchSca...  44.8 us
    pallas_call x4, Pallas kernels, rows_grads(): pl.pallas_call(lambda info_ref, *refs: rows_kernel(halves, left[3], count...  31.8 us
    ppermute x36, starting transfers between devices, exchange(): lax.ppermute(value, axis, [(i, i ^ apart(i)) for i in range(lax.axis_size...  31.4 us
    pallas_call x2, Pallas kernels, mixer_forward(): pl.pallas_call(wrap(lambda info_ref, after_ref, *refs: mixer_forward_kern...  31.2 us
    pallas_call x2, Pallas kernels, feed_backward(): pl.pallas_call(kernel, name='feed_backward', grid_spec=pltpu.PrefetchScal...  27.4 us
    pallas_call x2, Pallas kernels, second_layer(): pl.pallas_call(only_second(second_layer_kernel), name='second_layer', gri...  25.2 us
  transfers between devices with their start and end apart: 41, of which 22 were waited for; matrix products, arithmetic and copies ran while one was open for 8% of the time, Pallas kernels for 42%

profile of v4, /device:TPU:0, one launch (start us, length us, event | category | flops | bytes accessed | tf_op | source)
XLA Modules:
  0.0 435.6 jit_solution(18210759476407233153)
XLA Ops:
  1.7 3.1 collective-permute-start
  4.8 2.0 constant_dynamic-slice_fusion.6
  6.8 7.1 %collective-permute-done = bf16[3,128,512]{2,1,0:T(8,128)(2,1)S(1)} collective-permute-done((bf16[3,128,512]{2,1,0:T(8,128)(2,1)S(1)}, bf16[3,128,512]{2,1,0:T(8,128)(2,1)S(1)}, u32[]{:S(2)}, u32[]{:S(2)}) %collective-permute-start) | collective-permute-done | bytes 393248 | tf_op jit(solution)/shard_map/ppermute | solution.py:1375
  13.9 1.7 collective-permute-start.7
  16.8 1.6 collective-permute-start.6
  18.4 3.3 collective-permute-done.7
  21.8 1.7 collective-permute-start.8
  23.5 1.9 constant_dynamic-slice_fusion.5
  25.4 2.2 dynamic-slice_bitcast_fusion.2
  27.6 2.0 constant_dynamic-slice_fusion.4
  29.6 1.6 collective-permute-start.1
  34.8 10.9 %collective-permute-done.1 = bf16[2,128,1408]{2,1,0:T(8,128)(2,1)S(1)} collective-permute-done((bf16[2,128,1408]{2,1,0:T(8,128)(2,1)}, bf16[2,128,1408]{2,1,0:T(8,128)(2,1)S(1)}, u32[]{:S(2)}, u32[]{:S(2)}) %collective-permute-start.1) | collective-permute-done | bytes 720928 | tf_op jit(solution)/shard_map/ppermute | solution.py:1375
  47.8 1.4 collective-permute-start.4
  51.4 9.1 %collective-permute-done.4.refs_9_.refs_12_.refs_21_ = bf16[256,1024]{1,0:T(8,128)(2,1)S(1)} collective-permute-done((bf16[256,1024]{1,0:T(8,128)(2,1)}, bf16[256,1024]{1,0:T(8,128)(2,1)S(1)}, u32[]{:S(2)}, u32[]{:S(2)}) %collective-permute-start.4) | collective-permute-done | bytes 524320 | tf_op jit(solution)/shard_map/ppermute | solution.py:1375
  60.5 1.5 collective-permute-start.5
  64.1 15.5 %mixer_forward.2 = (f32[256,1024]{1,0:T(8,128)}, f32[256,128]{1,0:T(8,128)}, bf16[3,256,1024]{2,1,0:T(8,128)(2,1)}, bf16[256,1024]{1,0:T(8,128)(2,1)}, bf16[256,...) custom-call(s32[20]{0:T(128)} %stack.109.info_ref.refs_0_, ...), custom_call_target="tpu_custom_call" | custom-call | flops 15399999488 | bytes 1048576 | tf_op jit(solution)/shard_map/mixer_forward/pallas_call | solution.py:344
  79.7 1.5 collective-permute-done.3
  82.3 15.7 %mixer_forward.3 = (f32[256,1024]{1,0:T(8,128)}, f32[256,128]{1,0:T(8,128)}, bf16[3,256,1024]{2,1,0:T(8,128)(2,1)}, bf16[256,1024]{1,0:T(8,128)(2,1)}, bf16[256,...) custom-call(s32[20]{0:T(128)} %stack.109.info_ref.refs_0_, ...), custom_call_target="tpu_custom_call" | custom-call | flops 15399999488 | bytes 1048576 | tf_op jit(solution)/shard_map/mixer_forward/pallas_call | solution.py:344
  98.8 1.4 copy-done.31
  101.8 11.7 %feed_forward.2 = (bf16[256,1024]{1,0:T(8,128)(2,1)}, bf16[2,256,2816]{2,1,0:T(8,128)(2,1)}) custom-call(s32[20]{0:T(128)} %stack.109.info_ref.refs_0_, f32[256,1024]{1,0:T(8,128)} %get-tuple-element.118.after_ref.refs_1_.refs_2_, f32[1,1024]{1,0:T(1,128)} %get-tuple-element.266.refs_2_.refs_4_, bf16[2,1024,1408]{2,1,0:T(8,128)(2,1)} %refs_6_.7, ...), custom_call_target="tpu_custom_call" | custom-call | flops 11000000512 | bytes 1048576 | tf_op jit(solution)/shard_map/feed_forward/pallas_call | solution.py:848
  113.5 4.5 %collective-permute-start.14 = (bf16[256,1024]{1,0:T(8,128)(2,1)}, bf16[256,1024]{1,0:T(8,128)(2,1)S(1)}, u32[]{:S(2)}, u32[]{:S(2)}) collective-permute-start(bf16[256,1024]{1,0:T(8,128)(2,1)} %get-tuple-element.123), channel_id=1, source_target_pairs={{0,16},{8,24},{1,17},{9,25},{2,18},{10,26},{3,19},{11,27},{4,20},{... | collective-permute-start | bytes 1572872 | tf_op jit(solution)/shard_map/ppermute | solution.py:1503
  118.0 11.6 %feed_forward.3 = (bf16[256,1024]{1,0:T(8,128)(2,1)}, bf16[2,256,2816]{2,1,0:T(8,128)(2,1)}) custom-call(s32[20]{0:T(128)} %stack.109.info_ref.refs_0_, f32[256,1024]{1,0:T(8,128)} %get-tuple-element.124.refs_1_.refs_2_, f32[1,1024]{1,0:T(1,128)} %get-tuple-element.266.refs_2_.refs_4_, bf16[2,1024,1408]{2,1,0:T(8,128)(2,1)} %refs_6_.7, ...), custom_call_target="tpu_custom_call" | custom-call | flops 11000000512 | bytes 1048576 | tf_op jit(solution)/shard_map/feed_forward/pallas_call | solution.py:848
  130.0 13.5 %collective-permute-start.15 = (f32[20]{0:T(128)S(1)}, f32[20]{0:T(128)S(1)}, u32[]{:S(2)}, u32[]{:S(2)}) collective-permute-start(f32[20]{0:T(128)S(1)} %convert_element_type.12), channel_id=1, source_target_pairs={{0,8},{8,0},{1,9},{9,1},{2,10},{10,2},{3,11},{11,3},{4,12},{12,4},... | collective-permute-start | bytes 248 | tf_op jit(solution)/shard_map/ppermute | solution.py:1507
  145.1 1.3 collective-permute-start.16
  146.4 3.7 second_layer.2
  150.1 1.3 collective-permute-start.17
  151.4 1.4 copy.52
  152.8 4.2 collective-permute-done.16.refs_1_
  157.8 21.5 %second_layer.3 = (bf16[256,1024]{1,0:T(8,128)(2,1)}, bf16[256,1024]{1,0:T(8,128)(2,1)}, f32[1,1024]{1,0:T(1,128)}, f32[1,1024]{1,0:T(1,128)}, bf16[256,128]{1,0...) custom-call(s32[20]{0:T(128)} %stack.109.info_ref.refs_0_, ...), custom_call_target="tpu_custom_call" | custom-call | flops 54999998464 | bytes 1048576 | tf_op jit(solution)/shard_map/second_layer/pallas_call | solution.py:1208
  179.3 1.3 collective-permute-start.20
  180.6 25.0 %collective-permute-done.17.refs_3_ = bf16[256,1024]{1,0:T(8,128)(2,1)S(1)} collective-permute-done((bf16[256,1024]{1,0:T(8,128)(2,1)}, bf16[256,1024]{1,0:T(8,128)(2,1)S(1)}, u32[]{:S(2)}, u32[]{:S(2)}) %collective-permute-start.17) | collective-permute-done | bytes 524320 | tf_op jit(solution)/shard_map/ppermute | solution.py:1520
  206.4 13.5 %feed_backward.2 = (f32[256,1024]{1,0:T(8,128)}, f32[1,1024]{1,0:T(1,128)}, bf16[4,256,2816]{2,1,0:T(8,128)(2,1)}) custom-call(s32[20]{0:T(128)} %stack.109.info_ref.refs_0_, bf16[256,1024]{1,0:T(8,128)(2,1)} %get-tuple-element.133.refs_1_, f32[256,1024]{1,0:T(8,128)} %get-tuple-element.118.after_ref.refs_1_.refs_2_, ...), custom_call_target="tpu_custom_call", output_to_operand_aliasing={{2}: (13, {})} | custom-call | flops 14300000256 | bytes 1048576 | tf_op jit(solution)/shard_map/feed_backward/pallas_call | solution.py:983
  220.0 22.0 %mixer_backward.2 = (bf16[256,1024]{1,0:T(8,128)(2,1)}, f32[1,1024]{1,0:T(1,128)}, bf16[6,256,1024]{2,1,0:T(8,128)(2,1)}, bf16[256,128]{1,0:T(8,128)(2,1)}, f32[3,4,1024]{2,1,0:T(4,128)}, /*index=5*/f32[1,128]{1,0:T(1,128)}) custom-call(s32[20]{0:T(128)} %stack.109.info_ref.refs_0_, f32[3,4,1024]{2,1,0:T(4,128)} %copy-done.39, f32[3,4,1024]{2,1,0:T(4,128)} %copy-done.39, ...), custom_call_target="tpu_custom_call" | custom-call | flops 22000001024 | bytes 1048576 | tf_op jit(solution)/shard_map/mixer_backward/pallas_call | solution.py:684
  242.5 27.4 %collective-permute-done.20.refs_3_ = bf16[256,1024]{1,0:T(8,128)(2,1)S(1)} collective-permute-done((bf16[256,1024]{1,0:T(8,128)(2,1)}, bf16[256,1024]{1,0:T(8,128)(2,1)S(1)}, u32[]{:S(2)}, u32[]{:S(2)}) %collective-permute-start.20) | collective-permute-done | bytes 524320 | tf_op jit(solution)/shard_map/ppermute | solution.py:1520
  270.7 13.9 %feed_backward.3 = (f32[256,1024]{1,0:T(8,128)}, f32[1,1024]{1,0:T(1,128)}, bf16[4,256,2816]{2,1,0:T(8,128)(2,1)}) custom-call(s32[20]{0:T(128)} %stack.109.info_ref.refs_0_, bf16[256,1024]{1,0:T(8,128)(2,1)} %get-tuple-element.150.refs_1_, f32[256,1024]{1,0:T(8,128)} %get-tuple-element.124.refs_1_.refs_2_, ...), custom_call_target="tpu_custom_call", output_to_operand_aliasing={{2}: (13, {})} | custom-call | flops 14300000256 | bytes 1048576 | tf_op jit(solution)/shard_map/feed_backward/pallas_call | solution.py:983
  285.4 1.6 copy-done.8
  287.1 22.8 %mixer_backward.3 = (bf16[256,1024]{1,0:T(8,128)(2,1)}, f32[1,1024]{1,0:T(1,128)}, bf16[6,256,1024]{2,1,0:T(8,128)(2,1)}, bf16[256,128]{1,0:T(8,128)(2,1)}, f32[3,4,1024]{2,1,0:T(4,128)}, /*index=5*/f32[1,128]{1,0:T(1,128)}) custom-call(s32[20]{0:T(128)} %stack.109.info_ref.refs_0_, bf16[4,256,2816]{2,1,0:T(8,128)(2,1)} %collective-permute-done.18.refs_1_.refs_3_.refs_7_, ...), custom_call_target="tpu_custom_call" | custom-call | flops 22000001024 | bytes 1048576 | tf_op jit(solution)/shard_map/mixer_backward/pallas_call | solution.py:684
  313.4 12.0 %rows_grads.4 = (bf16[2,256,2816]{2,1,0:T(8,128)(2,1)S(1)}, bf16[2,256,2816]{2,1,0:T(8,128)(2,1)}) custom-call(s32[20]{0:T(128)S(1)} %copy-done.7, f32[1,1024]{1,0:T(1,128)S(1)} %copy-done.5, bf16[4,256,2816]{2,1,0:T(8,128)(2,1)S(1)} %bitcast.81, bf16[4,256,2816]{2,1,0:T(8,128)(2,1)} %get-tuple-element.172.refs_2_.refs_6_, ...), custom_call_target="tpu_custom_call" | custom-call | flops 11000000512 | bytes 1048576 | tf_op jit(solution)/shard_map/rows_grads/pallas_call | solution.py:1322
  325.4 2.0 collective-permute-start.24
  327.4 9.7 %rows_grads.5 = (bf16[1,704,1024]{2,1,0:T(8,128)(2,1)S(1)}, bf16[1,704,1024]{2,1,0:T(8,128)(2,1)}) custom-call(s32[20]{0:T(128)S(1)} %copy-done.7, bf16[2,256,2816]{2,1,0:T(8,128)(2,1)S(1)} %get-tuple-element.173.refs_0_.keep_ref, bf16[4,256,2816]{2,1,0:T(8,128)(2,1)S(1)} %bitcast.81, bf16[4,256,2816]{2,1,0:T(8,128)(2,1)} %get-tuple-element.172.refs_2_.refs_6_, ...), custom_call_target="tpu_custom_call" | custom-call | flops 11000000512 | bytes 1048576 | tf_op jit(solution)/shard_map/rows_grads/pallas_call | solution.py:1322
  337.6 1.9 copy-done.3
  339.5 1.9 copy-done.9
  341.4 6.4 %rows_grads.6 = (bf16[3,256,1024]{2,1,0:T(8,128)(2,1)S(1)}, bf16[3,256,1024]{2,1,0:T(8,128)(2,1)S(1)}) custom-call(s32[20]{0:T(128)S(1)} %copy-done.7, bf16[1,704,1024]{2,1,0:T(8,128)(2,1)S(1)} %get-tuple-element.174.refs_0_.keep_ref, bf16[6,256,1024]{2,1,0:T(8,128)(2,1)S(1)} %copy-done.2, bf16[6,256,1024]{2,1,0:T(8,128)(2,1)S(1)} %copy-done.3, ...), custom_call_target="tpu_custom_call" | custom-call | flops 11000000512 | bytes 1048576 | tf_op jit(solution)/shard_map/rows_grads/pallas_call | solution.py:1322
  347.9 3.6 rows_grads.7
  351.6 1.6 collective-permute-start.27
  354.2 6.0 %collective-permute-done.24.came_ref = bf16[2,256,2816]{2,1,0:T(8,128)(2,1)} collective-permute-done((bf16[2,256,2816]{2,1,0:T(8,128)(2,1)}, bf16[2,256,2816]{2,1,0:T(8,128)(2,1)}, u32[]{:S(2)}, u32[]{:S(2)}) %collective-permute-start.24) | collective-permute-done | bytes 2883616 | tf_op jit(solution)/shard_map/ppermute | solution.py:1375
  360.2 2.3 halve.12
  363.0 9.0 %collective-permute-done.25.came_ref = bf16[1,704,1024]{2,1,0:T(8,128)(2,1)} collective-permute-done((bf16[1,704,1024]{2,1,0:T(8,128)(2,1)}, bf16[1,704,1024]{2,1,0:T(8,128)(2,1)}, u32[]{:S(2)}, u32[]{:S(2)}) %collective-permute-start.25) | collective-permute-done | bytes 1441824 | tf_op jit(solution)/shard_map/ppermute | solution.py:1375
  372.0 1.7 halve.13
  373.7 1.5 select_bitcast_fusion
  377.8 5.3 %collective-permute-done.27.came_ref = bf16[1,256,1024]{2,1,0:T(8,128)(2,1)S(1)} collective-permute-done((bf16[1,256,1024]{2,1,0:T(8,128)(2,1)S(1)}, bf16[1,256,1024]{2,1,0:T(8,128)(2,1)S(1)}, u32[]{:S(2)}, u32[]{:S(2)}) %collective-permute-start.27) | collective-permute-done | bytes 524320 | tf_op jit(solution)/shard_map/ppermute | solution.py:1375
  384.8 8.1 %collective-permute-done.26 = bf16[2,2,256,256]{3,2,1,0:T(8,128)(2,1)S(1)} collective-permute-done((bf16[2,2,256,256]{3,2,1,0:T(8,128)(2,1)S(1)}, bf16[2,2,256,256]{3,2,1,0:T(8,128)(2,1)S(1)}, u32[]{:S(2)}, u32[]{:S(2)}) %collective-permute-start.26) | collective-permute-done | bytes 524320 | tf_op jit(solution)/shard_map/ppermute | solution.py:1375
  395.1 2.0 collective-permute-done.29.came_ref
  399.4 1.3 reshape.192
  401.3 1.7 collective-permute-done.30.came_ref
  405.2 1.3 halve.17
  407.1 1.6 collective-permute-done.31.came_ref
  410.3 2.0 collective-permute-start.38
  412.5 3.5 collective-permute-done.38
  416.0 1.9 collective-permute-start.39
  417.9 1.2 collective-permute-start.36
  420.5 1.4 copy-done.13
  425.3 4.6 %collective-permute-done.40 = f32[1416]{0:T(1024)S(1)} collective-permute-done((f32[1416]{0:T(1024)S(1)}, f32[1416]{0:T(1024)S(1)}, u32[]{:S(2)}, u32[]{:S(2)}) %collective-permute-start.40) | collective-permute-done | bytes 5696 | tf_op jit(solution)/shard_map/ppermute | solution.py:1375
  433.7 1.5 halve.23
  (246 shorter events, 49.1 us)
Async XLA Ops:
  0.6 16.1 %copy-start.32 = (f32[3,4,512]{2,1,0:T(4,128)S(1)}, f32[3,4,512]{2,1,0:T(4,128)}, u32[]{:S(2)}) copy-start(f32[3,4,512]{2,1,0:T(4,128)} %param.14) | copy-start | bytes 73732
  0.7 16.1 %copy-start.38 = (f32[2,512]{1,0:T(2,128)S(1)}, f32[2,512]{1,0:T(2,128)}, u32[]{:S(2)}) copy-start(f32[2,512]{1,0:T(2,128)} %param.18) | copy-start | bytes 12292
  0.7 16.1 %copy-start.43 = (f32[64]{0:T(128)S(1)}, f32[64]{0:T(128)}, u32[]{:S(2)}) copy-start(f32[64]{0:T(128)} %param.19) | copy-start | bytes 772
  1.7 12.2 %collective-permute-start = (bf16[3,128,512]{2,1,0:T(8,128)(2,1)S(1)}, bf16[3,128,512]{2,1,0:T(8,128)(2,1)S(1)}, u32[]{:S(2)}, u32[]{:S(2)}) collective-permute-start(bf16[3,128,512]{2,1,0:T(8,128)(2,1)S(1)} %constant_dynamic-slice_fusion.7), channel_id=1, source_target_pairs={{0,8},{8,0},{16,24},{24,16},{1,9},{9,1},{17,25},{25,17},{2,10},{10... | collective-permute-start | bytes 1179656 | tf_op jit(solution)/shard_map/ppermute | solution.py:1375
  13.9 7.8 %collective-permute-start.7 = (bf16[3,128,512]{2,1,0:T(8,128)(2,1)S(1)}, bf16[3,128,512]{2,1,0:T(8,128)(2,1)S(1)}, u32[]{:S(2)}, u32[]{:S(2)}) collective-permute-start(bf16[3,128,512]{2,1,0:T(8,128)(2,1)S(1)} %collective-permute-done), channel_id=1, source_target_pairs={{0,2},{1,5},{2,0},{3,7},{4,6},{5,1},{6,4},{7,3},{8,10},{9,13},{10,... | collective-permute-start | bytes 1179656 | tf_op jit(solution)/shard_map/ppermute | solution.py:1375
  16.8 15.3 %collective-permute-start.6 = (f32[11328]{0:T(1024)S(1)}, f32[11328]{0:T(1024)S(1)}, u32[]{:S(2)}, u32[]{:S(2)}) collective-permute-start(f32[11328]{0:T(1024)S(1)} %pad_maximum_fusion.4), channel_id=1, source_target_pairs={{0,8},{8,0},{16,24},{24,16},{1,9},{9,1},{17,25},{25,17},{2,10},{10... | collective-permute-start | bytes 135944 | tf_op jit(solution)/shard_map/ppermute | solution.py:1375
  18.4 12.8 %copy-start.37 = (bf16[1024,4]{0,1:T(4,128)(2,1)S(1)}, bf16[1024,4]{0,1:T(4,128)(2,1)}, u32[]{:S(2)}) copy-start(bf16[1024,4]{0,1:T(4,128)(2,1)} %param.13) | copy-start | bytes 24580
  21.8 12.1 %collective-permute-start.8 = (bf16[3,256,512]{2,1,0:T(8,128)(2,1)S(1)}, bf16[3,256,512]{2,1,0:T(8,128)(2,1)S(1)}, u32[]{:S(2)}, u32[]{:S(2)}) collective-permute-start(bf16[3,256,512]{2,1,0:T(8,128)(2,1)S(1)} %pad_maximum_fusion.2), channel_id=1, source_target_pairs={{0,4},{1,3},{2,6},{3,1},{4,0},{5,7},{6,2},{7,5},{8,12},{9,11},{10,... | collective-permute-start | bytes 2359304 | tf_op jit(solution)/shard_map/ppermute | solution.py:1375
  29.6 16.1 %collective-permute-start.1 = (bf16[2,128,1408]{2,1,0:T(8,128)(2,1)}, bf16[2,128,1408]{2,1,0:T(8,128)(2,1)S(1)}, u32[]{:S(2)}, u32[]{:S(2)}) collective-permute-start(bf16[2,128,1408]{2,1,0:T(8,128)(2,1)} %constant_dynamic-slice_fusion.6), channel_id=1, source_target_pairs={{0,8},{8,0},{16,24},{24,16},{1,9},{9,1},{17,25},{25,17},{2,10},{10... | collective-permute-start | bytes 2162696 | tf_op jit(solution)/shard_map/ppermute | solution.py:1375
  33.8 26.7 %copy-start.27 = (bf16[1408,256]{1,0:T(8,128)(2,1)S(1)}, bf16[1408,256]{1,0:T(8,128)(2,1)}, u32[]{:S(2)}) copy-start(bf16[1408,256]{1,0:T(8,128)(2,1)} %constant_dynamic-slice_fusion.4) | copy-start | bytes 2162692
  34.7 28.6 %collective-permute-start.9 = (bf16[3,512,512]{2,1,0:T(8,128)(2,1)}, bf16[3,512,512]{2,1,0:T(8,128)(2,1)}, u32[]{:S(2)}, u32[]{:S(2)}) collective-permute-start(bf16[3,512,512]{2,1,0:T(8,128)(2,1)} %constant_dynamic-update-slice_fusion.2.refs_7_.refs_10_.refs_19_), channel_id=1, source_target_pairs={{0,1},{1,0},{2,3},{3,2},{4,5},{5,4},{6,7},{7,6},{8,9},{9,8},{10,11... | collective-permute-start | bytes 4718600 | tf_op jit(solution)/shard_map/ppermute | solution.py:1375
  34.8 28.6 %copy-start.39 = (f32[3,4,1024]{2,1,0:T(4,128)}, f32[3,4,1024]{2,1,0:T(4,128)S(1)}, u32[]{:S(2)}) copy-start(f32[3,4,1024]{2,1,0:T(4,128)S(1)} %constant_dynamic-update-slice_fusion.refs_3_.refs_1_.refs_2_.refs_15_) | copy-start | bytes 147460
  45.7 16.3 %collective-permute-start.2 = (bf16[2,128,1408]{2,1,0:T(8,128)(2,1)S(1)}, bf16[2,128,1408]{2,1,0:T(8,128)(2,1)S(1)}, u32[]{:S(2)}, u32[]{:S(2)}) collective-permute-start(bf16[2,128,1408]{2,1,0:T(8,128)(2,1)S(1)} %collective-permute-done.1), channel_id=1, source_target_pairs={{0,2},{1,5},{2,0},{3,7},{4,6},{5,1},{6,4},{7,3},{8,10},{9,13},{10,... | collective-permute-start | bytes 2162696 | tf_op jit(solution)/shard_map/ppermute | solution.py:1375
  47.8 12.6 %collective-permute-start.4 = (bf16[256,1024]{1,0:T(8,128)(2,1)}, bf16[256,1024]{1,0:T(8,128)(2,1)S(1)}, u32[]{:S(2)}, u32[]{:S(2)}) collective-permute-start(bf16[256,1024]{1,0:T(8,128)(2,1)} %constant_dynamic-slice_fusion.5), channel_id=1, source_target_pairs={{0,8},{8,0},{16,24},{24,16},{1,9},{9,1},{17,25},{25,17},{2,10},{10... | collective-permute-start | bytes 1572872 | tf_op jit(solution)/shard_map/ppermute | solution.py:1375
  60.5 2.9 collective-permute-start.10
  60.5 19.2 %collective-permute-start.5 = (bf16[1408,256]{1,0:T(8,128)(2,1)S(1)}, bf16[1408,256]{1,0:T(8,128)(2,1)S(1)}, u32[]{:S(2)}, u32[]{:S(2)}) collective-permute-start(bf16[1408,256]{1,0:T(8,128)(2,1)S(1)} %copy-done.27), channel_id=1, source_target_pairs={{0,8},{8,0},{16,24},{24,16},{1,9},{9,1},{17,25},{25,17},{2,10},{10... | collective-permute-start | bytes 2162696 | tf_op jit(solution)/shard_map/ppermute | solution.py:1375
  62.1 19.1 %collective-permute-start.3 = (bf16[2,256,1408]{2,1,0:T(8,128)(2,1)S(1)}, bf16[2,256,1408]{2,1,0:T(8,128)(2,1)S(1)}, u32[]{:S(2)}, u32[]{:S(2)}) collective-permute-start(bf16[2,256,1408]{2,1,0:T(8,128)(2,1)S(1)} %pad_maximum_fusion), channel_id=1, source_target_pairs={{0,4},{1,3},{2,6},{3,1},{4,0},{5,7},{6,2},{7,5},{8,12},{9,11},{10,... | collective-permute-start | bytes 4325384 | tf_op jit(solution)/shard_map/ppermute | solution.py:1375
  81.2 16.9 %collective-permute-start.12 = (bf16[1408,256]{1,0:T(8,128)(2,1)S(1)}, bf16[1408,256]{1,0:T(8,128)(2,1)S(1)}, u32[]{:S(2)}, u32[]{:S(2)}) collective-permute-start(bf16[1408,256]{1,0:T(8,128)(2,1)S(1)} %collective-permute-done.5), channel_id=1, source_target_pairs={{0,2},{1,5},{2,0},{3,7},{4,6},{5,1},{6,4},{7,3},{8,10},{9,13},{10,... | collective-permute-start | bytes 2162696 | tf_op jit(solution)/shard_map/ppermute | solution.py:1375
  82.3 19.4 %collective-permute-start.11 = (bf16[2,512,1408]{2,1,0:T(8,128)(2,1)}, bf16[2,512,1408]{2,1,0:T(8,128)(2,1)}, u32[]{:S(2)}, u32[]{:S(2)}) collective-permute-start(bf16[2,512,1408]{2,1,0:T(8,128)(2,1)} %constant_dynamic-update-slice_fusion.5.refs_5_.refs_16_.refs_8_), channel_id=1, source_target_pairs={{0,1},{1,0},{2,3},{3,2},{4,5},{5,4},{6,7},{7,6},{8,9},{9,8},{10,11... | collective-permute-start | bytes 8650760 | tf_op jit(solution)/shard_map/ppermute | solution.py:1375
  98.2 3.6 collective-permute-start.13
  113.5 16.6 %collective-permute-start.14 = (bf16[256,1024]{1,0:T(8,128)(2,1)}, bf16[256,1024]{1,0:T(8,128)(2,1)S(1)}, u32[]{:S(2)}, u32[]{:S(2)}) collective-permute-start(bf16[256,1024]{1,0:T(8,128)(2,1)} %get-tuple-element.123), channel_id=1, source_target_pairs={{0,16},{8,24},{1,17},{9,25},{2,18},{10,26},{3,19},{11,27},{4,20},{... | collective-permute-start | bytes 1572872 | tf_op jit(solution)/shard_map/ppermute | solution.py:1503
  130.0 16.4 %copy-start.49 = (bf16[256,1024]{1,0:T(8,128)(2,1)}, bf16[256,1024]{1,0:T(8,128)(2,1)S(1)}, u32[]{:S(2)}) copy-start(bf16[256,1024]{1,0:T(8,128)(2,1)S(1)} %collective-permute-done.14.refs_1_) | copy-start | bytes 1572868
  130.0 15.1 %collective-permute-start.15 = (f32[20]{0:T(128)S(1)}, f32[20]{0:T(128)S(1)}, u32[]{:S(2)}, u32[]{:S(2)}) collective-permute-start(f32[20]{0:T(128)S(1)} %convert_element_type.12), channel_id=1, source_target_pairs={{0,8},{8,0},{1,9},{9,1},{2,10},{10,2},{3,11},{11,3},{4,12},{12,4},... | collective-permute-start | bytes 248 | tf_op jit(solution)/shard_map/ppermute | solution.py:1507
  145.1 11.9 %collective-permute-start.16 = (bf16[256,1024]{1,0:T(8,128)(2,1)}, bf16[256,1024]{1,0:T(8,128)(2,1)S(1)}, u32[]{:S(2)}, u32[]{:S(2)}) collective-permute-start(bf16[256,1024]{1,0:T(8,128)(2,1)} %get-tuple-element.132), channel_id=1, source_target_pairs={{0,16},{8,24},{1,17},{9,25},{2,18},{10,26},{3,19},{11,27},{4,20},{... | collective-permute-start | bytes 1572872 | tf_op jit(solution)/shard_map/ppermute | solution.py:1510
  150.1 55.5 %collective-permute-start.17 = (bf16[256,1024]{1,0:T(8,128)(2,1)}, bf16[256,1024]{1,0:T(8,128)(2,1)S(1)}, u32[]{:S(2)}, u32[]{:S(2)}) collective-permute-start(bf16[256,1024]{1,0:T(8,128)(2,1)} %get-tuple-element.131.refs_0_), channel_id=1, source_target_pairs={{16,0},{24,8},{17,1},{25,9},{18,2},{26,10},{19,3},{27,11},{20,4},{... | collective-permute-start | bytes 1572872 | tf_op jit(solution)/shard_map/ppermute | solution.py:1520
  179.3 90.6 %collective-permute-start.20 = (bf16[256,1024]{1,0:T(8,128)(2,1)}, bf16[256,1024]{1,0:T(8,128)(2,1)S(1)}, u32[]{:S(2)}, u32[]{:S(2)}) collective-permute-start(bf16[256,1024]{1,0:T(8,128)(2,1)} %get-tuple-element.133.refs_1_), channel_id=1, source_target_pairs={{16,0},{24,8},{17,1},{25,9},{18,2},{26,10},{19,3},{27,11},{20,4},{... | collective-permute-start | bytes 1572872 | tf_op jit(solution)/shard_map/ppermute | solution.py:1520
  219.9 65.5 %collective-permute-start.18 = (bf16[4,256,2816]{2,1,0:T(8,128)(2,1)}, bf16[4,256,2816]{2,1,0:T(8,128)(2,1)}, u32[]{:S(2)}, u32[]{:S(2)}) collective-permute-start(bf16[4,256,2816]{2,1,0:T(8,128)(2,1)} %get-tuple-element.152.refs_1_.refs_5_), channel_id=1, source_target_pairs={{0,1},{1,0},{2,3},{3,2},{4,5},{5,4},{6,7},{7,6},{8,9},{9,8},{10,11... | collective-permute-start | bytes 17301512 | tf_op jit(solution)/shard_map/ppermute | solution.py:1375
  242.0 43.4 %collective-permute-start.19 = (bf16[6,256,1024]{2,1,0:T(8,128)(2,1)}, bf16[6,256,1024]{2,1,0:T(8,128)(2,1)S(1)}, u32[]{:S(2)}, u32[]{:S(2)}) collective-permute-start(bf16[6,256,1024]{2,1,0:T(8,128)(2,1)} %get-tuple-element.153.refs_1_.refs_5_), channel_id=1, source_target_pairs={{0,1},{1,0},{2,3},{3,2},{4,5},{5,4},{6,7},{7,6},{8,9},{9,8},{10,11... | collective-permute-start | bytes 9437192 | tf_op jit(solution)/shard_map/ppermute | solution.py:1375
  270.7 14.1 %copy-start.35 = (f32[2,3,4,512]{3,2,1,0:T(4,128)S(1)}, f32[2,3,4,512]{3,2,1,0:T(4,128)}, u32[]{:S(2)}) copy-start(f32[2,3,4,512]{3,2,1,0:T(4,128)} %get-tuple-element.168) | copy-start | bytes 147460
  284.6 28.7 %collective-permute-start.22 = (bf16[4,256,2816]{2,1,0:T(8,128)(2,1)}, bf16[4,256,2816]{2,1,0:T(8,128)(2,1)}, u32[]{:S(2)}, u32[]{:S(2)}) collective-permute-start(bf16[4,256,2816]{2,1,0:T(8,128)(2,1)} %get-tuple-element.172.refs_2_.refs_6_), channel_id=1, source_target_pairs={{0,1},{1,0},{2,3},{3,2},{4,5},{5,4},{6,7},{7,6},{8,9},{9,8},{10,11... | collective-permute-start | bytes 17301512 | tf_op jit(solution)/shard_map/ppermute | solution.py:1375
  287.0 26.3 %slice-start = ((s8[5767168]{0:T(1024)(128)(4,1)}), s8[4194304]{0:T(1024)(128)(4,1)S(1)}, s32[]{:S(2)}) async-start(s8[5767168]{0:T(1024)(128)(4,1)} %bitcast.80), calls=%async_computation | async-start | bytes 8388608
  287.0 23.3 %copy-start.28 = (bf16[256,1024]{1,0:T(8,128)(2,1)S(1)}, bf16[256,1024]{1,0:T(8,128)(2,1)}, u32[]{:S(2)}) copy-start(bf16[256,1024]{1,0:T(8,128)(2,1)} %get-tuple-element.130) | copy-start | bytes 1572868
  287.0 23.3 %copy-start.30 = (bf16[256,1024]{1,0:T(8,128)(2,1)S(1)}, bf16[256,1024]{1,0:T(8,128)(2,1)}, u32[]{:S(2)}) copy-start(bf16[256,1024]{1,0:T(8,128)(2,1)} %get-tuple-element.150.refs_1_) | copy-start | bytes 1572868
  287.0 23.4 %copy-start.41 = (f32[1,1024]{1,0:T(1,128)S(1)}, f32[1,1024]{1,0:T(1,128)}, u32[]{:S(2)}) copy-start(f32[1,1024]{1,0:T(1,128)} %get-tuple-element.205) | copy-start | bytes 12292
  287.0 23.4 %copy-start.42 = (f32[1,1024]{1,0:T(1,128)S(1)}, f32[1,1024]{1,0:T(1,128)}, u32[]{:S(2)}) copy-start(f32[1,1024]{1,0:T(1,128)} %get-tuple-element.206) | copy-start | bytes 12292
  287.1 23.4 %copy-start.36 = (f32[3,4,1024]{2,1,0:T(4,128)S(1)}, f32[3,4,1024]{2,1,0:T(4,128)}, u32[]{:S(2)}) copy-start(f32[3,4,1024]{2,1,0:T(4,128)} %get-tuple-element.199) | copy-start | bytes 147460
  287.1 24.2 %copy-start.29 = (bf16[256,1024]{1,0:T(8,128)(2,1)S(1)}, bf16[256,1024]{1,0:T(8,128)(2,1)}, u32[]{:S(2)}) copy-start(bf16[256,1024]{1,0:T(8,128)(2,1)} %get-tuple-element.151) | copy-start | bytes 1572868
  287.1 26.3 %slice-start.1 = ((s8[5767168]{0:T(1024)(128)(4,1)}), s8[1572864]{0:T(1024)(128)(4,1)S(1)}, s32[]{:S(2)}) async-start(s8[5767168]{0:T(1024)(128)(4,1)} %bitcast.80), calls=%async_computation.1 | async-start | bytes 3145728
  309.9 27.7 %collective-permute-start.23 = (bf16[6,256,1024]{2,1,0:T(8,128)(2,1)}, bf16[6,256,1024]{2,1,0:T(8,128)(2,1)}, u32[]{:S(2)}, u32[]{:S(2)}) collective-permute-start(bf16[6,256,1024]{2,1,0:T(8,128)(2,1)} %get-tuple-element.175.refs_2_.refs_6_), channel_id=1, source_target_pairs={{0,1},{1,0},{2,3},{3,2},{4,5},{5,4},{6,7},{7,6},{8,9},{9,8},{10,11... | collective-permute-start | bytes 9437192 | tf_op jit(solution)/shard_map/ppermute | solution.py:1375
  313.3 60.4 %collective-permute-start.21 = (bf16[2,256,512]{2,1,0:T(8,128)(2,1)}, bf16[2,256,512]{2,1,0:T(8,128)(2,1)}, u32[]{:S(2)}, u32[]{:S(2)}) collective-permute-start(bf16[2,256,512]{2,1,0:T(8,128)(2,1)} %fusion.2), channel_id=1, source_target_pairs={{0,16},{8,24},{16,0},{24,8},{1,17},{9,25},{17,1},{25,9},{2,18},{10... | collective-permute-start | bytes 1572872 | tf_op jit(solution)/shard_map/ppermute | solution.py:1375
  325.4 11.7 %copy-start = (bf16[2,256,2816]{2,1,0:T(8,128)(2,1)}, bf16[2,256,2816]{2,1,0:T(8,128)(2,1)S(1)}, u32[]{:S(2)}) copy-start(bf16[2,256,2816]{2,1,0:T(8,128)(2,1)S(1)} %get-tuple-element.173.refs_0_.keep_ref) | copy-start | bytes 8650756
  325.4 34.8 %collective-permute-start.24 = (bf16[2,256,2816]{2,1,0:T(8,128)(2,1)}, bf16[2,256,2816]{2,1,0:T(8,128)(2,1)}, u32[]{:S(2)}, u32[]{:S(2)}) collective-permute-start(bf16[2,256,2816]{2,1,0:T(8,128)(2,1)} %get-tuple-element.178), channel_id=1, source_target_pairs={{0,2},{1,5},{2,0},{3,7},{4,6},{5,1},{6,4},{7,3},{8,10},{9,13},{10,... | collective-permute-start | bytes 8650760 | tf_op jit(solution)/shard_map/ppermute | solution.py:1375
  327.4 10.2 %copy-start.2 = (bf16[6,256,1024]{2,1,0:T(8,128)(2,1)S(1)}, bf16[6,256,1024]{2,1,0:T(8,128)(2,1)}, u32[]{:S(2)}) copy-start(bf16[6,256,1024]{2,1,0:T(8,128)(2,1)} %get-tuple-element.153.refs_1_.refs_5_) | copy-start | bytes 9437188
  337.1 10.8 %copy-start.11 = (bf16[1,704,1024]{2,1,0:T(8,128)(2,1)}, bf16[1,704,1024]{2,1,0:T(8,128)(2,1)S(1)}, u32[]{:S(2)}) copy-start(bf16[1,704,1024]{2,1,0:T(8,128)(2,1)S(1)} %get-tuple-element.174.refs_0_.keep_ref) | copy-start | bytes 4325380
  337.1 34.8 %collective-permute-start.25 = (bf16[1,704,1024]{2,1,0:T(8,128)(2,1)}, bf16[1,704,1024]{2,1,0:T(8,128)(2,1)}, u32[]{:S(2)}, u32[]{:S(2)}) collective-permute-start(bf16[1,704,1024]{2,1,0:T(8,128)(2,1)} %get-tuple-element.180), channel_id=1, source_target_pairs={{0,8},{8,0},{16,24},{24,16},{1,9},{9,1},{17,25},{25,17},{2,10},{10... | collective-permute-start | bytes 4325384 | tf_op jit(solution)/shard_map/ppermute | solution.py:1375
  347.9 12.3 %copy-start.1 = (bf16[2,256,2816]{2,1,0:T(8,128)(2,1)S(1)}, bf16[2,256,2816]{2,1,0:T(8,128)(2,1)}, u32[]{:S(2)}) copy-start(bf16[2,256,2816]{2,1,0:T(8,128)(2,1)} %copy-done) | copy-start | bytes 8650756
  351.6 31.5 %collective-permute-start.27 = (bf16[1,256,1024]{2,1,0:T(8,128)(2,1)S(1)}, bf16[1,256,1024]{2,1,0:T(8,128)(2,1)S(1)}, u32[]{:S(2)}, u32[]{:S(2)}) collective-permute-start(bf16[1,256,1024]{2,1,0:T(8,128)(2,1)S(1)} %get-tuple-element.183), channel_id=1, source_target_pairs={{0,8},{8,0},{16,24},{24,16},{1,9},{9,1},{17,25},{25,17},{2,10},{10... | collective-permute-start | bytes 1572872 | tf_op jit(solution)/shard_map/ppermute | solution.py:1375
  353.1 41.0 %collective-permute-start.28 = (bf16[3,256,1024]{2,1,0:T(8,128)(2,1)S(1)}, bf16[3,256,1024]{2,1,0:T(8,128)(2,1)S(1)}, u32[]{:S(2)}, u32[]{:S(2)}) collective-permute-start(bf16[3,256,1024]{2,1,0:T(8,128)(2,1)S(1)} %get-tuple-element.185), channel_id=1, source_target_pairs={{0,2},{1,5},{2,0},{3,7},{4,6},{5,1},{6,4},{7,3},{8,10},{9,13},{10,... | collective-permute-start | bytes 4718600 | tf_op jit(solution)/shard_map/ppermute | solution.py:1375
  360.2 11.8 %copy-start.12 = (bf16[1,704,1024]{2,1,0:T(8,128)(2,1)S(1)}, bf16[1,704,1024]{2,1,0:T(8,128)(2,1)}, u32[]{:S(2)}) copy-start(bf16[1,704,1024]{2,1,0:T(8,128)(2,1)} %copy-done.11) | copy-start | bytes 4325380
  362.4 34.6 %collective-permute-start.29 = (bf16[2,128,2816]{2,1,0:T(8,128)(2,1)S(1)}, bf16[2,128,2816]{2,1,0:T(8,128)(2,1)S(1)}, u32[]{:S(2)}, u32[]{:S(2)}) collective-permute-start(bf16[2,128,2816]{2,1,0:T(8,128)(2,1)S(1)} %get-tuple-element.187), channel_id=1, source_target_pairs={{0,4},{1,3},{2,6},{3,1},{4,0},{5,7},{6,2},{7,5},{8,12},{9,11},{10,... | collective-permute-start | bytes 4325384 | tf_op jit(solution)/shard_map/ppermute | solution.py:1375
  373.7 9.4 %copy-start.16 = (bf16[1,352,1024]{2,1,0:T(8,128)(2,1)}, bf16[1,352,1024]{2,1,0:T(8,128)(2,1)S(1)}, u32[]{:S(2)}) copy-start(bf16[1,352,1024]{2,1,0:T(8,128)(2,1)S(1)} %get-tuple-element.181.after_ref.keep_ref) | copy-start | bytes 2162692
  375.8 17.1 %collective-permute-start.26 = (bf16[2,2,256,256]{3,2,1,0:T(8,128)(2,1)S(1)}, bf16[2,2,256,256]{3,2,1,0:T(8,128)(2,1)S(1)}, u32[]{:S(2)}, u32[]{:S(2)}) collective-permute-start(bf16[2,2,256,256]{3,2,1,0:T(8,128)(2,1)S(1)} %get-tuple-element.261), channel_id=1, source_target_pairs={{0,8},{8,0},{16,24},{24,16},{1,9},{9,1},{17,25},{25,17},{2,10},{10... | collective-permute-start | bytes 1572872 | tf_op jit(solution)/shard_map/ppermute | solution.py:1375
  376.7 26.3 %collective-permute-start.30 = (bf16[1,352,1024]{2,1,0:T(8,128)(2,1)S(1)}, bf16[1,352,1024]{2,1,0:T(8,128)(2,1)}, u32[]{:S(2)}, u32[]{:S(2)}) collective-permute-start(bf16[1,352,1024]{2,1,0:T(8,128)(2,1)S(1)} %get-tuple-element.189), channel_id=1, source_target_pairs={{0,2},{1,5},{2,0},{3,7},{4,6},{5,1},{6,4},{7,3},{8,10},{9,13},{10,... | collective-permute-start | bytes 2162696 | tf_op jit(solution)/shard_map/ppermute | solution.py:1375
  383.9 10.7 %copy-start.23 = (bf16[1,128,1024]{2,1,0:T(8,128)(2,1)}, bf16[1,128,1024]{2,1,0:T(8,128)(2,1)S(1)}, u32[]{:S(2)}) copy-start(bf16[1,128,1024]{2,1,0:T(8,128)(2,1)S(1)} %get-tuple-element.184.after_ref.keep_ref) | copy-start | bytes 786436
  383.9 24.8 %collective-permute-start.31 = (bf16[1,128,1024]{2,1,0:T(8,128)(2,1)}, bf16[1,128,1024]{2,1,0:T(8,128)(2,1)}, u32[]{:S(2)}, u32[]{:S(2)}) collective-permute-start(bf16[1,128,1024]{2,1,0:T(8,128)(2,1)} %get-tuple-element.191), channel_id=1, source_target_pairs={{0,2},{1,5},{2,0},{3,7},{4,6},{5,1},{6,4},{7,3},{8,10},{9,13},{10,... | collective-permute-start | bytes 786440 | tf_op jit(solution)/shard_map/ppermute | solution.py:1375
  394.6 17.7 %collective-permute-start.32 = (bf16[3,128,1024]{2,1,0:T(8,128)(2,1)S(1)}, bf16[3,128,1024]{2,1,0:T(8,128)(2,1)S(1)}, u32[]{:S(2)}, u32[]{:S(2)}) collective-permute-start(bf16[3,128,1024]{2,1,0:T(8,128)(2,1)S(1)} %get-tuple-element.193), channel_id=1, source_target_pairs={{0,4},{1,3},{2,6},{3,1},{4,0},{5,7},{6,2},{7,5},{8,12},{9,11},{10,... | collective-permute-start | bytes 2359304 | tf_op jit(solution)/shard_map/ppermute | solution.py:1375
  400.6 9.6 %collective-permute-start.37 = (f32[22656]{0:T(1024)S(1)}, f32[22656]{0:T(1024)S(1)}, u32[]{:S(2)}, u32[]{:S(2)}) collective-permute-start(f32[22656]{0:T(1024)S(1)} %pad_maximum_fusion.3), channel_id=1, source_target_pairs={{0,1},{1,0},{2,3},{3,2},{4,5},{5,4},{6,7},{7,6},{8,9},{9,8},{10,11... | collective-permute-start | bytes 271880 | tf_op jit(solution)/shard_map/ppermute | solution.py:1375
  400.7 18.6 %collective-permute-start.33 = (bf16[2,128,1408]{2,1,0:T(8,128)(2,1)S(1)}, bf16[2,128,1408]{2,1,0:T(8,128)(2,1)S(1)}, u32[]{:S(2)}, u32[]{:S(2)}) collective-permute-start(bf16[2,128,1408]{2,1,0:T(8,128)(2,1)S(1)} %get-tuple-element.195), channel_id=1, source_target_pairs={{0,8},{8,0},{16,24},{24,16},{1,9},{9,1},{17,25},{25,17},{2,10},{10... | collective-permute-start | bytes 2162696 | tf_op jit(solution)/shard_map/ppermute | solution.py:1375
  406.6 13.9 %collective-permute-start.34 = (bf16[1,176,1024]{2,1,0:T(8,128)(2,1)S(1)}, bf16[1,176,1024]{2,1,0:T(8,128)(2,1)S(1)}, u32[]{:S(2)}, u32[]{:S(2)}) collective-permute-start(bf16[1,176,1024]{2,1,0:T(8,128)(2,1)S(1)} %get-tuple-element.196), channel_id=1, source_target_pairs={{0,4},{1,3},{2,6},{3,1},{4,0},{5,7},{6,2},{7,5},{8,12},{9,11},{10,... | collective-permute-start | bytes 1081352 | tf_op jit(solution)/shard_map/ppermute | solution.py:1375
  409.7 14.8 %collective-permute-start.35 = (bf16[1,64,1024]{2,1,0:T(8,128)(2,1)S(1)}, bf16[1,64,1024]{2,1,0:T(8,128)(2,1)S(1)}, u32[]{:S(2)}, u32[]{:S(2)}) collective-permute-start(bf16[1,64,1024]{2,1,0:T(8,128)(2,1)S(1)} %get-tuple-element.197), channel_id=1, source_target_pairs={{0,4},{1,3},{2,6},{3,1},{4,0},{5,7},{6,2},{7,5},{8,12},{9,11},{10,... | collective-permute-start | bytes 393224 | tf_op jit(solution)/shard_map/ppermute | solution.py:1375
  410.3 5.7 %collective-permute-start.38 = (f32[22656]{0:T(1024)S(1)}, f32[22656]{0:T(1024)S(1)}, u32[]{:S(2)}, u32[]{:S(2)}) collective-permute-start(f32[22656]{0:T(1024)S(1)} %fusion.14), channel_id=1, source_target_pairs={{0,2},{1,3},{2,0},{3,1},{4,6},{5,7},{6,4},{7,5},{8,10},{9,11},{10,... | collective-permute-start | bytes 271880 | tf_op jit(solution)/shard_map/ppermute | solution.py:1375
  416.0 6.8 %collective-permute-start.39 = (f32[22656]{0:T(1024)S(1)}, f32[22656]{0:T(1024)S(1)}, u32[]{:S(2)}, u32[]{:S(2)}) collective-permute-start(f32[22656]{0:T(1024)S(1)} %add.166), channel_id=1, source_target_pairs={{0,4},{1,5},{2,6},{3,7},{4,0},{5,1},{6,2},{7,3},{8,12},{9,13},{10,... | collective-permute-start | bytes 271880 | tf_op jit(solution)/shard_map/ppermute | solution.py:1375
  417.9 14.9 %collective-permute-start.36 = (bf16[3,128,512]{2,1,0:T(8,128)(2,1)S(1)}, bf16[3,128,512]{2,1,0:T(8,128)(2,1)S(1)}, u32[]{:S(2)}, u32[]{:S(2)}) collective-permute-start(bf16[3,128,512]{2,1,0:T(8,128)(2,1)S(1)} %get-tuple-element.198), channel_id=1, source_target_pairs={{0,8},{8,0},{16,24},{24,16},{1,9},{9,1},{17,25},{25,17},{2,10},{10... | collective-permute-start | bytes 1179656 | tf_op jit(solution)/shard_map/ppermute | solution.py:1375
  423.9 6.0 %collective-permute-start.40 = (f32[1416]{0:T(1024)S(1)}, f32[1416]{0:T(1024)S(1)}, u32[]{:S(2)}, u32[]{:S(2)}) collective-permute-start(f32[1416]{0:T(1024)S(1)} %pad_maximum_fusion.5), channel_id=1, source_target_pairs={{0,8},{8,0},{16,24},{24,16},{1,9},{9,1},{17,25},{25,17},{2,10},{10... | collective-permute-start | bytes 17000 | tf_op jit(solution)/shard_map/ppermute | solution.py:1375
  (32 other events, 80.4 us)

commit v5 on v4

--- a/solution.py
+++ b/solution.py
@@ -1011,6 +1011,59 @@
     )(info, *after, middle, grad, gain, lifted, *weights, *more)
 
 
+def feed_forward_half(which, units, lows_ref, w_gate_up_ref, w_down_ref, kept_ref, totals_ref):
+    normed = lows_ref[which]
+    lifted = []
+    tiles = unit_tiles(units)
+    for index in range(len(tiles) + 1):
+        if index < len(tiles):
+            start, size = tiles[index]
+            span, place = pl.ds(start, size), pl.ds(pl.multiple_of(which * units + start, LANES), size)
+            gate = mm(normed, w_gate_up_ref[which, 0, :, span])
+            up = mm(normed, w_gate_up_ref[which, 1, :, span])
+            kept_ref[0, :, place] = low(gate)
+            kept_ref[1, :, place] = low(up)
+            lifted.append((gate, up))
+        if index:
+            start, size = tiles[index - 1]
+            gate, up = lifted[index - 1]
+            part = mm(low(gate * sigmoid(gate) * up), w_down_ref[which, pl.ds(start, size), :])
+            if index > 1:
+                totals_ref[which] += part
+            else:
+                totals_ref[which] = part
+
+
+def feed_backward_half(which, units, lows_ref, w_gate_up_ref, w_down_ref, kept_ref, made_ref, totals_ref):
+    grads = lows_ref[which]
+    hidden_grads = []
+    tiles = unit_tiles(units)
+    for index in range(len(tiles) + 1):
+        if index < len(tiles):
+            start, size = tiles[index]
+            hidden_grads.append(mm_nt(grads, w_down_ref[which, pl.ds(start, size), :]))
+        if index:
+            start, size = tiles[index - 1]
+            span, place = pl.ds(start, size), pl.ds(pl.multiple_of(which * units + start, LANES), size)
+            hidden_grad = hidden_grads[index - 1]
+            gate = kept_ref[0, :, place].astype(WIDE)
+            up = kept_ref[1, :, place].astype(WIDE)
+            open_ = sigmoid(gate)
+            silu = gate * open_
+            up_grad = low(hidden_grad * silu)
+            gate_grad = low(hidden_grad * up * (open_ + silu * (1.0 - open_)))
+            kept_ref[0, :, place] = gate_grad
+            kept_ref[1, :, place] = up_grad
+            made_ref[0, :, place] = low(silu * up)
+            part = mm_nt(gate_grad, w_gate_up_ref[which, 0, :, span]) + mm_nt(
+                up_grad, w_gate_up_ref[which, 1, :, span]
+            )
+            if index > 1:
+                totals_ref[which] += part
+            else:
+                totals_ref[which] = part
+
+
 def second_layer_kernel(
     info_ref,
     after_ref,
@@ -1104,54 +1157,63 @@
             sems,
         )
 
-    @pl.when(turn == 0)
-    def ahead():
-        for item in tiles[:AHEAD]:
-            start_each(item[3] + item[4])
-
-    @pl.when(turn == 1)
+    units, width = down_own_ref.shape[0], middle_ref.shape[1]
+    half_tiles = len(tiles) // 2
+    whole_stack = [
+        pltpu.make_async_copy(kept_ref, feed_stack_ref.at[pl.ds(0, 2)], out_sems.at[0]),
+        pltpu.make_async_copy(made_ref, feed_stack_ref.at[pl.ds(2, 2)], out_sems.at[1]),
+    ]
+
+    for which in range(2):
+
+        @pl.when(turn == which)
+        def ahead():
+            for item in tiles[which * half_tiles : (which + 1) * half_tiles]:
+                start_each(item[3] + item[4])
+
+        @pl.when(turn == 2 + which)
+        def arrived():
+            for item in tiles[which * half_tiles : (which + 1) * half_tiles]:
+                wait_each(item[3] + item[4])
+
+    @pl.when(turn == 2)
+    def feed_first():
+        middle = middle_ref[...]
+        lows_ref[0] = low(middle * norm_scale(middle, 1e-6) * feed_gain_ref[...])
+        made_ref[1] = jnp.zeros(made_ref.shape[1:], LOW)
+        made_ref[1, :, :width] = lows_ref[0]
+        apart_order(info_ref, lows_ref.at[0], lows_ref.at[1])
+
+    @pl.when((turn == 2) | (turn == 3))
     def feed():
-        feed_forward_kernel(
-            False,
-            info_ref,
-            middle_ref,
-            feed_gain_ref,
-            *feed_weights,
-            result_ref,
-            None,
-            totals_ref,
-            lows_ref,
-            w_gate_up_ref,
-            w_down_ref,
-            kept_ref,
-            feed_sems,
-            None,
-        )
-        feed_backward_kernel(
-            False,
-            info_ref,
-            middle_ref,
-            grad_ref,
-            feed_gain_ref,
-            None,
-            *feed_weights,
-            branch_ref,
-            feed_gain_grad_ref,
-            feed_stack_ref,
-            totals_ref,
-            lows_ref,
-            w_gate_up_ref,
-            w_down_ref,
-            kept_ref,
-            made_ref,
-            feed_sems,
-            None,
-            out_sems,
-        )
-
-    @pl.when(turn >= 2)
+        feed_forward_half(turn - 2, units, lows_ref, w_gate_up_ref, w_down_ref, kept_ref, totals_ref)
+
+    @pl.when(turn == 3)
+    def feed_last():
+        add_from_apart(info_ref, totals_ref.at[1], totals_ref.at[0], DOWN)
+        result_ref[...] = low(totals_ref[0] + middle_ref[...])
+
+    @pl.when(turn == 4)
+    def feed_back_first():
+        made_ref[1, :, units : units + width] = grad_ref[...]
+        lows_ref[0] = grad_ref[...]
+        apart_order(info_ref, lows_ref.at[0], lows_ref.at[1], DOWN)
+
+    @pl.when((turn == 4) | (turn == 5))
+    def feed_back():
+        feed_backward_half(turn - 4, units, lows_ref, w_gate_up_ref, w_down_ref, kept_ref, made_ref, totals_ref)
+
+    @pl.when(turn == 5)
+    def feed_back_last():
+        start_each(whole_stack)
+        add_from_apart(info_ref, totals_ref.at[1], totals_ref.at[0])
+        value_grad, gain_grad = norm_back(middle_ref[...], feed_gain_ref[...], totals_ref[0], 1e-6)
+        branch_ref[...] = grad_ref[...].astype(WIDE) + value_grad
+        feed_gain_grad_ref[...] = gain_grad
+
+    @pl.when(turn >= 6)
     def backward():
-        half = turn - 2
+        half = turn - 6
         mixer_backward_kernel(
             half,
             False,
@@ -1187,12 +1249,13 @@
 
     for which in range(2):
 
-        @pl.when(turn == 2 + which)
+        @pl.when(turn == 6 + which)
         def start_leaving():
             leave(which).start()
 
-    @pl.when(turn == 3)
+    @pl.when(turn == 7)
     def wait_leaving():
+        wait_each(whole_stack)
         leave(0).wait()
         leave(1).wait()
 
@@ -1210,7 +1273,7 @@
         name="second_layer",
         grid_spec=pltpu.PrefetchScalarGridSpec(
             num_scalar_prefetch=1,
-            grid=(4,),
+            grid=(8,),
             in_specs=[
                 ANYWHERE,
                 whole((length, width)),
@@ -1258,7 +1321,7 @@
                 pltpu.VMEM((2, 6, length, tile), LOW),
                 pltpu.SemaphoreType.DMA((6,)),
                 pltpu.SemaphoreType.DMA((3 * count,)),
-                pltpu.SemaphoreType.DMA((2 * count + 1,)),
+                pltpu.SemaphoreType.DMA((2,)),
                 pltpu.SemaphoreType.DMA((2,)),
             ],
         ),

time: 440 us -> 439 us (level)
  transfers between devices with their start and end apart: 41 -> 41, of which waited for: 22 -> 22; matrix products, arithmetic and copies ran while one was open for 8% -> 8% of each run, Pallas kernels for 42% -> 41%
where the time goes in v5:
time: 439 us; the launch traced here: 435 us
  Pallas kernels  193 us (44%)
  waiting for transfers between devices  134 us (31%)
  starting transfers between devices  53.6 us (12%)
  local copies, waits for them, and re-layouts  41.6 us (9%)
  other arithmetic  9.49 us (2%)
    ppermute x36, waiting for transfers between devices, exchange(): lax.ppermute(value, axis, [(i, i ^ apart(i)) for i in range(lax.axis_size...  74.3 us
    ppermute x2, waiting for transfers between devices, local(): returned.append(lax.ppermute(after, 'section', [(2, 0), (3, 1)]))  54.1 us
    pallas_call x2, Pallas kernels, mixer_backward(): pl.pallas_call(kernel, name='mixer_backward', grid_spec=pltpu.PrefetchSca...  44.8 us
    pallas_call x4, Pallas kernels, rows_grads(): pl.pallas_call(lambda info_ref, *refs: rows_kernel(halves, left[3], count...  31.8 us
    ppermute x36, starting transfers between devices, exchange(): lax.ppermute(value, axis, [(i, i ^ apart(i)) for i in range(lax.axis_size...  31.6 us
    pallas_call x2, Pallas kernels, mixer_forward(): pl.pallas_call(wrap(lambda info_ref, after_ref, *refs: mixer_forward_kern...  31.2 us
    pallas_call x2, Pallas kernels, feed_backward(): pl.pallas_call(kernel, name='feed_backward', grid_spec=pltpu.PrefetchScal...  27.4 us
    pallas_call x2, Pallas kernels, feed_forward(): pl.pallas_call(wrap(lambda *refs: feed_forward_kernel(True, *refs)), name...  23.3 us
  transfers between devices with their start and end apart: 41, of which 22 were waited for; matrix products, arithmetic and copies ran while one was open for 8% of the time, Pallas kernels for 41%

profile of v5, /device:TPU:0, one launch (start us, length us, event | category | flops | bytes accessed | tf_op | source)
XLA Modules:
  0.0 434.7 jit_solution(15094618561347450161)
XLA Ops:
  1.7 3.1 collective-permute-start
  4.8 2.0 constant_dynamic-slice_fusion.6
  6.8 7.1 %collective-permute-done = bf16[3,128,512]{2,1,0:T(8,128)(2,1)S(1)} collective-permute-done((bf16[3,128,512]{2,1,0:T(8,128)(2,1)S(1)}, bf16[3,128,512]{2,1,0:T(8,128)(2,1)S(1)}, u32[]{:S(2)}, u32[]{:S(2)}) %collective-permute-start) | collective-permute-done | bytes 393248 | tf_op jit(solution)/shard_map/ppermute | solution.py:1438
  13.9 1.7 collective-permute-start.7
  16.8 1.6 collective-permute-start.6
  18.4 3.3 collective-permute-done.7
  21.8 1.7 collective-permute-start.8
  23.5 1.9 constant_dynamic-slice_fusion.5
  25.4 2.2 dynamic-slice_bitcast_fusion.2
  27.6 2.0 constant_dynamic-slice_fusion.4
  29.6 1.6 collective-permute-start.1
  34.8 10.9 %collective-permute-done.1 = bf16[2,128,1408]{2,1,0:T(8,128)(2,1)S(1)} collective-permute-done((bf16[2,128,1408]{2,1,0:T(8,128)(2,1)}, bf16[2,128,1408]{2,1,0:T(8,128)(2,1)S(1)}, u32[]{:S(2)}, u32[]{:S(2)}) %collective-permute-start.1) | collective-permute-done | bytes 720928 | tf_op jit(solution)/shard_map/ppermute | solution.py:1438
  47.8 1.4 collective-permute-start.4
  51.4 9.1 %collective-permute-done.4.refs_9_.refs_12_.refs_21_ = bf16[256,1024]{1,0:T(8,128)(2,1)S(1)} collective-permute-done((bf16[256,1024]{1,0:T(8,128)(2,1)}, bf16[256,1024]{1,0:T(8,128)(2,1)S(1)}, u32[]{:S(2)}, u32[]{:S(2)}) %collective-permute-start.4) | collective-permute-done | bytes 524320 | tf_op jit(solution)/shard_map/ppermute | solution.py:1438
  60.5 1.5 collective-permute-start.5
  64.1 15.5 %mixer_forward.2 = (f32[256,1024]{1,0:T(8,128)}, f32[256,128]{1,0:T(8,128)}, bf16[3,256,1024]{2,1,0:T(8,128)(2,1)}, bf16[256,1024]{1,0:T(8,128)(2,1)}, bf16[256,...) custom-call(s32[20]{0:T(128)} %stack.109.info_ref.refs_0_, ...), custom_call_target="tpu_custom_call" | custom-call | flops 15399999488 | bytes 1048576 | tf_op jit(solution)/shard_map/mixer_forward/pallas_call | solution.py:344
  79.7 1.5 collective-permute-done.3
  82.3 15.7 %mixer_forward.3 = (f32[256,1024]{1,0:T(8,128)}, f32[256,128]{1,0:T(8,128)}, bf16[3,256,1024]{2,1,0:T(8,128)(2,1)}, bf16[256,1024]{1,0:T(8,128)(2,1)}, bf16[256,...) custom-call(s32[20]{0:T(128)} %stack.109.info_ref.refs_0_, ...), custom_call_target="tpu_custom_call" | custom-call | flops 15399999488 | bytes 1048576 | tf_op jit(solution)/shard_map/mixer_forward/pallas_call | solution.py:344
  98.8 1.4 copy-done.31
  101.8 11.7 %feed_forward.2 = (bf16[256,1024]{1,0:T(8,128)(2,1)}, bf16[2,256,2816]{2,1,0:T(8,128)(2,1)}) custom-call(s32[20]{0:T(128)} %stack.109.info_ref.refs_0_, f32[256,1024]{1,0:T(8,128)} %get-tuple-element.118.after_ref.refs_1_.refs_2_, f32[1,1024]{1,0:T(1,128)} %get-tuple-element.266.refs_2_.refs_4_, bf16[2,1024,1408]{2,1,0:T(8,128)(2,1)} %refs_6_.7, ...), custom_call_target="tpu_custom_call" | custom-call | flops 11000000512 | bytes 1048576 | tf_op jit(solution)/shard_map/feed_forward/pallas_call | solution.py:848
  113.5 4.5 %collective-permute-start.14 = (bf16[256,1024]{1,0:T(8,128)(2,1)}, bf16[256,1024]{1,0:T(8,128)(2,1)S(1)}, u32[]{:S(2)}, u32[]{:S(2)}) collective-permute-start(bf16[256,1024]{1,0:T(8,128)(2,1)} %get-tuple-element.123), channel_id=1, source_target_pairs={{0,16},{8,24},{1,17},{9,25},{2,18},{10,26},{3,19},{11,27},{4,20},{... | collective-permute-start | bytes 1572872 | tf_op jit(solution)/shard_map/ppermute | solution.py:1566
  118.0 11.6 %feed_forward.3 = (bf16[256,1024]{1,0:T(8,128)(2,1)}, bf16[2,256,2816]{2,1,0:T(8,128)(2,1)}) custom-call(s32[20]{0:T(128)} %stack.109.info_ref.refs_0_, f32[256,1024]{1,0:T(8,128)} %get-tuple-element.124.refs_1_.refs_2_, f32[1,1024]{1,0:T(1,128)} %get-tuple-element.266.refs_2_.refs_4_, bf16[2,1024,1408]{2,1,0:T(8,128)(2,1)} %refs_6_.7, ...), custom_call_target="tpu_custom_call" | custom-call | flops 11000000512 | bytes 1048576 | tf_op jit(solution)/shard_map/feed_forward/pallas_call | solution.py:848
  130.0 13.5 %collective-permute-start.15 = (f32[20]{0:T(128)S(1)}, f32[20]{0:T(128)S(1)}, u32[]{:S(2)}, u32[]{:S(2)}) collective-permute-start(f32[20]{0:T(128)S(1)} %convert_element_type.12), channel_id=1, source_target_pairs={{0,8},{8,0},{1,9},{9,1},{2,10},{10,2},{3,11},{11,3},{4,12},{12,4},... | collective-permute-start | bytes 248 | tf_op jit(solution)/shard_map/ppermute | solution.py:1570
  145.1 1.3 collective-permute-start.16
  146.4 3.6 second_layer.2
  150.0 1.3 collective-permute-start.17
  151.3 1.4 copy.52
  152.7 4.3 collective-permute-done.16.refs_1_
  157.8 19.0 %second_layer.3 = (bf16[256,1024]{1,0:T(8,128)(2,1)}, bf16[256,1024]{1,0:T(8,128)(2,1)}, f32[1,1024]{1,0:T(1,128)}, f32[1,1024]{1,0:T(1,128)}, bf16[256,128]{1,0...) custom-call(s32[20]{0:T(128)} %stack.109.info_ref.refs_0_, ...), custom_call_target="tpu_custom_call" | custom-call | flops 54999998464 | bytes 1048576 | tf_op jit(solution)/shard_map/second_layer/pallas_call | solution.py:1271
  176.8 1.3 collective-permute-start.20
  178.1 28.3 %collective-permute-done.17.refs_3_ = bf16[256,1024]{1,0:T(8,128)(2,1)S(1)} collective-permute-done((bf16[256,1024]{1,0:T(8,128)(2,1)}, bf16[256,1024]{1,0:T(8,128)(2,1)S(1)}, u32[]{:S(2)}, u32[]{:S(2)}) %collective-permute-start.17) | collective-permute-done | bytes 524320 | tf_op jit(solution)/shard_map/ppermute | solution.py:1583
  207.2 13.5 %feed_backward.2 = (f32[256,1024]{1,0:T(8,128)}, f32[1,1024]{1,0:T(1,128)}, bf16[4,256,2816]{2,1,0:T(8,128)(2,1)}) custom-call(s32[20]{0:T(128)} %stack.109.info_ref.refs_0_, bf16[256,1024]{1,0:T(8,128)(2,1)} %get-tuple-element.133.refs_1_, f32[256,1024]{1,0:T(8,128)} %get-tuple-element.118.after_ref.refs_1_.refs_2_, ...), custom_call_target="tpu_custom_call", output_to_operand_aliasing={{2}: (13, {})} | custom-call | flops 14300000256 | bytes 1048576 | tf_op jit(solution)/shard_map/feed_backward/pallas_call | solution.py:983
  220.8 22.0 %mixer_backward.2 = (bf16[256,1024]{1,0:T(8,128)(2,1)}, f32[1,1024]{1,0:T(1,128)}, bf16[6,256,1024]{2,1,0:T(8,128)(2,1)}, bf16[256,128]{1,0:T(8,128)(2,1)}, f32[3,4,1024]{2,1,0:T(4,128)}, /*index=5*/f32[1,128]{1,0:T(1,128)}) custom-call(s32[20]{0:T(128)} %stack.109.info_ref.refs_0_, f32[3,4,1024]{2,1,0:T(4,128)} %copy-done.39, f32[3,4,1024]{2,1,0:T(4,128)} %copy-done.39, ...), custom_call_target="tpu_custom_call" | custom-call | flops 22000001024 | bytes 1048576 | tf_op jit(solution)/shard_map/mixer_backward/pallas_call | solution.py:684
  243.3 25.8 %collective-permute-done.20.refs_3_ = bf16[256,1024]{1,0:T(8,128)(2,1)S(1)} collective-permute-done((bf16[256,1024]{1,0:T(8,128)(2,1)}, bf16[256,1024]{1,0:T(8,128)(2,1)S(1)}, u32[]{:S(2)}, u32[]{:S(2)}) %collective-permute-start.20) | collective-permute-done | bytes 524320 | tf_op jit(solution)/shard_map/ppermute | solution.py:1583
  269.9 13.9 %feed_backward.3 = (f32[256,1024]{1,0:T(8,128)}, f32[1,1024]{1,0:T(1,128)}, bf16[4,256,2816]{2,1,0:T(8,128)(2,1)}) custom-call(s32[20]{0:T(128)} %stack.109.info_ref.refs_0_, bf16[256,1024]{1,0:T(8,128)(2,1)} %get-tuple-element.150.refs_1_, f32[256,1024]{1,0:T(8,128)} %get-tuple-element.124.refs_1_.refs_2_, ...), custom_call_target="tpu_custom_call", output_to_operand_aliasing={{2}: (13, {})} | custom-call | flops 14300000256 | bytes 1048576 | tf_op jit(solution)/shard_map/feed_backward/pallas_call | solution.py:983
  284.6 1.6 copy-done.8
  286.3 22.8 %mixer_backward.3 = (bf16[256,1024]{1,0:T(8,128)(2,1)}, f32[1,1024]{1,0:T(1,128)}, bf16[6,256,1024]{2,1,0:T(8,128)(2,1)}, bf16[256,128]{1,0:T(8,128)(2,1)}, f32[3,4,1024]{2,1,0:T(4,128)}, /*index=5*/f32[1,128]{1,0:T(1,128)}) custom-call(s32[20]{0:T(128)} %stack.109.info_ref.refs_0_, bf16[4,256,2816]{2,1,0:T(8,128)(2,1)} %collective-permute-done.18.refs_1_.refs_3_.refs_7_, ...), custom_call_target="tpu_custom_call" | custom-call | flops 22000001024 | bytes 1048576 | tf_op jit(solution)/shard_map/mixer_backward/pallas_call | solution.py:684
  312.5 12.0 %rows_grads.4 = (bf16[2,256,2816]{2,1,0:T(8,128)(2,1)S(1)}, bf16[2,256,2816]{2,1,0:T(8,128)(2,1)}) custom-call(s32[20]{0:T(128)S(1)} %copy-done.7, f32[1,1024]{1,0:T(1,128)S(1)} %copy-done.5, bf16[4,256,2816]{2,1,0:T(8,128)(2,1)S(1)} %bitcast.81, bf16[4,256,2816]{2,1,0:T(8,128)(2,1)} %get-tuple-element.172.refs_2_.refs_6_, ...), custom_call_target="tpu_custom_call" | custom-call | flops 11000000512 | bytes 1048576 | tf_op jit(solution)/shard_map/rows_grads/pallas_call | solution.py:1385
  324.6 2.0 collective-permute-start.24
  326.6 9.7 %rows_grads.5 = (bf16[1,704,1024]{2,1,0:T(8,128)(2,1)S(1)}, bf16[1,704,1024]{2,1,0:T(8,128)(2,1)}) custom-call(s32[20]{0:T(128)S(1)} %copy-done.7, bf16[2,256,2816]{2,1,0:T(8,128)(2,1)S(1)} %get-tuple-element.173.refs_0_.keep_ref, bf16[4,256,2816]{2,1,0:T(8,128)(2,1)S(1)} %bitcast.81, bf16[4,256,2816]{2,1,0:T(8,128)(2,1)} %get-tuple-element.172.refs_2_.refs_6_, ...), custom_call_target="tpu_custom_call" | custom-call | flops 11000000512 | bytes 1048576 | tf_op jit(solution)/shard_map/rows_grads/pallas_call | solution.py:1385
  336.8 1.9 copy-done.3
  338.7 1.9 copy-done.9
  340.6 6.4 %rows_grads.6 = (bf16[3,256,1024]{2,1,0:T(8,128)(2,1)S(1)}, bf16[3,256,1024]{2,1,0:T(8,128)(2,1)S(1)}) custom-call(s32[20]{0:T(128)S(1)} %copy-done.7, bf16[1,704,1024]{2,1,0:T(8,128)(2,1)S(1)} %get-tuple-element.174.refs_0_.keep_ref, bf16[6,256,1024]{2,1,0:T(8,128)(2,1)S(1)} %copy-done.2, bf16[6,256,1024]{2,1,0:T(8,128)(2,1)S(1)} %copy-done.3, ...), custom_call_target="tpu_custom_call" | custom-call | flops 11000000512 | bytes 1048576 | tf_op jit(solution)/shard_map/rows_grads/pallas_call | solution.py:1385
  347.1 3.6 rows_grads.7
  350.7 1.6 collective-permute-start.27
  353.4 6.0 %collective-permute-done.24.came_ref = bf16[2,256,2816]{2,1,0:T(8,128)(2,1)} collective-permute-done((bf16[2,256,2816]{2,1,0:T(8,128)(2,1)}, bf16[2,256,2816]{2,1,0:T(8,128)(2,1)}, u32[]{:S(2)}, u32[]{:S(2)}) %collective-permute-start.24) | collective-permute-done | bytes 2883616 | tf_op jit(solution)/shard_map/ppermute | solution.py:1438
  359.4 2.3 halve.12
  362.2 9.0 %collective-permute-done.25.came_ref = bf16[1,704,1024]{2,1,0:T(8,128)(2,1)} collective-permute-done((bf16[1,704,1024]{2,1,0:T(8,128)(2,1)}, bf16[1,704,1024]{2,1,0:T(8,128)(2,1)}, u32[]{:S(2)}, u32[]{:S(2)}) %collective-permute-start.25) | collective-permute-done | bytes 1441824 | tf_op jit(solution)/shard_map/ppermute | solution.py:1438
  371.2 1.7 halve.13
  372.9 1.5 select_bitcast_fusion
  376.9 5.3 %collective-permute-done.27.came_ref = bf16[1,256,1024]{2,1,0:T(8,128)(2,1)S(1)} collective-permute-done((bf16[1,256,1024]{2,1,0:T(8,128)(2,1)S(1)}, bf16[1,256,1024]{2,1,0:T(8,128)(2,1)S(1)}, u32[]{:S(2)}, u32[]{:S(2)}) %collective-permute-start.27) | collective-permute-done | bytes 524320 | tf_op jit(solution)/shard_map/ppermute | solution.py:1438
  384.0 8.0 %collective-permute-done.26 = bf16[2,2,256,256]{3,2,1,0:T(8,128)(2,1)S(1)} collective-permute-done((bf16[2,2,256,256]{3,2,1,0:T(8,128)(2,1)S(1)}, bf16[2,2,256,256]{3,2,1,0:T(8,128)(2,1)S(1)}, u32[]{:S(2)}, u32[]{:S(2)}) %collective-permute-start.26) | collective-permute-done | bytes 524320 | tf_op jit(solution)/shard_map/ppermute | solution.py:1438
  394.2 2.0 collective-permute-done.29.came_ref
  398.5 1.3 reshape.192
  400.5 1.7 collective-permute-done.30.came_ref
  404.4 1.3 halve.17
  406.2 1.5 collective-permute-done.31.came_ref
  409.4 2.0 collective-permute-start.38
  411.6 3.5 collective-permute-done.38
  415.2 1.9 collective-permute-start.39
  417.0 1.2 collective-permute-start.36
  419.6 1.4 copy-done.13
  424.4 4.6 %collective-permute-done.40 = f32[1416]{0:T(1024)S(1)} collective-permute-done((f32[1416]{0:T(1024)S(1)}, f32[1416]{0:T(1024)S(1)}, u32[]{:S(2)}, u32[]{:S(2)}) %collective-permute-start.40) | collective-permute-done | bytes 5696 | tf_op jit(solution)/shard_map/ppermute | solution.py:1438
  432.8 1.5 halve.23
  (246 shorter events, 49.3 us)
Async XLA Ops:
  0.6 16.1 %copy-start.32 = (f32[3,4,512]{2,1,0:T(4,128)S(1)}, f32[3,4,512]{2,1,0:T(4,128)}, u32[]{:S(2)}) copy-start(f32[3,4,512]{2,1,0:T(4,128)} %param.14) | copy-start | bytes 73732
  0.7 16.1 %copy-start.38 = (f32[2,512]{1,0:T(2,128)S(1)}, f32[2,512]{1,0:T(2,128)}, u32[]{:S(2)}) copy-start(f32[2,512]{1,0:T(2,128)} %param.18) | copy-start | bytes 12292
  0.7 16.1 %copy-start.43 = (f32[64]{0:T(128)S(1)}, f32[64]{0:T(128)}, u32[]{:S(2)}) copy-start(f32[64]{0:T(128)} %param.19) | copy-start | bytes 772
  1.7 12.2 %collective-permute-start = (bf16[3,128,512]{2,1,0:T(8,128)(2,1)S(1)}, bf16[3,128,512]{2,1,0:T(8,128)(2,1)S(1)}, u32[]{:S(2)}, u32[]{:S(2)}) collective-permute-start(bf16[3,128,512]{2,1,0:T(8,128)(2,1)S(1)} %constant_dynamic-slice_fusion.7), channel_id=1, source_target_pairs={{0,8},{8,0},{16,24},{24,16},{1,9},{9,1},{17,25},{25,17},{2,10},{10... | collective-permute-start | bytes 1179656 | tf_op jit(solution)/shard_map/ppermute | solution.py:1438
  13.9 7.8 %collective-permute-start.7 = (bf16[3,128,512]{2,1,0:T(8,128)(2,1)S(1)}, bf16[3,128,512]{2,1,0:T(8,128)(2,1)S(1)}, u32[]{:S(2)}, u32[]{:S(2)}) collective-permute-start(bf16[3,128,512]{2,1,0:T(8,128)(2,1)S(1)} %collective-permute-done), channel_id=1, source_target_pairs={{0,2},{1,5},{2,0},{3,7},{4,6},{5,1},{6,4},{7,3},{8,10},{9,13},{10,... | collective-permute-start | bytes 1179656 | tf_op jit(solution)/shard_map/ppermute | solution.py:1438
  16.8 15.3 %collective-permute-start.6 = (f32[11328]{0:T(1024)S(1)}, f32[11328]{0:T(1024)S(1)}, u32[]{:S(2)}, u32[]{:S(2)}) collective-permute-start(f32[11328]{0:T(1024)S(1)} %pad_maximum_fusion.4), channel_id=1, source_target_pairs={{0,8},{8,0},{16,24},{24,16},{1,9},{9,1},{17,25},{25,17},{2,10},{10... | collective-permute-start | bytes 135944 | tf_op jit(solution)/shard_map/ppermute | solution.py:1438
  18.4 12.8 %copy-start.37 = (bf16[1024,4]{0,1:T(4,128)(2,1)S(1)}, bf16[1024,4]{0,1:T(4,128)(2,1)}, u32[]{:S(2)}) copy-start(bf16[1024,4]{0,1:T(4,128)(2,1)} %param.13) | copy-start | bytes 24580
  21.8 12.1 %collective-permute-start.8 = (bf16[3,256,512]{2,1,0:T(8,128)(2,1)S(1)}, bf16[3,256,512]{2,1,0:T(8,128)(2,1)S(1)}, u32[]{:S(2)}, u32[]{:S(2)}) collective-permute-start(bf16[3,256,512]{2,1,0:T(8,128)(2,1)S(1)} %pad_maximum_fusion.2), channel_id=1, source_target_pairs={{0,4},{1,3},{2,6},{3,1},{4,0},{5,7},{6,2},{7,5},{8,12},{9,11},{10,... | collective-permute-start | bytes 2359304 | tf_op jit(solution)/shard_map/ppermute | solution.py:1438
  29.6 16.1 %collective-permute-start.1 = (bf16[2,128,1408]{2,1,0:T(8,128)(2,1)}, bf16[2,128,1408]{2,1,0:T(8,128)(2,1)S(1)}, u32[]{:S(2)}, u32[]{:S(2)}) collective-permute-start(bf16[2,128,1408]{2,1,0:T(8,128)(2,1)} %constant_dynamic-slice_fusion.6), channel_id=1, source_target_pairs={{0,8},{8,0},{16,24},{24,16},{1,9},{9,1},{17,25},{25,17},{2,10},{10... | collective-permute-start | bytes 2162696 | tf_op jit(solution)/shard_map/ppermute | solution.py:1438
  33.8 26.7 %copy-start.27 = (bf16[1408,256]{1,0:T(8,128)(2,1)S(1)}, bf16[1408,256]{1,0:T(8,128)(2,1)}, u32[]{:S(2)}) copy-start(bf16[1408,256]{1,0:T(8,128)(2,1)} %constant_dynamic-slice_fusion.4) | copy-start | bytes 2162692
  34.7 28.6 %collective-permute-start.9 = (bf16[3,512,512]{2,1,0:T(8,128)(2,1)}, bf16[3,512,512]{2,1,0:T(8,128)(2,1)}, u32[]{:S(2)}, u32[]{:S(2)}) collective-permute-start(bf16[3,512,512]{2,1,0:T(8,128)(2,1)} %constant_dynamic-update-slice_fusion.2.refs_7_.refs_10_.refs_19_), channel_id=1, source_target_pairs={{0,1},{1,0},{2,3},{3,2},{4,5},{5,4},{6,7},{7,6},{8,9},{9,8},{10,11... | collective-permute-start | bytes 4718600 | tf_op jit(solution)/shard_map/ppermute | solution.py:1438
  34.8 28.6 %copy-start.39 = (f32[3,4,1024]{2,1,0:T(4,128)}, f32[3,4,1024]{2,1,0:T(4,128)S(1)}, u32[]{:S(2)}) copy-start(f32[3,4,1024]{2,1,0:T(4,128)S(1)} %constant_dynamic-update-slice_fusion.refs_3_.refs_1_.refs_2_.refs_15_) | copy-start | bytes 147460
  45.7 16.3 %collective-permute-start.2 = (bf16[2,128,1408]{2,1,0:T(8,128)(2,1)S(1)}, bf16[2,128,1408]{2,1,0:T(8,128)(2,1)S(1)}, u32[]{:S(2)}, u32[]{:S(2)}) collective-permute-start(bf16[2,128,1408]{2,1,0:T(8,128)(2,1)S(1)} %collective-permute-done.1), channel_id=1, source_target_pairs={{0,2},{1,5},{2,0},{3,7},{4,6},{5,1},{6,4},{7,3},{8,10},{9,13},{10,... | collective-permute-start | bytes 2162696 | tf_op jit(solution)/shard_map/ppermute | solution.py:1438
  47.8 12.6 %collective-permute-start.4 = (bf16[256,1024]{1,0:T(8,128)(2,1)}, bf16[256,1024]{1,0:T(8,128)(2,1)S(1)}, u32[]{:S(2)}, u32[]{:S(2)}) collective-permute-start(bf16[256,1024]{1,0:T(8,128)(2,1)} %constant_dynamic-slice_fusion.5), channel_id=1, source_target_pairs={{0,8},{8,0},{16,24},{24,16},{1,9},{9,1},{17,25},{25,17},{2,10},{10... | collective-permute-start | bytes 1572872 | tf_op jit(solution)/shard_map/ppermute | solution.py:1438
  60.5 2.9 collective-permute-start.10
  60.5 19.2 %collective-permute-start.5 = (bf16[1408,256]{1,0:T(8,128)(2,1)S(1)}, bf16[1408,256]{1,0:T(8,128)(2,1)S(1)}, u32[]{:S(2)}, u32[]{:S(2)}) collective-permute-start(bf16[1408,256]{1,0:T(8,128)(2,1)S(1)} %copy-done.27), channel_id=1, source_target_pairs={{0,8},{8,0},{16,24},{24,16},{1,9},{9,1},{17,25},{25,17},{2,10},{10... | collective-permute-start | bytes 2162696 | tf_op jit(solution)/shard_map/ppermute | solution.py:1438
  62.1 19.1 %collective-permute-start.3 = (bf16[2,256,1408]{2,1,0:T(8,128)(2,1)S(1)}, bf16[2,256,1408]{2,1,0:T(8,128)(2,1)S(1)}, u32[]{:S(2)}, u32[]{:S(2)}) collective-permute-start(bf16[2,256,1408]{2,1,0:T(8,128)(2,1)S(1)} %pad_maximum_fusion), channel_id=1, source_target_pairs={{0,4},{1,3},{2,6},{3,1},{4,0},{5,7},{6,2},{7,5},{8,12},{9,11},{10,... | collective-permute-start | bytes 4325384 | tf_op jit(solution)/shard_map/ppermute | solution.py:1438
  81.2 16.9 %collective-permute-start.12 = (bf16[1408,256]{1,0:T(8,128)(2,1)S(1)}, bf16[1408,256]{1,0:T(8,128)(2,1)S(1)}, u32[]{:S(2)}, u32[]{:S(2)}) collective-permute-start(bf16[1408,256]{1,0:T(8,128)(2,1)S(1)} %collective-permute-done.5), channel_id=1, source_target_pairs={{0,2},{1,5},{2,0},{3,7},{4,6},{5,1},{6,4},{7,3},{8,10},{9,13},{10,... | collective-permute-start | bytes 2162696 | tf_op jit(solution)/shard_map/ppermute | solution.py:1438
  82.3 19.4 %collective-permute-start.11 = (bf16[2,512,1408]{2,1,0:T(8,128)(2,1)}, bf16[2,512,1408]{2,1,0:T(8,128)(2,1)}, u32[]{:S(2)}, u32[]{:S(2)}) collective-permute-start(bf16[2,512,1408]{2,1,0:T(8,128)(2,1)} %constant_dynamic-update-slice_fusion.5.refs_5_.refs_16_.refs_8_), channel_id=1, source_target_pairs={{0,1},{1,0},{2,3},{3,2},{4,5},{5,4},{6,7},{7,6},{8,9},{9,8},{10,11... | collective-permute-start | bytes 8650760 | tf_op jit(solution)/shard_map/ppermute | solution.py:1438
  98.2 3.6 collective-permute-start.13
  113.5 16.6 %collective-permute-start.14 = (bf16[256,1024]{1,0:T(8,128)(2,1)}, bf16[256,1024]{1,0:T(8,128)(2,1)S(1)}, u32[]{:S(2)}, u32[]{:S(2)}) collective-permute-start(bf16[256,1024]{1,0:T(8,128)(2,1)} %get-tuple-element.123), channel_id=1, source_target_pairs={{0,16},{8,24},{1,17},{9,25},{2,18},{10,26},{3,19},{11,27},{4,20},{... | collective-permute-start | bytes 1572872 | tf_op jit(solution)/shard_map/ppermute | solution.py:1566
  130.0 16.4 %copy-start.49 = (bf16[256,1024]{1,0:T(8,128)(2,1)}, bf16[256,1024]{1,0:T(8,128)(2,1)S(1)}, u32[]{:S(2)}) copy-start(bf16[256,1024]{1,0:T(8,128)(2,1)S(1)} %collective-permute-done.14.refs_1_) | copy-start | bytes 1572868
  130.0 15.1 %collective-permute-start.15 = (f32[20]{0:T(128)S(1)}, f32[20]{0:T(128)S(1)}, u32[]{:S(2)}, u32[]{:S(2)}) collective-permute-start(f32[20]{0:T(128)S(1)} %convert_element_type.12), channel_id=1, source_target_pairs={{0,8},{8,0},{1,9},{9,1},{2,10},{10,2},{3,11},{11,3},{4,12},{12,4},... | collective-permute-start | bytes 248 | tf_op jit(solution)/shard_map/ppermute | solution.py:1570
  145.1 11.9 %collective-permute-start.16 = (bf16[256,1024]{1,0:T(8,128)(2,1)}, bf16[256,1024]{1,0:T(8,128)(2,1)S(1)}, u32[]{:S(2)}, u32[]{:S(2)}) collective-permute-start(bf16[256,1024]{1,0:T(8,128)(2,1)} %get-tuple-element.132), channel_id=1, source_target_pairs={{0,16},{8,24},{1,17},{9,25},{2,18},{10,26},{3,19},{11,27},{4,20},{... | collective-permute-start | bytes 1572872 | tf_op jit(solution)/shard_map/ppermute | solution.py:1573
  150.0 56.4 %collective-permute-start.17 = (bf16[256,1024]{1,0:T(8,128)(2,1)}, bf16[256,1024]{1,0:T(8,128)(2,1)S(1)}, u32[]{:S(2)}, u32[]{:S(2)}) collective-permute-start(bf16[256,1024]{1,0:T(8,128)(2,1)} %get-tuple-element.131.refs_0_), channel_id=1, source_target_pairs={{16,0},{24,8},{17,1},{25,9},{18,2},{26,10},{19,3},{27,11},{20,4},{... | collective-permute-start | bytes 1572872 | tf_op jit(solution)/shard_map/ppermute | solution.py:1583
  176.8 92.3 %collective-permute-start.20 = (bf16[256,1024]{1,0:T(8,128)(2,1)}, bf16[256,1024]{1,0:T(8,128)(2,1)S(1)}, u32[]{:S(2)}, u32[]{:S(2)}) collective-permute-start(bf16[256,1024]{1,0:T(8,128)(2,1)} %get-tuple-element.133.refs_1_), channel_id=1, source_target_pairs={{16,0},{24,8},{17,1},{25,9},{18,2},{26,10},{19,3},{27,11},{20,4},{... | collective-permute-start | bytes 1572872 | tf_op jit(solution)/shard_map/ppermute | solution.py:1583
  220.7 63.9 %collective-permute-start.18 = (bf16[4,256,2816]{2,1,0:T(8,128)(2,1)}, bf16[4,256,2816]{2,1,0:T(8,128)(2,1)}, u32[]{:S(2)}, u32[]{:S(2)}) collective-permute-start(bf16[4,256,2816]{2,1,0:T(8,128)(2,1)} %get-tuple-element.152.refs_1_.refs_5_), channel_id=1, source_target_pairs={{0,1},{1,0},{2,3},{3,2},{4,5},{5,4},{6,7},{7,6},{8,9},{9,8},{10,11... | collective-permute-start | bytes 17301512 | tf_op jit(solution)/shard_map/ppermute | solution.py:1438
  242.8 41.8 %collective-permute-start.19 = (bf16[6,256,1024]{2,1,0:T(8,128)(2,1)}, bf16[6,256,1024]{2,1,0:T(8,128)(2,1)S(1)}, u32[]{:S(2)}, u32[]{:S(2)}) collective-permute-start(bf16[6,256,1024]{2,1,0:T(8,128)(2,1)} %get-tuple-element.153.refs_1_.refs_5_), channel_id=1, source_target_pairs={{0,1},{1,0},{2,3},{3,2},{4,5},{5,4},{6,7},{7,6},{8,9},{9,8},{10,11... | collective-permute-start | bytes 9437192 | tf_op jit(solution)/shard_map/ppermute | solution.py:1438
  269.9 14.1 %copy-start.35 = (f32[2,3,4,512]{3,2,1,0:T(4,128)S(1)}, f32[2,3,4,512]{3,2,1,0:T(4,128)}, u32[]{:S(2)}) copy-start(f32[2,3,4,512]{3,2,1,0:T(4,128)} %get-tuple-element.168) | copy-start | bytes 147460
  283.7 28.7 %collective-permute-start.22 = (bf16[4,256,2816]{2,1,0:T(8,128)(2,1)}, bf16[4,256,2816]{2,1,0:T(8,128)(2,1)}, u32[]{:S(2)}, u32[]{:S(2)}) collective-permute-start(bf16[4,256,2816]{2,1,0:T(8,128)(2,1)} %get-tuple-element.172.refs_2_.refs_6_), channel_id=1, source_target_pairs={{0,1},{1,0},{2,3},{3,2},{4,5},{5,4},{6,7},{7,6},{8,9},{9,8},{10,11... | collective-permute-start | bytes 17301512 | tf_op jit(solution)/shard_map/ppermute | solution.py:1438
  286.2 26.3 %slice-start = ((s8[5767168]{0:T(1024)(128)(4,1)}), s8[4194304]{0:T(1024)(128)(4,1)S(1)}, s32[]{:S(2)}) async-start(s8[5767168]{0:T(1024)(128)(4,1)} %bitcast.80), calls=%async_computation | async-start | bytes 8388608
  286.2 23.3 %copy-start.28 = (bf16[256,1024]{1,0:T(8,128)(2,1)S(1)}, bf16[256,1024]{1,0:T(8,128)(2,1)}, u32[]{:S(2)}) copy-start(bf16[256,1024]{1,0:T(8,128)(2,1)} %get-tuple-element.130) | copy-start | bytes 1572868
  286.2 23.3 %copy-start.30 = (bf16[256,1024]{1,0:T(8,128)(2,1)S(1)}, bf16[256,1024]{1,0:T(8,128)(2,1)}, u32[]{:S(2)}) copy-start(bf16[256,1024]{1,0:T(8,128)(2,1)} %get-tuple-element.150.refs_1_) | copy-start | bytes 1572868
  286.2 23.4 %copy-start.41 = (f32[1,1024]{1,0:T(1,128)S(1)}, f32[1,1024]{1,0:T(1,128)}, u32[]{:S(2)}) copy-start(f32[1,1024]{1,0:T(1,128)} %get-tuple-element.205) | copy-start | bytes 12292
  286.2 23.4 %copy-start.42 = (f32[1,1024]{1,0:T(1,128)S(1)}, f32[1,1024]{1,0:T(1,128)}, u32[]{:S(2)}) copy-start(f32[1,1024]{1,0:T(1,128)} %get-tuple-element.206) | copy-start | bytes 12292
  286.2 23.4 %copy-start.36 = (f32[3,4,1024]{2,1,0:T(4,128)S(1)}, f32[3,4,1024]{2,1,0:T(4,128)}, u32[]{:S(2)}) copy-start(f32[3,4,1024]{2,1,0:T(4,128)} %get-tuple-element.199) | copy-start | bytes 147460
  286.2 24.2 %copy-start.29 = (bf16[256,1024]{1,0:T(8,128)(2,1)S(1)}, bf16[256,1024]{1,0:T(8,128)(2,1)}, u32[]{:S(2)}) copy-start(bf16[256,1024]{1,0:T(8,128)(2,1)} %get-tuple-element.151) | copy-start | bytes 1572868
  286.2 26.3 %slice-start.1 = ((s8[5767168]{0:T(1024)(128)(4,1)}), s8[1572864]{0:T(1024)(128)(4,1)S(1)}, s32[]{:S(2)}) async-start(s8[5767168]{0:T(1024)(128)(4,1)} %bitcast.80), calls=%async_computation.1 | async-start | bytes 3145728
  309.1 27.7 %collective-permute-start.23 = (bf16[6,256,1024]{2,1,0:T(8,128)(2,1)}, bf16[6,256,1024]{2,1,0:T(8,128)(2,1)}, u32[]{:S(2)}, u32[]{:S(2)}) collective-permute-start(bf16[6,256,1024]{2,1,0:T(8,128)(2,1)} %get-tuple-element.175.refs_2_.refs_6_), channel_id=1, source_target_pairs={{0,1},{1,0},{2,3},{3,2},{4,5},{5,4},{6,7},{7,6},{8,9},{9,8},{10,11... | collective-permute-start | bytes 9437192 | tf_op jit(solution)/shard_map/ppermute | solution.py:1438
  312.4 60.4 %collective-permute-start.21 = (bf16[2,256,512]{2,1,0:T(8,128)(2,1)}, bf16[2,256,512]{2,1,0:T(8,128)(2,1)}, u32[]{:S(2)}, u32[]{:S(2)}) collective-permute-start(bf16[2,256,512]{2,1,0:T(8,128)(2,1)} %fusion.2), channel_id=1, source_target_pairs={{0,16},{8,24},{16,0},{24,8},{1,17},{9,25},{17,1},{25,9},{2,18},{10... | collective-permute-start | bytes 1572872 | tf_op jit(solution)/shard_map/ppermute | solution.py:1438
  324.6 11.7 %copy-start = (bf16[2,256,2816]{2,1,0:T(8,128)(2,1)}, bf16[2,256,2816]{2,1,0:T(8,128)(2,1)S(1)}, u32[]{:S(2)}) copy-start(bf16[2,256,2816]{2,1,0:T(8,128)(2,1)S(1)} %get-tuple-element.173.refs_0_.keep_ref) | copy-start | bytes 8650756
  324.6 34.8 %collective-permute-start.24 = (bf16[2,256,2816]{2,1,0:T(8,128)(2,1)}, bf16[2,256,2816]{2,1,0:T(8,128)(2,1)}, u32[]{:S(2)}, u32[]{:S(2)}) collective-permute-start(bf16[2,256,2816]{2,1,0:T(8,128)(2,1)} %get-tuple-element.178), channel_id=1, source_target_pairs={{0,2},{1,5},{2,0},{3,7},{4,6},{5,1},{6,4},{7,3},{8,10},{9,13},{10,... | collective-permute-start | bytes 8650760 | tf_op jit(solution)/shard_map/ppermute | solution.py:1438
  326.6 10.2 %copy-start.2 = (bf16[6,256,1024]{2,1,0:T(8,128)(2,1)S(1)}, bf16[6,256,1024]{2,1,0:T(8,128)(2,1)}, u32[]{:S(2)}) copy-start(bf16[6,256,1024]{2,1,0:T(8,128)(2,1)} %get-tuple-element.153.refs_1_.refs_5_) | copy-start | bytes 9437188
  336.3 10.8 %copy-start.11 = (bf16[1,704,1024]{2,1,0:T(8,128)(2,1)}, bf16[1,704,1024]{2,1,0:T(8,128)(2,1)S(1)}, u32[]{:S(2)}) copy-start(bf16[1,704,1024]{2,1,0:T(8,128)(2,1)S(1)} %get-tuple-element.174.refs_0_.keep_ref) | copy-start | bytes 4325380
  336.3 34.8 %collective-permute-start.25 = (bf16[1,704,1024]{2,1,0:T(8,128)(2,1)}, bf16[1,704,1024]{2,1,0:T(8,128)(2,1)}, u32[]{:S(2)}, u32[]{:S(2)}) collective-permute-start(bf16[1,704,1024]{2,1,0:T(8,128)(2,1)} %get-tuple-element.180), channel_id=1, source_target_pairs={{0,8},{8,0},{16,24},{24,16},{1,9},{9,1},{17,25},{25,17},{2,10},{10... | collective-permute-start | bytes 4325384 | tf_op jit(solution)/shard_map/ppermute | solution.py:1438
  347.1 12.2 %copy-start.1 = (bf16[2,256,2816]{2,1,0:T(8,128)(2,1)S(1)}, bf16[2,256,2816]{2,1,0:T(8,128)(2,1)}, u32[]{:S(2)}) copy-start(bf16[2,256,2816]{2,1,0:T(8,128)(2,1)} %copy-done) | copy-start | bytes 8650756
  350.7 31.5 %collective-permute-start.27 = (bf16[1,256,1024]{2,1,0:T(8,128)(2,1)S(1)}, bf16[1,256,1024]{2,1,0:T(8,128)(2,1)S(1)}, u32[]{:S(2)}, u32[]{:S(2)}) collective-permute-start(bf16[1,256,1024]{2,1,0:T(8,128)(2,1)S(1)} %get-tuple-element.183), channel_id=1, source_target_pairs={{0,8},{8,0},{16,24},{24,16},{1,9},{9,1},{17,25},{25,17},{2,10},{10... | collective-permute-start | bytes 1572872 | tf_op jit(solution)/shard_map/ppermute | solution.py:1438
  352.3 40.9 %collective-permute-start.28 = (bf16[3,256,1024]{2,1,0:T(8,128)(2,1)S(1)}, bf16[3,256,1024]{2,1,0:T(8,128)(2,1)S(1)}, u32[]{:S(2)}, u32[]{:S(2)}) collective-permute-start(bf16[3,256,1024]{2,1,0:T(8,128)(2,1)S(1)} %get-tuple-element.185), channel_id=1, source_target_pairs={{0,2},{1,5},{2,0},{3,7},{4,6},{5,1},{6,4},{7,3},{8,10},{9,13},{10,... | collective-permute-start | bytes 4718600 | tf_op jit(solution)/shard_map/ppermute | solution.py:1438
  359.4 11.8 %copy-start.12 = (bf16[1,704,1024]{2,1,0:T(8,128)(2,1)S(1)}, bf16[1,704,1024]{2,1,0:T(8,128)(2,1)}, u32[]{:S(2)}) copy-start(bf16[1,704,1024]{2,1,0:T(8,128)(2,1)} %copy-done.11) | copy-start | bytes 4325380
  361.6 34.6 %collective-permute-start.29 = (bf16[2,128,2816]{2,1,0:T(8,128)(2,1)S(1)}, bf16[2,128,2816]{2,1,0:T(8,128)(2,1)S(1)}, u32[]{:S(2)}, u32[]{:S(2)}) collective-permute-start(bf16[2,128,2816]{2,1,0:T(8,128)(2,1)S(1)} %get-tuple-element.187), channel_id=1, source_target_pairs={{0,4},{1,3},{2,6},{3,1},{4,0},{5,7},{6,2},{7,5},{8,12},{9,11},{10,... | collective-permute-start | bytes 4325384 | tf_op jit(solution)/shard_map/ppermute | solution.py:1438
  372.8 9.4 %copy-start.16 = (bf16[1,352,1024]{2,1,0:T(8,128)(2,1)}, bf16[1,352,1024]{2,1,0:T(8,128)(2,1)S(1)}, u32[]{:S(2)}) copy-start(bf16[1,352,1024]{2,1,0:T(8,128)(2,1)S(1)} %get-tuple-element.181.after_ref.keep_ref) | copy-start | bytes 2162692
  375.0 17.0 %collective-permute-start.26 = (bf16[2,2,256,256]{3,2,1,0:T(8,128)(2,1)S(1)}, bf16[2,2,256,256]{3,2,1,0:T(8,128)(2,1)S(1)}, u32[]{:S(2)}, u32[]{:S(2)}) collective-permute-start(bf16[2,2,256,256]{3,2,1,0:T(8,128)(2,1)S(1)} %get-tuple-element.261), channel_id=1, source_target_pairs={{0,8},{8,0},{16,24},{24,16},{1,9},{9,1},{17,25},{25,17},{2,10},{10... | collective-permute-start | bytes 1572872 | tf_op jit(solution)/shard_map/ppermute | solution.py:1438
  375.9 26.2 %collective-permute-start.30 = (bf16[1,352,1024]{2,1,0:T(8,128)(2,1)S(1)}, bf16[1,352,1024]{2,1,0:T(8,128)(2,1)}, u32[]{:S(2)}, u32[]{:S(2)}) collective-permute-start(bf16[1,352,1024]{2,1,0:T(8,128)(2,1)S(1)} %get-tuple-element.189), channel_id=1, source_target_pairs={{0,2},{1,5},{2,0},{3,7},{4,6},{5,1},{6,4},{7,3},{8,10},{9,13},{10,... | collective-permute-start | bytes 2162696 | tf_op jit(solution)/shard_map/ppermute | solution.py:1438
  383.0 10.7 %copy-start.23 = (bf16[1,128,1024]{2,1,0:T(8,128)(2,1)}, bf16[1,128,1024]{2,1,0:T(8,128)(2,1)S(1)}, u32[]{:S(2)}) copy-start(bf16[1,128,1024]{2,1,0:T(8,128)(2,1)S(1)} %get-tuple-element.184.after_ref.keep_ref) | copy-start | bytes 786436
  383.1 24.7 %collective-permute-start.31 = (bf16[1,128,1024]{2,1,0:T(8,128)(2,1)}, bf16[1,128,1024]{2,1,0:T(8,128)(2,1)}, u32[]{:S(2)}, u32[]{:S(2)}) collective-permute-start(bf16[1,128,1024]{2,1,0:T(8,128)(2,1)} %get-tuple-element.191), channel_id=1, source_target_pairs={{0,2},{1,5},{2,0},{3,7},{4,6},{5,1},{6,4},{7,3},{8,10},{9,13},{10,... | collective-permute-start | bytes 786440 | tf_op jit(solution)/shard_map/ppermute | solution.py:1438
  393.7 17.7 %collective-permute-start.32 = (bf16[3,128,1024]{2,1,0:T(8,128)(2,1)S(1)}, bf16[3,128,1024]{2,1,0:T(8,128)(2,1)S(1)}, u32[]{:S(2)}, u32[]{:S(2)}) collective-permute-start(bf16[3,128,1024]{2,1,0:T(8,128)(2,1)S(1)} %get-tuple-element.193), channel_id=1, source_target_pairs={{0,4},{1,3},{2,6},{3,1},{4,0},{5,7},{6,2},{7,5},{8,12},{9,11},{10,... | collective-permute-start | bytes 2359304 | tf_op jit(solution)/shard_map/ppermute | solution.py:1438
  399.8 9.6 %collective-permute-start.37 = (f32[22656]{0:T(1024)S(1)}, f32[22656]{0:T(1024)S(1)}, u32[]{:S(2)}, u32[]{:S(2)}) collective-permute-start(f32[22656]{0:T(1024)S(1)} %pad_maximum_fusion.3), channel_id=1, source_target_pairs={{0,1},{1,0},{2,3},{3,2},{4,5},{5,4},{6,7},{7,6},{8,9},{9,8},{10,11... | collective-permute-start | bytes 271880 | tf_op jit(solution)/shard_map/ppermute | solution.py:1438
  399.9 18.6 %collective-permute-start.33 = (bf16[2,128,1408]{2,1,0:T(8,128)(2,1)S(1)}, bf16[2,128,1408]{2,1,0:T(8,128)(2,1)S(1)}, u32[]{:S(2)}, u32[]{:S(2)}) collective-permute-start(bf16[2,128,1408]{2,1,0:T(8,128)(2,1)S(1)} %get-tuple-element.195), channel_id=1, source_target_pairs={{0,8},{8,0},{16,24},{24,16},{1,9},{9,1},{17,25},{25,17},{2,10},{10... | collective-permute-start | bytes 2162696 | tf_op jit(solution)/shard_map/ppermute | solution.py:1438
  405.7 13.9 %collective-permute-start.34 = (bf16[1,176,1024]{2,1,0:T(8,128)(2,1)S(1)}, bf16[1,176,1024]{2,1,0:T(8,128)(2,1)S(1)}, u32[]{:S(2)}, u32[]{:S(2)}) collective-permute-start(bf16[1,176,1024]{2,1,0:T(8,128)(2,1)S(1)} %get-tuple-element.196), channel_id=1, source_target_pairs={{0,4},{1,3},{2,6},{3,1},{4,0},{5,7},{6,2},{7,5},{8,12},{9,11},{10,... | collective-permute-start | bytes 1081352 | tf_op jit(solution)/shard_map/ppermute | solution.py:1438
  408.9 14.8 %collective-permute-start.35 = (bf16[1,64,1024]{2,1,0:T(8,128)(2,1)S(1)}, bf16[1,64,1024]{2,1,0:T(8,128)(2,1)S(1)}, u32[]{:S(2)}, u32[]{:S(2)}) collective-permute-start(bf16[1,64,1024]{2,1,0:T(8,128)(2,1)S(1)} %get-tuple-element.197), channel_id=1, source_target_pairs={{0,4},{1,3},{2,6},{3,1},{4,0},{5,7},{6,2},{7,5},{8,12},{9,11},{10,... | collective-permute-start | bytes 393224 | tf_op jit(solution)/shard_map/ppermute | solution.py:1438
  409.4 5.7 %collective-permute-start.38 = (f32[22656]{0:T(1024)S(1)}, f32[22656]{0:T(1024)S(1)}, u32[]{:S(2)}, u32[]{:S(2)}) collective-permute-start(f32[22656]{0:T(1024)S(1)} %fusion.14), channel_id=1, source_target_pairs={{0,2},{1,3},{2,0},{3,1},{4,6},{5,7},{6,4},{7,5},{8,10},{9,11},{10,... | collective-permute-start | bytes 271880 | tf_op jit(solution)/shard_map/ppermute | solution.py:1438
  415.2 6.8 %collective-permute-start.39 = (f32[22656]{0:T(1024)S(1)}, f32[22656]{0:T(1024)S(1)}, u32[]{:S(2)}, u32[]{:S(2)}) collective-permute-start(f32[22656]{0:T(1024)S(1)} %add.166), channel_id=1, source_target_pairs={{0,4},{1,5},{2,6},{3,7},{4,0},{5,1},{6,2},{7,3},{8,12},{9,13},{10,... | collective-permute-start | bytes 271880 | tf_op jit(solution)/shard_map/ppermute | solution.py:1438
  417.0 14.8 %collective-permute-start.36 = (bf16[3,128,512]{2,1,0:T(8,128)(2,1)S(1)}, bf16[3,128,512]{2,1,0:T(8,128)(2,1)S(1)}, u32[]{:S(2)}, u32[]{:S(2)}) collective-permute-start(bf16[3,128,512]{2,1,0:T(8,128)(2,1)S(1)} %get-tuple-element.198), channel_id=1, source_target_pairs={{0,8},{8,0},{16,24},{24,16},{1,9},{9,1},{17,25},{25,17},{2,10},{10... | collective-permute-start | bytes 1179656 | tf_op jit(solution)/shard_map/ppermute | solution.py:1438
  423.0 6.0 %collective-permute-start.40 = (f32[1416]{0:T(1024)S(1)}, f32[1416]{0:T(1024)S(1)}, u32[]{:S(2)}, u32[]{:S(2)}) collective-permute-start(f32[1416]{0:T(1024)S(1)} %pad_maximum_fusion.5), channel_id=1, source_target_pairs={{0,8},{8,0},{16,24},{24,16},{1,9},{9,1},{17,25},{25,17},{2,10},{10... | collective-permute-start | bytes 17000 | tf_op jit(solution)/shard_map/ppermute | solution.py:1438
  (32 other events, 80.4 us)
